TPU v7x, 128 devices: a whole 4x4x4 slice. The times are simulated.
128 devices in a mesh: enc: 4 (over x), seq: 16 (over z, y), tp: 2 (over core).
Axes of the slice: x: 4, y: 4, z: 4, core: 2. Of those that a mesh axis runs over, the one named last changes fastest.
Arguments:
- audio_rows: bfloat16 [8192, 1280], P(('enc', 'seq')), may hold values from -6 to 6
- vision_rows: bfloat16 [4096, 5120], P(('enc', 'seq')), may hold values from -6 to 6
- audio_weight: bfloat16 [1280, 3584], P('seq', 'tp'), may hold values from -0.15625 to 0.15625
- vision_weight: bfloat16 [1280, 4, 3584], P('seq', None, 'tp'), may hold values from -0.078125 to 0.078125
- text_rows: bfloat16 [16384, 3584], P(('enc', 'seq'), 'tp'), may hold values from -6 to 6
- row_target: int32 [64, 192], replicated, may hold values from 0 to 16383, as said below
- segment_ids: int32 [64, 256], P(('enc', 'seq')), may hold values from 0 to 3, never falling along the last dimension, each value on 1 to 128 neighbouring positions
- norm_gain: float32 [3584], replicated, may hold values from 0.1 to 1.9
- qkv_weight: bfloat16 [3584, 2304], P(None, 'tp'), may hold values from -1 to 1
- attn_grad: bfloat16 [16384, 1792], P(('enc', 'seq'), 'tp'), may hold values from -6 to 6
Outputs:
- audio_grad: bfloat16 [8192, 3584], P(('enc', 'seq'), 'tp')
- vision_grad: bfloat16 [4096, 3584], P(('enc', 'seq'), 'tp')
Inputs may be any that keep to these rules, and one draw needn't show every extreme that they name: `row_target`: no two entries are equal. Every sample (positions s * 256 to (s + 1) * 256 - 1) receives exactly 192 encoder rows. The rows of one sending device name the positions of one sample between 2 and 4 times; every sending device sends exactly 4 rows to some sample, and every sample receives exactly 4 rows from some sending device.
All inputs are finite; a program needn't handle non-finite values.
Results may differ from a plain program's by a relative error of at most 0.018.
Values may be sent and summed in bfloat16 or wider, within the bound.
No kernel may reach another device: no remote copies, remote signals or barrier semaphores. Data moves between devices by JAX's collectives and lax.ppermute only.
A program may use at most 128 MiB of HBM per device.

v0:
```python
import jax
import jax.numpy as jnp
from jax import lax
from jax.sharding import PartitionSpec as P

HEADS = 14
KV_HEADS = 2
HEAD_DIM = 128


epsilon = 1e-06


def group_grads(query_rows, key_rows, value_rows, upstream, allowed, score_scale):
    scores = (
        jnp.einsum("qhd,kd->hqk", query_rows, key_rows, preferred_element_type=jnp.float32)
        * score_scale
    )
    scores = jnp.where(allowed[None], scores, -1e30)
    row_max = jnp.max(scores, axis=2, keepdims=True)
    weights = jnp.exp(scores - row_max)
    weights = weights / jnp.sum(weights, axis=2, keepdims=True)
    probs_low = weights.astype(jnp.bfloat16)
    weight_grad = jnp.einsum(
        "qhd,kd->hqk", upstream, value_rows, preferred_element_type=jnp.float32
    )
    row_delta = jnp.sum(weight_grad * weights, axis=2, keepdims=True)
    score_grad = (weights * (weight_grad - row_delta) * score_scale).astype(jnp.bfloat16)
    grad_query = jnp.einsum("hqk,kd->qhd", score_grad, key_rows, preferred_element_type=jnp.float32)
    grad_key = jnp.einsum("hqk,qhd->kd", score_grad, query_rows, preferred_element_type=jnp.float32)
    grad_value = jnp.einsum("hqk,qhd->kd", probs_low, upstream, preferred_element_type=jnp.float32)
    return (grad_query, grad_key, grad_value)


def head_grads(scaled, upstream, segments, heads_per_group, head_size):
    length = scaled.shape[0]
    groups = scaled.shape[1] // ((heads_per_group + 2) * head_size)
    blocks = scaled.reshape(length, groups, heads_per_group + 2, head_size)
    query_rows = jnp.moveaxis(blocks[:, :, :heads_per_group], 1, 0)
    key_rows = jnp.moveaxis(blocks[:, :, heads_per_group], 1, 0)
    value_rows = jnp.moveaxis(blocks[:, :, heads_per_group + 1], 1, 0)
    upstream_rows = jnp.moveaxis(upstream.reshape(length, groups, heads_per_group, head_size), 1, 0)
    positions = jnp.arange(length)
    allowed = (segments[:, None] == segments[None, :]) & (positions[None, :] <= positions[:, None])
    score_scale = head_size ** (-0.5)

    def per_group(group_items):
        grad_query, grad_key, grad_value = group_grads(
            group_items[0], group_items[1], group_items[2], group_items[3], allowed, score_scale
        )
        return jnp.concatenate([grad_query, grad_key[:, None], grad_value[:, None]], axis=1)

    stacked = lax.map(per_group, (query_rows, key_rows, value_rows, upstream_rows))
    return jnp.moveaxis(stacked, 0, 1).reshape(length, groups * (heads_per_group + 2) * head_size)


def local(
    audio_rows,
    vision_rows,
    audio_weight,
    vision_weight,
    text_rows,
    row_target,
    segment_ids,
    norm_gain,
    qkv_weight,
    attn_grad,
):
    tp_count = lax.axis_size("tp")
    tp_rank = lax.axis_index("tp")
    seq_count = lax.axis_size("seq")
    self_index = lax.axis_index("enc") * seq_count + lax.axis_index("seq")
    senders = row_target.shape[0]
    enc_rows = row_target.shape[1]
    slab_cols = text_rows.shape[1]
    model_width = slab_cols * tp_count
    length = text_rows.shape[0]
    audio_count = audio_rows.shape[0]
    merge_factor = vision_weight.shape[1]
    per_pair = enc_rows // senders
    capacity = per_pair + per_pair // 2
    audio_piece = lax.all_gather(audio_weight, "seq", axis=0, tiled=True)
    vision_piece = lax.all_gather(vision_weight, "seq", axis=0, tiled=True)
    piece_rows = audio_piece.shape[0]
    audio_total = jnp.dot(audio_rows, audio_piece, preferred_element_type=jnp.float32)
    vision_total = jnp.dot(
        vision_rows,
        vision_piece.reshape(piece_rows * merge_factor, slab_cols),
        preferred_element_type=jnp.float32,
    )
    encoded = jnp.concatenate(
        [audio_total.astype(jnp.bfloat16), vision_total.astype(jnp.bfloat16)], axis=0
    )
    own_target = lax.dynamic_index_in_dim(row_target, self_index, 0, keepdims=False)
    own_dest = own_target // length
    dest_hot = (own_dest[:, None] == jnp.arange(senders)[None, :]).astype(jnp.int32)
    own_slot = jnp.sum((jnp.cumsum(dest_hot, axis=0) - 1) * dest_hot, axis=1)
    own_cell = own_dest * capacity + own_slot
    selector = (own_cell[:, None] == jnp.arange(senders * capacity)[None, :]).astype(jnp.bfloat16)
    outgoing = lax.dot_general(
        selector, encoded, (((0,), (0,)), ((), ())), preferred_element_type=jnp.float32
    )
    outgoing = outgoing.astype(jnp.bfloat16).reshape(senders, capacity, slab_cols)
    mine_mask = (row_target // length == self_index).astype(jnp.int32)
    slot_all = jnp.cumsum(mine_mask, axis=1) - 1
    local_pos = row_target % length
    slot_hot = (slot_all[:, :, None] == jnp.arange(capacity)[None, None, :]) & (
        mine_mask[:, :, None] == 1
    )
    incoming_pos = jnp.sum(jnp.where(slot_hot, local_pos[:, :, None] + 1, 0), axis=1) - 1
    placement = (jnp.arange(length)[:, None] == incoming_pos.reshape(1, senders * capacity)).astype(
        jnp.bfloat16
    )
    arrived = lax.all_to_all(outgoing, ("enc", "seq"), split_axis=0, concat_axis=0, tiled=True)
    arrived = arrived.reshape(senders * capacity, slab_cols)
    placed = jnp.dot(placement, arrived, preferred_element_type=jnp.float32).astype(jnp.bfloat16)
    filled = jnp.max(placement, axis=1) > 0
    row_slab = jnp.where(filled[:, None], placed, text_rows)
    full_rows = lax.all_gather(row_slab, "tp", axis=1, tiled=True)
    inv_rms = lax.rsqrt(
        jnp.mean(
            full_rows.astype(jnp.float32) * full_rows.astype(jnp.float32), axis=1, keepdims=True
        )
        + epsilon
    )
    normed = (full_rows.astype(jnp.float32) * norm_gain).astype(jnp.bfloat16)
    unscaled = jnp.dot(normed, qkv_weight, preferred_element_type=jnp.float32)
    scaled = (unscaled * inv_rms).astype(jnp.bfloat16)
    grads = head_grads(scaled, attn_grad, segment_ids[0], HEADS // KV_HEADS, HEAD_DIM)
    scaled_grad = (grads * inv_rms).astype(jnp.bfloat16)
    row_part = jnp.sum(grads * unscaled, axis=1, keepdims=True)
    partial_proj = lax.dot_general(
        scaled_grad, qkv_weight, (((1,), (1,)), ((), ())), preferred_element_type=jnp.float32
    )
    spread_stat = jnp.broadcast_to(row_part, (length, tp_count))
    back_slab, stat_total = (
        lax.psum_scatter(
            partial_proj.astype(jnp.bfloat16), "tp", scatter_dimension=1, tiled=True
        ).astype(jnp.float32),
        lax.psum_scatter(
            spread_stat.astype(jnp.bfloat16), "tp", scatter_dimension=1, tiled=True
        ).astype(jnp.float32),
    )
    gain_slab = lax.dynamic_slice_in_dim(norm_gain, tp_rank * slab_cols, slab_cols, 0)
    row_grads = (
        gain_slab * back_slab
        - row_slab.astype(jnp.float32) * (inv_rms**3 / model_width) * stat_total
    )
    row_grads = row_grads.astype(jnp.bfloat16)
    outgoing_grads = lax.dot_general(
        placement, row_grads, (((0,), (0,)), ((), ())), preferred_element_type=jnp.float32
    )
    outgoing_grads = outgoing_grads.astype(jnp.bfloat16).reshape(senders, capacity, slab_cols)
    returned = lax.all_to_all(
        outgoing_grads, ("enc", "seq"), split_axis=0, concat_axis=0, tiled=True
    )
    returned = returned.reshape(senders * capacity, slab_cols)
    own_grads = jnp.dot(selector, returned, preferred_element_type=jnp.float32).astype(jnp.bfloat16)
    return (own_grads[:audio_count], own_grads[audio_count:])


def solution(mesh):
    in_specs = (
        P(("enc", "seq"), None),
        P(("enc", "seq"), None),
        P("seq", "tp"),
        P("seq", None, "tp"),
        P(("enc", "seq"), "tp"),
        P(),
        P(("enc", "seq"), None),
        P(),
        P(None, "tp"),
        P(("enc", "seq"), "tp"),
    )
    out_specs = (P(("enc", "seq"), "tp"), P(("enc", "seq"), "tp"))
    return jax.shard_map(local, mesh=mesh, in_specs=in_specs, out_specs=out_specs, check_vma=False)
```

profile of v0, /device:TPU:0, one launch (start us, length us, event | category | flops | bytes accessed | tf_op | source)
XLA Modules:
  0.0 346.9 jit_solution(18337905429011846856)
XLA Ops:
  7.2 0.0 copy-start
  7.2 0.0 all-gather.4.cloned.1.call-start
  7.2 0.7 all-gather.4.cloned.1.call-update
  7.9 0.0 all-gather.6.cloned.1.call-start
  8.0 0.7 all-gather.6.cloned.1.call-update
  8.7 0.7 constant_dynamic-slice_fusion
  9.4 0.6 reduce-window.14
  10.0 0.2 slice_reduce_fusion.1
  10.3 0.9 broadcast_compare_fusion
  11.2 0.6 reduce-window.16
  11.8 0.2 slice_reduce_fusion
  12.0 0.1 bitcast_bitcast_fusion
  12.2 0.1 copy_bitcast_fusion
  12.3 53.9 %all-gather.4.cloned.1.call-done = bf16[1280,1792]{1,0:T(8,128)(2,1)} async-done(((bf16[80,1792]{1,0:T(8,128)(2,1)}), bf16[1280,1792]{1,0:T(8,128)(2,1)}) %all-gather.4.cloned.1.call-update) | async-done | bytes 4587536 | tf_op jit(solution)/shard_map/all_gather | solution.py:82
  66.2 3.1 convolution_convert_fusion.5
  69.3 118.1 %all-gather.6.cloned.1.call-done = bf16[1280,4,1792]{2,1,0:T(4,128)(2,1)} async-done(((bf16[80,4,1792]{2,1,0:T(4,128)(2,1)}), bf16[1280,4,1792]{2,1,0:T(4,128)(2,1)}) %all-gather.6.cloned.1.call-update) | async-done | bytes 18350096 | tf_op jit(solution)/shard_map/all_gather | solution.py:83
  187.4 28.7 %reshape.174 = bf16[5120,1792]{1,0:T(8,128)(2,1)} reshape(bf16[1280,4,1792]{2,1,0:T(4,128)(2,1)} %all-gather.6.cloned.1.call-done) | data formatting | bytes 36700160 | tf_op jit(solution)/shard_map/reshape | solution.py:88
  216.1 9.5 %convolution_convert_fusion.6 = bf16[64,1792]{1,0:T(8,128)(2,1)S(1)} fusion(bf16[64,5120]{1,0:T(8,128)(2,1)S(1)} %copy-done, bf16[5120,1792]{1,0:T(8,128)(2,1)} %reshape.174), kind=kOutput, calls=%fused_computation.13 | convolution fusion | flops 1174519808 | bytes 19234816 | tf_op jit(solution)/shard_map/dot_general | solution.py:86
  225.6 0.6 convolution_convert_fusion.3
  226.1 0.0 copy-start.7
  226.1 1.1 reshape.175
  227.3 8.8 %all-to-all-start = ((bf16[64,4,1792]{2,1,0:T(4,128)(2,1)}), bf16[64,4,1792]{2,1,0:T(4,128)(2,1)S(1)}, u32[]{:S(2)}, u32[]{:S(2)}) async-start(bf16[64,4,1792]{2,1,0:T(4,128)(2,1)} %reshape.175), calls=%async_computation | async-start | bytes 1835008 | tf_op jit(solution)/shard_map/all_to_all | solution.py:114
  236.1 0.0 all-gather.8.cloned.1.call-start
  236.2 0.2 select_reduce_fusion
  236.3 0.1 copy.62
  236.4 0.1 sub.58
  236.5 0.1 fusion.30
  236.7 16.6 %all-to-all-done = bf16[64,4,1792]{2,1,0:T(4,128)(2,1)S(1)} async-done(((bf16[64,4,1792]{2,1,0:T(4,128)(2,1)}), bf16[64,4,1792]{2,1,0:T(4,128)(2,1)S(1)}, u32[]{:S(2)}, u32[]{:S(2)}) %all-to-all-start) | async-done | bytes 917536 | tf_op jit(solution)/shard_map/all_to_all | solution.py:114
  253.3 0.2 reshape.176
  253.5 0.0 copy-start.5
  253.5 0.0 copy-start.8
  253.5 1.3 fusion.4
  254.8 0.0 all-gather.8.cloned.1.call-update
  254.9 0.2 reduce-scatter.2.cloned.1.call-start
  255.1 0.2 copy.67
  255.3 0.1 fusion.29
  255.4 8.2 %all-gather.8.cloned.1.call-done = bf16[256,3584]{1,0:T(8,128)(2,1)} async-done(((bf16[256,1792]{1,0:T(8,128)(2,1)}), bf16[256,3584]{1,0:T(8,128)(2,1)}) %all-gather.8.cloned.1.call-update) | async-done | bytes 1835024 | tf_op jit(solution)/shard_map/all_gather | solution.py:119
  263.7 2.1 fusion.3
  265.8 6.9 %multiply_convert_fusion.1 = (bf16[256,1152]{1,0:T(8,128)(2,1)S(1)}, f32[256,1152]{1,0:T(8,128)}) fusion(f32[256]{0:T(256)S(1)} %get-tuple-element.19, bf16[3584,1152]{1,0:T(8,128)(2,1)} %param.18, bf16[256,3584]{1,0:T(8,128)(2,1)S(1)} %copy-done.3, f32[3584]{0:T(1024)S(1)} %copy-done.9), kind=kOutput, calls=%fused_computation.29 | convolution fusion | flops 2117271552 | bytes 11877376 | tf_op jit(solution)/shard_map/dot_general | solution.py:127
  272.7 0.2 copy.63
  272.9 2.0 fusion.52
  274.9 0.4 fusion.37
  275.3 1.1 copy-done.11
  276.4 0.5 convolution_bitcast_fusion.1
  276.9 2.8 convolution_bitcast_fusion.2
  279.7 3.7 %convolution_bitcast_fusion = f32[256,7,128]{0,2,1:T(8,128)} fusion(f32[256,256,7]{1,0,2:T(8,128)S(1)} %fusion.37, bf16[256,1,9,128]{0,3,2,1:T(8,128)(2,1)S(1)} %bitcast.114, f32[7,256,256]{1,2,0:T(8,128)} %get-tuple-element.30, f32[7,256]{1,0:T(8,128)S(1)} %get-tuple-element.29), kind=kOutput, calls=%fused_computation.25 | convolution fusion | flops 120653824 | bytes 8339456 | tf_op jit(solution)/shard_map/while/body/eval_jaxpr/hqk,kd->qhd/dot_general | solution.py:29
  283.4 1.3 pad_maximum_fusion
  284.7 0.4 copy.74
  285.0 7.2 %convolution_convert_fusion = bf16[256,3584]{1,0:T(8,128)(2,1)} fusion(bf16[3584,1152]{1,0:T(8,128)(2,1)} %param.18, f32[256,1152]{1,0:T(8,128)S(1)} %copy.74, f32[256]{0:T(256)S(1)} %get-tuple-element.19), kind=kOutput, calls=%fused_computation.2 | convolution fusion | flops 2115436544 | bytes 11273216 | tf_op jit(solution)/shard_map/dot_general | solution.py:132
  292.2 0.0 reduce-scatter.2.cloned.1.call-update
  292.3 0.1 dynamic_slice.18
  292.3 0.5 copy-done.10
  292.9 0.6 dynamic-slice
  293.5 1.5 multiply_reduce_fusion
  294.9 2.5 all-reduce.2
  297.4 0.6 dynamic-slice_convert_fusion
  298.1 7.6 %reduce-scatter.2.cloned.1.call-done = bf16[256,1792]{1,0:T(8,128)(2,1)} async-done(((bf16[256,3584]{1,0:T(8,128)(2,1)}), bf16[256,1792]{1,0:T(8,128)(2,1)}) %reduce-scatter.2.cloned.1.call-update) | async-done | bytes 917520 | tf_op jit(solution)/shard_map/reduce_scatter | solution.py:137
  305.7 2.8 convolution_convert_fusion.1
  308.5 1.8 reshape.178
  310.2 28.0 %all_to_all.10 = bf16[64,4,1792]{2,1,0:T(4,128)(2,1)S(1)} all-to-all(bf16[64,4,1792]{2,1,0:T(4,128)(2,1)S(1)} %reshape.178), channel_id=1, replica_groups=mesh['enc'=4,'seq'=16,'tp'=2] {'enc','seq'}, dimensions={0} | all-to-all | bytes 1835008 | tf_op jit(solution)/shard_map/all_to_all | solution.py:154
  338.3 0.2 reshape.179
  338.5 0.4 convolution_convert_fusion.4
  338.9 0.8 slice.51
  339.7 0.7 slice.52
  (33 shorter events, 0.3 us)
Async XLA Ops:
  7.2 208.9 %copy-start = (bf16[64,5120]{1,0:T(8,128)(2,1)S(1)}, bf16[64,5120]{1,0:T(8,128)(2,1)}, u32[]{:S(2)}) copy-start(bf16[64,5120]{1,0:T(8,128)(2,1)} %param.11) | copy-start | bytes 1966084
  7.2 59.0 %copy-start.6 = (bf16[128,1280]{1,0:T(8,128)(2,1)S(1)}, bf16[128,1280]{1,0:T(8,128)(2,1)}, u32[]{:S(2)}) copy-start(bf16[128,1280]{1,0:T(8,128)(2,1)} %param.10) | copy-start | bytes 983044
  7.2 59.0 %all-gather.4.cloned.1.call-start = ((), (), s32[]{:S(2)}) async-start(), calls=%async_computation.3 | async-start | bytes 4874240 | tf_op jit(solution)/shard_map/all_gather | solution.py:82
  7.9 179.5 %all-gather.6.cloned.1.call-start = ((), (), s32[]{:S(2)}) async-start(), calls=%async_computation.4 | async-start | bytes 19496960 | tf_op jit(solution)/shard_map/all_gather | solution.py:83
  226.1 10.0 %copy-start.7 = (s32[64,192]{1,0:T(8,128)S(1)}, s32[64,192]{1,0:T(8,128)}, u32[]{:S(2)}) copy-start(s32[64,192]{1,0:T(8,128)} %param.15) | copy-start | bytes 147460
  227.3 26.2 %copy-start.4 = (bf16[256,1792]{1,0:T(8,128)(2,1)S(1)}, bf16[256,1792]{1,0:T(8,128)(2,1)}, u32[]{:S(2)}) copy-start(bf16[256,1792]{1,0:T(8,128)(2,1)} %param.14) | copy-start | bytes 2752516
  227.3 26.0 %all-to-all-start = ((bf16[64,4,1792]{2,1,0:T(4,128)(2,1)}), bf16[64,4,1792]{2,1,0:T(4,128)(2,1)S(1)}, u32[]{:S(2)}, u32[]{:S(2)}) async-start(bf16[64,4,1792]{2,1,0:T(4,128)(2,1)} %reshape.175), calls=%async_computation | async-start | bytes 1835008 | tf_op jit(solution)/shard_map/all_to_all | solution.py:114
  236.1 27.6 %all-gather.8.cloned.1.call-start = ((), (), s32[]{:S(2)}) async-start(), calls=%async_computation.5 | async-start | bytes 2752512 | tf_op jit(solution)/shard_map/all_gather | solution.py:119
  253.5 1.6 copy-start.5
  253.5 1.8 copy-start.8
  254.8 10.9 %copy-start.9 = (f32[3584]{0:T(1024)S(1)}, f32[3584]{0:T(1024)}, u32[]{:S(2)}) copy-start(f32[3584]{0:T(1024)} %param.17) | copy-start | bytes 43012
  254.9 50.8 %reduce-scatter.2.cloned.1.call-start = ((), (), s32[]{:S(2)}) async-start(), calls=%async_computation.6 | async-start | bytes 2752512 | tf_op jit(solution)/shard_map/reduce_scatter | solution.py:137
  263.7 2.1 copy-start.3
  274.9 1.5 copy-start.11
  292.2 0.7 copy-start.10
  292.2 13.4 %copy-start.2 = (bf16[256,1792]{1,0:T(8,128)(2,1)S(1)}, bf16[256,1792]{1,0:T(8,128)(2,1)}, u32[]{:S(2)}) copy-start(bf16[256,1792]{1,0:T(8,128)(2,1)} %fusion.4) | copy-start | bytes 2752516
  338.3 2.1 copy-start.1
Sparse Core Ops, SparseCore 0:
  10.2 55.9 all-gather.3
  68.3 119.0 all-gather.5
  255.0 8.6 all-gather.7
  292.4 13.2 reduce-scatter.1
where the time goes:
time: 348 us; the launch traced here: 347 us
  waiting for transfers between devices  206 us (59%)
  matrix products  41.1 us (12%)
  local copies, waits for them, and re-layouts  38 us (11%)
  blocking collectives  30.5 us (9%)
  between operations  14 us (4%)
  starting transfers between devices  9.12 us (3%)
  other arithmetic  8.36 us (2%)
    all_gather x1, waiting for transfers between devices, local(): vision_piece = lax.all_gather(vision_weight, 'seq', axis=0, tiled=True)  118 us
    all_gather x1, waiting for transfers between devices, local(): audio_piece = lax.all_gather(audio_weight, 'seq', axis=0, tiled=True)  53.9 us
    reshape x1, local copies, waits for them, and re-layouts, local(): vision_piece.reshape(piece_rows * merge_factor, slab_cols)  28.7 us
    all_to_all x1, blocking collectives, local(): lax.all_to_all(outgoing_grads, ('enc', 'seq'), split_axis=0, concat_axis=...  28 us
    all_to_all x1, waiting for transfers between devices, local(): lax.all_to_all(outgoing, ('enc', 'seq'), split_axis=0, concat_axis=0, til...  16.6 us
    dot_general x1, matrix products, local(): jnp.dot(vision_rows, vision_piece.reshape(piece_rows * merge_factor, slab...  9.48 us
    all_to_all x1, starting transfers between devices, local(): lax.all_to_all(outgoing, ('enc', 'seq'), split_axis=0, concat_axis=0, til...  8.78 us
    all_gather x1, waiting for transfers between devices, local(): full_rows = lax.all_gather(row_slab, 'tp', axis=1, tiled=True)  8.23 us
  transfers between devices with their start and end apart: 5, of which 5 were waited for; matrix products, arithmetic and copies ran while one was open for 3% of the time, Pallas kernels for 0%

commit v1 on v0

v1 whole, which is shorter than its diff:
```python
import jax
import jax.numpy as jnp
from jax import lax
from jax.sharding import PartitionSpec as P

HEADS = 14
KV_HEADS = 2
HEAD_DIM = 128

epsilon = 1e-06


def group_grads(query_rows, key_rows, value_rows, upstream, allowed, score_scale):
    scores = (
        jnp.einsum("qhd,kd->hqk", query_rows, key_rows, preferred_element_type=jnp.float32)
        * score_scale
    )
    scores = jnp.where(allowed[None], scores, -1e30)
    row_max = jnp.max(scores, axis=2, keepdims=True)
    weights = jnp.exp(scores - row_max)
    weights = weights / jnp.sum(weights, axis=2, keepdims=True)
    probs_low = weights.astype(jnp.bfloat16)
    weight_grad = jnp.einsum(
        "qhd,kd->hqk", upstream, value_rows, preferred_element_type=jnp.float32
    )
    row_delta = jnp.sum(weight_grad * weights, axis=2, keepdims=True)
    score_grad = (weights * (weight_grad - row_delta) * score_scale).astype(jnp.bfloat16)
    grad_query = jnp.einsum("hqk,kd->qhd", score_grad, key_rows, preferred_element_type=jnp.float32)
    grad_key = jnp.einsum("hqk,qhd->kd", score_grad, query_rows, preferred_element_type=jnp.float32)
    grad_value = jnp.einsum("hqk,qhd->kd", probs_low, upstream, preferred_element_type=jnp.float32)
    return (grad_query, grad_key, grad_value)


def head_grads(scaled, upstream, segments, heads_per_group, head_size):
    length = scaled.shape[0]
    blocks = scaled.reshape(length, heads_per_group + 2, head_size)
    positions = jnp.arange(length)
    allowed = (segments[:, None] == segments[None, :]) & (positions[None, :] <= positions[:, None])
    grad_query, grad_key, grad_value = group_grads(
        blocks[:, :heads_per_group],
        blocks[:, heads_per_group],
        blocks[:, heads_per_group + 1],
        upstream.reshape(length, heads_per_group, head_size),
        allowed,
        head_size ** (-0.5),
    )
    stacked = jnp.concatenate([grad_query, grad_key[:, None], grad_value[:, None]], axis=1)
    return stacked.reshape(length, (heads_per_group + 2) * head_size)


def swap(x):
    return lax.ppermute(x, "tp", [(0, 1), (1, 0)])


def ranks(dest):
    count = dest.shape[1]
    same = dest[:, :, None] == dest[:, None, :]
    earlier = jnp.arange(count)[None, :] < jnp.arange(count)[:, None]
    return jnp.sum((same & earlier[None]).astype(jnp.int32), axis=2)


def local(
    audio_rows,
    vision_rows,
    audio_weight,
    vision_weight,
    text_rows,
    row_target,
    segment_ids,
    norm_gain,
    qkv_weight,
    attn_grad,
):
    bf16, f32 = jnp.bfloat16, jnp.float32
    t = lax.axis_index("tp")
    e = lax.axis_index("enc")
    j = lax.axis_index("seq")
    n_enc = 4
    n_seq = 16
    self_index = e * n_seq + j
    senders, enc_rows = row_target.shape
    length, slab = text_rows.shape
    audio_count, audio_width = audio_rows.shape
    vision_count = vision_rows.shape[0]
    merge = vision_weight.shape[1]
    k_rows = audio_weight.shape[0]
    cap = 4
    wide = slab // 128 // n_enc * 128
    tail = slab // n_enc - wide

    def columns(w):
        w = w.reshape(-1, slab)
        main = lax.dynamic_slice_in_dim(w, e * wide, wide, 1)
        last = lax.dynamic_slice_in_dim(w, n_enc * wide + e * tail, tail, 1)
        return jnp.concatenate([main, last], axis=1)

    shard = jnp.concatenate([columns(audio_weight), columns(vision_weight)], axis=0)
    gathered = lax.all_gather(shard, "seq", axis=0, tiled=False)
    w_audio = gathered[:, :k_rows].reshape(audio_width, wide + tail)
    w_vision = gathered[:, k_rows:].reshape(audio_width * merge, wide + tail)

    ah, vh = audio_count // 2, vision_count // 2
    audio_half = lax.dynamic_slice_in_dim(audio_rows, t * ah, ah, 0)
    vision_half = lax.dynamic_slice_in_dim(vision_rows, t * vh, vh, 0)
    packed = jnp.concatenate(
        [audio_half] + [vision_half[:, i * audio_width : (i + 1) * audio_width] for i in range(merge)],
        axis=0,
    )
    own = [packed] + [
        lax.ppermute(packed, "enc", [(i, (i + k) % n_enc) for i in range(n_enc)])
        for k in range(1, n_enc)
    ]
    other = [swap(b) for b in own]
    blocks = jnp.stack(own + other)
    x_audio = blocks[:, :ah].reshape(2 * n_enc * ah, audio_width)
    x_vision = jnp.concatenate(
        [
            blocks[:, ah + i * vh : ah + (i + 1) * vh].reshape(2 * n_enc * vh, audio_width)
            for i in range(merge)
        ],
        axis=1,
    )
    audio_proj = jnp.dot(x_audio, w_audio, preferred_element_type=f32).astype(bf16)
    vision_proj = jnp.dot(x_vision, w_vision, preferred_element_type=f32).astype(bf16)
    encoded = jnp.concatenate([audio_proj, vision_proj], axis=0)

    order = (e - jnp.arange(n_enc)) % n_enc
    line = row_target.reshape(n_enc, n_seq, enc_rows)[:, j]
    line_dest = line // length
    line_slot = line_dest * (n_enc * cap) + jnp.arange(n_enc)[:, None] * cap + ranks(line_dest)
    line_slot = line_slot[order]
    a_slot = line_slot[:, :audio_count].reshape(n_enc, 2, ah)
    v_slot = line_slot[:, audio_count:].reshape(n_enc, 2, vh)
    halves = jnp.stack([t, 1 - t])
    a_slot = jnp.moveaxis(a_slot, 1, 0)[halves].reshape(-1)
    v_slot = jnp.moveaxis(v_slot, 1, 0)[halves].reshape(-1)
    row_slot = jnp.concatenate([a_slot, v_slot])
    selector = (jnp.arange(senders * n_enc * cap)[:, None] == row_slot[None, :]).astype(bf16)
    outgoing = jnp.dot(selector, encoded, preferred_element_type=f32).astype(bf16)
    outgoing = outgoing.reshape(senders, n_enc * cap, wide + tail)

    dest = row_target // length
    mine = (dest == self_index).astype(jnp.int32)
    rank_all = jnp.cumsum(mine, axis=1) - 1
    hot = (rank_all[:, :, None] == jnp.arange(cap)[None, None, :]) & (mine[:, :, None] == 1)
    incoming = jnp.sum(jnp.where(hot, (row_target % length)[:, :, None] + 1, 0), axis=1) - 1
    by_line = incoming.reshape(n_enc, n_seq, cap).transpose(1, 0, 2).reshape(1, senders * cap)
    placement = (jnp.arange(length)[:, None] == by_line).astype(bf16)
    filled = jnp.max(placement, axis=1) > 0

    arrived = lax.all_to_all(outgoing, ("enc", "seq"), split_axis=0, concat_axis=0, tiled=True)
    arrived = arrived.reshape(n_enc, senders * cap, wide + tail)
    placed = jnp.einsum("ps,esc->epc", placement, arrived, preferred_element_type=f32).astype(bf16)
    placed = jnp.concatenate(
        [placed[i, :, :wide] for i in range(n_enc)] + [placed[i, :, wide:] for i in range(n_enc)],
        axis=1,
    )
    row_slab = jnp.where(filled[:, None], placed, text_rows)

    other_slab = swap(row_slab)
    full_rows = jnp.concatenate(
        [jnp.where(t == 0, row_slab, other_slab), jnp.where(t == 0, other_slab, row_slab)], axis=1
    )
    model_width = full_rows.shape[1]
    inv_rms = lax.rsqrt(
        jnp.mean(full_rows.astype(f32) * full_rows.astype(f32), axis=1, keepdims=True) + epsilon
    )
    normed = (full_rows.astype(f32) * norm_gain).astype(bf16)
    unscaled = jnp.dot(normed, qkv_weight, preferred_element_type=f32)
    scaled = (unscaled * inv_rms).astype(bf16)
    grads = head_grads(scaled, attn_grad, segment_ids[0], HEADS // KV_HEADS, HEAD_DIM)
    scaled_grad = (grads * inv_rms).astype(bf16)
    row_part = jnp.sum(grads * unscaled, axis=1, keepdims=True)
    partial_proj = lax.dot_general(
        scaled_grad, qkv_weight, (((1,), (1,)), ((), ())), preferred_element_type=f32
    )
    low, high = partial_proj[:, :slab], partial_proj[:, slab:]
    keep = jnp.where(t == 0, low, high)
    give = jnp.where(t == 0, high, low).astype(bf16)
    back = keep + swap(give).astype(f32)
    stat = row_part + swap(row_part)
    gain_slab = lax.dynamic_slice_in_dim(norm_gain, t * slab, slab, 0)
    row_grads = gain_slab * back - row_slab.astype(f32) * (inv_rms**3 / model_width) * stat
    row_grads = row_grads.astype(bf16)

    half = slab // 2
    flat = jnp.arange(senders * 2 * cap)
    slot_pos = incoming.reshape(-1)
    pos8 = jnp.broadcast_to(incoming[:, None, :], (senders, 2, cap)).reshape(-1, 1)
    part8 = (flat // cap % 2)[:, None]
    hits = pos8 == jnp.arange(length)[None, :]
    out8 = jnp.dot(
        (hits & (part8 == 0)).astype(bf16), row_grads[:, :half], preferred_element_type=f32
    ) + jnp.dot((hits & (part8 == 1)).astype(bf16), row_grads[:, half:], preferred_element_type=f32)
    out8 = out8.astype(bf16).reshape(senders, 2 * cap, half)
    returned = lax.all_to_all(out8, ("enc", "seq"), split_axis=0, concat_axis=0, tiled=True)
    returned = returned.reshape(senders * 2 * cap, half)
    own_target = lax.dynamic_index_in_dim(row_target, self_index, 0, keepdims=True)
    own_dest = own_target // length
    own_cell = (own_dest * (2 * cap) + ranks(own_dest)).reshape(-1, 1)
    result = jnp.concatenate(
        [
            jnp.dot(
                (own_cell + h * cap == flat[None, :]).astype(bf16),
                returned,
                preferred_element_type=f32,
            ).astype(bf16)
            for h in range(2)
        ],
        axis=1,
    )
    return (result[:audio_count], result[audio_count:])


def solution(mesh):
    in_specs = (
        P(("enc", "seq"), None),
        P(("enc", "seq"), None),
        P("seq", "tp"),
        P("seq", None, "tp"),
        P(("enc", "seq"), "tp"),
        P(),
        P(("enc", "seq"), None),
        P(),
        P(None, "tp"),
        P(("enc", "seq"), "tp"),
    )
    out_specs = (P(("enc", "seq"), "tp"), P(("enc", "seq"), "tp"))
    return jax.shard_map(local, mesh=mesh, in_specs=in_specs, out_specs=out_specs, check_vma=False)
```

time: 348 us -> 189 us (0.54)
  waiting for transfers between devices: 206 us -> 89.1 us
  blocking collectives: 30.5 us -> 0 us
  local copies, waits for them, and re-layouts: 38 us -> 18.5 us
  starting transfers between devices: 9.12 us -> 20.5 us
  matrix products: 41.1 us -> 33.5 us
    all_gather x3 -> x1, waiting for transfers between devices: 180 us -> 35.3 us  [local(): gathered = lax.all_gather(shard, 'seq', axis=0, tiled=False)]
    all_to_all x1 -> x0, blocking collectives: 28 us -> none  [local(): lax.all_to_all(outgoing_grads, ('enc', 'seq'), split_axis=0, concat_axis=...]
    reshape x5 -> x9, local copies, waits for them, and re-layouts: 32 us -> 4.34 us  [the longest x1 2.36 us: columns(): w = w.reshape(-1, slab)]
    ppermute x0 -> x10, waiting for transfers between devices: none -> 20.5 us  [the longest x3 16.2 us: local(): lax.ppermute(packed, 'enc', [(i, (i + k) % n_enc) for i in range(n_enc)])]
    all_to_all x0 -> x1, waiting for transfers between devices: none -> 15.9 us  [local(): lax.all_to_all(out8, ('enc', 'seq'), split_axis=0, concat_axis=0, tiled=T...]
    dot_general x7 -> x9, matrix products: 24.5 us -> 14.1 us  [the longest x1 7.06 us: local(): unscaled = jnp.dot(normed, qkv_weight, preferred_element_type=f32)]
    reduce_scatter x1 -> x0, waiting for transfers between devices: 7.59 us -> none  [local(): lax.psum_scatter(partial_proj.astype(jnp.bfloat16), 'tp', scatter_dimensi...]
    ppermute x0 -> x10, starting transfers between devices: none -> 7.01 us  [the longest x3 5.81 us: local(): lax.ppermute(packed, 'enc', [(i, (i + k) % n_enc) for i in range(n_enc)])]
  transfers between devices with their start and end apart: 5 -> 13, of which waited for: 5 -> 10; matrix products, arithmetic and copies ran while one was open for 3% -> 5% of each run, Pallas kernels for 0% -> 0%
where the time goes in v1:
time: 189 us; the launch traced here: 188 us
  waiting for transfers between devices  89.1 us (47%)
  matrix products  33.5 us (18%)
  starting transfers between devices  20.5 us (11%)
  local copies, waits for them, and re-layouts  18.5 us (10%)
  between operations  14.7 us (8%)
  other arithmetic  11.6 us (6%)
    all_gather x1, waiting for transfers between devices, local(): gathered = lax.all_gather(shard, 'seq', axis=0, tiled=False)  35.3 us
    all_to_all x1, waiting for transfers between devices, local(): lax.all_to_all(outgoing, ('enc', 'seq'), split_axis=0, concat_axis=0, til...  17.3 us
    ppermute x3, waiting for transfers between devices, local(): lax.ppermute(packed, 'enc', [(i, (i + k) % n_enc) for i in range(n_enc)])  16.2 us
    all_to_all x1, waiting for transfers between devices, local(): lax.all_to_all(out8, ('enc', 'seq'), split_axis=0, concat_axis=0, tiled=T...  15.9 us
    all_to_all x1, starting transfers between devices, local(): lax.all_to_all(outgoing, ('enc', 'seq'), split_axis=0, concat_axis=0, til...  8.61 us
    dot_general x1, matrix products, local(): unscaled = jnp.dot(normed, qkv_weight, preferred_element_type=f32)  7.06 us
    dot_general x1, matrix products, local(): lax.dot_general(scaled_grad, qkv_weight, (((1,), (1,)), ((), ())), prefer...  6.12 us
    ppermute x3, starting transfers between devices, local(): lax.ppermute(packed, 'enc', [(i, (i + k) % n_enc) for i in range(n_enc)])  5.81 us
  transfers between devices with their start and end apart: 13, of which 10 were waited for; matrix products, arithmetic and copies ran while one was open for 5% of the time, Pallas kernels for 0%

profile of v1, /device:TPU:0, one launch (start us, length us, event | category | flops | bytes accessed | tf_op | source)
XLA Modules:
  0.0 187.9 jit_solution(2316045132091038207)
XLA Ops:
  7.3 2.4 %reshape.464 = bf16[320,1792]{1,0:T(8,128)(2,1)S(1)} reshape(bf16[80,4,1792]{2,1,0:T(4,128)(2,1)} %param.13) | data formatting | bytes 2293760 | tf_op jit(solution)/shard_map/reshape | solution.py:92
  9.9 0.8 maximum_maximum_fusion
  10.9 1.6 collective-permute-start
  12.5 2.7 %collective-permute-start.1 = (bf16[192,1280]{1,0:T(8,128)(2,1)S(1)}, bf16[192,1280]{1,0:T(8,128)(2,1)S(1)}, u32[]{:S(2)}, u32[]{:S(2)}) collective-permute-start(bf16[192,1280]{1,0:T(8,128)(2,1)S(1)} %dynamic-slice_dynamic-update-slice_fusion.1), channel_id=1, source_target_pairs={{0,64},{32,96},{64,0},{96,32},{1,65},{33,97},{65,1},{97,33},{2,66}... | collective-permute-start | bytes 1474568 | tf_op jit(solution)/shard_map/ppermute | solution.py:110
  15.3 1.4 collective-permute-start.2
  16.9 0.4 convert_reduce_fusion
  17.3 0.6 gather_fusion
  18.0 0.6 gather_fusion.1
  18.7 0.6 gather_fusion.2
  19.5 0.6 reduce-window.6
  20.1 0.2 slice_reduce_fusion
  20.5 4.5 %collective-permute-done = bf16[192,1280]{1,0:T(8,128)(2,1)S(1)} collective-permute-done((bf16[192,1280]{1,0:T(8,128)(2,1)S(1)}, bf16[192,1280]{1,0:T(8,128)(2,1)S(1)}, u32[]{:S(2)}, u32[]{:S(2)}) %collective-permute-start) | collective-permute-done | bytes 491552 | tf_op jit(solution)/shard_map/ppermute | solution.py:110
  25.1 11.7 %collective-permute-done.1 = bf16[192,1280]{1,0:T(8,128)(2,1)S(1)} collective-permute-done((bf16[192,1280]{1,0:T(8,128)(2,1)S(1)}, bf16[192,1280]{1,0:T(8,128)(2,1)S(1)}, u32[]{:S(2)}, u32[]{:S(2)}) %collective-permute-start.1) | collective-permute-done | bytes 491552 | tf_op jit(solution)/shard_map/ppermute | solution.py:110
  36.8 0.6 collective-permute-start.6
  37.5 1.1 collective-permute-done.5
  38.6 0.7 collective-permute-done.6
  39.4 1.2 fusion.106
  40.7 35.3 %all-gather.3.cloned.1.call-done = bf16[6400,448]{1,0:T(8,128)(2,1)} async-done(((bf16[400,448]{1,0:T(8,128)(2,1)}), bf16[6400,448]{1,0:T(8,128)(2,1)}) %all-gather.3.cloned.1.call-update) | async-done | bytes 5734416 | tf_op jit(solution)/shard_map/all_gather | solution.py:98
  75.9 1.4 slice.143
  77.3 3.0 %slice.148 = bf16[16,320,448]{2,1,0:T(8,128)(2,1)S(1)} slice(bf16[16,400,448]{2,1,0:T(8,128)(2,1)} %bitcast.188), slice={[0:16], [80:400], [0:448]} | slice | bytes 9175040 | tf_op jit(solution)/shard_map/slice | solution.py:100
  80.4 0.8 convolution_convert_fusion.1
  81.2 0.3 copy-done.6
  81.4 0.2 copy-done.7
  81.6 2.1 %fusion.24 = bf16[256,448]{0,1:T(8,128)(2,1)S(1)} fusion(bf16[5120,448]{1,0:T(8,128)(2,1)S(1)} %bitcast.189, bf16[256,1280]{1,0:T(8,128)(2,1)S(1)} %bitcast.201, bf16[256,1280]{1,0:T(8,128)(2,1)S(1)} %bitcast.202, bf16[256,1280]{1,0:T(8,128)(2,1)S(1)} %bitcast.203, bf16[256,1280]{1,0:T(8,128)(2,1)S(1)} %bitcast.200), kind=kOutput, calls=%fused_computation.42 | convolution fusion | flops 1185005568 | bytes 7438336 | tf_op jit(solution)/shard_map/dot_general | solution.py:124
  83.7 0.9 fusion.21
  84.7 1.3 copy.83
  86.0 8.6 %all-to-all-start = ((bf16[64,16,448]{2,1,0:T(8,128)(2,1)}), bf16[64,16,448]{2,1,0:T(8,128)(2,1)S(1)}, u32[]{:S(2)}, u32[]{:S(2)}) async-start(bf16[64,16,448]{2,1,0:T(8,128)(2,1)} %bitcast.29), calls=%async_computation | async-start | bytes 2097152 | tf_op jit(solution)/shard_map/all_to_all | solution.py:151
  95.2 0.5 copy.85
  95.8 17.3 %all-to-all-done = bf16[64,16,448]{2,1,0:T(8,128)(2,1)S(1)} async-done(((bf16[64,16,448]{2,1,0:T(8,128)(2,1)}), bf16[64,16,448]{2,1,0:T(8,128)(2,1)S(1)}, u32[]{:S(2)}, u32[]{:S(2)}) %all-to-all-start) | async-done | bytes 917536 | tf_op jit(solution)/shard_map/all_to_all | solution.py:151
  113.2 0.5 fusion.23
  113.9 0.3 collective-permute-start.7
  114.2 0.5 copy-done.8
  114.7 0.2 copy.90
  115.1 1.6 collective-permute-done.7
  116.8 0.5 fusion.3
  117.3 0.2 copy-done.13
  117.5 7.1 %multiply_convert_fusion.1 = (bf16[256,1152]{1,0:T(8,128)(2,1)S(1)}, f32[256,1152]{1,0:T(8,128)}) fusion(f32[256]{0:T(256)S(1)} %get-tuple-element.11, bf16[3584,1152]{1,0:T(8,128)(2,1)} %param.18, f32[3584]{0:T(1024)S(1)} %copy-done.13, bf16[256,1792]{0,1:T(8,128)(2,1)S(1)} %get-tuple-element.9, bf16[256,1792]{0,1:T(8,128)(2,1)S(1)} %get-tuple-element.8), kind=kOutput, calls=%fused_computation.46 | convolution fusion | flops 2120024064 | bytes 11877376 | tf_op jit(solution)/shard_map/dot_general | solution.py:169
  124.6 1.1 copy.86
  125.7 1.3 fusion.76
  126.9 3.1 %fusion.107 = (f32[7,256]{1,0:T(8,128)S(1)}, f32[7,256,256]{1,2,0:T(8,128)}) fusion(pred[256,256]{0,1:T(8,128)(4,1)S(1)} %fusion.60, bf16[256,9,128]{0,2,1:T(8,128)(2,1)} %bitcast.197), kind=kOutput, calls=%fused_computation.226 | convolution fusion | flops 119275776 | bytes 2432000 | tf_op jit(solution)/shard_map/sub | solution.py:20
  130.0 3.9 %convolution_bitcast_fusion = f32[256,7,128]{0,2,1:T(8,128)} fusion(f32[256,256,7]{1,0,2:T(8,128)S(1)} %fusion.76, bf16[256,9,128]{0,2,1:T(8,128)(2,1)} %bitcast.198, f32[7,256,256]{1,2,0:T(8,128)} %get-tuple-element.15, f32[7,256]{1,0:T(8,128)S(1)} %get-tuple-element.14), kind=kOutput, calls=%fused_computation.38 | convolution fusion | flops 120653824 | bytes 8339456 | tf_op jit(solution)/shard_map/hqk,kd->qhd/dot_general | solution.py:28
  133.9 3.0 %convolution_bitcast_fusion.2 = f32[256,1,128]{0,2,1:T(8,128)S(1)} fusion(f32[256,256,7]{1,0,2:T(8,128)S(1)} %fusion.76, bf16[256,9,128]{0,2,1:T(8,128)(2,1)} %bitcast.199, f32[7,256,256]{1,2,0:T(8,128)} %get-tuple-element.15, f32[7,256]{1,0:T(8,128)S(1)} %get-tuple-element.14), kind=kOutput, calls=%fused_computation.48 | convolution fusion | flops 120653824 | bytes 7946240 | tf_op jit(solution)/shard_map/hqk,qhd->kd/dot_general | solution.py:29
  136.9 2.1 %convolution_bitcast_fusion.1 = f32[256,1,128]{0,2,1:T(8,128)S(1)} fusion(bf16[256,7,128]{0,2,1:T(8,128)(2,1)S(1)} %bitcast.193, f32[7,256,256]{1,2,0:T(8,128)} %get-tuple-element.15, f32[7,256]{1,0:T(8,128)S(1)} %get-tuple-element.14), kind=kOutput, calls=%fused_computation.47 | convolution fusion | flops 118358016 | bytes 2432000 | tf_op jit(solution)/shard_map/hqk,qhd->kd/dot_general | solution.py:30
  138.9 1.1 pad_maximum_fusion.2
  140.0 1.6 copy.97
  141.7 6.1 %fusion.39 = f32[256,3584]{0,1:T(8,128)S(1)} fusion(bf16[3584,1152]{1,0:T(8,128)(2,1)} %param.18, f32[256,1152]{1,0:T(8,128)S(1)} %copy.97, f32[256]{0:T(256)S(1)} %get-tuple-element.11), kind=kOutput, calls=%fused_computation.68 | convolution fusion | flops 2114519040 | bytes 13108224 | tf_op jit(solution)/shard_map/dot_general | solution.py:174
  147.8 1.1 select_convert_fusion
  149.1 0.9 copy-done.3
  150.0 0.2 multiply_reduce_fusion
  150.2 0.2 collective-permute-start.9
  150.7 0.7 collective-permute-done.9
  151.4 0.2 collective-permute-done.8
  151.6 2.6 %subtract_convert_fusion = bf16[256,1792]{0,1:T(8,128)(2,1)S(1)} fusion(bf16[256,1792]{0,1:T(8,128)(2,1)S(1)} %broadcast_select_fusion, bf16[256,1792]{0,1:T(8,128)(2,1)S(1)} %collective-permute-done.8, f32[256,3584]{0,1:T(8,128)} %copy-done.2, f32[256]{0:T(256)S(1)} %bitcast.213, f32[256]{0:T(256)S(1)} %get-tuple-element.10, f32[1792]{0:T(1024)S(1)} %dynamic_slice.29, ...), kind=kLoop, calls=%fused_computation.28 | loop fusion | flops 4128768 | bytes 6431745 | tf_op jit(solution)/shard_map/convert_element_type | solution.py:184
  154.3 0.5 fusion.44
  154.8 1.4 fusion.22
  156.2 4.9 %all-to-all-start.1 = ((bf16[64,8,896]{2,1,0:T(8,128)(2,1)}), bf16[64,8,896]{2,1,0:T(8,128)(2,1)S(1)}, u32[]{:S(2)}, u32[]{:S(2)}) async-start(bf16[64,8,896]{2,1,0:T(8,128)(2,1)} %fusion.22), calls=%async_computation.1 | async-start | bytes 1835008 | tf_op jit(solution)/shard_map/all_to_all | solution.py:196
  161.1 0.7 and_select_fusion
  161.8 0.2 convert_reduce_fusion.1
  162.0 0.7 multiply_add_fusion
  162.7 15.9 %all-to-all-done.1 = bf16[64,8,896]{2,1,0:T(8,128)(2,1)S(1)} async-done(((bf16[64,8,896]{2,1,0:T(8,128)(2,1)}), bf16[64,8,896]{2,1,0:T(8,128)(2,1)S(1)}, u32[]{:S(2)}, u32[]{:S(2)}) %all-to-all-start.1) | async-done | bytes 917536 | tf_op jit(solution)/shard_map/all_to_all | solution.py:196
  178.7 0.4 convolution_convert_fusion.3
  179.1 0.4 convolution_convert_fusion.2
  179.5 0.7 pad_maximum_fusion.3
  180.2 0.8 fusion.46
  (101 shorter events, 3.1 us)
Async XLA Ops:
  7.2 2.6 %copy-start = (bf16[80,1792]{1,0:T(8,128)(2,1)S(1)}, bf16[80,1792]{1,0:T(8,128)(2,1)}, u32[]{:S(2)}) copy-start(bf16[80,1792]{1,0:T(8,128)(2,1)} %param.12) | copy-start | bytes 860164
  7.2 68.7 %all-gather.3.cloned.1.call-start = ((), (), s32[]{:S(2)}) async-start(), calls=%async_computation.2 | async-start | bytes 6963200 | tf_op jit(solution)/shard_map/all_gather | solution.py:98
  7.2 3.5 %copy-start.11 = (bf16[128,1280]{1,0:T(8,128)(2,1)S(1)}, bf16[128,1280]{1,0:T(8,128)(2,1)}, u32[]{:S(2)}) copy-start(bf16[128,1280]{1,0:T(8,128)(2,1)} %param.10) | copy-start | bytes 983044
  7.2 3.5 %copy-start.10 = (bf16[64,5120]{1,0:T(8,128)(2,1)S(1)}, bf16[64,5120]{1,0:T(8,128)(2,1)}, u32[]{:S(2)}) copy-start(bf16[64,5120]{1,0:T(8,128)(2,1)} %param.11) | copy-start | bytes 1966084
  9.6 7.2 %copy-start.9 = (s32[64,192]{1,0:T(8,128)S(1)}, s32[64,192]{1,0:T(8,128)}, u32[]{:S(2)}) copy-start(s32[64,192]{1,0:T(8,128)} %param.15) | copy-start | bytes 147460
  10.9 14.1 %collective-permute-start = (bf16[192,1280]{1,0:T(8,128)(2,1)S(1)}, bf16[192,1280]{1,0:T(8,128)(2,1)S(1)}, u32[]{:S(2)}, u32[]{:S(2)}) collective-permute-start(bf16[192,1280]{1,0:T(8,128)(2,1)S(1)} %dynamic-slice_dynamic-update-slice_fusion.1), channel_id=1, source_target_pairs={{0,32},{32,64},{64,96},{96,0},{1,33},{33,65},{65,97},{97,1},{2,34}... | collective-permute-start | bytes 1474568 | tf_op jit(solution)/shard_map/ppermute | solution.py:110
  12.5 24.2 %collective-permute-start.1 = (bf16[192,1280]{1,0:T(8,128)(2,1)S(1)}, bf16[192,1280]{1,0:T(8,128)(2,1)S(1)}, u32[]{:S(2)}, u32[]{:S(2)}) collective-permute-start(bf16[192,1280]{1,0:T(8,128)(2,1)S(1)} %dynamic-slice_dynamic-update-slice_fusion.1), channel_id=1, source_target_pairs={{0,64},{32,96},{64,0},{96,32},{1,65},{33,97},{65,1},{97,33},{2,66}... | collective-permute-start | bytes 1474568 | tf_op jit(solution)/shard_map/ppermute | solution.py:110
  15.3 21.5 %collective-permute-start.2 = (bf16[192,1280]{1,0:T(8,128)(2,1)S(1)}, bf16[192,1280]{1,0:T(8,128)(2,1)S(1)}, u32[]{:S(2)}, u32[]{:S(2)}) collective-permute-start(bf16[192,1280]{1,0:T(8,128)(2,1)S(1)} %dynamic-slice_dynamic-update-slice_fusion.1), channel_id=1, source_target_pairs={{0,96},{32,0},{64,32},{96,64},{1,97},{33,1},{65,33},{97,65},{2,98}... | collective-permute-start | bytes 1474568 | tf_op jit(solution)/shard_map/ppermute | solution.py:110
  16.7 20.7 %collective-permute-start.3 = (bf16[192,1280]{1,0:T(8,128)(2,1)S(1)}, bf16[192,1280]{1,0:T(8,128)(2,1)S(1)}, u32[]{:S(2)}, u32[]{:S(2)}) collective-permute-start(bf16[192,1280]{1,0:T(8,128)(2,1)S(1)} %dynamic-slice_dynamic-update-slice_fusion.1), channel_id=1, source_target_pairs={{0,1},{1,0},{2,3},{3,2},{4,5},{5,4},{6,7},{7,6},{8,9},{9,8},{10,11... | collective-permute-start | bytes 1474568 | tf_op jit(solution)/shard_map/ppermute | solution.py:52
  25.0 12.4 %collective-permute-start.4 = (bf16[192,1280]{1,0:T(8,128)(2,1)S(1)}, bf16[192,1280]{1,0:T(8,128)(2,1)S(1)}, u32[]{:S(2)}, u32[]{:S(2)}) collective-permute-start(bf16[192,1280]{1,0:T(8,128)(2,1)S(1)} %collective-permute-done), channel_id=1, source_target_pairs={{0,1},{1,0},{2,3},{3,2},{4,5},{5,4},{6,7},{7,6},{8,9},{9,8},{10,11... | collective-permute-start | bytes 1474568 | tf_op jit(solution)/shard_map/ppermute | solution.py:52
  36.7 1.9 collective-permute-start.5
  36.8 2.5 %collective-permute-start.6 = (bf16[192,1280]{1,0:T(8,128)(2,1)S(1)}, bf16[192,1280]{1,0:T(8,128)(2,1)S(1)}, u32[]{:S(2)}, u32[]{:S(2)}) collective-permute-start(bf16[192,1280]{1,0:T(8,128)(2,1)S(1)} %collective-permute-done.2), channel_id=1, source_target_pairs={{0,1},{1,0},{2,3},{3,2},{4,5},{5,4},{6,7},{7,6},{8,9},{9,8},{10,11... | collective-permute-start | bytes 1474568 | tf_op jit(solution)/shard_map/ppermute | solution.py:52
  80.3 1.1 copy-start.6
  80.4 1.3 copy-start.7
  84.7 10.5 %copy-start.4 = (bf16[256,1792]{1,0:T(8,128)(2,1)S(1)}, bf16[256,1792]{1,0:T(8,128)(2,1)}, u32[]{:S(2)}) copy-start(bf16[256,1792]{1,0:T(8,128)(2,1)} %param.14) | copy-start | bytes 2752516
  86.0 27.2 %all-to-all-start = ((bf16[64,16,448]{2,1,0:T(8,128)(2,1)}), bf16[64,16,448]{2,1,0:T(8,128)(2,1)S(1)}, u32[]{:S(2)}, u32[]{:S(2)}) async-start(bf16[64,16,448]{2,1,0:T(8,128)(2,1)} %bitcast.29), calls=%async_computation | async-start | bytes 2097152 | tf_op jit(solution)/shard_map/all_to_all | solution.py:151
  113.7 1.0 copy-start.8
  113.8 1.1 copy-start.12
  113.9 2.7 %collective-permute-start.7 = (bf16[256,1792]{0,1:T(8,128)(2,1)S(1)}, bf16[256,1792]{0,1:T(8,128)(2,1)S(1)}, u32[]{:S(2)}, u32[]{:S(2)}) collective-permute-start(bf16[256,1792]{0,1:T(8,128)(2,1)S(1)} %broadcast_select_fusion), channel_id=1, source_target_pairs={{0,1},{1,0},{2,3},{3,2},{4,5},{5,4},{6,7},{7,6},{8,9},{9,8},{10,11... | collective-permute-start | bytes 2752520 | tf_op jit(solution)/shard_map/ppermute | solution.py:52
  116.8 0.7 copy-start.13
  136.9 2.1 %copy-start.5 = (f32[256,7,128]{0,2,1:T(8,128)S(1)}, f32[256,7,128]{0,2,1:T(8,128)}, u32[]{:S(2)}) copy-start(f32[256,7,128]{0,2,1:T(8,128)} %convolution_bitcast_fusion) | copy-start | bytes 2752516
  147.8 2.3 %copy-start.2 = (f32[256,3584]{0,1:T(8,128)}, f32[256,3584]{0,1:T(8,128)S(1)}, u32[]{:S(2)}) copy-start(f32[256,3584]{0,1:T(8,128)S(1)} %fusion.39) | copy-start | bytes 11010052
  147.8 2.1 %copy-start.3 = (f32[256,1152]{1,0:T(8,128)S(1)}, f32[256,1152]{1,0:T(8,128)}, u32[]{:S(2)}) copy-start(f32[256,1152]{1,0:T(8,128)} %get-tuple-element.13) | copy-start | bytes 3538948
  149.0 2.7 %collective-permute-start.8 = (bf16[256,1792]{0,1:T(8,128)(2,1)}, bf16[256,1792]{0,1:T(8,128)(2,1)S(1)}, u32[]{:S(2)}, u32[]{:S(2)}) collective-permute-start(bf16[256,1792]{0,1:T(8,128)(2,1)} %select_convert_fusion), channel_id=1, source_target_pairs={{0,1},{1,0},{2,3},{3,2},{4,5},{5,4},{6,7},{7,6},{8,9},{9,8},{10,11... | collective-permute-start | bytes 2752520 | tf_op jit(solution)/shard_map/ppermute | solution.py:52
  150.2 1.3 collective-permute-start.9
  156.2 22.4 %all-to-all-start.1 = ((bf16[64,8,896]{2,1,0:T(8,128)(2,1)}), bf16[64,8,896]{2,1,0:T(8,128)(2,1)S(1)}, u32[]{:S(2)}, u32[]{:S(2)}) async-start(bf16[64,8,896]{2,1,0:T(8,128)(2,1)} %fusion.22), calls=%async_computation.1 | async-start | bytes 1835008 | tf_op jit(solution)/shard_map/all_to_all | solution.py:196
  178.7 2.4 %copy-start.1 = (bf16[80,1792]{1,0:T(8,128)(2,1)S(1)}, bf16[80,1792]{1,0:T(8,128)(2,1)}, u32[]{:S(2)}) copy-start(bf16[80,1792]{1,0:T(8,128)(2,1)} %param.12) | copy-start | bytes 860164
Sparse Core Ops, SparseCore 0:
  10.9 65.0 all-gather.2

commit v2 on v1

--- a/solution.py
+++ b/solution.py
@@ -1,51 +1,159 @@
 import jax
 import jax.numpy as jnp
 from jax import lax
+from jax.experimental import pallas as pl
+from jax.experimental.pallas import tpu as pltpu
 from jax.sharding import PartitionSpec as P
 
-HEADS = 14
-KV_HEADS = 2
 HEAD_DIM = 128
 
 epsilon = 1e-06
 
 
-def group_grads(query_rows, key_rows, value_rows, upstream, allowed, score_scale):
-    scores = (
-        jnp.einsum("qhd,kd->hqk", query_rows, key_rows, preferred_element_type=jnp.float32)
-        * score_scale
-    )
-    scores = jnp.where(allowed[None], scores, -1e30)
-    row_max = jnp.max(scores, axis=2, keepdims=True)
-    weights = jnp.exp(scores - row_max)
-    weights = weights / jnp.sum(weights, axis=2, keepdims=True)
-    probs_low = weights.astype(jnp.bfloat16)
-    weight_grad = jnp.einsum(
-        "qhd,kd->hqk", upstream, value_rows, preferred_element_type=jnp.float32
-    )
-    row_delta = jnp.sum(weight_grad * weights, axis=2, keepdims=True)
-    score_grad = (weights * (weight_grad - row_delta) * score_scale).astype(jnp.bfloat16)
-    grad_query = jnp.einsum("hqk,kd->qhd", score_grad, key_rows, preferred_element_type=jnp.float32)
-    grad_key = jnp.einsum("hqk,qhd->kd", score_grad, query_rows, preferred_element_type=jnp.float32)
-    grad_value = jnp.einsum("hqk,qhd->kd", probs_low, upstream, preferred_element_type=jnp.float32)
-    return (grad_query, grad_key, grad_value)
-
-
-def head_grads(scaled, upstream, segments, heads_per_group, head_size):
-    length = scaled.shape[0]
-    blocks = scaled.reshape(length, heads_per_group + 2, head_size)
-    positions = jnp.arange(length)
-    allowed = (segments[:, None] == segments[None, :]) & (positions[None, :] <= positions[:, None])
-    grad_query, grad_key, grad_value = group_grads(
-        blocks[:, :heads_per_group],
-        blocks[:, heads_per_group],
-        blocks[:, heads_per_group + 1],
-        upstream.reshape(length, heads_per_group, head_size),
-        allowed,
-        head_size ** (-0.5),
-    )
-    stacked = jnp.concatenate([grad_query, grad_key[:, None], grad_value[:, None]], axis=1)
-    return stacked.reshape(length, (heads_per_group + 2) * head_size)
+NT = (((1,), (1,)), ((), ()))
+NN = (((1,), (0,)), ((), ()))
+TAIL = 128
+
+
+def dot(x, y, dims=NN):
+    return lax.dot_general(x, y, dims, preferred_element_type=jnp.float32)
+
+
+def attend_kernel(
+    half_ref,
+    own_ref,
+    other_ref,
+    gain_ref,
+    weight_ref,
+    upstream_ref,
+    seg_row_ref,
+    seg_col_ref,
+    give_ref,
+    keep_ref,
+    inv_ref,
+    stat_ref,
+    normed_ref,
+    unscaled_ref,
+    scaled_ref,
+    sgrad_ref,
+    bias_ref,
+):
+    bf16, f32 = jnp.bfloat16, jnp.float32
+    rows, slab = own_ref.shape
+    group = weight_ref.shape[1]
+    heads = group // HEAD_DIM - 2
+    t = half_ref[0]
+    own_at = pl.multiple_of(t * slab, HEAD_DIM)
+    other_at = pl.multiple_of((1 - t) * slab, HEAD_DIM)
+    score_scale = HEAD_DIM ** (-0.5)
+
+    squares = jnp.zeros((rows, HEAD_DIM), f32)
+    for part, ref in ((t, own_ref), (1 - t, other_ref)):
+        gain = gain_ref[pl.ds(part, 1), :]
+        for c in range(0, slab, HEAD_DIM):
+            x = ref[:, c : c + HEAD_DIM].astype(f32)
+            squares = squares + x * x
+            at = pl.multiple_of(part * slab + c, HEAD_DIM)
+            normed_ref[:, pl.ds(at, HEAD_DIM)] = (x * gain[:, c : c + HEAD_DIM]).astype(bf16)
+    inv = lax.rsqrt(jnp.sum(squares, axis=1, keepdims=True) / (2 * slab) + epsilon)
+    inv_ref[...] = inv
+
+    width = 384
+
+    @pl.loop(0, group // width)
+    def _(n):
+        cols = pl.ds(pl.multiple_of(n * width, width), width)
+        value = dot(normed_ref[...], weight_ref[:, cols])
+        unscaled_ref[:, cols] = value
+        scaled_ref[:, cols] = (value * inv).astype(bf16)
+
+    place_u = lax.broadcasted_iota(jnp.int32, (rows, rows), 0)
+    place_t = lax.broadcasted_iota(jnp.int32, (rows, rows), 1)
+    allowed = (seg_col_ref[...] == seg_row_ref[...]) & (place_u <= place_t)
+    bias_ref[...] = jnp.where(allowed, 0.0, -1e30)
+
+    key = scaled_ref[:, heads * HEAD_DIM : (heads + 1) * HEAD_DIM]
+    val = scaled_ref[:, (heads + 1) * HEAD_DIM :]
+    grad_key = jnp.zeros((rows, HEAD_DIM), f32)
+    grad_val = jnp.zeros((rows, HEAD_DIM), f32)
+    stat = jnp.zeros((rows, HEAD_DIM), f32)
+    for h in range(heads):
+        cols = slice(h * HEAD_DIM, (h + 1) * HEAD_DIM)
+        query = scaled_ref[:, cols]
+        up = upstream_ref[:, cols]
+        scores = dot(key, query, NT) * score_scale + bias_ref[...]
+        scores = jnp.exp(scores - jnp.max(scores, axis=0, keepdims=True))
+        probs = scores * (1.0 / jnp.sum(scores, axis=0, keepdims=True))
+        dprobs = dot(val, up, NT)
+        delta = jnp.sum(probs * dprobs, axis=0, keepdims=True)
+        sgrad = (probs * (dprobs - delta) * score_scale).astype(bf16)
+        grad_val = grad_val + dot(probs.astype(bf16), up)
+        grad_key = grad_key + dot(sgrad, query)
+        grad_query = dot(sgrad.T, key)
+        stat = stat + grad_query * unscaled_ref[:, cols]
+        sgrad_ref[:, cols] = (grad_query * inv).astype(bf16)
+    cols = slice(heads * HEAD_DIM, (heads + 1) * HEAD_DIM)
+    stat = stat + grad_key * unscaled_ref[:, cols]
+    sgrad_ref[:, cols] = (grad_key * inv).astype(bf16)
+    cols = slice((heads + 1) * HEAD_DIM, (heads + 2) * HEAD_DIM)
+    stat = stat + grad_val * unscaled_ref[:, cols]
+    sgrad_ref[:, cols] = (grad_val * inv).astype(bf16)
+    total = jnp.sum(stat, axis=1, keepdims=True)
+    stat_ref[...] = total
+    lane = lax.broadcasted_iota(jnp.int32, (rows, TAIL), 1)
+    high = total.astype(bf16)
+    low = (total - high.astype(f32)).astype(bf16)
+    give_ref[:, slab:] = jnp.where(lane == 0, high.astype(f32), low.astype(f32)).astype(bf16)
+
+    step = 256
+
+    @pl.loop(0, slab // step)
+    def _(n):
+        at = pl.multiple_of(n * step, step)
+        rows_at = pl.ds(pl.multiple_of(other_at + at, HEAD_DIM), step)
+        give_ref[:, pl.ds(at, step)] = dot(sgrad_ref[...], weight_ref[rows_at, :], NT).astype(bf16)
+
+    @pl.loop(0, slab // step)
+    def _(n):
+        at = pl.multiple_of(n * step, step)
+        rows_at = pl.ds(pl.multiple_of(own_at + at, HEAD_DIM), step)
+        keep_ref[:, pl.ds(at, step)] = dot(sgrad_ref[...], weight_ref[rows_at, :], NT)
+
+
+def attend(half, own, other, norm_gain, qkv_weight, upstream, segments):
+    rows, slab = own.shape
+    group = qkv_weight.shape[1]
+    f32, bf16 = jnp.float32, jnp.bfloat16
+    vmem = pl.BlockSpec(memory_space=pltpu.VMEM)
+    return pl.pallas_call(
+        attend_kernel,
+        out_shape=(
+            jax.ShapeDtypeStruct((rows, slab + TAIL), bf16),
+            jax.ShapeDtypeStruct((rows, slab), f32),
+            jax.ShapeDtypeStruct((rows, 1), f32),
+            jax.ShapeDtypeStruct((rows, 1), f32),
+        ),
+        in_specs=[pl.BlockSpec(memory_space=pltpu.SMEM)] + [vmem] * 7,
+        out_specs=(vmem,) * 4,
+        scratch_shapes=[
+            pltpu.VMEM((rows, 2 * slab), bf16),
+            pltpu.VMEM((rows, group), f32),
+            pltpu.VMEM((rows, group), bf16),
+            pltpu.VMEM((rows, group), bf16),
+            pltpu.VMEM((rows, rows), f32),
+        ],
+        compiler_params=pltpu.CompilerParams(vmem_limit_bytes=40 * 1024 * 1024),
+        cost_estimate=pl.CostEstimate(flops=5_000_000_000, bytes_accessed=14_000_000, transcendentals=500_000),
+    )(
+        half.reshape(1),
+        own,
+        other,
+        norm_gain.reshape(2, slab),
+        qkv_weight,
+        upstream,
+        segments.reshape(1, rows),
+        segments.reshape(rows, 1),
+    )
 
 
 def swap(x):
@@ -158,27 +266,13 @@
     row_slab = jnp.where(filled[:, None], placed, text_rows)
 
     other_slab = swap(row_slab)
-    full_rows = jnp.concatenate(
-        [jnp.where(t == 0, row_slab, other_slab), jnp.where(t == 0, other_slab, row_slab)], axis=1
-    )
-    model_width = full_rows.shape[1]
-    inv_rms = lax.rsqrt(
-        jnp.mean(full_rows.astype(f32) * full_rows.astype(f32), axis=1, keepdims=True) + epsilon
-    )
-    normed = (full_rows.astype(f32) * norm_gain).astype(bf16)
-    unscaled = jnp.dot(normed, qkv_weight, preferred_element_type=f32)
-    scaled = (unscaled * inv_rms).astype(bf16)
-    grads = head_grads(scaled, attn_grad, segment_ids[0], HEADS // KV_HEADS, HEAD_DIM)
-    scaled_grad = (grads * inv_rms).astype(bf16)
-    row_part = jnp.sum(grads * unscaled, axis=1, keepdims=True)
-    partial_proj = lax.dot_general(
-        scaled_grad, qkv_weight, (((1,), (1,)), ((), ())), preferred_element_type=f32
-    )
-    low, high = partial_proj[:, :slab], partial_proj[:, slab:]
-    keep = jnp.where(t == 0, low, high)
-    give = jnp.where(t == 0, high, low).astype(bf16)
-    back = keep + swap(give).astype(f32)
-    stat = row_part + swap(row_part)
+    give, keep, inv_rms, row_part = attend(
+        t, row_slab, other_slab, norm_gain, qkv_weight, attn_grad, segment_ids[0]
+    )
+    model_width = 2 * slab
+    taken = swap(give)
+    back = keep + taken[:, :slab].astype(f32)
+    stat = row_part + taken[:, slab : slab + 1].astype(f32) + taken[:, slab + 1 : slab + 2].astype(f32)
     gain_slab = lax.dynamic_slice_in_dim(norm_gain, t * slab, slab, 0)
     row_grads = gain_slab * back - row_slab.astype(f32) * (inv_rms**3 / model_width) * stat
     row_grads = row_grads.astype(bf16)

time: 189 us -> 179 us (0.947)
  matrix products: 33.5 us -> 7.08 us
  Pallas kernels: 0 us -> 12.9 us
  local copies, waits for them, and re-layouts: 18.5 us -> 23.3 us
  other arithmetic: 11.6 us -> 7.35 us
  waiting for transfers between devices: 89.1 us -> 93 us
    dot_general x6 -> x0, matrix products: 23.4 us -> none  [the longest x1 7.06 us: local(): unscaled = jnp.dot(normed, qkv_weight, preferred_element_type=f32)]
    pallas_call x0 -> x1, Pallas kernels: none -> 12.9 us  [attend(): pl.pallas_call(attend_kernel, out_shape=(jax.ShapeDtypeStruct((rows, slab...]
    unnamed x48 -> x37, local copies, waits for them, and re-layouts: 3.19 us -> 7.28 us
    sub x1 -> x0, matrix products: 3.06 us -> none  [group_grads(): weights = jnp.exp(scores - row_max)]
    ppermute x7 -> x6, waiting for transfers between devices: 4.31 us -> 6.33 us  [swap(): return lax.ppermute(x, 'tp', [(0, 1), (1, 0)])]
  transfers between devices with their start and end apart: 13 -> 12, of which waited for: 10 -> 9; matrix products, arithmetic and copies ran while one was open for 5% -> 4% of each run, Pallas kernels for 0% -> 0%
where the time goes in v2:
time: 179 us
  waiting for transfers between devices  93 us (52%)
  local copies, waits for them, and re-layouts  23.3 us (13%)
  starting transfers between devices  20.3 us (11%)
  between operations  14.6 us (8%)
  Pallas kernels  12.9 us (7%)
  other arithmetic  7.35 us (4%)
  matrix products  7.08 us (4%)
    all_gather x1, waiting for transfers between devices, local(): gathered = lax.all_gather(shard, 'seq', axis=0, tiled=False)  35.3 us
    all_to_all x1, waiting for transfers between devices, local(): lax.all_to_all(outgoing, ('enc', 'seq'), split_axis=0, concat_axis=0, til...  17.9 us
    all_to_all x1, waiting for transfers between devices, local(): lax.all_to_all(out8, ('enc', 'seq'), split_axis=0, concat_axis=0, tiled=T...  17.3 us
    ppermute x3, waiting for transfers between devices, local(): lax.ppermute(packed, 'enc', [(i, (i + k) % n_enc) for i in range(n_enc)])  16.2 us
    pallas_call x1, Pallas kernels, attend(): pl.pallas_call(attend_kernel, out_shape=(jax.ShapeDtypeStruct((rows, slab...  12.9 us
    all_to_all x1, starting transfers between devices, local(): lax.all_to_all(outgoing, ('enc', 'seq'), split_axis=0, concat_axis=0, til...  8.61 us
    unnamed x37, local copies, waits for them, and re-layouts  7.28 us
    ppermute x6, waiting for transfers between devices, swap(): return lax.ppermute(x, 'tp', [(0, 1), (1, 0)])  6.33 us
  transfers between devices with their start and end apart: 12, of which 9 were waited for; matrix products, arithmetic and copies ran while one was open for 4% of the time, Pallas kernels for 0%

profile of v2, /device:TPU:0, one launch (start us, length us, event | category | flops | bytes accessed | tf_op | source)
XLA Modules:
  0.0 178.6 jit_solution(7089948823314603441)
XLA Ops:
  7.3 2.4 %reshape.399 = bf16[320,1792]{1,0:T(8,128)(2,1)S(1)} reshape(bf16[80,4,1792]{2,1,0:T(4,128)(2,1)} %param.13) | data formatting | bytes 2293760 | tf_op jit(solution)/shard_map/reshape | solution.py:200
  9.7 0.1 constant_dynamic-slice_fusion
  9.9 0.8 maximum_maximum_fusion
  10.9 1.6 collective-permute-start
  12.5 2.7 %collective-permute-start.1 = (bf16[192,1280]{1,0:T(8,128)(2,1)S(1)}, bf16[192,1280]{1,0:T(8,128)(2,1)S(1)}, u32[]{:S(2)}, u32[]{:S(2)}) collective-permute-start(bf16[192,1280]{1,0:T(8,128)(2,1)S(1)} %dynamic-slice_dynamic-update-slice_fusion.1), channel_id=1, source_target_pairs={{0,64},{32,96},{64,0},{96,32},{1,65},{33,97},{65,1},{97,33},{2,66}... | collective-permute-start | bytes 1474568 | tf_op jit(solution)/shard_map/ppermute | solution.py:218
  15.3 1.4 collective-permute-start.2
  16.9 0.4 convert_reduce_fusion
  17.3 0.6 gather_fusion
  18.0 0.6 gather_fusion.1
  18.7 0.6 gather_fusion.2
  19.5 0.6 reduce-window.6
  20.1 0.2 slice_reduce_fusion
  20.5 4.5 %collective-permute-done = bf16[192,1280]{1,0:T(8,128)(2,1)S(1)} collective-permute-done((bf16[192,1280]{1,0:T(8,128)(2,1)S(1)}, bf16[192,1280]{1,0:T(8,128)(2,1)S(1)}, u32[]{:S(2)}, u32[]{:S(2)}) %collective-permute-start) | collective-permute-done | bytes 491552 | tf_op jit(solution)/shard_map/ppermute | solution.py:218
  25.1 11.7 %collective-permute-done.1 = bf16[192,1280]{1,0:T(8,128)(2,1)S(1)} collective-permute-done((bf16[192,1280]{1,0:T(8,128)(2,1)S(1)}, bf16[192,1280]{1,0:T(8,128)(2,1)S(1)}, u32[]{:S(2)}, u32[]{:S(2)}) %collective-permute-start.1) | collective-permute-done | bytes 491552 | tf_op jit(solution)/shard_map/ppermute | solution.py:218
  36.8 0.6 collective-permute-start.6
  37.5 1.1 collective-permute-done.5
  38.6 0.7 collective-permute-done.6
  39.3 0.1 slice.134
  39.4 1.2 fusion.64
  40.6 35.3 %all-gather.3.cloned.1.call-done = bf16[6400,448]{1,0:T(8,128)(2,1)} async-done(((bf16[400,448]{1,0:T(8,128)(2,1)}), bf16[6400,448]{1,0:T(8,128)(2,1)}) %all-gather.3.cloned.1.call-update) | async-done | bytes 5734416 | tf_op jit(solution)/shard_map/all_gather | solution.py:206
  75.9 1.4 slice.135
  77.3 3.0 %slice.140 = bf16[16,320,448]{2,1,0:T(8,128)(2,1)S(1)} slice(bf16[16,400,448]{2,1,0:T(8,128)(2,1)} %bitcast.110), slice={[0:16], [80:400], [0:448]} | slice | bytes 9175040 | tf_op jit(solution)/shard_map/slice | solution.py:208
  80.4 0.8 convolution_convert_fusion.1
  81.2 0.3 copy-done.7
  81.4 0.2 copy-done.8
  81.6 2.1 %fusion.12 = bf16[256,448]{0,1:T(8,128)(2,1)S(1)} fusion(bf16[5120,448]{1,0:T(8,128)(2,1)S(1)} %bitcast.111, bf16[256,1280]{1,0:T(8,128)(2,1)S(1)} %bitcast.118, bf16[256,1280]{1,0:T(8,128)(2,1)S(1)} %bitcast.119, bf16[256,1280]{1,0:T(8,128)(2,1)S(1)} %bitcast.120, bf16[256,1280]{1,0:T(8,128)(2,1)S(1)} %bitcast.117), kind=kOutput, calls=%fused_computation.22 | convolution fusion | flops 1185005568 | bytes 7438336 | tf_op jit(solution)/shard_map/dot_general | solution.py:232
  83.7 0.9 fusion.10
  84.7 1.3 copy.53
  86.0 8.6 %all-to-all-start = ((bf16[64,16,448]{2,1,0:T(8,128)(2,1)}), bf16[64,16,448]{2,1,0:T(8,128)(2,1)S(1)}, u32[]{:S(2)}, u32[]{:S(2)}) async-start(bf16[64,16,448]{2,1,0:T(8,128)(2,1)} %bitcast.30), calls=%async_computation | async-start | bytes 2097152 | tf_op jit(solution)/shard_map/all_to_all | solution.py:259
  94.6 0.2 select_reduce_fusion
  94.9 0.1 copy.49
  95.0 0.1 eq.173
  95.1 0.1 fusion.41
  95.2 17.9 %all-to-all-done = bf16[64,16,448]{2,1,0:T(8,128)(2,1)S(1)} async-done(((bf16[64,16,448]{2,1,0:T(8,128)(2,1)}), bf16[64,16,448]{2,1,0:T(8,128)(2,1)S(1)}, u32[]{:S(2)}, u32[]{:S(2)}) %all-to-all-start) | async-done | bytes 917536 | tf_op jit(solution)/shard_map/all_to_all | solution.py:259
  113.1 0.5 convolution_convert_fusion
  113.6 0.5 copy.55
  114.2 0.8 slice_bitcast_fusion
  115.0 0.7 slice_bitcast_fusion.4
  115.7 1.3 concatenate.53
  117.0 0.2 broadcast_select_fusion.own_ref
  117.2 0.3 collective-permute-start.7
  117.5 0.1 copy.56.seg_col_ref
  117.6 2.3 %collective-permute-done.7.other_ref = bf16[256,1792]{1,0:T(8,128)(2,1)S(1)} collective-permute-done((bf16[256,1792]{1,0:T(8,128)(2,1)S(1)}, bf16[256,1792]{1,0:T(8,128)(2,1)S(1)}, u32[]{:S(2)}, u32[]{:S(2)}) %collective-permute-start.7) | collective-permute-done | bytes 917536 | tf_op jit(solution)/shard_map/ppermute | solution.py:160
  119.9 0.9 copy-done.3
  120.8 3.3 %copy-done.2 = bf16[3584,1152]{1,0:T(8,128)(2,1)S(1)} copy-done((bf16[3584,1152]{1,0:T(8,128)(2,1)S(1)}, bf16[3584,1152]{1,0:T(8,128)(2,1)}, u32[]{:S(2)}) %copy-start.2) | copy-done | bytes 8257560
  124.2 1.2 copy-done.4
  125.4 1.0 copy-done.5
  126.4 12.9 %shard_map.113 = (bf16[256,1920]{1,0:T(8,128)(2,1)}, f32[256,1792]{1,0:T(8,128)S(1)}, f32[256,1]{1,0:T(8,128)S(1)}, f32[256,1]{1,0:T(8,128)S(1)}) custom-call(s32[1]{0:T(128)} %bitcast.3.half_ref, bf16[256,1792]{1,0:T(8,128)(2,1)S(1)} %broadcast_select_fusion.own_ref, bf16[256,1792]{1,0:T(8,128)(2,1)S(1)} %copy-done.4, f32[2,1792]{1,0:T(2,128)S(1)} %reshape.408.gain_ref, ...), custom_call_target="tpu_custom_call" | custom-call | flops 5000000000 | bytes 14000000 | tf_op jit(solution)/shard_map/pallas_call | solution.py:128
  139.3 0.1 collective-permute-start.8
  139.5 0.1 copy.48
  139.6 0.1 eq.167
  139.8 0.1 fusion.40
  139.9 2.3 %collective-permute-done.8 = bf16[256,1920]{1,0:T(8,128)(2,1)} collective-permute-done((bf16[256,1920]{1,0:T(8,128)(2,1)}, bf16[256,1920]{1,0:T(8,128)(2,1)}, u32[]{:S(2)}, u32[]{:S(2)}) %collective-permute-start.8) | collective-permute-done | bytes 983072 | tf_op jit(solution)/shard_map/ppermute | solution.py:160
  142.2 1.1 add_reduce_fusion
  143.3 1.7 subtract_convert_fusion
  145.0 0.5 fusion.23
  145.5 1.4 fusion.11
  147.0 4.9 %all-to-all-start.1 = ((bf16[64,8,896]{2,1,0:T(8,128)(2,1)}), bf16[64,8,896]{2,1,0:T(8,128)(2,1)S(1)}, u32[]{:S(2)}, u32[]{:S(2)}) async-start(bf16[64,8,896]{2,1,0:T(8,128)(2,1)} %fusion.11), calls=%async_computation.1 | async-start | bytes 1835008 | tf_op jit(solution)/shard_map/all_to_all | solution.py:290
  151.9 0.2 convert_reduce_fusion.1
  152.1 17.3 %all-to-all-done.1 = bf16[64,8,896]{2,1,0:T(8,128)(2,1)S(1)} async-done(((bf16[64,8,896]{2,1,0:T(8,128)(2,1)}), bf16[64,8,896]{2,1,0:T(8,128)(2,1)S(1)}, u32[]{:S(2)}, u32[]{:S(2)}) %all-to-all-start.1) | async-done | bytes 917536 | tf_op jit(solution)/shard_map/all_to_all | solution.py:290
  169.4 0.4 convolution_convert_fusion.3
  169.8 0.4 convolution_convert_fusion.2
  170.3 0.7 pad_maximum_fusion
  171.0 0.8 fusion.25
  (79 shorter events, 1.7 us)
Async XLA Ops:
  7.2 2.6 %copy-start = (bf16[80,1792]{1,0:T(8,128)(2,1)S(1)}, bf16[80,1792]{1,0:T(8,128)(2,1)}, u32[]{:S(2)}) copy-start(bf16[80,1792]{1,0:T(8,128)(2,1)} %param.12) | copy-start | bytes 860164
  7.2 3.6 %copy-start.11 = (bf16[128,1280]{1,0:T(8,128)(2,1)S(1)}, bf16[128,1280]{1,0:T(8,128)(2,1)}, u32[]{:S(2)}) copy-start(bf16[128,1280]{1,0:T(8,128)(2,1)} %param.10) | copy-start | bytes 983044
  7.2 3.6 %copy-start.10 = (bf16[64,5120]{1,0:T(8,128)(2,1)S(1)}, bf16[64,5120]{1,0:T(8,128)(2,1)}, u32[]{:S(2)}) copy-start(bf16[64,5120]{1,0:T(8,128)(2,1)} %param.11) | copy-start | bytes 1966084
  7.2 9.6 %copy-start.9 = (s32[64,192]{1,0:T(8,128)S(1)}, s32[64,192]{1,0:T(8,128)}, u32[]{:S(2)}) copy-start(s32[64,192]{1,0:T(8,128)} %param.15) | copy-start | bytes 147460
  7.2 68.7 %all-gather.3.cloned.1.call-start = ((), (), s32[]{:S(2)}) async-start(), calls=%async_computation.2 | async-start | bytes 6963200 | tf_op jit(solution)/shard_map/all_gather | solution.py:206
  10.9 14.1 %collective-permute-start = (bf16[192,1280]{1,0:T(8,128)(2,1)S(1)}, bf16[192,1280]{1,0:T(8,128)(2,1)S(1)}, u32[]{:S(2)}, u32[]{:S(2)}) collective-permute-start(bf16[192,1280]{1,0:T(8,128)(2,1)S(1)} %dynamic-slice_dynamic-update-slice_fusion.1), channel_id=1, source_target_pairs={{0,32},{32,64},{64,96},{96,0},{1,33},{33,65},{65,97},{97,1},{2,34}... | collective-permute-start | bytes 1474568 | tf_op jit(solution)/shard_map/ppermute | solution.py:218
  12.5 24.2 %collective-permute-start.1 = (bf16[192,1280]{1,0:T(8,128)(2,1)S(1)}, bf16[192,1280]{1,0:T(8,128)(2,1)S(1)}, u32[]{:S(2)}, u32[]{:S(2)}) collective-permute-start(bf16[192,1280]{1,0:T(8,128)(2,1)S(1)} %dynamic-slice_dynamic-update-slice_fusion.1), channel_id=1, source_target_pairs={{0,64},{32,96},{64,0},{96,32},{1,65},{33,97},{65,1},{97,33},{2,66}... | collective-permute-start | bytes 1474568 | tf_op jit(solution)/shard_map/ppermute | solution.py:218
  15.3 21.5 %collective-permute-start.2 = (bf16[192,1280]{1,0:T(8,128)(2,1)S(1)}, bf16[192,1280]{1,0:T(8,128)(2,1)S(1)}, u32[]{:S(2)}, u32[]{:S(2)}) collective-permute-start(bf16[192,1280]{1,0:T(8,128)(2,1)S(1)} %dynamic-slice_dynamic-update-slice_fusion.1), channel_id=1, source_target_pairs={{0,96},{32,0},{64,32},{96,64},{1,97},{33,1},{65,33},{97,65},{2,98}... | collective-permute-start | bytes 1474568 | tf_op jit(solution)/shard_map/ppermute | solution.py:218
  16.7 20.7 %collective-permute-start.3 = (bf16[192,1280]{1,0:T(8,128)(2,1)S(1)}, bf16[192,1280]{1,0:T(8,128)(2,1)S(1)}, u32[]{:S(2)}, u32[]{:S(2)}) collective-permute-start(bf16[192,1280]{1,0:T(8,128)(2,1)S(1)} %dynamic-slice_dynamic-update-slice_fusion.1), channel_id=1, source_target_pairs={{0,1},{1,0},{2,3},{3,2},{4,5},{5,4},{6,7},{7,6},{8,9},{9,8},{10,11... | collective-permute-start | bytes 1474568 | tf_op jit(solution)/shard_map/ppermute | solution.py:160
  25.0 12.4 %collective-permute-start.4 = (bf16[192,1280]{1,0:T(8,128)(2,1)S(1)}, bf16[192,1280]{1,0:T(8,128)(2,1)S(1)}, u32[]{:S(2)}, u32[]{:S(2)}) collective-permute-start(bf16[192,1280]{1,0:T(8,128)(2,1)S(1)} %collective-permute-done), channel_id=1, source_target_pairs={{0,1},{1,0},{2,3},{3,2},{4,5},{5,4},{6,7},{7,6},{8,9},{9,8},{10,11... | collective-permute-start | bytes 1474568 | tf_op jit(solution)/shard_map/ppermute | solution.py:160
  36.7 1.9 %collective-permute-start.5 = (bf16[192,1280]{1,0:T(8,128)(2,1)S(1)}, bf16[192,1280]{1,0:T(8,128)(2,1)S(1)}, u32[]{:S(2)}, u32[]{:S(2)}) collective-permute-start(bf16[192,1280]{1,0:T(8,128)(2,1)S(1)} %collective-permute-done.1), channel_id=1, source_target_pairs={{0,1},{1,0},{2,3},{3,2},{4,5},{5,4},{6,7},{7,6},{8,9},{9,8},{10,11... | collective-permute-start | bytes 1474568 | tf_op jit(solution)/shard_map/ppermute | solution.py:160
  36.8 2.5 %collective-permute-start.6 = (bf16[192,1280]{1,0:T(8,128)(2,1)S(1)}, bf16[192,1280]{1,0:T(8,128)(2,1)S(1)}, u32[]{:S(2)}, u32[]{:S(2)}) collective-permute-start(bf16[192,1280]{1,0:T(8,128)(2,1)S(1)} %collective-permute-done.2), channel_id=1, source_target_pairs={{0,1},{1,0},{2,3},{3,2},{4,5},{5,4},{6,7},{7,6},{8,9},{9,8},{10,11... | collective-permute-start | bytes 1474568 | tf_op jit(solution)/shard_map/ppermute | solution.py:160
  80.3 1.1 copy-start.7
  80.4 1.3 copy-start.8
  86.0 27.2 %all-to-all-start = ((bf16[64,16,448]{2,1,0:T(8,128)(2,1)}), bf16[64,16,448]{2,1,0:T(8,128)(2,1)S(1)}, u32[]{:S(2)}, u32[]{:S(2)}) async-start(bf16[64,16,448]{2,1,0:T(8,128)(2,1)} %bitcast.30), calls=%async_computation | async-start | bytes 2097152 | tf_op jit(solution)/shard_map/all_to_all | solution.py:259
  114.1 2.9 %copy-start.6 = (bf16[256,1792]{1,0:T(8,128)(2,1)S(1)}, bf16[256,1792]{1,0:T(8,128)(2,1)}, u32[]{:S(2)}) copy-start(bf16[256,1792]{1,0:T(8,128)(2,1)} %param.14) | copy-start | bytes 2752516
  114.2 3.3 %copy-start.1 = (s32[1,256]{1,0:T(1,128)S(1)}, s32[1,256]{1,0:T(1,128)}, u32[]{:S(2)}) copy-start(s32[1,256]{1,0:T(1,128)} %seg_row_ref.1) | copy-start | bytes 3076
  114.2 3.4 %copy-start.12 = (f32[3584]{0:T(1024)S(1)}, f32[3584]{0:T(1024)}, u32[]{:S(2)}) copy-start(f32[3584]{0:T(1024)} %param.17) | copy-start | bytes 43012
  117.2 2.7 %collective-permute-start.7 = (bf16[256,1792]{1,0:T(8,128)(2,1)S(1)}, bf16[256,1792]{1,0:T(8,128)(2,1)S(1)}, u32[]{:S(2)}, u32[]{:S(2)}) collective-permute-start(bf16[256,1792]{1,0:T(8,128)(2,1)S(1)} %broadcast_select_fusion.own_ref), channel_id=1, source_target_pairs={{0,1},{1,0},{2,3},{3,2},{4,5},{5,4},{6,7},{7,6},{8,9},{9,8},{10,11... | collective-permute-start | bytes 2752520 | tf_op jit(solution)/shard_map/ppermute | solution.py:160
  119.9 0.9 copy-start.3
  120.8 3.3 %copy-start.2 = (bf16[3584,1152]{1,0:T(8,128)(2,1)S(1)}, bf16[3584,1152]{1,0:T(8,128)(2,1)}, u32[]{:S(2)}) copy-start(bf16[3584,1152]{1,0:T(8,128)(2,1)} %weight_ref.1) | copy-start | bytes 24772612
  124.2 1.2 copy-start.4
  125.4 1.0 copy-start.5
  139.3 2.9 %collective-permute-start.8 = (bf16[256,1920]{1,0:T(8,128)(2,1)}, bf16[256,1920]{1,0:T(8,128)(2,1)}, u32[]{:S(2)}, u32[]{:S(2)}) collective-permute-start(bf16[256,1920]{1,0:T(8,128)(2,1)} %get-tuple-element.7), channel_id=1, source_target_pairs={{0,1},{1,0},{2,3},{3,2},{4,5},{5,4},{6,7},{7,6},{8,9},{9,8},{10,11... | collective-permute-start | bytes 2949128 | tf_op jit(solution)/shard_map/ppermute | solution.py:160
  147.0 22.4 %all-to-all-start.1 = ((bf16[64,8,896]{2,1,0:T(8,128)(2,1)}), bf16[64,8,896]{2,1,0:T(8,128)(2,1)S(1)}, u32[]{:S(2)}, u32[]{:S(2)}) async-start(bf16[64,8,896]{2,1,0:T(8,128)(2,1)} %fusion.11), calls=%async_computation.1 | async-start | bytes 1835008 | tf_op jit(solution)/shard_map/all_to_all | solution.py:290
Sparse Core Ops, SparseCore 0:
  10.8 65.0 all-gather.2

commit v3 on v2

--- a/solution.py
+++ b/solution.py
@@ -37,11 +37,23 @@
     scaled_ref,
     sgrad_ref,
     bias_ref,
+    held_ref,
+    sems,
 ):
     bf16, f32 = jnp.bfloat16, jnp.float32
     rows, slab = own_ref.shape
     group = weight_ref.shape[1]
     heads = group // HEAD_DIM - 2
+    width = held_ref.shape[2]
+    pieces = group // width
+    copies = [
+        pltpu.make_async_copy(
+            weight_ref.at[:, n * width : (n + 1) * width], held_ref.at[n], sems.at[n]
+        )
+        for n in range(pieces)
+    ]
+    for copy in copies:
+        copy.start()
     t = half_ref[0]
     own_at = pl.multiple_of(t * slab, HEAD_DIM)
     other_at = pl.multiple_of((1 - t) * slab, HEAD_DIM)
@@ -58,14 +70,11 @@
     inv = lax.rsqrt(jnp.sum(squares, axis=1, keepdims=True) / (2 * slab) + epsilon)
     inv_ref[...] = inv
 
-    width = 384
-
-    @pl.loop(0, group // width)
-    def _(n):
-        cols = pl.ds(pl.multiple_of(n * width, width), width)
-        value = dot(normed_ref[...], weight_ref[:, cols])
-        unscaled_ref[:, cols] = value
-        scaled_ref[:, cols] = (value * inv).astype(bf16)
+    for n in range(pieces):
+        copies[n].wait()
+        value = dot(normed_ref[...], held_ref[n])
+        unscaled_ref[:, n * width : (n + 1) * width] = value
+        scaled_ref[:, n * width : (n + 1) * width] = (value * inv).astype(bf16)
 
     place_u = lax.broadcasted_iota(jnp.int32, (rows, rows), 0)
     place_t = lax.broadcasted_iota(jnp.int32, (rows, rows), 1)
@@ -107,17 +116,20 @@
 
     step = 256
 
+    def rows_of(rows_at):
+        return jnp.concatenate([held_ref[n, rows_at, :] for n in range(pieces)], axis=1)
+
     @pl.loop(0, slab // step)
     def _(n):
         at = pl.multiple_of(n * step, step)
         rows_at = pl.ds(pl.multiple_of(other_at + at, HEAD_DIM), step)
-        give_ref[:, pl.ds(at, step)] = dot(sgrad_ref[...], weight_ref[rows_at, :], NT).astype(bf16)
+        give_ref[:, pl.ds(at, step)] = dot(sgrad_ref[...], rows_of(rows_at), NT).astype(bf16)
 
     @pl.loop(0, slab // step)
     def _(n):
         at = pl.multiple_of(n * step, step)
         rows_at = pl.ds(pl.multiple_of(own_at + at, HEAD_DIM), step)
-        keep_ref[:, pl.ds(at, step)] = dot(sgrad_ref[...], weight_ref[rows_at, :], NT)
+        keep_ref[:, pl.ds(at, step)] = dot(sgrad_ref[...], rows_of(rows_at), NT)
 
 
 def attend(half, own, other, norm_gain, qkv_weight, upstream, segments):
@@ -133,7 +145,8 @@
             jax.ShapeDtypeStruct((rows, 1), f32),
             jax.ShapeDtypeStruct((rows, 1), f32),
         ),
-        in_specs=[pl.BlockSpec(memory_space=pltpu.SMEM)] + [vmem] * 7,
+        in_specs=[pl.BlockSpec(memory_space=pltpu.SMEM), vmem, vmem, vmem]
+        + [pl.BlockSpec(memory_space=pl.ANY), vmem, vmem, vmem],
         out_specs=(vmem,) * 4,
         scratch_shapes=[
             pltpu.VMEM((rows, 2 * slab), bf16),
@@ -141,8 +154,10 @@
             pltpu.VMEM((rows, group), bf16),
             pltpu.VMEM((rows, group), bf16),
             pltpu.VMEM((rows, rows), f32),
+            pltpu.VMEM((group // 384, 2 * slab, 384), bf16),
+            pltpu.SemaphoreType.DMA((group // 384,)),
         ],
-        compiler_params=pltpu.CompilerParams(vmem_limit_bytes=40 * 1024 * 1024),
+        compiler_params=pltpu.CompilerParams(vmem_limit_bytes=28 * 1024 * 1024),
         cost_estimate=pl.CostEstimate(flops=5_000_000_000, bytes_accessed=14_000_000, transcendentals=500_000),
     )(
         half.reshape(1),
@@ -156,8 +171,254 @@
     )
 
 
+def roll_half(x):
+    return pltpu.roll(x.astype(jnp.float32), 64, 1).astype(x.dtype)
+
+
+A_ROWS, A_TAIL = 192, 96
+B_ROWS, B_TAIL = 208, 112
+A_PIECE = 3 * A_ROWS + A_TAIL
+B_PIECE = 3 * B_ROWS + B_TAIL
+
+
+def pack_kernel(e_ref, am_ref, at_ref, vm_ref, vt_ref, a_ref, b_ref):
+    k = am_ref.shape[0]
+    cut = A_ROWS - k
+    for n in range(3):
+        cols = slice(n * 128, (n + 1) * 128)
+        a_ref[n * A_ROWS : n * A_ROWS + k, :] = am_ref[:, cols]
+        a_ref[n * A_ROWS + k : (n + 1) * A_ROWS, :] = vm_ref[:cut, cols]
+        b_ref[n * B_ROWS : (n + 1) * B_ROWS, :] = vm_ref[cut:, cols]
+    odd = e_ref[0] % 2 == 1
+    tail = jnp.concatenate([at_ref[...], vt_ref[...]], axis=0).astype(jnp.float32)
+    moved = pltpu.roll(tail, 64, 1)
+    first = jnp.where(odd, moved, tail)
+    second = jnp.where(odd, tail, moved)
+    lane = lax.broadcasted_iota(jnp.int32, (B_TAIL, 128), 1)
+    a_ref[3 * A_ROWS :, :] = jnp.where(
+        lane[:A_TAIL] < 64, first[:A_TAIL], second[A_TAIL:A_ROWS]
+    ).astype(a_ref.dtype)
+    high = jnp.concatenate(
+        [second[A_ROWS + B_TAIL :], jnp.zeros((2 * B_TAIL - B_ROWS, 128), jnp.float32)], axis=0
+    )
+    b_ref[3 * B_ROWS :, :] = jnp.where(
+        lane < 64, first[A_ROWS : A_ROWS + B_TAIL], high
+    ).astype(b_ref.dtype)
+
+
+def pack_weights(e, audio_main, audio_tail, vision_main, vision_tail):
+    vmem = pl.BlockSpec(memory_space=pltpu.VMEM)
+    return pl.pallas_call(
+        pack_kernel,
+        out_shape=(
+            jax.ShapeDtypeStruct((A_PIECE, 128), jnp.bfloat16),
+            jax.ShapeDtypeStruct((B_PIECE, 128), jnp.bfloat16),
+        ),
+        in_specs=[pl.BlockSpec(memory_space=pltpu.SMEM)] + [vmem] * 4,
+        out_specs=(vmem,) * 2,
+        compiler_params=pltpu.CompilerParams(vmem_limit_bytes=8 * 1024 * 1024),
+        cost_estimate=pl.CostEstimate(flops=0, bytes_accessed=800_000, transcendentals=0),
+    )(e.reshape(1), audio_main, audio_tail, vision_main, vision_tail)
+
+
+def encode_kernel(
+    a_at_ref,
+    b_at_ref,
+    ga0,
+    ga1,
+    ga2,
+    ga3,
+    gb0,
+    gb1,
+    gb2,
+    gb3,
+    own_ref,
+    other_ref,
+    cell_ref,
+    out_ref,
+    w_ref,
+    ta_ref,
+    tb_ref,
+    x_ref,
+    enc_ref,
+    sems,
+):
+    bf16, f32 = jnp.bfloat16, jnp.float32
+    audio_width = x_ref.shape[3]
+    audio_k = audio_width // 16
+    vision_k = 4 * audio_k
+    cut = A_ROWS - audio_k
+    pltpu.make_async_copy(own_ref, x_ref.at[0], sems.at[0]).start()
+    pltpu.make_async_copy(other_ref, x_ref.at[1], sems.at[1]).start()
+    for m, (ga, gb) in enumerate(((ga0, gb0), (ga1, gb1), (ga2, gb2), (ga3, gb3))):
+
+        @pl.loop(0, 4)
+        def _(n):
+            p = m * 4 + n
+            a_at = a_at_ref[p]
+            b_at = b_at_ref[p]
+            base_a = pl.multiple_of(n * A_PIECE, 16)
+            base_b = pl.multiple_of(n * B_PIECE, 16)
+            audio_at = pl.multiple_of(a_at * audio_k, 16)
+            low_at = pl.multiple_of(audio_width + a_at * vision_k, 16)
+            high_at = pl.multiple_of(audio_width + b_at * vision_k + cut, 16)
+            for c in range(3):
+                pltpu.make_async_copy(
+                    ga.at[pl.ds(base_a + c * A_ROWS, audio_k), :],
+                    w_ref.at[c, pl.ds(audio_at, audio_k), :],
+                    sems.at[2],
+                ).start()
+                pltpu.make_async_copy(
+                    ga.at[pl.ds(base_a + c * A_ROWS + audio_k, cut), :],
+                    w_ref.at[c, pl.ds(low_at, cut), :],
+                    sems.at[2],
+                ).start()
+                pltpu.make_async_copy(
+                    gb.at[pl.ds(base_b + c * B_ROWS, B_ROWS), :],
+                    w_ref.at[c, pl.ds(high_at, B_ROWS), :],
+                    sems.at[2],
+                ).start()
+            pltpu.make_async_copy(
+                ga.at[pl.ds(base_a + 3 * A_ROWS, A_TAIL), :], ta_ref.at[p], sems.at[3]
+            ).start()
+            pltpu.make_async_copy(
+                gb.at[pl.ds(base_b + 3 * B_ROWS, B_TAIL), :], tb_ref.at[p], sems.at[4]
+            ).start()
+
+    count = cell_ref.shape[1]
+    cells = out_ref.shape[0]
+    line = lax.broadcasted_iota(jnp.int32, (cells, count), 0)
+    first = jnp.where(line == cell_ref[0:1, :], 1.0, 0.0).astype(bf16)
+    second = jnp.where(line == cell_ref[1:2, :], 1.0, 0.0).astype(bf16)
+
+    pltpu.make_async_copy(ta_ref, ta_ref, sems.at[3]).wait()
+    pltpu.make_async_copy(tb_ref, tb_ref, sems.at[4]).wait()
+
+    @pl.loop(0, 16)
+    def _(p):
+        a_at = a_at_ref[p]
+        b_at = b_at_ref[p]
+        audio_at = pl.multiple_of(a_at * audio_k, 16)
+        low_at = pl.multiple_of(audio_width + a_at * vision_k, 16)
+        high_at = pl.multiple_of(audio_width + b_at * vision_k + cut, 16)
+        ta = ta_ref[p]
+        w_ref[3, pl.ds(audio_at, audio_k), :] = ta[:audio_k]
+        w_ref[3, pl.ds(low_at, A_TAIL - audio_k), :] = ta[audio_k:]
+        w_ref[3, pl.ds(low_at + (A_TAIL - audio_k), A_TAIL), :] = roll_half(ta)
+        tb = tb_ref[p]
+        w_ref[3, pl.ds(high_at, B_TAIL), :] = tb
+        w_ref[3, pl.ds(high_at + B_TAIL, B_ROWS - B_TAIL), :] = roll_half(tb)[: B_ROWS - B_TAIL]
+
+    pltpu.make_async_copy(own_ref, x_ref.at[0], sems.at[0]).wait()
+    pltpu.make_async_copy(other_ref, x_ref.at[1], sems.at[1]).wait()
+    pltpu.make_async_copy(w_ref.at[0:3], w_ref.at[0:3], sems.at[2]).wait()
+
+    halves, n_enc = x_ref.shape[:2]
+    audio = 64
+    vision = 32
+    n_audio = halves * n_enc * audio
+    for c in (0, 2):
+        cols = slice(c * 128, (c + 2) * 128)
+
+        def weights(at, size):
+            return jnp.concatenate([w_ref[c, at : at + size, :], w_ref[c + 1, at : at + size, :]], axis=1)
+
+        rows = x_ref[:, :, :audio, :].reshape(n_audio, audio_width)
+        enc_ref[:n_audio, cols] = dot(rows, weights(0, audio_width)).astype(bf16)
+        total = jnp.zeros((halves * n_enc * vision, 256), f32)
+        for i in range(4):
+            rows = x_ref[:, :, audio + i * vision : audio + (i + 1) * vision, :]
+            rows = rows.reshape(halves * n_enc * vision, audio_width)
+            total = total + dot(rows, weights((i + 1) * audio_width, audio_width))
+        enc_ref[n_audio:, cols] = total.astype(bf16)
+
+    main = enc_ref[:, :384]
+    out_ref[:, :384] = dot(first, main).astype(bf16)
+    out_ref[:, 384:768] = dot(second, main).astype(bf16)
+    last = enc_ref[:, 384:].astype(f32)
+    lane = lax.broadcasted_iota(jnp.int32, last.shape, 1)
+    last = jnp.where(lane < 64, last, 0.0)
+    moved = pltpu.roll(last, 64, 1)
+    out_ref[:, 768:] = (dot(first, last.astype(bf16)) + dot(second, moved.astype(bf16))).astype(bf16)
+
+
+def encode(a_at, b_at, pieces_a, pieces_b, own, other, cells, n_cells):
+    bf16 = jnp.bfloat16
+    n_enc, rows, width = own.shape
+    smem = pl.BlockSpec(memory_space=pltpu.SMEM)
+    vmem = pl.BlockSpec(memory_space=pltpu.VMEM)
+    anywhere = pl.BlockSpec(memory_space=pl.ANY)
+    return pl.pallas_call(
+        encode_kernel,
+        out_shape=jax.ShapeDtypeStruct((n_cells, 896), bf16),
+        in_specs=[smem, smem] + [anywhere] * 10 + [vmem],
+        out_specs=vmem,
+        scratch_shapes=[
+            pltpu.VMEM((4, 5 * width, 128), bf16),
+            pltpu.VMEM((16, A_TAIL, 128), bf16),
+            pltpu.VMEM((16, B_TAIL, 128), bf16),
+            pltpu.VMEM((2, n_enc, rows, width), bf16),
+            pltpu.VMEM((cells.shape[1], 512), bf16),
+            pltpu.SemaphoreType.DMA((5,)),
+        ],
+        compiler_params=pltpu.CompilerParams(vmem_limit_bytes=28 * 1024 * 1024),
+        cost_estimate=pl.CostEstimate(
+            flops=3_000_000_000, bytes_accessed=11_000_000, transcendentals=0
+        ),
+    )(a_at, b_at, *pieces_a, *pieces_b, own, other, cells)
+
+
+def place_kernel(e_row_ref, arrived_ref, text_ref, filled_ref, out_ref):
+    bf16, f32 = jnp.bfloat16, jnp.float32
+    rows = out_ref.shape[0]
+    each = arrived_ref.shape[0] // 4
+    line = lax.broadcasted_iota(jnp.int32, (rows, each), 0)
+    first = jnp.where(line == e_row_ref[0:1, :], 1.0, 0.0).astype(bf16)
+    second = jnp.where(line == e_row_ref[1:2, :], 1.0, 0.0).astype(bf16)
+    both = jnp.concatenate([first, second], axis=1)
+    taken = filled_ref[...] > 0.5
+    lane = lax.broadcasted_iota(jnp.int32, (rows, 128), 1)
+    low = []
+    high = []
+    for e in range(4):
+        at = slice(e * each, (e + 1) * each)
+        main = jnp.concatenate([arrived_ref[at, :384], arrived_ref[at, 384:768]], axis=0)
+        cols = slice(e * 384, (e + 1) * 384)
+        text = text_ref[:, cols].astype(f32)
+        out_ref[:, cols] = jnp.where(taken, dot(both, main), text).astype(bf16)
+        last = arrived_ref[at, 768:]
+        low.append(dot(first, last))
+        high.append(dot(second, last))
+    for q in range(2):
+        left = low[2 * q] + pltpu.roll(high[2 * q], 64, 1)
+        right = pltpu.roll(low[2 * q + 1], 64, 1) + high[2 * q + 1]
+        cols = slice(1536 + q * 128, 1536 + (q + 1) * 128)
+        text = text_ref[:, cols].astype(f32)
+        out_ref[:, cols] = jnp.where(taken, jnp.where(lane < 64, left, right), text).astype(bf16)
+
+
+def place(spots, arrived, text, filled):
+    vmem = pl.BlockSpec(memory_space=pltpu.VMEM)
+    return pl.pallas_call(
+        place_kernel,
+        out_shape=jax.ShapeDtypeStruct(text.shape, text.dtype),
+        in_specs=[vmem] * 4,
+        out_specs=vmem,
+        compiler_params=pltpu.CompilerParams(vmem_limit_bytes=12 * 1024 * 1024),
+        cost_estimate=pl.CostEstimate(flops=300_000_000, bytes_accessed=3_000_000, transcendentals=0),
+    )(spots, arrived, text, filled)
+
+
 def swap(x):
     return lax.ppermute(x, "tp", [(0, 1), (1, 0)])
+
+
+def shift_y(x, k):
+    return lax.ppermute(x, "seq", [(i, i // 4 * 4 + (i % 4 + k) % 4) for i in range(16)])
+
+
+def shift_z(x, k):
+    return lax.ppermute(x, "seq", [(i, (i // 4 + k) % 4 * 4 + i % 4) for i in range(16)])
 
 
 def ranks(dest):
@@ -191,21 +452,29 @@
     audio_count, audio_width = audio_rows.shape
     vision_count = vision_rows.shape[0]
     merge = vision_weight.shape[1]
-    k_rows = audio_weight.shape[0]
     cap = 4
     wide = slab // 128 // n_enc * 128
-    tail = slab // n_enc - wide
 
     def columns(w):
-        w = w.reshape(-1, slab)
-        main = lax.dynamic_slice_in_dim(w, e * wide, wide, 1)
-        last = lax.dynamic_slice_in_dim(w, n_enc * wide + e * tail, tail, 1)
-        return jnp.concatenate([main, last], axis=1)
-
-    shard = jnp.concatenate([columns(audio_weight), columns(vision_weight)], axis=0)
-    gathered = lax.all_gather(shard, "seq", axis=0, tiled=False)
-    w_audio = gathered[:, :k_rows].reshape(audio_width, wide + tail)
-    w_vision = gathered[:, k_rows:].reshape(audio_width * merge, wide + tail)
+        axis = w.ndim - 1
+        main = lax.dynamic_slice_in_dim(w, e * wide, wide, axis)
+        last = lax.dynamic_slice_in_dim(w, n_enc * wide + (e // 2) * 128, 128, axis)
+        return main.reshape(-1, wide), last.reshape(-1, 128)
+
+    piece_a, piece_b = pack_weights(e, *columns(audio_weight), *columns(vision_weight))
+    hops = (1, 3, 2)
+    along_y = [piece_a] + [shift_y(piece_a, k) for k in hops]
+    along_z = [piece_b] + [shift_z(piece_b, k) for k in hops]
+    along_y, along_z = lax.optimization_barrier((along_y, along_z))
+    stack_a = jnp.concatenate(along_y, axis=0)
+    stack_b = jnp.concatenate(along_z, axis=0)
+    stack_a, stack_b = lax.optimization_barrier((stack_a, stack_b))
+    pieces_a = [stack_a] + [shift_z(stack_a, k) for k in hops]
+    pieces_b = [stack_b] + [shift_y(stack_b, k) for k in hops]
+    z, y = j // 4, j % 4
+    back = jnp.array((0,) + hops, jnp.int32)
+    a_at = (((z - back) % 4)[:, None] * 4 + ((y - back) % 4)[None, :]).reshape(-1)
+    b_at = (((y - back) % 4)[:, None] + ((z - back) % 4)[None, :] * 4).reshape(-1)
 
     ah, vh = audio_count // 2, vision_count // 2
     audio_half = lax.dynamic_slice_in_dim(audio_rows, t * ah, ah, 0)
@@ -214,56 +483,36 @@
         [audio_half] + [vision_half[:, i * audio_width : (i + 1) * audio_width] for i in range(merge)],
         axis=0,
     )
-    own = [packed] + [
-        lax.ppermute(packed, "enc", [(i, (i + k) % n_enc) for i in range(n_enc)])
-        for k in range(1, n_enc)
-    ]
-    other = [swap(b) for b in own]
-    blocks = jnp.stack(own + other)
-    x_audio = blocks[:, :ah].reshape(2 * n_enc * ah, audio_width)
-    x_vision = jnp.concatenate(
-        [
-            blocks[:, ah + i * vh : ah + (i + 1) * vh].reshape(2 * n_enc * vh, audio_width)
-            for i in range(merge)
-        ],
-        axis=1,
-    )
-    audio_proj = jnp.dot(x_audio, w_audio, preferred_element_type=f32).astype(bf16)
-    vision_proj = jnp.dot(x_vision, w_vision, preferred_element_type=f32).astype(bf16)
-    encoded = jnp.concatenate([audio_proj, vision_proj], axis=0)
-
-    order = (e - jnp.arange(n_enc)) % n_enc
+    own = lax.all_gather(packed, "enc", axis=0, tiled=False)
+    other = swap(own)
+
     line = row_target.reshape(n_enc, n_seq, enc_rows)[:, j]
     line_dest = line // length
     line_slot = line_dest * (n_enc * cap) + jnp.arange(n_enc)[:, None] * cap + ranks(line_dest)
-    line_slot = line_slot[order]
     a_slot = line_slot[:, :audio_count].reshape(n_enc, 2, ah)
     v_slot = line_slot[:, audio_count:].reshape(n_enc, 2, vh)
     halves = jnp.stack([t, 1 - t])
     a_slot = jnp.moveaxis(a_slot, 1, 0)[halves].reshape(-1)
     v_slot = jnp.moveaxis(v_slot, 1, 0)[halves].reshape(-1)
     row_slot = jnp.concatenate([a_slot, v_slot])
-    selector = (jnp.arange(senders * n_enc * cap)[:, None] == row_slot[None, :]).astype(bf16)
-    outgoing = jnp.dot(selector, encoded, preferred_element_type=f32).astype(bf16)
-    outgoing = outgoing.reshape(senders, n_enc * cap, wide + tail)
+    cell = row_slot // 16 * 8 + row_slot % 8
+    part = row_slot // 8 % 2
+    cells = jnp.stack([jnp.where(part == 0, cell, -1), jnp.where(part == 1, cell, -1)])
 
     dest = row_target // length
     mine = (dest == self_index).astype(jnp.int32)
     rank_all = jnp.cumsum(mine, axis=1) - 1
     hot = (rank_all[:, :, None] == jnp.arange(cap)[None, None, :]) & (mine[:, :, None] == 1)
     incoming = jnp.sum(jnp.where(hot, (row_target % length)[:, :, None] + 1, 0), axis=1) - 1
-    by_line = incoming.reshape(n_enc, n_seq, cap).transpose(1, 0, 2).reshape(1, senders * cap)
-    placement = (jnp.arange(length)[:, None] == by_line).astype(bf16)
-    filled = jnp.max(placement, axis=1) > 0
-
-    arrived = lax.all_to_all(outgoing, ("enc", "seq"), split_axis=0, concat_axis=0, tiled=True)
-    arrived = arrived.reshape(n_enc, senders * cap, wide + tail)
-    placed = jnp.einsum("ps,esc->epc", placement, arrived, preferred_element_type=f32).astype(bf16)
-    placed = jnp.concatenate(
-        [placed[i, :, :wide] for i in range(n_enc)] + [placed[i, :, wide:] for i in range(n_enc)],
-        axis=1,
-    )
-    row_slab = jnp.where(filled[:, None], placed, text_rows)
+    by_line = incoming.reshape(2, 2, n_seq, cap).transpose(0, 2, 1, 3).reshape(2, -1)
+    filled = jnp.max(
+        (jnp.arange(length)[:, None] == incoming.reshape(1, -1)).astype(jnp.float32), axis=1, keepdims=True
+    )
+    outgoing = encode(a_at, b_at, pieces_a, pieces_b, own, other, cells, senders * 8)
+    arrived = lax.all_to_all(
+        outgoing.reshape(senders, 8, slab // 2), ("enc", "seq"), split_axis=0, concat_axis=0, tiled=True
+    )
+    row_slab = place(by_line, arrived.reshape(senders * 8, slab // 2), text_rows, filled)
 
     other_slab = swap(row_slab)
     give, keep, inv_rms, row_part = attend(
@@ -279,7 +528,6 @@
 
     half = slab // 2
     flat = jnp.arange(senders * 2 * cap)
-    slot_pos = incoming.reshape(-1)
     pos8 = jnp.broadcast_to(incoming[:, None, :], (senders, 2, cap)).reshape(-1, 1)
     part8 = (flat // cap % 2)[:, None]
     hits = pos8 == jnp.arange(length)[None, :]

time: 179 us -> 192 us (1.073)
  Pallas kernels: 12.9 us -> 25.1 us
  starting transfers between devices: 20.3 us -> 32.4 us
  waiting for transfers between devices: 93 us -> 86.2 us
  matrix products: 7.08 us -> 2.76 us
  local copies, waits for them, and re-layouts: 23.3 us -> 20.5 us
  other arithmetic: 7.35 us -> 9.42 us
    all_gather x1, waiting for transfers between devices: 35.3 us -> 10.7 us  [local(): own = lax.all_gather(packed, 'enc', axis=0, tiled=False)]
    ppermute x3 -> x12, waiting for transfers between devices: 16.2 us -> 38.7 us  [the longest x6 26.1 us: shift_z(): lax.ppermute(x, 'seq', [(i, (i // 4 + k) % 4 * 4 + i % 4) for i in range(...]
    ppermute x3 -> x12, starting transfers between devices: 5.81 us -> 21.6 us  [the longest x6 11.3 us: shift_z(): lax.ppermute(x, 'seq', [(i, (i // 4 + k) % 4 * 4 + i % 4) for i in range(...]
    pallas_call x0 -> x3, Pallas kernels: none -> 12.1 us  [the longest x1 11.4 us: encode(): pl.pallas_call(encode_kernel, out_shape=jax.ShapeDtypeStruct((n_cells, 89...]
    unnamed x37 -> x33, local copies, waits for them, and re-layouts: 7.28 us -> 15 us
    slice x5 -> x1, local copies, waits for them, and re-layouts: 5.92 us -> 0.18 us  [the longest x1 3.02 us: local(): w_vision = gathered[:, k_rows:].reshape(audio_width * merge, wide + tail)]
    dot_general x4 -> x0, matrix products: 4.31 us -> none  [the longest x1 2.08 us: local(): jnp.dot(x_vision, w_vision, preferred_element_type=f32).astype(bf16)]
    all_to_all x1, starting transfers between devices: 8.61 us -> 5.57 us  [local(): lax.all_to_all(outgoing.reshape(senders, 8, slab // 2), ('enc', 'seq'), s...]
  transfers between devices with their start and end apart: 12 -> 18, of which waited for: 9 -> 11; matrix products, arithmetic and copies ran while one was open for 4% -> 5% of each run, Pallas kernels for 0% -> 0%
where the time goes in v3:
time: 192 us; the launch traced here: 191 us
  waiting for transfers between devices  86.2 us (45%)
  starting transfers between devices  32.4 us (17%)
  Pallas kernels  25.1 us (13%)
  local copies, waits for them, and re-layouts  20.5 us (11%)
  between operations  14.4 us (8%)
  other arithmetic  9.42 us (5%)
  matrix products  2.76 us (1%)
    ppermute x6, waiting for transfers between devices, shift_z(): lax.ppermute(x, 'seq', [(i, (i // 4 + k) % 4 * 4 + i % 4) for i in range(...  26.1 us
    all_to_all x1, waiting for transfers between devices, local(): lax.all_to_all(outgoing.reshape(senders, 8, slab // 2), ('enc', 'seq'), s...  16.2 us
    all_to_all x1, waiting for transfers between devices, local(): lax.all_to_all(out8, ('enc', 'seq'), split_axis=0, concat_axis=0, tiled=T...  16 us
    unnamed x33, local copies, waits for them, and re-layouts  15 us
    pallas_call x1, Pallas kernels, attend(): pl.pallas_call(attend_kernel, out_shape=(jax.ShapeDtypeStruct((rows, slab...  13.1 us
    ppermute x6, waiting for transfers between devices, shift_y(): lax.ppermute(x, 'seq', [(i, i // 4 * 4 + (i % 4 + k) % 4) for i in range(...  12.6 us
    pallas_call x1, Pallas kernels, encode(): pl.pallas_call(encode_kernel, out_shape=jax.ShapeDtypeStruct((n_cells, 89...  11.4 us
    ppermute x6, starting transfers between devices, shift_z(): lax.ppermute(x, 'seq', [(i, (i // 4 + k) % 4 * 4 + i % 4) for i in range(...  11.3 us
  transfers between devices with their start and end apart: 18, of which 11 were waited for; matrix products, arithmetic and copies ran while one was open for 5% of the time, Pallas kernels for 0%

profile of v3, /device:TPU:0, one launch (start us, length us, event | category | flops | bytes accessed | tf_op | source)
XLA Modules:
  0.0 190.8 jit_solution(12182093825613667976)
XLA Ops:
  7.2 1.0 dynamic-slice_dynamic-update-slice_fusion
  8.3 0.9 dynamic-slice_dynamic-update-slice_fusion.4
  9.2 0.9 dynamic-slice_dynamic-update-slice_fusion.3
  10.1 0.9 dynamic-slice_dynamic-update-slice_fusion.2
  10.9 0.9 dynamic-slice_dynamic-update-slice_fusion.1
  11.8 0.8 copy-done.9
  12.9 0.7 constant_dynamic-slice_fusion.3.at_ref
  13.6 0.8 constant_dynamic-slice_fusion.4.am_ref
  14.6 2.1 %collective-permute-start.3 = (bf16[736,128]{1,0:T(8,128)(2,1)S(1)}, bf16[736,128]{1,0:T(8,128)(2,1)S(1)}, u32[]{:S(2)}, u32[]{:S(2)}) collective-permute-start(bf16[736,128]{1,0:T(8,128)(2,1)S(1)} %get-tuple-element.24), channel_id=1, source_target_pairs={{0,8},{2,10},{4,12},{6,14},{8,16},{10,18},{12,20},{14,22},{16,24},... | collective-permute-start | bytes 565256 | tf_op jit(solution)/shard_map/ppermute | solution.py:421
  16.7 2.2 %collective-permute-start.4 = (bf16[736,128]{1,0:T(8,128)(2,1)S(1)}, bf16[736,128]{1,0:T(8,128)(2,1)S(1)}, u32[]{:S(2)}, u32[]{:S(2)}) collective-permute-start(bf16[736,128]{1,0:T(8,128)(2,1)S(1)} %get-tuple-element.24), channel_id=1, source_target_pairs={{0,24},{2,26},{4,28},{6,30},{8,0},{10,2},{12,4},{14,6},{16,8},{18,... | collective-permute-start | bytes 565256 | tf_op jit(solution)/shard_map/ppermute | solution.py:421
  18.9 1.8 collective-permute-start.5
  20.7 1.6 collective-permute-start
  22.2 1.7 collective-permute-start.1
  24.1 0.4 convert_reduce_fusion
  24.5 2.8 %collective-permute-done = bf16[672,128]{1,0:T(8,128)(2,1)S(1)} collective-permute-done((bf16[672,128]{1,0:T(8,128)(2,1)S(1)}, bf16[672,128]{1,0:T(8,128)(2,1)S(1)}, u32[]{:S(2)}, u32[]{:S(2)}) %collective-permute-start) | collective-permute-done | bytes 172064 | tf_op jit(solution)/shard_map/ppermute | solution.py:417
  27.3 2.0 %collective-permute-start.2 = (bf16[672,128]{1,0:T(8,128)(2,1)S(1)}, bf16[672,128]{1,0:T(8,128)(2,1)}, u32[]{:S(2)}, u32[]{:S(2)}) collective-permute-start(bf16[672,128]{1,0:T(8,128)(2,1)S(1)} %get-tuple-element.20), channel_id=1, source_target_pairs={{0,4},{2,6},{4,0},{6,2},{8,12},{10,14},{12,8},{14,10},{16,20},{18,... | collective-permute-start | bytes 516104 | tf_op jit(solution)/shard_map/ppermute | solution.py:417
  29.3 5.0 %collective-permute-done.2 = bf16[672,128]{1,0:T(8,128)(2,1)} collective-permute-done((bf16[672,128]{1,0:T(8,128)(2,1)S(1)}, bf16[672,128]{1,0:T(8,128)(2,1)}, u32[]{:S(2)}, u32[]{:S(2)}) %collective-permute-start.2) | collective-permute-done | bytes 172064 | tf_op jit(solution)/shard_map/ppermute | solution.py:417
  34.3 10.7 %all-gather.3.cloned.1.call-done = bf16[768,1280]{1,0:T(8,128)(2,1)} async-done(((bf16[192,1280]{1,0:T(8,128)(2,1)}), bf16[768,1280]{1,0:T(8,128)(2,1)}) %all-gather.3.cloned.1.call-update) | async-done | bytes 1966096 | tf_op jit(solution)/shard_map/all_gather | solution.py:486
  45.1 1.0 pad_maximum_fusion.1.ga0
  46.0 1.6 collective-permute-start.6
  47.7 1.7 collective-permute-start.7
  49.4 0.6 gather_fusion
  50.1 0.6 reduce-window.6
  50.7 0.2 slice_reduce_fusion
  51.0 2.8 %collective-permute-start.10 = (bf16[2944,128]{1,0:T(8,128)(2,1)S(1)}, bf16[2944,128]{1,0:T(8,128)(2,1)S(1)}, u32[]{:S(2)}, u32[]{:S(2)}) collective-permute-start(bf16[2944,128]{1,0:T(8,128)(2,1)S(1)} %pad_maximum_fusion.gb0), channel_id=1, source_target_pairs={{0,6},{2,0},{4,2},{6,4},{8,14},{10,8},{12,10},{14,12},{16,22},{18,... | collective-permute-start | bytes 2261000 | tf_op jit(solution)/shard_map/ppermute | solution.py:417
  53.8 0.8 collective-permute-start.11
  54.6 10.7 %collective-permute-done.6.ga1 = bf16[2688,128]{1,0:T(8,128)(2,1)} collective-permute-done((bf16[2688,128]{1,0:T(8,128)(2,1)S(1)}, bf16[2688,128]{1,0:T(8,128)(2,1)}, u32[]{:S(2)}, u32[]{:S(2)}) %collective-permute-start.6) | collective-permute-done | bytes 688160 | tf_op jit(solution)/shard_map/ppermute | solution.py:421
  65.3 1.5 collective-permute-start.9
  66.8 1.9 %collective-permute-start.8 = (bf16[2688,128]{1,0:T(8,128)(2,1)S(1)}, bf16[2688,128]{1,0:T(8,128)(2,1)}, u32[]{:S(2)}, u32[]{:S(2)}) collective-permute-start(bf16[2688,128]{1,0:T(8,128)(2,1)S(1)} %pad_maximum_fusion.1.ga0), channel_id=1, source_target_pairs={{0,16},{2,18},{4,20},{6,22},{8,24},{10,26},{12,28},{14,30},{16,0},... | collective-permute-start | bytes 2064392 | tf_op jit(solution)/shard_map/ppermute | solution.py:421
  68.8 0.6 gather_fusion.1
  69.8 15.4 %collective-permute-done.8.ga3 = bf16[2688,128]{1,0:T(8,128)(2,1)} collective-permute-done((bf16[2688,128]{1,0:T(8,128)(2,1)S(1)}, bf16[2688,128]{1,0:T(8,128)(2,1)}, u32[]{:S(2)}, u32[]{:S(2)}) %collective-permute-start.8) | collective-permute-done | bytes 688160 | tf_op jit(solution)/shard_map/ppermute | solution.py:421
  85.2 1.1 collective-permute-done.10.gb2
  86.2 3.8 %collective-permute-done.9.gb1 = bf16[2944,128]{1,0:T(8,128)(2,1)} collective-permute-done((bf16[2944,128]{1,0:T(8,128)(2,1)S(1)}, bf16[2944,128]{1,0:T(8,128)(2,1)}, u32[]{:S(2)}, u32[]{:S(2)}) %collective-permute-start.9) | collective-permute-done | bytes 753696 | tf_op jit(solution)/shard_map/ppermute | solution.py:417
  90.0 1.5 copy-done.5
  91.6 11.4 %shard_map.123 = bf16[512,896]{1,0:T(8,128)(2,1)} custom-call(s32[16]{0:T(128)S(1)} %add.274.a_at_ref, s32[16]{0:T(128)S(1)} %add.278.b_at_ref, bf16[2688,128]{1,0:T(8,128)(2,1)S(1)} %pad_maximum_fusion.1.ga0, bf16[2688,128]{1,0:T(8,128)(2,1)} %collective-permute-done.6.ga1, bf16[2688,128]{1,0:T(8,128)(2,1)} %collective-permute-done.7.ga2, ...), custom_call_target="tpu_custom_call" | custom-call | flops 3000000000 | bytes 11000000 | tf_op jit(solution)/shard_map/pallas_call | solution.py:351
  102.9 5.6 %all-to-all-start = ((bf16[64,8,896]{2,1,0:T(8,128)(2,1)}), bf16[64,8,896]{2,1,0:T(8,128)(2,1)S(1)}, u32[]{:S(2)}, u32[]{:S(2)}) async-start(bf16[64,8,896]{2,1,0:T(8,128)(2,1)} %bitcast.16), calls=%async_computation | async-start | bytes 1835008 | tf_op jit(solution)/shard_map/all_to_all | solution.py:512
  108.7 0.2 select_reduce_fusion
  109.3 0.1 copy.36.filled_ref
  109.6 16.2 %all-to-all-done = bf16[64,8,896]{2,1,0:T(8,128)(2,1)S(1)} async-done(((bf16[64,8,896]{2,1,0:T(8,128)(2,1)}), bf16[64,8,896]{2,1,0:T(8,128)(2,1)S(1)}, u32[]{:S(2)}, u32[]{:S(2)}) %all-to-all-start) | async-done | bytes 917536 | tf_op jit(solution)/shard_map/all_to_all | solution.py:512
  125.9 1.2 copy-done.2
  127.1 0.6 shard_map.124.own_ref
  127.7 0.3 collective-permute-start.13
  128.0 0.1 copy.37.seg_col_ref
  128.1 2.3 %collective-permute-done.13.other_ref = bf16[256,1792]{1,0:T(8,128)(2,1)S(1)} collective-permute-done((bf16[256,1792]{1,0:T(8,128)(2,1)S(1)}, bf16[256,1792]{1,0:T(8,128)(2,1)S(1)}, u32[]{:S(2)}, u32[]{:S(2)}) %collective-permute-start.13) | collective-permute-done | bytes 917536 | tf_op jit(solution)/shard_map/ppermute | solution.py:413
  130.4 0.9 copy-done.6
  131.3 3.3 %copy-done.4 = bf16[3584,1152]{1,0:T(8,128)(2,1)S(1)} copy-done((bf16[3584,1152]{1,0:T(8,128)(2,1)S(1)}, bf16[3584,1152]{1,0:T(8,128)(2,1)}, u32[]{:S(2)}) %copy-start.4) | copy-done | bytes 8257560
  134.7 1.2 copy-done.7
  135.9 1.0 copy-done.8
  136.9 13.1 %shard_map.125 = (bf16[256,1920]{1,0:T(8,128)(2,1)S(1)}, f32[256,1792]{1,0:T(8,128)S(1)}, f32[256,1]{1,0:T(8,128)S(1)}, f32[256,1]{1,0:T(8,128)S(1)}) custom-call(s32[1]{0:T(128)} %bitcast.3.half_ref, bf16[256,1792]{1,0:T(8,128)(2,1)S(1)} %shard_map.124.own_ref, bf16[256,1792]{1,0:T(8,128)(2,1)S(1)} %copy-done.7, f32[2,1792]{1,0:T(2,128)S(1)} %reshape.686.gain_ref, ...), custom_call_target="tpu_custom_call" | custom-call | flops 5000000000 | bytes 14000000 | tf_op jit(solution)/shard_map/pallas_call | solution.py:140
  150.0 1.2 copy-done.1
  151.7 2.2 %collective-permute-done.14 = bf16[256,1920]{1,0:T(8,128)(2,1)} collective-permute-done((bf16[256,1920]{1,0:T(8,128)(2,1)S(1)}, bf16[256,1920]{1,0:T(8,128)(2,1)}, u32[]{:S(2)}, u32[]{:S(2)}) %collective-permute-start.14) | collective-permute-done | bytes 983072 | tf_op jit(solution)/shard_map/ppermute | solution.py:413
  153.9 1.1 add_reduce_fusion
  155.0 2.2 %subtract_convert_fusion = bf16[256,1792]{1,0:T(8,128)(2,1)S(1)} fusion(bf16[256,1792]{1,0:T(8,128)(2,1)S(1)} %shard_map.124.own_ref, f32[256,1792]{1,0:T(8,128)} %copy-done.1, bf16[256,1920]{1,0:T(8,128)(2,1)} %collective-permute-done.14, f32[256]{0:T(256)S(1)} %add_reduce_fusion, f32[256]{0:T(256)S(1)} %fusion.20, f32[1792]{0:T(1024)S(1)} %dynamic_slice.29), kind=kLoop, calls=%fused_computation.3 | loop fusion | flops 3670016 | bytes 4596736 | tf_op jit(solution)/shard_map/convert_element_type | solution.py:527
  157.2 0.5 fusion.6
  157.7 1.4 fusion
  159.2 4.8 %all-to-all-start.1 = ((bf16[64,8,896]{2,1,0:T(8,128)(2,1)}), bf16[64,8,896]{2,1,0:T(8,128)(2,1)S(1)}, u32[]{:S(2)}, u32[]{:S(2)}) async-start(bf16[64,8,896]{2,1,0:T(8,128)(2,1)} %fusion), calls=%async_computation.1 | async-start | bytes 1835008 | tf_op jit(solution)/shard_map/all_to_all | solution.py:538
  164.0 0.7 and_select_fusion.4
  164.7 0.2 convert_reduce_fusion.2
  164.9 0.7 multiply_add_fusion
  165.6 16.0 %all-to-all-done.1 = bf16[64,8,896]{2,1,0:T(8,128)(2,1)S(1)} async-done(((bf16[64,8,896]{2,1,0:T(8,128)(2,1)}), bf16[64,8,896]{2,1,0:T(8,128)(2,1)S(1)}, u32[]{:S(2)}, u32[]{:S(2)}) %all-to-all-start.1) | async-done | bytes 917536 | tf_op jit(solution)/shard_map/all_to_all | solution.py:538
  181.6 0.4 convolution_convert_fusion.1
  182.0 0.4 convolution_convert_fusion
  182.4 0.7 pad_maximum_fusion.2
  183.2 0.8 fusion.8
  (83 shorter events, 2.7 us)
Async XLA Ops:
  7.2 5.5 %copy-start = (bf16[80,4,1792]{2,1,0:T(4,128)(2,1)S(1)}, bf16[80,4,1792]{2,1,0:T(4,128)(2,1)}, u32[]{:S(2)}) copy-start(bf16[80,4,1792]{2,1,0:T(4,128)(2,1)} %param.14) | copy-start | bytes 3440644
  7.2 16.7 %copy-start.10 = (s32[64,192]{1,0:T(8,128)S(1)}, s32[64,192]{1,0:T(8,128)}, u32[]{:S(2)}) copy-start(s32[64,192]{1,0:T(8,128)} %param.16) | copy-start | bytes 147460
  7.2 37.8 %all-gather.3.cloned.1.call-start = ((), (), s32[]{:S(2)}) async-start(), calls=%async_computation.2 | async-start | bytes 2457600 | tf_op jit(solution)/shard_map/all_gather | solution.py:486
  11.8 0.8 copy-start.9
  14.6 36.3 %copy-start.13 = (s32[4]{0:T(128)S(1)}, s32[4]{0:T(128)}, u32[]{:S(2)}) copy-start(s32[4]{0:T(128)} %constant.230) | copy-start | bytes 52
  14.6 19.7 %collective-permute-start.3 = (bf16[736,128]{1,0:T(8,128)(2,1)S(1)}, bf16[736,128]{1,0:T(8,128)(2,1)S(1)}, u32[]{:S(2)}, u32[]{:S(2)}) collective-permute-start(bf16[736,128]{1,0:T(8,128)(2,1)S(1)} %get-tuple-element.24), channel_id=1, source_target_pairs={{0,8},{2,10},{4,12},{6,14},{8,16},{10,18},{12,20},{14,22},{16,24},... | collective-permute-start | bytes 565256 | tf_op jit(solution)/shard_map/ppermute | solution.py:421
  16.7 17.6 %collective-permute-start.4 = (bf16[736,128]{1,0:T(8,128)(2,1)S(1)}, bf16[736,128]{1,0:T(8,128)(2,1)S(1)}, u32[]{:S(2)}, u32[]{:S(2)}) collective-permute-start(bf16[736,128]{1,0:T(8,128)(2,1)S(1)} %get-tuple-element.24), channel_id=1, source_target_pairs={{0,24},{2,26},{4,28},{6,30},{8,0},{10,2},{12,4},{14,6},{16,8},{18,... | collective-permute-start | bytes 565256 | tf_op jit(solution)/shard_map/ppermute | solution.py:421
  18.9 15.4 %collective-permute-start.5 = (bf16[736,128]{1,0:T(8,128)(2,1)S(1)}, bf16[736,128]{1,0:T(8,128)(2,1)S(1)}, u32[]{:S(2)}, u32[]{:S(2)}) collective-permute-start(bf16[736,128]{1,0:T(8,128)(2,1)S(1)} %get-tuple-element.24), channel_id=1, source_target_pairs={{0,16},{2,18},{4,20},{6,22},{8,24},{10,26},{12,28},{14,30},{16,0},... | collective-permute-start | bytes 565256 | tf_op jit(solution)/shard_map/ppermute | solution.py:421
  20.7 6.6 %collective-permute-start = (bf16[672,128]{1,0:T(8,128)(2,1)S(1)}, bf16[672,128]{1,0:T(8,128)(2,1)S(1)}, u32[]{:S(2)}, u32[]{:S(2)}) collective-permute-start(bf16[672,128]{1,0:T(8,128)(2,1)S(1)} %get-tuple-element.20), channel_id=1, source_target_pairs={{0,2},{2,4},{4,6},{6,0},{8,10},{10,12},{12,14},{14,8},{16,18},{18,... | collective-permute-start | bytes 516104 | tf_op jit(solution)/shard_map/ppermute | solution.py:417
  22.2 7.1 %collective-permute-start.1 = (bf16[672,128]{1,0:T(8,128)(2,1)S(1)}, bf16[672,128]{1,0:T(8,128)(2,1)S(1)}, u32[]{:S(2)}, u32[]{:S(2)}) collective-permute-start(bf16[672,128]{1,0:T(8,128)(2,1)S(1)} %get-tuple-element.20), channel_id=1, source_target_pairs={{0,6},{2,0},{4,2},{6,4},{8,14},{10,8},{12,10},{14,12},{16,22},{18,... | collective-permute-start | bytes 516104 | tf_op jit(solution)/shard_map/ppermute | solution.py:417
  27.3 7.0 %collective-permute-start.2 = (bf16[672,128]{1,0:T(8,128)(2,1)S(1)}, bf16[672,128]{1,0:T(8,128)(2,1)}, u32[]{:S(2)}, u32[]{:S(2)}) collective-permute-start(bf16[672,128]{1,0:T(8,128)(2,1)S(1)} %get-tuple-element.20), channel_id=1, source_target_pairs={{0,4},{2,6},{4,0},{6,2},{8,12},{10,14},{12,8},{14,10},{16,20},{18,... | collective-permute-start | bytes 516104 | tf_op jit(solution)/shard_map/ppermute | solution.py:417
  45.0 45.0 %collective-permute-start.12 = (bf16[4,192,1280]{2,1,0:T(8,128)(2,1)}, bf16[4,192,1280]{2,1,0:T(8,128)(2,1)}, u32[]{:S(2)}, u32[]{:S(2)}) collective-permute-start(bf16[4,192,1280]{2,1,0:T(8,128)(2,1)} %bitcast.65), channel_id=1, source_target_pairs={{0,1},{1,0},{2,3},{3,2},{4,5},{5,4},{6,7},{7,6},{8,9},{9,8},{10,11... | collective-permute-start | bytes 5898248 | tf_op jit(solution)/shard_map/ppermute | solution.py:413
  46.0 19.2 %collective-permute-start.6 = (bf16[2688,128]{1,0:T(8,128)(2,1)S(1)}, bf16[2688,128]{1,0:T(8,128)(2,1)}, u32[]{:S(2)}, u32[]{:S(2)}) collective-permute-start(bf16[2688,128]{1,0:T(8,128)(2,1)S(1)} %pad_maximum_fusion.1.ga0), channel_id=1, source_target_pairs={{0,8},{2,10},{4,12},{6,14},{8,16},{10,18},{12,20},{14,22},{16,24},... | collective-permute-start | bytes 2064392 | tf_op jit(solution)/shard_map/ppermute | solution.py:421
  47.7 19.1 %collective-permute-start.7 = (bf16[2688,128]{1,0:T(8,128)(2,1)S(1)}, bf16[2688,128]{1,0:T(8,128)(2,1)}, u32[]{:S(2)}, u32[]{:S(2)}) collective-permute-start(bf16[2688,128]{1,0:T(8,128)(2,1)S(1)} %pad_maximum_fusion.1.ga0), channel_id=1, source_target_pairs={{0,24},{2,26},{4,28},{6,30},{8,0},{10,2},{12,4},{14,6},{16,8},{18,... | collective-permute-start | bytes 2064392 | tf_op jit(solution)/shard_map/ppermute | solution.py:421
  51.0 35.2 %collective-permute-start.10 = (bf16[2944,128]{1,0:T(8,128)(2,1)S(1)}, bf16[2944,128]{1,0:T(8,128)(2,1)S(1)}, u32[]{:S(2)}, u32[]{:S(2)}) collective-permute-start(bf16[2944,128]{1,0:T(8,128)(2,1)S(1)} %pad_maximum_fusion.gb0), channel_id=1, source_target_pairs={{0,6},{2,0},{4,2},{6,4},{8,14},{10,8},{12,10},{14,12},{16,22},{18,... | collective-permute-start | bytes 2261000 | tf_op jit(solution)/shard_map/ppermute | solution.py:417
  53.8 32.5 %collective-permute-start.11 = (bf16[2944,128]{1,0:T(8,128)(2,1)S(1)}, bf16[2944,128]{1,0:T(8,128)(2,1)}, u32[]{:S(2)}, u32[]{:S(2)}) collective-permute-start(bf16[2944,128]{1,0:T(8,128)(2,1)S(1)} %pad_maximum_fusion.gb0), channel_id=1, source_target_pairs={{0,4},{2,6},{4,0},{6,2},{8,12},{10,14},{12,8},{14,10},{16,20},{18,... | collective-permute-start | bytes 2261000 | tf_op jit(solution)/shard_map/ppermute | solution.py:417
  65.3 24.7 %collective-permute-start.9 = (bf16[2944,128]{1,0:T(8,128)(2,1)S(1)}, bf16[2944,128]{1,0:T(8,128)(2,1)}, u32[]{:S(2)}, u32[]{:S(2)}) collective-permute-start(bf16[2944,128]{1,0:T(8,128)(2,1)S(1)} %pad_maximum_fusion.gb0), channel_id=1, source_target_pairs={{0,2},{2,4},{4,6},{6,0},{8,10},{10,12},{12,14},{14,8},{16,18},{18,... | collective-permute-start | bytes 2261000 | tf_op jit(solution)/shard_map/ppermute | solution.py:417
  66.8 18.4 %collective-permute-start.8 = (bf16[2688,128]{1,0:T(8,128)(2,1)S(1)}, bf16[2688,128]{1,0:T(8,128)(2,1)}, u32[]{:S(2)}, u32[]{:S(2)}) collective-permute-start(bf16[2688,128]{1,0:T(8,128)(2,1)S(1)} %pad_maximum_fusion.1.ga0), channel_id=1, source_target_pairs={{0,16},{2,18},{4,20},{6,22},{8,24},{10,26},{12,28},{14,30},{16,0},... | collective-permute-start | bytes 2064392 | tf_op jit(solution)/shard_map/ppermute | solution.py:421
  69.7 33.3 %copy-start.12 = (s32[64,3]{0,1:T(4,128)}, s32[64,3]{0,1:T(4,128)S(1)}, u32[]{:S(2)}) copy-start(s32[64,3]{0,1:T(4,128)S(1)} %reduce-window.9) | copy-start | bytes 2308
  90.0 1.5 copy-start.5
  102.9 5.6 %slice-start = ((s32[64,3]{0,1:T(4,128)}), s32[64,2]{0,1:T(2,128)S(1)}, s32[]{:S(2)}) async-start(s32[64,3]{0,1:T(4,128)} %copy-done.12), calls=%async_computation.3 | async-start | bytes 2048 | tf_op jit(solution)/shard_map/slice.1
  102.9 23.0 %all-to-all-start = ((bf16[64,8,896]{2,1,0:T(8,128)(2,1)}), bf16[64,8,896]{2,1,0:T(8,128)(2,1)S(1)}, u32[]{:S(2)}, u32[]{:S(2)}) async-start(bf16[64,8,896]{2,1,0:T(8,128)(2,1)} %bitcast.16), calls=%async_computation | async-start | bytes 1835008 | tf_op jit(solution)/shard_map/all_to_all | solution.py:512
  108.5 19.4 %copy-start.3 = (s32[1,256]{1,0:T(1,128)S(1)}, s32[1,256]{1,0:T(1,128)}, u32[]{:S(2)}) copy-start(s32[1,256]{1,0:T(1,128)} %seg_row_ref.1) | copy-start | bytes 3076
  108.6 19.5 %copy-start.11 = (f32[3584]{0:T(1024)S(1)}, f32[3584]{0:T(1024)}, u32[]{:S(2)}) copy-start(f32[3584]{0:T(1024)} %param.18) | copy-start | bytes 43012
  125.9 1.2 copy-start.2
  127.7 2.7 %collective-permute-start.13 = (bf16[256,1792]{1,0:T(8,128)(2,1)S(1)}, bf16[256,1792]{1,0:T(8,128)(2,1)S(1)}, u32[]{:S(2)}, u32[]{:S(2)}) collective-permute-start(bf16[256,1792]{1,0:T(8,128)(2,1)S(1)} %shard_map.124.own_ref), channel_id=1, source_target_pairs={{0,1},{1,0},{2,3},{3,2},{4,5},{5,4},{6,7},{7,6},{8,9},{9,8},{10,11... | collective-permute-start | bytes 2752520 | tf_op jit(solution)/shard_map/ppermute | solution.py:413
  130.4 0.9 copy-start.6
  131.3 3.3 %copy-start.4 = (bf16[3584,1152]{1,0:T(8,128)(2,1)S(1)}, bf16[3584,1152]{1,0:T(8,128)(2,1)}, u32[]{:S(2)}) copy-start(bf16[3584,1152]{1,0:T(8,128)(2,1)} %weight_ref.1) | copy-start | bytes 24772612
  134.7 1.2 copy-start.7
  135.9 1.0 copy-start.8
  150.0 1.3 copy-start.1
  151.2 2.7 %collective-permute-start.14 = (bf16[256,1920]{1,0:T(8,128)(2,1)S(1)}, bf16[256,1920]{1,0:T(8,128)(2,1)}, u32[]{:S(2)}, u32[]{:S(2)}) collective-permute-start(bf16[256,1920]{1,0:T(8,128)(2,1)S(1)} %get-tuple-element.31), channel_id=1, source_target_pairs={{0,1},{1,0},{2,3},{3,2},{4,5},{5,4},{6,7},{7,6},{8,9},{9,8},{10,11... | collective-permute-start | bytes 2949128 | tf_op jit(solution)/shard_map/ppermute | solution.py:413
  159.2 22.4 %all-to-all-start.1 = ((bf16[64,8,896]{2,1,0:T(8,128)(2,1)}), bf16[64,8,896]{2,1,0:T(8,128)(2,1)S(1)}, u32[]{:S(2)}, u32[]{:S(2)}) async-start(bf16[64,8,896]{2,1,0:T(8,128)(2,1)} %fusion), calls=%async_computation.1 | async-start | bytes 1835008 | tf_op jit(solution)/shard_map/all_to_all | solution.py:538
Sparse Core Ops, SparseCore 0:
  12.8 32.1 all-gather.2

commit v4 on v3

--- a/solution.py
+++ b/solution.py
@@ -13,6 +13,7 @@
 NT = (((1,), (1,)), ((), ()))
 NN = (((1,), (0,)), ((), ()))
 TAIL = 128
+BIG = 56 * 1024 * 1024
 
 
 def dot(x, y, dims=NN):
@@ -21,11 +22,11 @@
 
 def attend_kernel(
     half_ref,
-    own_ref,
-    other_ref,
+    own_hbm,
+    other_hbm,
     gain_ref,
     weight_ref,
-    upstream_ref,
+    upstream_hbm,
     seg_row_ref,
     seg_col_ref,
     give_ref,
@@ -38,10 +39,13 @@
     sgrad_ref,
     bias_ref,
     held_ref,
+    own_ref,
+    other_ref,
+    upstream_ref,
     sems,
 ):
     bf16, f32 = jnp.bfloat16, jnp.float32
-    rows, slab = own_ref.shape
+    rows, slab = own_hbm.shape
     group = weight_ref.shape[1]
     heads = group // HEAD_DIM - 2
     width = held_ref.shape[2]
@@ -52,8 +56,15 @@
         )
         for n in range(pieces)
     ]
-    for copy in copies:
+    small = [
+        pltpu.make_async_copy(own_hbm, own_ref, sems.at[pieces]),
+        pltpu.make_async_copy(other_hbm, other_ref, sems.at[pieces + 1]),
+        pltpu.make_async_copy(upstream_hbm, upstream_ref, sems.at[pieces + 2]),
+    ]
+    for copy in small[:2] + copies + small[2:]:
         copy.start()
+    small[0].wait()
+    small[1].wait()
     t = half_ref[0]
     own_at = pl.multiple_of(t * slab, HEAD_DIM)
     other_at = pl.multiple_of((1 - t) * slab, HEAD_DIM)
@@ -81,6 +92,7 @@
     allowed = (seg_col_ref[...] == seg_row_ref[...]) & (place_u <= place_t)
     bias_ref[...] = jnp.where(allowed, 0.0, -1e30)
 
+    small[2].wait()
     key = scaled_ref[:, heads * HEAD_DIM : (heads + 1) * HEAD_DIM]
     val = scaled_ref[:, (heads + 1) * HEAD_DIM :]
     grad_key = jnp.zeros((rows, HEAD_DIM), f32)
@@ -137,6 +149,7 @@
     group = qkv_weight.shape[1]
     f32, bf16 = jnp.float32, jnp.bfloat16
     vmem = pl.BlockSpec(memory_space=pltpu.VMEM)
+    anywhere = pl.BlockSpec(memory_space=pl.ANY)
     return pl.pallas_call(
         attend_kernel,
         out_shape=(
@@ -145,8 +158,8 @@
             jax.ShapeDtypeStruct((rows, 1), f32),
             jax.ShapeDtypeStruct((rows, 1), f32),
         ),
-        in_specs=[pl.BlockSpec(memory_space=pltpu.SMEM), vmem, vmem, vmem]
-        + [pl.BlockSpec(memory_space=pl.ANY), vmem, vmem, vmem],
+        in_specs=[pl.BlockSpec(memory_space=pltpu.SMEM), anywhere, anywhere, vmem]
+        + [anywhere, anywhere, vmem, vmem],
         out_specs=(vmem,) * 4,
         scratch_shapes=[
             pltpu.VMEM((rows, 2 * slab), bf16),
@@ -155,9 +168,12 @@
             pltpu.VMEM((rows, group), bf16),
             pltpu.VMEM((rows, rows), f32),
             pltpu.VMEM((group // 384, 2 * slab, 384), bf16),
-            pltpu.SemaphoreType.DMA((group // 384,)),
+            pltpu.VMEM((rows, slab), bf16),
+            pltpu.VMEM((rows, slab), bf16),
+            pltpu.VMEM(upstream.shape, bf16),
+            pltpu.SemaphoreType.DMA((group // 384 + 3,)),
         ],
-        compiler_params=pltpu.CompilerParams(vmem_limit_bytes=28 * 1024 * 1024),
+        compiler_params=pltpu.CompilerParams(vmem_limit_bytes=BIG),
         cost_estimate=pl.CostEstimate(flops=5_000_000_000, bytes_accessed=14_000_000, transcendentals=500_000),
     )(
         half.reshape(1),
@@ -181,7 +197,26 @@
 B_PIECE = 3 * B_ROWS + B_TAIL
 
 
-def pack_kernel(e_ref, am_ref, at_ref, vm_ref, vt_ref, a_ref, b_ref):
+def pack_kernel(
+    place_ref, am_ref, at_ref, vm_ref, vt_ref, audio_ref, vision_ref, a_ref, b_ref, rows_ref, sems
+):
+    t = place_ref[1]
+    width = rows_ref.shape[1]
+    ah, vh = audio_ref.shape[0] // 2, vision_ref.shape[0] // 2
+    copies = [
+        pltpu.make_async_copy(
+            audio_ref.at[pl.ds(pl.multiple_of(t * ah, 16), ah), :], rows_ref.at[:ah], sems.at[0]
+        )
+    ] + [
+        pltpu.make_async_copy(
+            vision_ref.at[pl.ds(pl.multiple_of(t * vh, 16), vh), i * width : (i + 1) * width],
+            rows_ref.at[ah + i * vh : ah + (i + 1) * vh],
+            sems.at[1 + i],
+        )
+        for i in range(4)
+    ]
+    for copy in copies:
+        copy.start()
     k = am_ref.shape[0]
     cut = A_ROWS - k
     for n in range(3):
@@ -189,7 +224,7 @@
         a_ref[n * A_ROWS : n * A_ROWS + k, :] = am_ref[:, cols]
         a_ref[n * A_ROWS + k : (n + 1) * A_ROWS, :] = vm_ref[:cut, cols]
         b_ref[n * B_ROWS : (n + 1) * B_ROWS, :] = vm_ref[cut:, cols]
-    odd = e_ref[0] % 2 == 1
+    odd = place_ref[0] % 2 == 1
     tail = jnp.concatenate([at_ref[...], vt_ref[...]], axis=0).astype(jnp.float32)
     moved = pltpu.roll(tail, 64, 1)
     first = jnp.where(odd, moved, tail)
@@ -204,21 +239,28 @@
     b_ref[3 * B_ROWS :, :] = jnp.where(
         lane < 64, first[A_ROWS : A_ROWS + B_TAIL], high
     ).astype(b_ref.dtype)
-
-
-def pack_weights(e, audio_main, audio_tail, vision_main, vision_tail):
+    for copy in copies:
+        copy.wait()
+
+
+def pack(where, audio_main, audio_tail, vision_main, vision_tail, audio_rows, vision_rows):
     vmem = pl.BlockSpec(memory_space=pltpu.VMEM)
+    anywhere = pl.BlockSpec(memory_space=pl.ANY)
     return pl.pallas_call(
         pack_kernel,
         out_shape=(
             jax.ShapeDtypeStruct((A_PIECE, 128), jnp.bfloat16),
             jax.ShapeDtypeStruct((B_PIECE, 128), jnp.bfloat16),
+            jax.ShapeDtypeStruct(
+                (audio_rows.shape[0] // 2 + 2 * vision_rows.shape[0], audio_rows.shape[1]), jnp.bfloat16
+            ),
         ),
-        in_specs=[pl.BlockSpec(memory_space=pltpu.SMEM)] + [vmem] * 4,
-        out_specs=(vmem,) * 2,
+        in_specs=[pl.BlockSpec(memory_space=pltpu.SMEM)] + [vmem] * 4 + [anywhere] * 2,
+        out_specs=(vmem, vmem, anywhere),
+        scratch_shapes=[pltpu.SemaphoreType.DMA((5,))],
         compiler_params=pltpu.CompilerParams(vmem_limit_bytes=8 * 1024 * 1024),
         cost_estimate=pl.CostEstimate(flops=0, bytes_accessed=800_000, transcendentals=0),
-    )(e.reshape(1), audio_main, audio_tail, vision_main, vision_tail)
+    )(where, audio_main, audio_tail, vision_main, vision_tail, audio_rows, vision_rows)
 
 
 def encode_kernel(
@@ -228,10 +270,12 @@
     ga1,
     ga2,
     ga3,
+    ga4,
     gb0,
     gb1,
     gb2,
     gb3,
+    gb4,
     own_ref,
     other_ref,
     cell_ref,
@@ -250,11 +294,12 @@
     cut = A_ROWS - audio_k
     pltpu.make_async_copy(own_ref, x_ref.at[0], sems.at[0]).start()
     pltpu.make_async_copy(other_ref, x_ref.at[1], sems.at[1]).start()
-    for m, (ga, gb) in enumerate(((ga0, gb0), (ga1, gb1), (ga2, gb2), (ga3, gb3))):
-
-        @pl.loop(0, 4)
+    sources = ((ga0, gb0, 0, 4), (ga1, gb1, 4, 4), (ga2, gb2, 8, 4), (ga3, gb3, 12, 2), (ga4, gb4, 14, 2))
+    for ga, gb, start, count in sources:
+
+        @pl.loop(0, count)
         def _(n):
-            p = m * 4 + n
+            p = start + n
             a_at = a_at_ref[p]
             b_at = b_at_ref[p]
             base_a = pl.multiple_of(n * A_PIECE, 16)
@@ -266,23 +311,23 @@
                 pltpu.make_async_copy(
                     ga.at[pl.ds(base_a + c * A_ROWS, audio_k), :],
                     w_ref.at[c, pl.ds(audio_at, audio_k), :],
-                    sems.at[2],
+                    sems.at[2 + c],
                 ).start()
                 pltpu.make_async_copy(
                     ga.at[pl.ds(base_a + c * A_ROWS + audio_k, cut), :],
                     w_ref.at[c, pl.ds(low_at, cut), :],
-                    sems.at[2],
+                    sems.at[2 + c],
                 ).start()
                 pltpu.make_async_copy(
                     gb.at[pl.ds(base_b + c * B_ROWS, B_ROWS), :],
                     w_ref.at[c, pl.ds(high_at, B_ROWS), :],
-                    sems.at[2],
+                    sems.at[2 + c],
                 ).start()
             pltpu.make_async_copy(
-                ga.at[pl.ds(base_a + 3 * A_ROWS, A_TAIL), :], ta_ref.at[p], sems.at[3]
+                ga.at[pl.ds(base_a + 3 * A_ROWS, A_TAIL), :], ta_ref.at[p], sems.at[5]
             ).start()
             pltpu.make_async_copy(
-                gb.at[pl.ds(base_b + 3 * B_ROWS, B_TAIL), :], tb_ref.at[p], sems.at[4]
+                gb.at[pl.ds(base_b + 3 * B_ROWS, B_TAIL), :], tb_ref.at[p], sems.at[6]
             ).start()
 
     count = cell_ref.shape[1]
@@ -291,8 +336,35 @@
     first = jnp.where(line == cell_ref[0:1, :], 1.0, 0.0).astype(bf16)
     second = jnp.where(line == cell_ref[1:2, :], 1.0, 0.0).astype(bf16)
 
-    pltpu.make_async_copy(ta_ref, ta_ref, sems.at[3]).wait()
-    pltpu.make_async_copy(tb_ref, tb_ref, sems.at[4]).wait()
+    halves, n_enc = x_ref.shape[:2]
+    audio = 64
+    vision = 32
+    n_audio = halves * n_enc * audio
+    n_vision = halves * n_enc * vision
+
+    def project(c):
+        cols = slice(c * 128, (c + 2) * 128)
+
+        def weights(at, size):
+            return jnp.concatenate([w_ref[c, at : at + size, :], w_ref[c + 1, at : at + size, :]], axis=1)
+
+        rows = x_ref[:, :, :audio, :].reshape(n_audio, audio_width)
+        enc_ref[:n_audio, cols] = dot(rows, weights(0, audio_width)).astype(bf16)
+        total = jnp.zeros((n_vision, 256), f32)
+        for i in range(4):
+            rows = x_ref[:, :, audio + i * vision : audio + (i + 1) * vision, :]
+            rows = rows.reshape(n_vision, audio_width)
+            total = total + dot(rows, weights((i + 1) * audio_width, audio_width))
+        enc_ref[n_audio:, cols] = total.astype(bf16)
+
+    pltpu.make_async_copy(own_ref, x_ref.at[0], sems.at[0]).wait()
+    pltpu.make_async_copy(other_ref, x_ref.at[1], sems.at[1]).wait()
+    pltpu.make_async_copy(w_ref.at[0], w_ref.at[0], sems.at[2]).wait()
+    pltpu.make_async_copy(w_ref.at[1], w_ref.at[1], sems.at[3]).wait()
+    project(0)
+
+    pltpu.make_async_copy(ta_ref, ta_ref, sems.at[5]).wait()
+    pltpu.make_async_copy(tb_ref, tb_ref, sems.at[6]).wait()
 
     @pl.loop(0, 16)
     def _(p):
@@ -309,28 +381,8 @@
         w_ref[3, pl.ds(high_at, B_TAIL), :] = tb
         w_ref[3, pl.ds(high_at + B_TAIL, B_ROWS - B_TAIL), :] = roll_half(tb)[: B_ROWS - B_TAIL]
 
-    pltpu.make_async_copy(own_ref, x_ref.at[0], sems.at[0]).wait()
-    pltpu.make_async_copy(other_ref, x_ref.at[1], sems.at[1]).wait()
-    pltpu.make_async_copy(w_ref.at[0:3], w_ref.at[0:3], sems.at[2]).wait()
-
-    halves, n_enc = x_ref.shape[:2]
-    audio = 64
-    vision = 32
-    n_audio = halves * n_enc * audio
-    for c in (0, 2):
-        cols = slice(c * 128, (c + 2) * 128)
-
-        def weights(at, size):
-            return jnp.concatenate([w_ref[c, at : at + size, :], w_ref[c + 1, at : at + size, :]], axis=1)
-
-        rows = x_ref[:, :, :audio, :].reshape(n_audio, audio_width)
-        enc_ref[:n_audio, cols] = dot(rows, weights(0, audio_width)).astype(bf16)
-        total = jnp.zeros((halves * n_enc * vision, 256), f32)
-        for i in range(4):
-            rows = x_ref[:, :, audio + i * vision : audio + (i + 1) * vision, :]
-            rows = rows.reshape(halves * n_enc * vision, audio_width)
-            total = total + dot(rows, weights((i + 1) * audio_width, audio_width))
-        enc_ref[n_audio:, cols] = total.astype(bf16)
+    pltpu.make_async_copy(w_ref.at[2], w_ref.at[2], sems.at[4]).wait()
+    project(2)
 
     main = enc_ref[:, :384]
     out_ref[:, :384] = dot(first, main).astype(bf16)
@@ -351,7 +403,7 @@
     return pl.pallas_call(
         encode_kernel,
         out_shape=jax.ShapeDtypeStruct((n_cells, 896), bf16),
-        in_specs=[smem, smem] + [anywhere] * 10 + [vmem],
+        in_specs=[smem, smem] + [anywhere] * 12 + [vmem],
         out_specs=vmem,
         scratch_shapes=[
             pltpu.VMEM((4, 5 * width, 128), bf16),
@@ -359,9 +411,9 @@
             pltpu.VMEM((16, B_TAIL, 128), bf16),
             pltpu.VMEM((2, n_enc, rows, width), bf16),
             pltpu.VMEM((cells.shape[1], 512), bf16),
-            pltpu.SemaphoreType.DMA((5,)),
+            pltpu.SemaphoreType.DMA((7,)),
         ],
-        compiler_params=pltpu.CompilerParams(vmem_limit_bytes=28 * 1024 * 1024),
+        compiler_params=pltpu.CompilerParams(vmem_limit_bytes=BIG),
         cost_estimate=pl.CostEstimate(
             flops=3_000_000_000, bytes_accessed=11_000_000, transcendentals=0
         ),
@@ -409,6 +461,77 @@
     )(spots, arrived, text, filled)
 
 
+def finish_kernel(
+    half_ref, rows_ref, keep_ref, taken_ref, inv_ref, stat_ref, gain_ref, spot_ref, out_ref
+):
+    bf16, f32 = jnp.bfloat16, jnp.float32
+    rows, slab = rows_ref.shape
+    cells = out_ref.shape[0]
+    half = slab // 2
+    inv = inv_ref[...]
+    sent = taken_ref[:, slab:].astype(f32)
+    stat = stat_ref[...] + sent[:, 0:1] + sent[:, 1:2]
+    factor = inv * inv * inv / (2 * slab) * stat
+    gain = gain_ref[pl.ds(half_ref[0], 1), :]
+    line = lax.broadcasted_iota(jnp.int32, (cells, rows), 1)
+    first = jnp.where(line == spot_ref[:, 0:1], 1.0, 0.0).astype(bf16)
+    second = jnp.where(line == spot_ref[:, 1:2], 1.0, 0.0).astype(bf16)
+
+    def grads(cols):
+        total = keep_ref[:, cols] + taken_ref[:, cols].astype(f32)
+        return (gain[:, cols] * total - rows_ref[:, cols].astype(f32) * factor).astype(bf16)
+
+    for c in range(0, half, 128):
+        low = grads(slice(c, c + 128))
+        high = grads(slice(half + c, half + c + 128))
+        out_ref[:, c : c + 128] = (dot(first, low) + dot(second, high)).astype(bf16)
+
+
+def finish(half, rows, keep, taken, inv, stat, norm_gain, spots):
+    vmem = pl.BlockSpec(memory_space=pltpu.VMEM)
+    cells = spots.shape[0]
+    slab = rows.shape[1]
+    return pl.pallas_call(
+        finish_kernel,
+        out_shape=jax.ShapeDtypeStruct((cells, slab // 2), jnp.bfloat16),
+        in_specs=[pl.BlockSpec(memory_space=pltpu.SMEM)] + [vmem] * 7,
+        out_specs=vmem,
+        compiler_params=pltpu.CompilerParams(vmem_limit_bytes=16 * 1024 * 1024),
+        cost_estimate=pl.CostEstimate(flops=500_000_000, bytes_accessed=4_000_000, transcendentals=0),
+    )(half.reshape(1), rows, keep, taken, inv, stat, norm_gain.reshape(2, slab), spots)
+
+
+def collect_kernel(cell_ref, returned_ref, audio_ref, vision_ref):
+    bf16 = jnp.bfloat16
+    count = cell_ref.shape[0]
+    cells, half = returned_ref.shape
+    audio = audio_ref.shape[0]
+    line = lax.broadcasted_iota(jnp.int32, (count, cells), 1)
+    for h in range(2):
+        hot = jnp.where(line == cell_ref[...] + 4 * h, 1.0, 0.0).astype(bf16)
+        value = dot(hot, returned_ref[...]).astype(bf16)
+        cols = slice(h * half, (h + 1) * half)
+        audio_ref[:, cols] = value[:audio]
+        vision_ref[:, cols] = value[audio:]
+
+
+def collect(cell, returned, audio):
+    vmem = pl.BlockSpec(memory_space=pltpu.VMEM)
+    count = cell.shape[0]
+    width = 2 * returned.shape[1]
+    return pl.pallas_call(
+        collect_kernel,
+        out_shape=(
+            jax.ShapeDtypeStruct((audio, width), jnp.bfloat16),
+            jax.ShapeDtypeStruct((count - audio, width), jnp.bfloat16),
+        ),
+        in_specs=[vmem] * 2,
+        out_specs=(vmem,) * 2,
+        compiler_params=pltpu.CompilerParams(vmem_limit_bytes=12 * 1024 * 1024),
+        cost_estimate=pl.CostEstimate(flops=400_000_000, bytes_accessed=2_000_000, transcendentals=0),
+    )(cell, returned)
+
+
 def swap(x):
     return lax.ppermute(x, "tp", [(0, 1), (1, 0)])
 
@@ -461,7 +584,13 @@
         last = lax.dynamic_slice_in_dim(w, n_enc * wide + (e // 2) * 128, 128, axis)
         return main.reshape(-1, wide), last.reshape(-1, 128)
 
-    piece_a, piece_b = pack_weights(e, *columns(audio_weight), *columns(vision_weight))
+    piece_a, piece_b, packed = pack(
+        jnp.stack([e, t]),
+        *columns(audio_weight),
+        *columns(vision_weight),
+        audio_rows,
+        vision_rows,
+    )
     hops = (1, 3, 2)
     along_y = [piece_a] + [shift_y(piece_a, k) for k in hops]
     along_z = [piece_b] + [shift_z(piece_b, k) for k in hops]
@@ -469,22 +598,20 @@
     stack_a = jnp.concatenate(along_y, axis=0)
     stack_b = jnp.concatenate(along_z, axis=0)
     stack_a, stack_b = lax.optimization_barrier((stack_a, stack_b))
-    pieces_a = [stack_a] + [shift_z(stack_a, k) for k in hops]
-    pieces_b = [stack_b] + [shift_y(stack_b, k) for k in hops]
+    near = [shift_z(stack_a, 1), shift_z(stack_a, 3), shift_y(stack_b, 1), shift_y(stack_b, 3)]
+    own = lax.all_gather(packed, "enc", axis=0, tiled=False)
+    near, own = lax.optimization_barrier((near, own))
+    far_a = [shift_z(near[0][: 2 * A_PIECE], 1), shift_z(near[1][2 * A_PIECE :], 3)]
+    far_b = [shift_y(near[2][: 2 * B_PIECE], 1), shift_y(near[3][2 * B_PIECE :], 3)]
+    other = swap(own)
+    pieces_a = [stack_a] + near[:2] + far_a
+    pieces_b = [stack_b] + near[2:] + far_b
     z, y = j // 4, j % 4
     back = jnp.array((0,) + hops, jnp.int32)
     a_at = (((z - back) % 4)[:, None] * 4 + ((y - back) % 4)[None, :]).reshape(-1)
     b_at = (((y - back) % 4)[:, None] + ((z - back) % 4)[None, :] * 4).reshape(-1)
 
     ah, vh = audio_count // 2, vision_count // 2
-    audio_half = lax.dynamic_slice_in_dim(audio_rows, t * ah, ah, 0)
-    vision_half = lax.dynamic_slice_in_dim(vision_rows, t * vh, vh, 0)
-    packed = jnp.concatenate(
-        [audio_half] + [vision_half[:, i * audio_width : (i + 1) * audio_width] for i in range(merge)],
-        axis=0,
-    )
-    own = lax.all_gather(packed, "enc", axis=0, tiled=False)
-    other = swap(own)
 
     line = row_target.reshape(n_enc, n_seq, enc_rows)[:, j]
     line_dest = line // length
@@ -518,40 +645,25 @@
     give, keep, inv_rms, row_part = attend(
         t, row_slab, other_slab, norm_gain, qkv_weight, attn_grad, segment_ids[0]
     )
-    model_width = 2 * slab
     taken = swap(give)
-    back = keep + taken[:, :slab].astype(f32)
-    stat = row_part + taken[:, slab : slab + 1].astype(f32) + taken[:, slab + 1 : slab + 2].astype(f32)
-    gain_slab = lax.dynamic_slice_in_dim(norm_gain, t * slab, slab, 0)
-    row_grads = gain_slab * back - row_slab.astype(f32) * (inv_rms**3 / model_width) * stat
-    row_grads = row_grads.astype(bf16)
 
     half = slab // 2
-    flat = jnp.arange(senders * 2 * cap)
-    pos8 = jnp.broadcast_to(incoming[:, None, :], (senders, 2, cap)).reshape(-1, 1)
-    part8 = (flat // cap % 2)[:, None]
-    hits = pos8 == jnp.arange(length)[None, :]
-    out8 = jnp.dot(
-        (hits & (part8 == 0)).astype(bf16), row_grads[:, :half], preferred_element_type=f32
-    ) + jnp.dot((hits & (part8 == 1)).astype(bf16), row_grads[:, half:], preferred_element_type=f32)
-    out8 = out8.astype(bf16).reshape(senders, 2 * cap, half)
-    returned = lax.all_to_all(out8, ("enc", "seq"), split_axis=0, concat_axis=0, tiled=True)
-    returned = returned.reshape(senders * 2 * cap, half)
+    nowhere = jnp.full_like(incoming, -1)
+    spots = jnp.stack(
+        [
+            jnp.stack([incoming, nowhere], axis=1).reshape(-1),
+            jnp.stack([nowhere, incoming], axis=1).reshape(-1),
+        ],
+        axis=1,
+    )
     own_target = lax.dynamic_index_in_dim(row_target, self_index, 0, keepdims=True)
     own_dest = own_target // length
     own_cell = (own_dest * (2 * cap) + ranks(own_dest)).reshape(-1, 1)
-    result = jnp.concatenate(
-        [
-            jnp.dot(
-                (own_cell + h * cap == flat[None, :]).astype(bf16),
-                returned,
-                preferred_element_type=f32,
-            ).astype(bf16)
-            for h in range(2)
-        ],
-        axis=1,
-    )
-    return (result[:audio_count], result[audio_count:])
+    out8 = finish(t, row_slab, keep, taken, inv_rms, row_part, norm_gain, spots)
+    returned = lax.all_to_all(
+        out8.reshape(senders, 2 * cap, half), ("enc", "seq"), split_axis=0, concat_axis=0, tiled=True
+    )
+    return collect(own_cell, returned.reshape(senders * 2 * cap, half), audio_count)
 
 
 def solution(mesh):

time: 192 us -> 168 us (0.88)
  waiting for transfers between devices: 86.2 us -> 58.5 us
  Pallas kernels: 25.1 us -> 33.7 us
  other arithmetic: 9.42 us -> 2.83 us
  starting transfers between devices: 32.4 us -> 37.6 us
  matrix products: 2.76 us -> 0 us
    all_gather x1, waiting for transfers between devices: 10.7 us -> 0.01 us  [local(): own = lax.all_gather(packed, 'enc', axis=0, tiled=False)]
    ppermute x6 -> x7, waiting for transfers between devices: 26.1 us -> 18.2 us  [shift_z(): lax.ppermute(x, 'seq', [(i, (i // 4 + k) % 4 * 4 + i % 4) for i in range(...]
    ppermute x6 -> x7, waiting for transfers between devices: 12.6 us -> 4.9 us  [shift_y(): lax.ppermute(x, 'seq', [(i, i // 4 * 4 + (i % 4 + k) % 4) for i in range(...]
    unnamed x33 -> x48, local copies, waits for them, and re-layouts: 15 us -> 9.77 us
    pallas_call x1 -> x3, Pallas kernels: 0.11 us -> 5.14 us  [the longest x1 2.31 us: finish(): pl.pallas_call(finish_kernel, out_shape=jax.ShapeDtypeStruct((cells, slab...]
    pallas_call x1, Pallas kernels: 13.1 us -> 16.1 us  [attend(): pl.pallas_call(attend_kernel, out_shape=(jax.ShapeDtypeStruct((rows, slab...]
    slice x1 -> x5, local copies, waits for them, and re-layouts: 0.18 us -> 3.09 us  [the longest x1 1.76 us: local(): near[3][2 * B_PIECE:]]
    dot_general x4 -> x0, matrix products: 2.76 us -> none  [the longest x1 1.44 us: local(): jnp.dot((hits & (part8 == 0)).astype(bf16), row_grads[:, :half], preferre...]
  transfers between devices with their start and end apart: 18 -> 20, of which waited for: 11 -> 8; matrix products, arithmetic and copies ran while one was open for 5% -> 7% of each run, Pallas kernels for 0% -> 0%
where the time goes in v4:
time: 168 us; the launch traced here: 167 us
  waiting for transfers between devices  58.5 us (35%)
  starting transfers between devices  37.6 us (22%)
  Pallas kernels  33.7 us (20%)
  local copies, waits for them, and re-layouts  20.2 us (12%)
  between operations  14.5 us (9%)
  other arithmetic  2.83 us (2%)
    ppermute x7, waiting for transfers between devices, shift_z(): lax.ppermute(x, 'seq', [(i, (i // 4 + k) % 4 * 4 + i % 4) for i in range(...  18.2 us
    all_to_all x1, waiting for transfers between devices, local(): lax.all_to_all(out8.reshape(senders, 2 * cap, half), ('enc', 'seq'), spli...  17.3 us
    pallas_call x1, Pallas kernels, attend(): pl.pallas_call(attend_kernel, out_shape=(jax.ShapeDtypeStruct((rows, slab...  16.1 us
    all_to_all x1, waiting for transfers between devices, local(): lax.all_to_all(outgoing.reshape(senders, 8, slab // 2), ('enc', 'seq'), s...  15 us
    ppermute x7, starting transfers between devices, shift_z(): lax.ppermute(x, 'seq', [(i, (i // 4 + k) % 4 * 4 + i % 4) for i in range(...  12.6 us
    ppermute x7, starting transfers between devices, shift_y(): lax.ppermute(x, 'seq', [(i, i // 4 * 4 + (i % 4 + k) % 4) for i in range(...  12 us
    pallas_call x1, Pallas kernels, encode(): pl.pallas_call(encode_kernel, out_shape=jax.ShapeDtypeStruct((n_cells, 89...  11.9 us
    unnamed x48, local copies, waits for them, and re-layouts  9.77 us
  transfers between devices with their start and end apart: 20, of which 8 were waited for; matrix products, arithmetic and copies ran while one was open for 7% of the time, Pallas kernels for 0%

profile of v4, /device:TPU:0, one launch (start us, length us, event | category | flops | bytes accessed | tf_op | source)
XLA Modules:
  0.0 167.3 jit_solution(1800590506173016516)
XLA Ops:
  7.3 1.2 copy-done
  8.5 0.7 constant_dynamic-slice_fusion.3.at_ref
  9.3 0.8 constant_dynamic-slice_fusion.4.am_ref
  10.3 1.4 shard_map.122
  11.7 1.7 %collective-permute-start = (bf16[672,128]{1,0:T(8,128)(2,1)S(1)}, bf16[672,128]{1,0:T(8,128)(2,1)S(1)}, u32[]{:S(2)}, u32[]{:S(2)}) collective-permute-start(bf16[672,128]{1,0:T(8,128)(2,1)S(1)} %get-tuple-element.26), channel_id=1, source_target_pairs={{0,2},{2,4},{4,6},{6,0},{8,10},{10,12},{12,14},{14,8},{16,18},{18,... | collective-permute-start | bytes 516104 | tf_op jit(solution)/shard_map/ppermute | solution.py:540
  13.4 1.9 %collective-permute-start.3 = (bf16[736,128]{1,0:T(8,128)(2,1)S(1)}, bf16[736,128]{1,0:T(8,128)(2,1)S(1)}, u32[]{:S(2)}, u32[]{:S(2)}) collective-permute-start(bf16[736,128]{1,0:T(8,128)(2,1)S(1)} %get-tuple-element.30), channel_id=1, source_target_pairs={{0,8},{2,10},{4,12},{6,14},{8,16},{10,18},{12,20},{14,22},{16,24},... | collective-permute-start | bytes 565256 | tf_op jit(solution)/shard_map/ppermute | solution.py:544
  15.4 2.1 %collective-permute-start.4 = (bf16[736,128]{1,0:T(8,128)(2,1)S(1)}, bf16[736,128]{1,0:T(8,128)(2,1)S(1)}, u32[]{:S(2)}, u32[]{:S(2)}) collective-permute-start(bf16[736,128]{1,0:T(8,128)(2,1)S(1)} %get-tuple-element.30), channel_id=1, source_target_pairs={{0,24},{2,26},{4,28},{6,30},{8,0},{10,2},{12,4},{14,6},{16,8},{18,... | collective-permute-start | bytes 565256 | tf_op jit(solution)/shard_map/ppermute | solution.py:544
  17.5 1.9 %collective-permute-start.5 = (bf16[736,128]{1,0:T(8,128)(2,1)S(1)}, bf16[736,128]{1,0:T(8,128)(2,1)S(1)}, u32[]{:S(2)}, u32[]{:S(2)}) collective-permute-start(bf16[736,128]{1,0:T(8,128)(2,1)S(1)} %get-tuple-element.30), channel_id=1, source_target_pairs={{0,16},{2,18},{4,20},{6,22},{8,24},{10,26},{12,28},{14,30},{16,0},... | collective-permute-start | bytes 565256 | tf_op jit(solution)/shard_map/ppermute | solution.py:544
  19.3 1.7 collective-permute-start.1
  21.0 2.0 %collective-permute-start.2 = (bf16[672,128]{1,0:T(8,128)(2,1)S(1)}, bf16[672,128]{1,0:T(8,128)(2,1)S(1)}, u32[]{:S(2)}, u32[]{:S(2)}) collective-permute-start(bf16[672,128]{1,0:T(8,128)(2,1)S(1)} %get-tuple-element.26), channel_id=1, source_target_pairs={{0,4},{2,6},{4,0},{6,2},{8,12},{10,14},{12,8},{14,10},{16,20},{18,... | collective-permute-start | bytes 516104 | tf_op jit(solution)/shard_map/ppermute | solution.py:540
  23.0 3.3 %collective-permute-done.1 = bf16[672,128]{1,0:T(8,128)(2,1)S(1)} collective-permute-done((bf16[672,128]{1,0:T(8,128)(2,1)S(1)}, bf16[672,128]{1,0:T(8,128)(2,1)S(1)}, u32[]{:S(2)}, u32[]{:S(2)}) %collective-permute-start.1) | collective-permute-done | bytes 172064 | tf_op jit(solution)/shard_map/ppermute | solution.py:540
  26.4 1.6 collective-permute-done.2
  28.1 2.5 %collective-permute-start.8 = (bf16[2944,128]{1,0:T(8,128)(2,1)S(1)}, bf16[2944,128]{1,0:T(8,128)(2,1)S(1)}, u32[]{:S(2)}, u32[]{:S(2)}) collective-permute-start(bf16[2944,128]{1,0:T(8,128)(2,1)S(1)} %pad_maximum_fusion.gb0), channel_id=1, source_target_pairs={{0,2},{2,4},{4,6},{6,0},{8,10},{10,12},{12,14},{14,8},{16,18},{18,... | collective-permute-start | bytes 2261000 | tf_op jit(solution)/shard_map/ppermute | solution.py:540
  30.5 0.8 collective-permute-start.9
  31.4 1.1 collective-permute-start.6
  32.5 2.2 %collective-permute-start.7 = (bf16[2688,128]{1,0:T(8,128)(2,1)S(1)}, bf16[2688,128]{1,0:T(8,128)(2,1)S(1)}, u32[]{:S(2)}, u32[]{:S(2)}) collective-permute-start(bf16[2688,128]{1,0:T(8,128)(2,1)S(1)} %pad_maximum_fusion.1.ga0), channel_id=1, source_target_pairs={{0,24},{2,26},{4,28},{6,30},{8,0},{10,2},{12,4},{14,6},{16,8},{18,... | collective-permute-start | bytes 2064392 | tf_op jit(solution)/shard_map/ppermute | solution.py:544
  34.7 0.4 convert_reduce_fusion
  35.1 12.5 %collective-permute-done.6.ga1 = bf16[2688,128]{1,0:T(8,128)(2,1)S(1)} collective-permute-done((bf16[2688,128]{1,0:T(8,128)(2,1)S(1)}, bf16[2688,128]{1,0:T(8,128)(2,1)S(1)}, u32[]{:S(2)}, u32[]{:S(2)}) %collective-permute-start.6) | collective-permute-done | bytes 688160 | tf_op jit(solution)/shard_map/ppermute | solution.py:544
  47.6 0.9 copy-done.14
  48.5 0.3 copy-done.16
  48.7 0.9 copy-done.13
  49.9 0.6 gather_fusion
  50.6 0.6 gather_fusion.1
  51.4 0.6 reduce-window.6
  52.2 1.1 slice.32
  53.3 0.9 collective-permute-start.12
  54.2 1.8 %slice.33 = bf16[1472,128]{1,0:T(8,128)(2,1)} slice(bf16[2944,128]{1,0:T(8,128)(2,1)} %collective-permute-done.9.gb2), slice={[1472:2944], [0:128]} | slice | bytes 753664 | tf_op jit(solution)/shard_map/slice | solution.py:605
  56.0 2.4 %collective-permute-start.13 = (bf16[1472,128]{1,0:T(8,128)(2,1)}, bf16[1472,128]{1,0:T(8,128)(2,1)}, u32[]{:S(2)}, u32[]{:S(2)}) collective-permute-start(bf16[1472,128]{1,0:T(8,128)(2,1)} %slice.33), channel_id=1, source_target_pairs={{0,6},{2,0},{4,2},{6,4},{8,14},{10,8},{12,10},{14,12},{16,22},{18,... | collective-permute-start | bytes 1130504 | tf_op jit(solution)/shard_map/ppermute | solution.py:540
  58.4 1.0 collective-permute-start.10
  59.4 2.4 %collective-permute-start.11 = (bf16[1344,128]{1,0:T(8,128)(2,1)S(1)}, bf16[1344,128]{1,0:T(8,128)(2,1)}, u32[]{:S(2)}, u32[]{:S(2)}) collective-permute-start(bf16[1344,128]{1,0:T(8,128)(2,1)S(1)} %slice.31), channel_id=1, source_target_pairs={{0,24},{2,26},{4,28},{6,30},{8,0},{10,2},{12,4},{14,6},{16,8},{18,... | collective-permute-start | bytes 1032200 | tf_op jit(solution)/shard_map/ppermute | solution.py:544
  61.8 0.2 slice_reduce_fusion
  62.0 0.6 add.225.a_at_ref
  62.6 0.7 add.229.b_at_ref
  63.3 0.6 pad_add_fusion.cell_ref
  63.9 5.8 %collective-permute-done.10.ga3 = bf16[1344,128]{1,0:T(8,128)(2,1)} collective-permute-done((bf16[1344,128]{1,0:T(8,128)(2,1)S(1)}, bf16[1344,128]{1,0:T(8,128)(2,1)}, u32[]{:S(2)}, u32[]{:S(2)}) %collective-permute-start.10) | collective-permute-done | bytes 344096 | tf_op jit(solution)/shard_map/ppermute | solution.py:544
  69.7 0.7 copy-done.22
  70.4 11.9 %shard_map.123 = bf16[512,896]{1,0:T(8,128)(2,1)} custom-call(s32[16]{0:T(128)} %add.225.a_at_ref, s32[16]{0:T(128)} %add.229.b_at_ref, bf16[2688,128]{1,0:T(8,128)(2,1)} %copy-done.11, bf16[2688,128]{1,0:T(8,128)(2,1)} %copy-done.14, bf16[2688,128]{1,0:T(8,128)(2,1)} %copy-done.16, bf16[1344,128]{1,0:T(8,128)(2,1)} %collective-permute-done.10.ga3, ...), custom_call_target="tpu_custom_call" | custom-call | flops 3000000000 | bytes 11000000 | tf_op jit(solution)/shard_map/pallas_call | solution.py:403
  82.3 7.8 %all-to-all-start = ((bf16[64,8,896]{2,1,0:T(8,128)(2,1)}), bf16[64,8,896]{2,1,0:T(8,128)(2,1)S(1)}, u32[]{:S(2)}, u32[]{:S(2)}) async-start(bf16[64,8,896]{2,1,0:T(8,128)(2,1)} %bitcast.63), calls=%async_computation | async-start | bytes 1835008 | tf_op jit(solution)/shard_map/all_to_all | solution.py:639
  90.3 0.2 select_reduce_fusion
  90.7 0.1 convert_reduce_fusion.1
  90.9 0.1 copy.49.filled_ref
  91.1 0.1 reshape.644.e_row_ref
  91.3 15.0 %all-to-all-done = bf16[64,8,896]{2,1,0:T(8,128)(2,1)S(1)} async-done(((bf16[64,8,896]{2,1,0:T(8,128)(2,1)}), bf16[64,8,896]{2,1,0:T(8,128)(2,1)S(1)}, u32[]{:S(2)}, u32[]{:S(2)}) %all-to-all-start) | async-done | bytes 917536 | tf_op jit(solution)/shard_map/all_to_all | solution.py:639
  106.3 1.2 copy-done.4
  107.5 0.6 shard_map.124.own_hbm.rows_ref
  108.2 0.8 reshape.652.gain_ref
  109.0 0.8 copy.50.seg_col_ref
  109.8 1.0 collective-permute-done.15.other_hbm
  110.8 16.1 %shard_map.125 = (bf16[256,1920]{1,0:T(8,128)(2,1)}, f32[256,1792]{1,0:T(8,128)}, f32[256,1]{1,0:T(8,128)}, f32[256,1]{1,0:T(8,128)}) custom-call(s32[1]{0:T(128)} %bitcast.3.half_ref, bf16[256,1792]{1,0:T(8,128)(2,1)} %copy-done.1, bf16[256,1792]{1,0:T(8,128)(2,1)} %collective-permute-done.15.other_hbm, f32[2,1792]{1,0:T(2,128)} %reshape.652.gain_ref, ...), custom_call_target="tpu_custom_call" | custom-call | flops 5000000000 | bytes 14000000 | tf_op jit(solution)/shard_map/pallas_call | solution.py:153
  126.9 0.2 collective-permute-start.16
  127.3 0.1 stack_reshape.6
  127.5 0.1 stack_reshape.7
  127.6 0.2 copy.53.spot_ref
  127.8 2.0 %collective-permute-done.16.taken_ref = bf16[256,1920]{1,0:T(8,128)(2,1)S(1)} collective-permute-done((bf16[256,1920]{1,0:T(8,128)(2,1)}, bf16[256,1920]{1,0:T(8,128)(2,1)S(1)}, u32[]{:S(2)}, u32[]{:S(2)}) %collective-permute-start.16) | collective-permute-done | bytes 983072 | tf_op jit(solution)/shard_map/ppermute | solution.py:536
  129.8 1.2 copy-done.2
  131.0 1.5 copy-done.3
  132.5 0.9 copy-done.7
  133.4 0.9 copy-done.8
  134.3 2.3 %shard_map.126 = bf16[512,896]{1,0:T(8,128)(2,1)} custom-call(s32[1]{0:T(128)} %bitcast.3.half_ref, bf16[256,1792]{1,0:T(8,128)(2,1)S(1)} %copy-done.2, f32[256,1792]{1,0:T(8,128)S(1)} %copy-done.3, bf16[256,1920]{1,0:T(8,128)(2,1)S(1)} %collective-permute-done.16.taken_ref, f32[256,1]{1,0:T(8,128)S(1)} %copy-done.7, f32[256,1]{1,0:T(8,128)S(1)} %copy-done.8, ...), custom_call_target="tpu_custom_call" | custom-call | flops 500000000 | bytes 4000000 | tf_op jit(solution)/shard_map/pallas_call | solution.py:494
  136.6 4.8 %all-to-all-start.1 = ((bf16[64,8,896]{2,1,0:T(8,128)(2,1)}), bf16[64,8,896]{2,1,0:T(8,128)(2,1)S(1)}, u32[]{:S(2)}, u32[]{:S(2)}) async-start(bf16[64,8,896]{2,1,0:T(8,128)(2,1)} %bitcast.21), calls=%async_computation.1 | async-start | bytes 1835008 | tf_op jit(solution)/shard_map/all_to_all | solution.py:663
  141.4 0.2 convert_reduce_fusion.2
  141.7 0.1 copy.54.cell_ref
  141.8 17.3 %all-to-all-done.1 = bf16[64,8,896]{2,1,0:T(8,128)(2,1)S(1)} async-done(((bf16[64,8,896]{2,1,0:T(8,128)(2,1)}), bf16[64,8,896]{2,1,0:T(8,128)(2,1)S(1)}, u32[]{:S(2)}, u32[]{:S(2)}) %all-to-all-start.1) | async-done | bytes 917536 | tf_op jit(solution)/shard_map/all_to_all | solution.py:663
  159.0 1.5 shard_map.127
  (99 shorter events, 2.2 us)
Async XLA Ops:
  7.2 1.3 copy-start
  7.2 3.1 %copy-start.6 = (bf16[128,1280]{1,0:T(8,128)(2,1)S(1)}, bf16[128,1280]{1,0:T(8,128)(2,1)}, u32[]{:S(2)}) copy-start(bf16[128,1280]{1,0:T(8,128)(2,1)} %audio_ref.1) | copy-start | bytes 983044
  7.2 3.1 %copy-start.5 = (bf16[64,5120]{1,0:T(8,128)(2,1)S(1)}, bf16[64,5120]{1,0:T(8,128)(2,1)}, u32[]{:S(2)}) copy-start(bf16[64,5120]{1,0:T(8,128)(2,1)} %vision_ref.1) | copy-start | bytes 1966084
  7.2 42.4 %all-gather.3.cloned.1.call-start = ((), (), s32[]{:S(2)}) async-start(), calls=%async_computation.2 | async-start | bytes 2457600 | tf_op jit(solution)/shard_map/all_gather | solution.py:602
  11.7 19.7 %copy-start.12 = (s32[64,192]{1,0:T(8,128)S(1)}, s32[64,192]{1,0:T(8,128)}, u32[]{:S(2)}) copy-start(s32[64,192]{1,0:T(8,128)} %param.16) | copy-start | bytes 147460
  11.7 9.3 %collective-permute-start = (bf16[672,128]{1,0:T(8,128)(2,1)S(1)}, bf16[672,128]{1,0:T(8,128)(2,1)S(1)}, u32[]{:S(2)}, u32[]{:S(2)}) collective-permute-start(bf16[672,128]{1,0:T(8,128)(2,1)S(1)} %get-tuple-element.26), channel_id=1, source_target_pairs={{0,2},{2,4},{4,6},{6,0},{8,10},{10,12},{12,14},{14,8},{16,18},{18,... | collective-permute-start | bytes 516104 | tf_op jit(solution)/shard_map/ppermute | solution.py:540
  13.4 14.5 %collective-permute-start.3 = (bf16[736,128]{1,0:T(8,128)(2,1)S(1)}, bf16[736,128]{1,0:T(8,128)(2,1)S(1)}, u32[]{:S(2)}, u32[]{:S(2)}) collective-permute-start(bf16[736,128]{1,0:T(8,128)(2,1)S(1)} %get-tuple-element.30), channel_id=1, source_target_pairs={{0,8},{2,10},{4,12},{6,14},{8,16},{10,18},{12,20},{14,22},{16,24},... | collective-permute-start | bytes 565256 | tf_op jit(solution)/shard_map/ppermute | solution.py:544
  15.4 12.6 %collective-permute-start.4 = (bf16[736,128]{1,0:T(8,128)(2,1)S(1)}, bf16[736,128]{1,0:T(8,128)(2,1)S(1)}, u32[]{:S(2)}, u32[]{:S(2)}) collective-permute-start(bf16[736,128]{1,0:T(8,128)(2,1)S(1)} %get-tuple-element.30), channel_id=1, source_target_pairs={{0,24},{2,26},{4,28},{6,30},{8,0},{10,2},{12,4},{14,6},{16,8},{18,... | collective-permute-start | bytes 565256 | tf_op jit(solution)/shard_map/ppermute | solution.py:544
  17.5 10.4 %collective-permute-start.5 = (bf16[736,128]{1,0:T(8,128)(2,1)S(1)}, bf16[736,128]{1,0:T(8,128)(2,1)S(1)}, u32[]{:S(2)}, u32[]{:S(2)}) collective-permute-start(bf16[736,128]{1,0:T(8,128)(2,1)S(1)} %get-tuple-element.30), channel_id=1, source_target_pairs={{0,16},{2,18},{4,20},{6,22},{8,24},{10,26},{12,28},{14,30},{16,0},... | collective-permute-start | bytes 565256 | tf_op jit(solution)/shard_map/ppermute | solution.py:544
  19.3 7.0 %collective-permute-start.1 = (bf16[672,128]{1,0:T(8,128)(2,1)S(1)}, bf16[672,128]{1,0:T(8,128)(2,1)S(1)}, u32[]{:S(2)}, u32[]{:S(2)}) collective-permute-start(bf16[672,128]{1,0:T(8,128)(2,1)S(1)} %get-tuple-element.26), channel_id=1, source_target_pairs={{0,6},{2,0},{4,2},{6,4},{8,14},{10,8},{12,10},{14,12},{16,22},{18,... | collective-permute-start | bytes 516104 | tf_op jit(solution)/shard_map/ppermute | solution.py:540
  21.0 6.9 %collective-permute-start.2 = (bf16[672,128]{1,0:T(8,128)(2,1)S(1)}, bf16[672,128]{1,0:T(8,128)(2,1)S(1)}, u32[]{:S(2)}, u32[]{:S(2)}) collective-permute-start(bf16[672,128]{1,0:T(8,128)(2,1)S(1)} %get-tuple-element.26), channel_id=1, source_target_pairs={{0,4},{2,6},{4,0},{6,2},{8,12},{10,14},{12,8},{14,10},{16,20},{18,... | collective-permute-start | bytes 516104 | tf_op jit(solution)/shard_map/ppermute | solution.py:540
  23.0 29.0 %copy-start.21 = (s32[4]{0:T(128)S(1)}, s32[4]{0:T(128)}, u32[]{:S(2)}) copy-start(s32[4]{0:T(128)} %constant.203) | copy-start | bytes 52
  28.0 28.0 %copy-start.10 = (bf16[2944,128]{1,0:T(8,128)(2,1)}, bf16[2944,128]{1,0:T(8,128)(2,1)S(1)}, u32[]{:S(2)}) copy-start(bf16[2944,128]{1,0:T(8,128)(2,1)S(1)} %pad_maximum_fusion.gb0) | copy-start | bytes 2260996
  28.1 31.4 %copy-start.11 = (bf16[2688,128]{1,0:T(8,128)(2,1)}, bf16[2688,128]{1,0:T(8,128)(2,1)S(1)}, u32[]{:S(2)}) copy-start(bf16[2688,128]{1,0:T(8,128)(2,1)S(1)} %pad_maximum_fusion.1.ga0) | copy-start | bytes 2064388
  28.1 19.5 %collective-permute-start.8 = (bf16[2944,128]{1,0:T(8,128)(2,1)S(1)}, bf16[2944,128]{1,0:T(8,128)(2,1)S(1)}, u32[]{:S(2)}, u32[]{:S(2)}) collective-permute-start(bf16[2944,128]{1,0:T(8,128)(2,1)S(1)} %pad_maximum_fusion.gb0), channel_id=1, source_target_pairs={{0,2},{2,4},{4,6},{6,0},{8,10},{10,12},{12,14},{14,8},{16,18},{18,... | collective-permute-start | bytes 2261000 | tf_op jit(solution)/shard_map/ppermute | solution.py:540
  30.5 19.1 %collective-permute-start.9 = (bf16[2944,128]{1,0:T(8,128)(2,1)S(1)}, bf16[2944,128]{1,0:T(8,128)(2,1)}, u32[]{:S(2)}, u32[]{:S(2)}) collective-permute-start(bf16[2944,128]{1,0:T(8,128)(2,1)S(1)} %pad_maximum_fusion.gb0), channel_id=1, source_target_pairs={{0,6},{2,0},{4,2},{6,4},{8,14},{10,8},{12,10},{14,12},{16,22},{18,... | collective-permute-start | bytes 2261000 | tf_op jit(solution)/shard_map/ppermute | solution.py:540
  31.4 16.2 %collective-permute-start.6 = (bf16[2688,128]{1,0:T(8,128)(2,1)S(1)}, bf16[2688,128]{1,0:T(8,128)(2,1)S(1)}, u32[]{:S(2)}, u32[]{:S(2)}) collective-permute-start(bf16[2688,128]{1,0:T(8,128)(2,1)S(1)} %pad_maximum_fusion.1.ga0), channel_id=1, source_target_pairs={{0,8},{2,10},{4,12},{6,14},{8,16},{10,18},{12,20},{14,22},{16,24},... | collective-permute-start | bytes 2064392 | tf_op jit(solution)/shard_map/ppermute | solution.py:544
  32.5 15.1 %collective-permute-start.7 = (bf16[2688,128]{1,0:T(8,128)(2,1)S(1)}, bf16[2688,128]{1,0:T(8,128)(2,1)S(1)}, u32[]{:S(2)}, u32[]{:S(2)}) collective-permute-start(bf16[2688,128]{1,0:T(8,128)(2,1)S(1)} %pad_maximum_fusion.1.ga0), channel_id=1, source_target_pairs={{0,24},{2,26},{4,28},{6,30},{8,0},{10,2},{12,4},{14,6},{16,8},{18,... | collective-permute-start | bytes 2064392 | tf_op jit(solution)/shard_map/ppermute | solution.py:544
  47.6 0.9 copy-start.14
  47.6 1.2 copy-start.16
  48.7 0.9 copy-start.13
  49.6 20.1 %collective-permute-start.14 = (bf16[4,192,1280]{2,1,0:T(8,128)(2,1)}, bf16[4,192,1280]{2,1,0:T(8,128)(2,1)}, u32[]{:S(2)}, u32[]{:S(2)}) collective-permute-start(bf16[4,192,1280]{2,1,0:T(8,128)(2,1)} %bitcast.72), channel_id=1, source_target_pairs={{0,1},{1,0},{2,3},{3,2},{4,5},{5,4},{6,7},{7,6},{8,9},{9,8},{10,11... | collective-permute-start | bytes 5898248 | tf_op jit(solution)/shard_map/ppermute | solution.py:536
  52.0 6.4 %copy-start.15 = (bf16[2688,128]{1,0:T(8,128)(2,1)S(1)}, bf16[2688,128]{1,0:T(8,128)(2,1)}, u32[]{:S(2)}) copy-start(bf16[2688,128]{1,0:T(8,128)(2,1)} %copy-done.14) | copy-start | bytes 2064388
  52.0 7.4 %copy-start.17 = (bf16[2688,128]{1,0:T(8,128)(2,1)S(1)}, bf16[2688,128]{1,0:T(8,128)(2,1)}, u32[]{:S(2)}) copy-start(bf16[2688,128]{1,0:T(8,128)(2,1)} %copy-done.16) | copy-start | bytes 2064388
  53.3 16.4 %collective-permute-start.12 = (bf16[1472,128]{1,0:T(8,128)(2,1)S(1)}, bf16[1472,128]{1,0:T(8,128)(2,1)S(1)}, u32[]{:S(2)}, u32[]{:S(2)}) collective-permute-start(bf16[1472,128]{1,0:T(8,128)(2,1)S(1)} %slice.32), channel_id=1, source_target_pairs={{0,2},{2,4},{4,6},{6,0},{8,10},{10,12},{12,14},{14,8},{16,18},{18,... | collective-permute-start | bytes 1130504 | tf_op jit(solution)/shard_map/ppermute | solution.py:540
  56.0 13.7 %collective-permute-start.13 = (bf16[1472,128]{1,0:T(8,128)(2,1)}, bf16[1472,128]{1,0:T(8,128)(2,1)}, u32[]{:S(2)}, u32[]{:S(2)}) collective-permute-start(bf16[1472,128]{1,0:T(8,128)(2,1)} %slice.33), channel_id=1, source_target_pairs={{0,6},{2,0},{4,2},{6,4},{8,14},{10,8},{12,10},{14,12},{16,22},{18,... | collective-permute-start | bytes 1130504 | tf_op jit(solution)/shard_map/ppermute | solution.py:540
  58.4 11.3 %collective-permute-start.10 = (bf16[1344,128]{1,0:T(8,128)(2,1)S(1)}, bf16[1344,128]{1,0:T(8,128)(2,1)}, u32[]{:S(2)}, u32[]{:S(2)}) collective-permute-start(bf16[1344,128]{1,0:T(8,128)(2,1)S(1)} %slice.30), channel_id=1, source_target_pairs={{0,8},{2,10},{4,12},{6,14},{8,16},{10,18},{12,20},{14,22},{16,24},... | collective-permute-start | bytes 1032200 | tf_op jit(solution)/shard_map/ppermute | solution.py:544
  59.4 10.2 %collective-permute-start.11 = (bf16[1344,128]{1,0:T(8,128)(2,1)S(1)}, bf16[1344,128]{1,0:T(8,128)(2,1)}, u32[]{:S(2)}, u32[]{:S(2)}) collective-permute-start(bf16[1344,128]{1,0:T(8,128)(2,1)S(1)} %slice.31), channel_id=1, source_target_pairs={{0,24},{2,26},{4,28},{6,30},{8,0},{10,2},{12,4},{14,6},{16,8},{18,... | collective-permute-start | bytes 1032200 | tf_op jit(solution)/shard_map/ppermute | solution.py:544
  63.3 19.0 %copy-start.19 = (s32[64,3]{0,1:T(4,128)}, s32[64,3]{0,1:T(4,128)S(1)}, u32[]{:S(2)}) copy-start(s32[64,3]{0,1:T(4,128)S(1)} %reduce-window.9) | copy-start | bytes 2308
  69.7 0.7 copy-start.22
  82.3 7.9 %slice-start = ((s32[64,3]{0,1:T(4,128)}), s32[64,2]{0,1:T(2,128)S(1)}, s32[]{:S(2)}) async-start(s32[64,3]{0,1:T(4,128)} %copy-done.19), calls=%async_computation.3 | async-start | bytes 2048 | tf_op jit(solution)/shard_map/slice.1
  82.3 24.0 %all-to-all-start = ((bf16[64,8,896]{2,1,0:T(8,128)(2,1)}), bf16[64,8,896]{2,1,0:T(8,128)(2,1)S(1)}, u32[]{:S(2)}, u32[]{:S(2)}) async-start(bf16[64,8,896]{2,1,0:T(8,128)(2,1)} %bitcast.63), calls=%async_computation | async-start | bytes 1835008 | tf_op jit(solution)/shard_map/all_to_all | solution.py:639
  91.0 17.2 %copy-start.18 = (f32[3584]{0:T(1024)S(1)}, f32[3584]{0:T(1024)}, u32[]{:S(2)}) copy-start(f32[3584]{0:T(1024)} %param.18) | copy-start | bytes 43012
  91.0 17.9 %copy-start.20 = (s32[1,256]{1,0:T(1,128)S(1)}, s32[1,256]{1,0:T(1,128)}, u32[]{:S(2)}) copy-start(s32[1,256]{1,0:T(1,128)} %seg_row_ref.1) | copy-start | bytes 3076
  106.3 1.2 copy-start.4
  108.1 2.7 %copy-start.1 = (bf16[256,1792]{1,0:T(8,128)(2,1)}, bf16[256,1792]{1,0:T(8,128)(2,1)S(1)}, u32[]{:S(2)}) copy-start(bf16[256,1792]{1,0:T(8,128)(2,1)S(1)} %shard_map.124.own_hbm.rows_ref) | copy-start | bytes 2752516
  108.1 2.7 %collective-permute-start.15 = (bf16[256,1792]{1,0:T(8,128)(2,1)S(1)}, bf16[256,1792]{1,0:T(8,128)(2,1)}, u32[]{:S(2)}, u32[]{:S(2)}) collective-permute-start(bf16[256,1792]{1,0:T(8,128)(2,1)S(1)} %shard_map.124.own_hbm.rows_ref), channel_id=1, source_target_pairs={{0,1},{1,0},{2,3},{3,2},{4,5},{5,4},{6,7},{7,6},{8,9},{9,8},{10,11... | collective-permute-start | bytes 2752520 | tf_op jit(solution)/shard_map/ppermute | solution.py:536
  109.8 20.0 %copy-start.9 = (f32[2,1792]{1,0:T(2,128)S(1)}, f32[2,1792]{1,0:T(2,128)}, u32[]{:S(2)}) copy-start(f32[2,1792]{1,0:T(2,128)} %reshape.652.gain_ref) | copy-start | bytes 43012
  126.9 2.9 %collective-permute-start.16 = (bf16[256,1920]{1,0:T(8,128)(2,1)}, bf16[256,1920]{1,0:T(8,128)(2,1)S(1)}, u32[]{:S(2)}, u32[]{:S(2)}) collective-permute-start(bf16[256,1920]{1,0:T(8,128)(2,1)} %get-tuple-element.43), channel_id=1, source_target_pairs={{0,1},{1,0},{2,3},{3,2},{4,5},{5,4},{6,7},{7,6},{8,9},{9,8},{10,11... | collective-permute-start | bytes 2949128 | tf_op jit(solution)/shard_map/ppermute | solution.py:536
  129.8 1.2 copy-start.2
  131.0 1.5 copy-start.3
  132.5 0.9 copy-start.7
  133.4 0.9 copy-start.8
  136.6 22.4 %all-to-all-start.1 = ((bf16[64,8,896]{2,1,0:T(8,128)(2,1)}), bf16[64,8,896]{2,1,0:T(8,128)(2,1)S(1)}, u32[]{:S(2)}, u32[]{:S(2)}) async-start(bf16[64,8,896]{2,1,0:T(8,128)(2,1)} %bitcast.21), calls=%async_computation.1 | async-start | bytes 1835008 | tf_op jit(solution)/shard_map/all_to_all | solution.py:663
Sparse Core Ops, SparseCore 0:
  11.8 32.1 all-gather.2

commit v5 on v4

v5 whole, which is shorter than its diff:
```python
import jax
import jax.numpy as jnp
from jax import lax
from jax.experimental import pallas as pl
from jax.experimental.pallas import tpu as pltpu
from jax.sharding import PartitionSpec as P

HEAD_DIM = 128

epsilon = 1e-06


NT = (((1,), (1,)), ((), ()))
NN = (((1,), (0,)), ((), ()))
TAIL = 128
BIG = 60 * 1024 * 1024


def dot(x, y, dims=NN):
    return lax.dot_general(x, y, dims, preferred_element_type=jnp.float32)


def attend_kernel(
    half_ref,
    own_hbm,
    other_hbm,
    gain_ref,
    weight_ref,
    upstream_hbm,
    seg_row_ref,
    seg_col_ref,
    give_hbm,
    keep_hbm,
    inv_ref,
    stat_ref,
    normed_ref,
    unscaled_ref,
    scaled_ref,
    sgrad_ref,
    bias_ref,
    held_ref,
    own_ref,
    other_ref,
    upstream_ref,
    give_ref,
    keep_ref,
    sems,
):
    bf16, f32 = jnp.bfloat16, jnp.float32
    rows, slab = own_hbm.shape
    group = weight_ref.shape[1]
    heads = group // HEAD_DIM - 2
    chunks = [(at, min(512, group - at)) for at in range(0, group, 512)]
    pieces = len(chunks)
    copies = [
        pltpu.make_async_copy(
            weight_ref.at[:, at : at + size], held_ref.at[:, at : at + size], sems.at[n]
        )
        for n, (at, size) in enumerate(chunks)
    ]
    small = [
        pltpu.make_async_copy(own_hbm, own_ref, sems.at[pieces]),
        pltpu.make_async_copy(other_hbm, other_ref, sems.at[pieces + 1]),
        pltpu.make_async_copy(upstream_hbm, upstream_ref, sems.at[pieces + 2]),
    ]
    for copy in small[:2] + copies + small[2:]:
        copy.start()
    place_u = lax.broadcasted_iota(jnp.int32, (rows, rows), 0)
    place_t = lax.broadcasted_iota(jnp.int32, (rows, rows), 1)
    allowed = (seg_col_ref[...] == seg_row_ref[...]) & (place_u <= place_t)
    bias_ref[...] = jnp.where(allowed, 0.0, -1e30)

    small[0].wait()
    small[1].wait()
    t = half_ref[0]
    own_at = pl.multiple_of(t * slab, HEAD_DIM)
    other_at = pl.multiple_of((1 - t) * slab, HEAD_DIM)
    score_scale = HEAD_DIM ** (-0.5)

    squares = jnp.zeros((rows, HEAD_DIM), f32)
    for part, ref in ((t, own_ref), (1 - t, other_ref)):
        gain = gain_ref[pl.ds(part, 1), :]
        for c in range(0, slab, HEAD_DIM):
            x = ref[:, c : c + HEAD_DIM].astype(f32)
            squares = squares + x * x
            at = pl.multiple_of(part * slab + c, HEAD_DIM)
            normed_ref[:, pl.ds(at, HEAD_DIM)] = (x * gain[:, c : c + HEAD_DIM]).astype(bf16)
    inv = lax.rsqrt(jnp.sum(squares, axis=1, keepdims=True) / (2 * slab) + epsilon)
    inv_ref[...] = inv

    for n, (at, size) in enumerate(chunks):
        copies[n].wait()
        value = dot(normed_ref[...], held_ref[:, at : at + size])
        unscaled_ref[:, at : at + size] = value
        scaled_ref[:, at : at + size] = (value * inv).astype(bf16)

    small[2].wait()
    key = scaled_ref[:, heads * HEAD_DIM : (heads + 1) * HEAD_DIM]
    val = scaled_ref[:, (heads + 1) * HEAD_DIM :]
    grad_key = jnp.zeros((rows, HEAD_DIM), f32)
    grad_val = jnp.zeros((rows, HEAD_DIM), f32)
    stat = jnp.zeros((rows, HEAD_DIM), f32)
    for h in range(heads):
        cols = slice(h * HEAD_DIM, (h + 1) * HEAD_DIM)
        query = scaled_ref[:, cols]
        up = upstream_ref[:, cols]
        scores = dot(key, query, NT) * score_scale + bias_ref[...]
        scores = jnp.exp(scores - jnp.max(scores, axis=0, keepdims=True))
        probs = scores * (1.0 / jnp.sum(scores, axis=0, keepdims=True))
        dprobs = dot(val, up, NT)
        delta = jnp.sum(probs * dprobs, axis=0, keepdims=True)
        sgrad = (probs * (dprobs - delta) * score_scale).astype(bf16)
        grad_val = grad_val + dot(probs.astype(bf16), up)
        grad_key = grad_key + dot(sgrad, query)
        grad_query = dot(sgrad.T, key)
        stat = stat + grad_query * unscaled_ref[:, cols]
        sgrad_ref[:, cols] = (grad_query * inv).astype(bf16)
    cols = slice(heads * HEAD_DIM, (heads + 1) * HEAD_DIM)
    stat = stat + grad_key * unscaled_ref[:, cols]
    sgrad_ref[:, cols] = (grad_key * inv).astype(bf16)
    cols = slice((heads + 1) * HEAD_DIM, (heads + 2) * HEAD_DIM)
    stat = stat + grad_val * unscaled_ref[:, cols]
    sgrad_ref[:, cols] = (grad_val * inv).astype(bf16)
    total = jnp.sum(stat, axis=1, keepdims=True)
    stat_ref[...] = total
    lane = lax.broadcasted_iota(jnp.int32, (rows, TAIL), 1)
    high = total.astype(bf16)
    low = (total - high.astype(f32)).astype(bf16)
    give_ref[:, slab:] = jnp.where(lane == 0, high.astype(f32), low.astype(f32)).astype(bf16)

    keep_ref[...] = dot(sgrad_ref[...], held_ref[pl.ds(own_at, slab), :], NT).astype(bf16)
    keep_out = pltpu.make_async_copy(keep_ref, keep_hbm, sems.at[pieces + 3])
    keep_out.start()
    give_ref[:, :slab] = dot(sgrad_ref[...], held_ref[pl.ds(other_at, slab), :], NT).astype(bf16)
    give_out = pltpu.make_async_copy(give_ref, give_hbm, sems.at[pieces + 4])
    give_out.start()
    keep_out.wait()
    give_out.wait()


def attend(half, own, other, gain, qkv_weight, upstream, seg_row, seg_col):
    rows, slab = own.shape
    group = qkv_weight.shape[1]
    f32, bf16 = jnp.float32, jnp.bfloat16
    vmem = pl.BlockSpec(memory_space=pltpu.VMEM)
    anywhere = pl.BlockSpec(memory_space=pl.ANY)
    return pl.pallas_call(
        attend_kernel,
        out_shape=(
            jax.ShapeDtypeStruct((rows, slab + TAIL), bf16),
            jax.ShapeDtypeStruct((rows, slab), bf16),
            jax.ShapeDtypeStruct((rows, 1), f32),
            jax.ShapeDtypeStruct((rows, 1), f32),
        ),
        in_specs=[pl.BlockSpec(memory_space=pltpu.SMEM), anywhere, anywhere, vmem]
        + [anywhere, anywhere, vmem, vmem],
        out_specs=(anywhere, anywhere, vmem, vmem),
        scratch_shapes=[
            pltpu.VMEM((rows, 2 * slab), bf16),
            pltpu.VMEM((rows, group), f32),
            pltpu.VMEM((rows, group), bf16),
            pltpu.VMEM((rows, group), bf16),
            pltpu.VMEM((rows, rows), f32),
            pltpu.VMEM((2 * slab, group), bf16),
            pltpu.VMEM((rows, slab), bf16),
            pltpu.VMEM((rows, slab), bf16),
            pltpu.VMEM(upstream.shape, bf16),
            pltpu.VMEM((rows, slab + TAIL), bf16),
            pltpu.VMEM((rows, slab), bf16),
            pltpu.SemaphoreType.DMA((8,)),
        ],
        compiler_params=pltpu.CompilerParams(vmem_limit_bytes=BIG),
        cost_estimate=pl.CostEstimate(flops=5_000_000_000, bytes_accessed=14_000_000, transcendentals=500_000),
    )(
        half.reshape(1),
        own,
        other,
        gain,
        qkv_weight,
        upstream,
        seg_row,
        seg_col,
    )


def roll_half(x):
    return pltpu.roll(x.astype(jnp.float32), 64, 1).astype(x.dtype)


A_ROWS, A_TAIL = 192, 32
B_ROWS, B_TAIL = 208, 48
A_PIECE = A_ROWS + A_TAIL
B_PIECE = B_ROWS + B_TAIL


def pack_kernel(
    place_ref,
    audio_w_ref,
    vision_w_ref,
    audio_ref,
    vision_ref,
    a_ref,
    b_ref,
    rows_ref,
    am_ref,
    at_ref,
    vm_ref,
    vt_ref,
    sems,
    row_sems,
):
    e = place_ref[0]
    t = place_ref[1]
    main_at = pl.multiple_of(e * 384, 128)
    tail_at = pl.multiple_of(1536 + e // 2 * 128, 128)
    loads = [
        pltpu.make_async_copy(vision_w_ref.at[:, :, pl.ds(main_at, 384)], vm_ref, sems.at[0]),
        pltpu.make_async_copy(vision_w_ref.at[:, :, pl.ds(tail_at, 128)], vt_ref, sems.at[1]),
        pltpu.make_async_copy(audio_w_ref.at[:, pl.ds(main_at, 384)], am_ref, sems.at[2]),
        pltpu.make_async_copy(audio_w_ref.at[:, pl.ds(tail_at, 128)], at_ref, sems.at[3]),
    ]
    for copy in loads:
        copy.start()
    width = rows_ref.shape[1]
    ah, vh = audio_ref.shape[0] // 2, vision_ref.shape[0] // 2
    copies = [
        pltpu.make_async_copy(
            audio_ref.at[pl.ds(pl.multiple_of(t * ah, 16), ah), :], rows_ref.at[:ah], row_sems.at[0]
        )
    ] + [
        pltpu.make_async_copy(
            vision_ref.at[pl.ds(pl.multiple_of(t * vh, 16), vh), i * width : (i + 1) * width],
            rows_ref.at[ah + i * vh : ah + (i + 1) * vh],
            row_sems.at[1 + i],
        )
        for i in range(4)
    ]
    for copy in copies:
        copy.start()
    for copy in loads:
        copy.wait()
    k = am_ref.shape[0]
    cut = A_ROWS - k
    vision_main = vm_ref[...].reshape(4 * k, 384)
    a_ref[:k, :] = am_ref[...]
    a_ref[k:A_ROWS, :] = vision_main[:cut]
    b_ref[:B_ROWS, :] = vision_main[cut:]
    odd = e % 2 == 1
    vision_tail = vt_ref[...].reshape(4 * k, 128)
    tail = jnp.concatenate([at_ref[...], vision_tail], axis=0).astype(jnp.float32)
    moved = pltpu.roll(tail, 64, 1)
    first = jnp.where(odd, moved, tail)
    second = jnp.where(odd, tail, moved)
    lane = lax.broadcasted_iota(jnp.int32, (B_TAIL, 128), 1)
    for q in range(3):
        cols = slice(q * 128, (q + 1) * 128)
        low = first[q * A_TAIL : (q + 1) * A_TAIL]
        high = second[96 + q * A_TAIL : 96 + (q + 1) * A_TAIL]
        a_ref[A_ROWS:, cols] = jnp.where(lane[:A_TAIL] < 64, low, high).astype(a_ref.dtype)
    base = A_ROWS
    for q in range(2):
        cols = slice(q * 128, (q + 1) * 128)
        low = first[base + q * B_TAIL : base + (q + 1) * B_TAIL]
        high = second[base + 112 + q * B_TAIL : base + 112 + (q + 1) * B_TAIL]
        b_ref[B_ROWS:, cols] = jnp.where(lane < 64, low, high).astype(b_ref.dtype)
    b_ref[B_ROWS : B_ROWS + 16, 256:] = first[base + 96 : base + 112].astype(b_ref.dtype)
    b_ref[B_ROWS + 16 :, 256:] = jnp.zeros((B_TAIL - 16, 128), b_ref.dtype)
    for copy in copies:
        copy.wait()


def pack(where, audio_weight, vision_weight, audio_rows, vision_rows):
    bf16 = jnp.bfloat16
    vmem = pl.BlockSpec(memory_space=pltpu.VMEM)
    anywhere = pl.BlockSpec(memory_space=pl.ANY)
    k = audio_weight.shape[0]
    return pl.pallas_call(
        pack_kernel,
        out_shape=(
            jax.ShapeDtypeStruct((A_PIECE, 384), bf16),
            jax.ShapeDtypeStruct((B_PIECE, 384), bf16),
            jax.ShapeDtypeStruct(
                (audio_rows.shape[0] // 2 + 2 * vision_rows.shape[0], audio_rows.shape[1]), bf16
            ),
        ),
        in_specs=[pl.BlockSpec(memory_space=pltpu.SMEM)] + [anywhere] * 4,
        out_specs=(vmem, vmem, anywhere),
        scratch_shapes=[
            pltpu.VMEM((k, 384), bf16),
            pltpu.VMEM((k, 128), bf16),
            pltpu.VMEM((k, 4, 384), bf16),
            pltpu.VMEM((k, 4, 128), bf16),
            pltpu.SemaphoreType.DMA((4,)),
            pltpu.SemaphoreType.DMA((5,)),
        ],
        compiler_params=pltpu.CompilerParams(vmem_limit_bytes=BIG),
        cost_estimate=pl.CostEstimate(flops=0, bytes_accessed=1_800_000, transcendentals=0),
    )(where, audio_weight, vision_weight, audio_rows, vision_rows)


def encode_kernel(
    a_at_ref,
    b_at_ref,
    ga0,
    ga1,
    ga2,
    ga3,
    gb0,
    gb1,
    gb2,
    gb3,
    own_ref,
    other_ref,
    cell_ref,
    out_ref,
    w_ref,
    wt_ref,
    ta_ref,
    tb_ref,
    x_ref,
    enc_ref,
    sems,
):
    bf16, f32 = jnp.bfloat16, jnp.float32
    audio_width = x_ref.shape[3]
    audio_k = audio_width // 16
    vision_k = 4 * audio_k
    cut = A_ROWS - audio_k
    sources = ((ga0, gb0), (ga1, gb1), (ga2, gb2), (ga3, gb3))

    def spots(p):
        audio_at = pl.multiple_of(a_at_ref[p] * audio_k, 16)
        low_at = pl.multiple_of(audio_width + a_at_ref[p] * vision_k, 16)
        high_at = pl.multiple_of(audio_width + b_at_ref[p] * vision_k + cut, 16)
        return audio_at, low_at, high_at

    def bases(n):
        return pl.multiple_of(n * A_PIECE, 16), pl.multiple_of(n * B_PIECE, 16)

    for m, (ga, gb) in enumerate(sources):

        @pl.loop(0, 4)
        def _(n):
            p = m * 4 + n
            base_a, base_b = bases(n)
            pltpu.make_async_copy(
                ga.at[pl.ds(base_a + A_ROWS, A_TAIL), :], ta_ref.at[p], sems.at[2]
            ).start()
            pltpu.make_async_copy(
                gb.at[pl.ds(base_b + B_ROWS, B_TAIL), :], tb_ref.at[p], sems.at[3]
            ).start()

    pltpu.make_async_copy(own_ref, x_ref.at[0], sems.at[0]).start()
    pltpu.make_async_copy(other_ref, x_ref.at[1], sems.at[1]).start()
    for m, (ga, gb) in enumerate(sources):

        @pl.loop(0, 4)
        def _(n):
            base_a, base_b = bases(n)
            audio_at, low_at, high_at = spots(m * 4 + n)
            pltpu.make_async_copy(
                ga.at[pl.ds(base_a, audio_k), :], w_ref.at[pl.ds(audio_at, audio_k), :], sems.at[4]
            ).start()
            pltpu.make_async_copy(
                ga.at[pl.ds(base_a + audio_k, cut), :], w_ref.at[pl.ds(low_at, cut), :], sems.at[5]
            ).start()
            pltpu.make_async_copy(
                gb.at[pl.ds(base_b, B_ROWS), :], w_ref.at[pl.ds(high_at, B_ROWS), :], sems.at[5]
            ).start()

    count = cell_ref.shape[1]
    cells = out_ref.shape[0]
    line = lax.broadcasted_iota(jnp.int32, (cells, count), 0)
    first = jnp.where(line == cell_ref[0:1, :], 1.0, 0.0).astype(bf16)
    second = jnp.where(line == cell_ref[1:2, :], 1.0, 0.0).astype(bf16)

    pltpu.make_async_copy(ta_ref, ta_ref, sems.at[2]).wait()
    pltpu.make_async_copy(tb_ref, tb_ref, sems.at[3]).wait()

    @pl.loop(0, 16)
    def _(p):
        audio_at, low_at, high_at = spots(p)
        ta = jnp.concatenate([ta_ref[p, :, q * 128 : (q + 1) * 128] for q in range(3)], axis=0)
        wt_ref[pl.ds(audio_at, audio_k), :] = ta[:audio_k]
        wt_ref[pl.ds(low_at, 96 - audio_k), :] = ta[audio_k:]
        wt_ref[pl.ds(low_at + (96 - audio_k), 96), :] = roll_half(ta)
        tb = jnp.concatenate([tb_ref[p, :, q * 128 : (q + 1) * 128] for q in range(2)], axis=0)
        wt_ref[pl.ds(high_at, 96), :] = tb
        wt_ref[pl.ds(high_at + 96, 16), :] = tb_ref[p, :16, 256:]
        wt_ref[pl.ds(high_at + 112, 96), :] = roll_half(tb)

    halves, n_enc = x_ref.shape[:2]
    audio = 64
    vision = 32
    n_audio = halves * n_enc * audio
    n_vision = halves * n_enc * vision

    def weights(at):
        return jnp.concatenate([w_ref[at : at + audio_width, :], wt_ref[at : at + audio_width, :]], axis=1)

    pltpu.make_async_copy(own_ref, x_ref.at[0], sems.at[0]).wait()
    pltpu.make_async_copy(other_ref, x_ref.at[1], sems.at[1]).wait()
    pltpu.make_async_copy(w_ref.at[:audio_width], w_ref.at[:audio_width], sems.at[4]).wait()
    rows = x_ref[:, :, :audio, :].reshape(n_audio, audio_width)
    enc_ref[:n_audio, :] = dot(rows, weights(0)).astype(bf16)
    pltpu.make_async_copy(w_ref.at[audio_width:], w_ref.at[audio_width:], sems.at[5]).wait()
    total = jnp.zeros((n_vision, 512), f32)
    for i in range(4):
        rows = x_ref[:, :, audio + i * vision : audio + (i + 1) * vision, :]
        total = total + dot(rows.reshape(n_vision, audio_width), weights((i + 1) * audio_width))
    enc_ref[n_audio:, :] = total.astype(bf16)

    main = enc_ref[:, :384]
    out_ref[:, :384] = dot(first, main).astype(bf16)
    out_ref[:, 384:768] = dot(second, main).astype(bf16)
    last = enc_ref[:, 384:].astype(f32)
    lane = lax.broadcasted_iota(jnp.int32, last.shape, 1)
    last = jnp.where(lane < 64, last, 0.0)
    moved = pltpu.roll(last, 64, 1)
    out_ref[:, 768:] = (dot(first, last.astype(bf16)) + dot(second, moved.astype(bf16))).astype(bf16)


def encode(a_at, b_at, pieces_a, pieces_b, own, other, cells, n_cells):
    bf16 = jnp.bfloat16
    n_enc, rows, width = own.shape
    smem = pl.BlockSpec(memory_space=pltpu.SMEM)
    vmem = pl.BlockSpec(memory_space=pltpu.VMEM)
    anywhere = pl.BlockSpec(memory_space=pl.ANY)
    return pl.pallas_call(
        encode_kernel,
        out_shape=jax.ShapeDtypeStruct((n_cells, 896), bf16),
        in_specs=[smem, smem] + [anywhere] * 10 + [vmem],
        out_specs=vmem,
        scratch_shapes=[
            pltpu.VMEM((5 * width, 384), bf16),
            pltpu.VMEM((5 * width, 128), bf16),
            pltpu.VMEM((16, A_TAIL, 384), bf16),
            pltpu.VMEM((16, B_TAIL, 384), bf16),
            pltpu.VMEM((2, n_enc, rows, width), bf16),
            pltpu.VMEM((cells.shape[1], 512), bf16),
            pltpu.SemaphoreType.DMA((6,)),
        ],
        compiler_params=pltpu.CompilerParams(vmem_limit_bytes=BIG),
        cost_estimate=pl.CostEstimate(
            flops=3_000_000_000, bytes_accessed=11_000_000, transcendentals=0
        ),
    )(a_at, b_at, *pieces_a, *pieces_b, own, other, cells)


def place_kernel(e_row_ref, arrived_ref, text_hbm, filled_ref, out_ref, text_ref, sem):
    bf16, f32 = jnp.bfloat16, jnp.float32
    load = pltpu.make_async_copy(text_hbm, text_ref, sem)
    load.start()
    rows = out_ref.shape[0]
    each = arrived_ref.shape[0] // 4
    line = lax.broadcasted_iota(jnp.int32, (rows, each), 0)
    first = jnp.where(line == e_row_ref[0:1, :], 1.0, 0.0).astype(bf16)
    second = jnp.where(line == e_row_ref[1:2, :], 1.0, 0.0).astype(bf16)
    both = jnp.concatenate([first, second], axis=1)
    taken = filled_ref[...] > 0.5
    lane = lax.broadcasted_iota(jnp.int32, (rows, 128), 1)
    low = []
    high = []
    load.wait()
    for e in range(4):
        at = slice(e * each, (e + 1) * each)
        main = jnp.concatenate([arrived_ref[at, :384], arrived_ref[at, 384:768]], axis=0)
        cols = slice(e * 384, (e + 1) * 384)
        text = text_ref[:, cols].astype(f32)
        out_ref[:, cols] = jnp.where(taken, dot(both, main), text).astype(bf16)
        last = arrived_ref[at, 768:]
        low.append(dot(first, last))
        high.append(dot(second, last))
    for q in range(2):
        left = low[2 * q] + pltpu.roll(high[2 * q], 64, 1)
        right = pltpu.roll(low[2 * q + 1], 64, 1) + high[2 * q + 1]
        cols = slice(1536 + q * 128, 1536 + (q + 1) * 128)
        text = text_ref[:, cols].astype(f32)
        out_ref[:, cols] = jnp.where(taken, jnp.where(lane < 64, left, right), text).astype(bf16)


def place(spots, arrived, text, filled):
    vmem = pl.BlockSpec(memory_space=pltpu.VMEM)
    return pl.pallas_call(
        place_kernel,
        out_shape=jax.ShapeDtypeStruct(text.shape, text.dtype),
        in_specs=[vmem, vmem, pl.BlockSpec(memory_space=pl.ANY), vmem],
        out_specs=vmem,
        scratch_shapes=[pltpu.VMEM(text.shape, text.dtype), pltpu.SemaphoreType.DMA],
        compiler_params=pltpu.CompilerParams(vmem_limit_bytes=12 * 1024 * 1024),
        cost_estimate=pl.CostEstimate(flops=300_000_000, bytes_accessed=3_000_000, transcendentals=0),
    )(spots, arrived, text, filled)


def finish_kernel(
    half_ref,
    rows_hbm,
    keep_hbm,
    taken_hbm,
    inv_ref,
    stat_ref,
    gain_ref,
    spot_ref,
    out_ref,
    rows_ref,
    keep_ref,
    taken_ref,
    grad_ref,
    sems,
):
    bf16, f32 = jnp.bfloat16, jnp.float32
    copies = [
        pltpu.make_async_copy(taken_hbm, taken_ref, sems.at[0]),
        pltpu.make_async_copy(rows_hbm, rows_ref, sems.at[1]),
        pltpu.make_async_copy(keep_hbm, keep_ref, sems.at[2]),
    ]
    for copy in copies:
        copy.start()
    rows, slab = rows_ref.shape
    cells = out_ref.shape[0]
    half = slab // 2
    inv = inv_ref[...]
    gain = gain_ref[pl.ds(half_ref[0], 1), :]
    line = lax.broadcasted_iota(jnp.int32, (cells, rows), 1)
    first = jnp.where(line == spot_ref[:, 0:1], 1.0, 0.0).astype(bf16)
    second = jnp.where(line == spot_ref[:, 1:2], 1.0, 0.0).astype(bf16)
    both = jnp.concatenate([first, second], axis=1)
    for copy in copies:
        copy.wait()
    sent = taken_ref[:, slab:].astype(f32)
    stat = stat_ref[...] + sent[:, 0:1] + sent[:, 1:2]
    factor = inv * inv * inv / (2 * slab) * stat
    for c in range(0, slab, 128):
        cols = slice(c, c + 128)
        total = keep_ref[:, cols].astype(f32) + taken_ref[:, cols].astype(f32)
        value = (gain[:, cols] * total - rows_ref[:, cols].astype(f32) * factor).astype(bf16)
        at = c // half
        grad_ref[at * rows : (at + 1) * rows, c - at * half : c - at * half + 128] = value
    out_ref[...] = dot(both, grad_ref[...]).astype(bf16)


def finish(half, rows, keep, taken, inv, stat, gain, spots):
    bf16 = jnp.bfloat16
    vmem = pl.BlockSpec(memory_space=pltpu.VMEM)
    anywhere = pl.BlockSpec(memory_space=pl.ANY)
    cells = spots.shape[0]
    count, slab = rows.shape
    return pl.pallas_call(
        finish_kernel,
        out_shape=jax.ShapeDtypeStruct((cells, slab // 2), bf16),
        in_specs=[pl.BlockSpec(memory_space=pltpu.SMEM)] + [anywhere] * 3 + [vmem] * 4,
        out_specs=vmem,
        scratch_shapes=[
            pltpu.VMEM((count, slab), bf16),
            pltpu.VMEM((count, slab), bf16),
            pltpu.VMEM((count, slab + TAIL), bf16),
            pltpu.VMEM((2 * count, slab // 2), bf16),
            pltpu.SemaphoreType.DMA((3,)),
        ],
        compiler_params=pltpu.CompilerParams(vmem_limit_bytes=BIG),
        cost_estimate=pl.CostEstimate(flops=500_000_000, bytes_accessed=4_000_000, transcendentals=0),
    )(half.reshape(1), rows, keep, taken, inv, stat, gain, spots)


def collect_kernel(cell_ref, returned_ref, audio_ref, vision_ref):
    bf16 = jnp.bfloat16
    count = cell_ref.shape[0]
    cells, half = returned_ref.shape
    audio = audio_ref.shape[0]
    line = lax.broadcasted_iota(jnp.int32, (count, cells), 1)
    for h in range(2):
        hot = jnp.where(line == cell_ref[...] + 4 * h, 1.0, 0.0).astype(bf16)
        value = dot(hot, returned_ref[...]).astype(bf16)
        cols = slice(h * half, (h + 1) * half)
        audio_ref[:, cols] = value[:audio]
        vision_ref[:, cols] = value[audio:]


def collect(cell, returned, audio):
    vmem = pl.BlockSpec(memory_space=pltpu.VMEM)
    count = cell.shape[0]
    width = 2 * returned.shape[1]
    return pl.pallas_call(
        collect_kernel,
        out_shape=(
            jax.ShapeDtypeStruct((audio, width), jnp.bfloat16),
            jax.ShapeDtypeStruct((count - audio, width), jnp.bfloat16),
        ),
        in_specs=[vmem] * 2,
        out_specs=(vmem,) * 2,
        compiler_params=pltpu.CompilerParams(vmem_limit_bytes=12 * 1024 * 1024),
        cost_estimate=pl.CostEstimate(flops=400_000_000, bytes_accessed=2_000_000, transcendentals=0),
    )(cell, returned)


def swap(x):
    return lax.ppermute(x, "tp", [(0, 1), (1, 0)])


def shift_y(x, k):
    return lax.ppermute(x, "seq", [(i, i // 4 * 4 + (i % 4 + k) % 4) for i in range(16)])


def shift_z(x, k):
    return lax.ppermute(x, "seq", [(i, (i // 4 + k) % 4 * 4 + i % 4) for i in range(16)])


def ranks(dest):
    count = dest.shape[1]
    same = dest[:, :, None] == dest[:, None, :]
    earlier = jnp.arange(count)[None, :] < jnp.arange(count)[:, None]
    return jnp.sum((same & earlier[None]).astype(jnp.int32), axis=2)


def local(
    audio_rows,
    vision_rows,
    audio_weight,
    vision_weight,
    text_rows,
    row_target,
    segment_ids,
    norm_gain,
    qkv_weight,
    attn_grad,
):
    bf16, f32 = jnp.bfloat16, jnp.float32
    t = lax.axis_index("tp")
    e = lax.axis_index("enc")
    j = lax.axis_index("seq")
    n_enc = 4
    n_seq = 16
    self_index = e * n_seq + j
    senders, enc_rows = row_target.shape
    length, slab = text_rows.shape
    audio_count, audio_width = audio_rows.shape
    vision_count = vision_rows.shape[0]
    merge = vision_weight.shape[1]
    cap = 4
    wide = slab // 128 // n_enc * 128

    piece_a, piece_b, packed = pack(
        jnp.stack([e, t]),
        audio_weight,
        vision_weight,
        audio_rows,
        vision_rows,
    )
    hops = (1, 3, 2)
    along_y = [piece_a] + [shift_y(piece_a, k) for k in hops]
    along_z = [piece_b] + [shift_z(piece_b, k) for k in hops]
    along_y, along_z = lax.optimization_barrier((along_y, along_z))
    stack_a = jnp.concatenate(along_y, axis=0)
    stack_b = jnp.concatenate(along_z, axis=0)
    stack_a, stack_b = lax.optimization_barrier((stack_a, stack_b))
    pieces_a = [stack_a] + [shift_z(stack_a, k) for k in hops]
    pieces_b = [stack_b] + [shift_y(stack_b, k) for k in hops]
    own = lax.all_gather(packed, "enc", axis=0, tiled=False)
    z, y = j // 4, j % 4
    back = jnp.array((0,) + hops, jnp.int32)
    a_at = (((z - back) % 4)[:, None] * 4 + ((y - back) % 4)[None, :]).reshape(-1)
    b_at = (((y - back) % 4)[:, None] + ((z - back) % 4)[None, :] * 4).reshape(-1)

    ah, vh = audio_count // 2, vision_count // 2

    line = row_target.reshape(n_enc, n_seq, enc_rows)[:, j]
    line_dest = line // length
    line_slot = line_dest * (n_enc * cap) + jnp.arange(n_enc)[:, None] * cap + ranks(line_dest)
    a_slot = line_slot[:, :audio_count].reshape(n_enc, 2, ah)
    v_slot = line_slot[:, audio_count:].reshape(n_enc, 2, vh)
    halves = jnp.stack([t, 1 - t])
    a_slot = jnp.moveaxis(a_slot, 1, 0)[halves].reshape(-1)
    v_slot = jnp.moveaxis(v_slot, 1, 0)[halves].reshape(-1)
    row_slot = jnp.concatenate([a_slot, v_slot])
    cell = row_slot // 16 * 8 + row_slot % 8
    part = row_slot // 8 % 2
    cells = jnp.stack([jnp.where(part == 0, cell, -1), jnp.where(part == 1, cell, -1)])

    dest = row_target // length
    mine = (dest == self_index).astype(jnp.int32)
    rank_all = jnp.cumsum(mine, axis=1) - 1
    hot = (rank_all[:, :, None] == jnp.arange(cap)[None, None, :]) & (mine[:, :, None] == 1)
    incoming = jnp.sum(jnp.where(hot, (row_target % length)[:, :, None] + 1, 0), axis=1) - 1
    by_line = incoming.reshape(2, 2, n_seq, cap).transpose(0, 2, 1, 3).reshape(2, -1)
    filled = jnp.max(
        (jnp.arange(length)[:, None] == incoming.reshape(1, -1)).astype(jnp.float32), axis=1, keepdims=True
    )
    half = slab // 2
    nowhere = jnp.full_like(incoming, -1)
    spots = jnp.stack(
        [
            jnp.stack([incoming, nowhere], axis=1).reshape(-1),
            jnp.stack([nowhere, incoming], axis=1).reshape(-1),
        ],
        axis=1,
    )
    own_target = lax.dynamic_index_in_dim(row_target, self_index, 0, keepdims=True)
    own_dest = own_target // length
    own_cell = (own_dest * (2 * cap) + ranks(own_dest)).reshape(-1, 1)
    gain = norm_gain.reshape(2, slab)
    seg_row = segment_ids
    seg_col = segment_ids.reshape(length, 1)
    pieces_a, pieces_b, own, cells, by_line, filled, spots, own_cell, gain, seg_col, a_at, b_at = (
        lax.optimization_barrier(
            (pieces_a, pieces_b, own, cells, by_line, filled, spots, own_cell, gain, seg_col, a_at, b_at)
        )
    )
    other = swap(own)
    outgoing = encode(a_at, b_at, pieces_a, pieces_b, own, other, cells, senders * 8)
    arrived = lax.all_to_all(
        outgoing.reshape(senders, 8, slab // 2), ("enc", "seq"), split_axis=0, concat_axis=0, tiled=True
    )
    row_slab = place(by_line, arrived.reshape(senders * 8, slab // 2), text_rows, filled)

    other_slab = swap(row_slab)
    give, keep, inv_rms, row_part = attend(
        t, row_slab, other_slab, gain, qkv_weight, attn_grad, seg_row, seg_col
    )
    taken = swap(give)

    out8 = finish(t, row_slab, keep, taken, inv_rms, row_part, gain, spots)
    returned = lax.all_to_all(
        out8.reshape(senders, 2 * cap, half), ("enc", "seq"), split_axis=0, concat_axis=0, tiled=True
    )
    return collect(own_cell, returned.reshape(senders * 2 * cap, half), audio_count)


def solution(mesh):
    in_specs = (
        P(("enc", "seq"), None),
        P(("enc", "seq"), None),
        P("seq", "tp"),
        P("seq", None, "tp"),
        P(("enc", "seq"), "tp"),
        P(),
        P(("enc", "seq"), None),
        P(),
        P(None, "tp"),
        P(("enc", "seq"), "tp"),
    )
    out_specs = (P(("enc", "seq"), "tp"), P(("enc", "seq"), "tp"))
    return jax.shard_map(local, mesh=mesh, in_specs=in_specs, out_specs=out_specs, check_vma=False)
```

time: 168 us -> 180 us (1.071)
  waiting for transfers between devices: 58.5 us -> 73.7 us
  Pallas kernels: 33.7 us -> 48 us
  local copies, waits for them, and re-layouts: 20.2 us -> 8.35 us
  starting transfers between devices: 37.6 us -> 31.5 us
    pallas_call x1, Pallas kernels: 1.38 us -> 17.5 us  [pack(): pl.pallas_call(pack_kernel, out_shape=(jax.ShapeDtypeStruct((A_PIECE, 384...]
    unnamed x48 -> x28, local copies, waits for them, and re-layouts: 9.77 us -> 2.05 us
    ppermute x7 -> x6, waiting for transfers between devices: 4.9 us -> 9.91 us  [shift_y(): lax.ppermute(x, 'seq', [(i, i // 4 * 4 + (i % 4 + k) % 4) for i in range(...]
    ppermute x3, waiting for transfers between devices: 3.04 us -> 7.69 us  [swap(): return lax.ppermute(x, 'tp', [(0, 1), (1, 0)])]
    ppermute x7 -> x6, waiting for transfers between devices: 18.2 us -> 21.5 us  [shift_z(): lax.ppermute(x, 'seq', [(i, (i // 4 + k) % 4 * 4 + i % 4) for i in range(...]
    ppermute x7 -> x6, starting transfers between devices: 12 us -> 8.77 us  [shift_y(): lax.ppermute(x, 'seq', [(i, i // 4 * 4 + (i % 4 + k) % 4) for i in range(...]
    slice x5 -> x1, local copies, waits for them, and re-layouts: 3.09 us -> 0.19 us  [the longest x1 1.76 us: local(): near[3][2 * B_PIECE:]]
    pallas_call x1, Pallas kernels: 16.1 us -> 13.4 us  [attend(): pl.pallas_call(attend_kernel, out_shape=(jax.ShapeDtypeStruct((rows, slab...]
  transfers between devices with their start and end apart: 20 -> 18, of which waited for: 8 -> 10; matrix products, arithmetic and copies ran while one was open for 7% -> 5% of each run, Pallas kernels for 0% -> 0%
where the time goes in v5:
time: 180 us; the launch traced here: 179 us
  waiting for transfers between devices  73.7 us (41%)
  Pallas kernels  48 us (27%)
  starting transfers between devices  31.5 us (18%)
  between operations  14.4 us (8%)
  local copies, waits for them, and re-layouts  8.35 us (5%)
  other arithmetic  3.47 us (2%)
    ppermute x6, waiting for transfers between devices, shift_z(): lax.ppermute(x, 'seq', [(i, (i // 4 + k) % 4 * 4 + i % 4) for i in range(...  21.5 us
    all_to_all x1, waiting for transfers between devices, local(): lax.all_to_all(out8.reshape(senders, 2 * cap, half), ('enc', 'seq'), spli...  17.5 us
    pallas_call x1, Pallas kernels, pack(): pl.pallas_call(pack_kernel, out_shape=(jax.ShapeDtypeStruct((A_PIECE, 384...  17.5 us
    all_to_all x1, waiting for transfers between devices, local(): lax.all_to_all(outgoing.reshape(senders, 8, slab // 2), ('enc', 'seq'), s...  17.2 us
    pallas_call x1, Pallas kernels, attend(): pl.pallas_call(attend_kernel, out_shape=(jax.ShapeDtypeStruct((rows, slab...  13.4 us
    ppermute x6, starting transfers between devices, shift_z(): lax.ppermute(x, 'seq', [(i, (i // 4 + k) % 4 * 4 + i % 4) for i in range(...  10.2 us
    pallas_call x1, Pallas kernels, encode(): pl.pallas_call(encode_kernel, out_shape=jax.ShapeDtypeStruct((n_cells, 89...  9.91 us
    ppermute x6, waiting for transfers between devices, shift_y(): lax.ppermute(x, 'seq', [(i, i // 4 * 4 + (i % 4 + k) % 4) for i in range(...  9.91 us
  transfers between devices with their start and end apart: 18, of which 10 were waited for; matrix products, arithmetic and copies ran while one was open for 5% of the time, Pallas kernels for 0%

profile of v5, /device:TPU:0, one launch (start us, length us, event | category | flops | bytes accessed | tf_op | source)
XLA Modules:
  0.0 179.4 jit_solution(17290560304916629275)
XLA Ops:
  7.2 0.6 pad_add_fusion.2.place_ref
  7.9 17.5 %shard_map.122 = (bf16[224,384]{1,0:T(8,128)(2,1)}, bf16[256,384]{1,0:T(8,128)(2,1)}, bf16[192,1280]{1,0:T(8,128)(2,1)}) custom-call(s32[2]{0:T(128)} %pad_add_fusion.2.place_ref, bf16[80,1792]{1,0:T(8,128)(2,1)} %audio_w_ref.1, bf16[80,4,1792]{2,1,0:T(4,128)(2,1)} %vision_w_ref.1, bf16[128,1280]{1,0:T(8,128)(2,1)} %audio_ref.1, bf16[64,5120]{1,0:T(8,128)(2,1)} %vision_ref.1), custom_call_target="tpu_custom_call" | custom-call | bytes 1800000 | tf_op jit(solution)/shard_map/pallas_call | solution.py:277
  25.4 2.1 %collective-permute-start.3 = (bf16[256,384]{1,0:T(8,128)(2,1)}, bf16[256,384]{1,0:T(8,128)(2,1)S(1)}, u32[]{:S(2)}, u32[]{:S(2)}) collective-permute-start(bf16[256,384]{1,0:T(8,128)(2,1)} %get-tuple-element.43), channel_id=1, source_target_pairs={{0,8},{2,10},{4,12},{6,14},{8,16},{10,18},{12,20},{14,22},{16,24},... | collective-permute-start | bytes 589832 | tf_op jit(solution)/shard_map/ppermute | solution.py:605
  27.5 2.2 %collective-permute-start.4 = (bf16[256,384]{1,0:T(8,128)(2,1)}, bf16[256,384]{1,0:T(8,128)(2,1)S(1)}, u32[]{:S(2)}, u32[]{:S(2)}) collective-permute-start(bf16[256,384]{1,0:T(8,128)(2,1)} %get-tuple-element.43), channel_id=1, source_target_pairs={{0,24},{2,26},{4,28},{6,30},{8,0},{10,2},{12,4},{14,6},{16,8},{18,... | collective-permute-start | bytes 589832 | tf_op jit(solution)/shard_map/ppermute | solution.py:605
  29.7 1.8 collective-permute-start.5
  31.4 1.6 collective-permute-start
  33.0 1.7 collective-permute-start.1
  34.8 0.4 convert_reduce_fusion
  35.3 0.1 reshape.635
  35.5 0.6 reduce-window.6
  36.1 0.2 slice_reduce_fusion
  36.3 0.1 copy_bitcast_fusion
  36.5 0.6 gather_fusion
  37.0 0.1 concatenate.81
  37.2 0.6 gather_fusion.1
  37.8 0.1 concatenate.82
  37.9 0.2 select_reduce_fusion
  38.1 0.1 copy.56
  38.3 2.1 %collective-permute-start.2 = (bf16[224,384]{1,0:T(8,128)(2,1)S(1)}, bf16[224,384]{1,0:T(8,128)(2,1)S(1)}, u32[]{:S(2)}, u32[]{:S(2)}) collective-permute-start(bf16[224,384]{1,0:T(8,128)(2,1)S(1)} %copy-done.7), channel_id=1, source_target_pairs={{0,4},{2,6},{4,0},{6,2},{8,12},{10,14},{12,8},{14,10},{16,20},{18,... | collective-permute-start | bytes 516104 | tf_op jit(solution)/shard_map/ppermute | solution.py:601
  40.4 4.9 %collective-permute-done.2 = bf16[224,384]{1,0:T(8,128)(2,1)S(1)} collective-permute-done((bf16[224,384]{1,0:T(8,128)(2,1)S(1)}, bf16[224,384]{1,0:T(8,128)(2,1)S(1)}, u32[]{:S(2)}, u32[]{:S(2)}) %collective-permute-start.2) | collective-permute-done | bytes 172064 | tf_op jit(solution)/shard_map/ppermute | solution.py:601
  45.4 0.1 pad_maximum_fusion.gb0
  45.5 1.1 collective-permute-start.6
  46.7 1.9 %collective-permute-start.10 = (bf16[1024,384]{1,0:T(8,128)(2,1)S(1)}, bf16[1024,384]{1,0:T(8,128)(2,1)S(1)}, u32[]{:S(2)}, u32[]{:S(2)}) collective-permute-start(bf16[1024,384]{1,0:T(8,128)(2,1)S(1)} %pad_maximum_fusion.gb0), channel_id=1, source_target_pairs={{0,6},{2,0},{4,2},{6,4},{8,14},{10,8},{12,10},{14,12},{16,22},{18,... | collective-permute-start | bytes 2359304 | tf_op jit(solution)/shard_map/ppermute | solution.py:601
  48.6 0.6 collective-permute-start.11
  49.2 1.0 collective-permute-start.9
  50.2 2.2 %collective-permute-start.7 = (bf16[896,384]{1,0:T(8,128)(2,1)S(1)}, bf16[896,384]{1,0:T(8,128)(2,1)}, u32[]{:S(2)}, u32[]{:S(2)}) collective-permute-start(bf16[896,384]{1,0:T(8,128)(2,1)S(1)} %pad_maximum_fusion.1.ga0), channel_id=1, source_target_pairs={{0,24},{2,26},{4,28},{6,30},{8,0},{10,2},{12,4},{14,6},{16,8},{18,... | collective-permute-start | bytes 2064392 | tf_op jit(solution)/shard_map/ppermute | solution.py:605
  52.4 9.1 %collective-permute-done.6.ga1 = bf16[896,384]{1,0:T(8,128)(2,1)} collective-permute-done((bf16[896,384]{1,0:T(8,128)(2,1)S(1)}, bf16[896,384]{1,0:T(8,128)(2,1)}, u32[]{:S(2)}, u32[]{:S(2)}) %collective-permute-start.6) | collective-permute-done | bytes 688160 | tf_op jit(solution)/shard_map/ppermute | solution.py:605
  61.6 0.8 collective-permute-start.8
  62.4 0.1 sub.75
  62.5 0.1 copy.48
  62.6 0.6 add.218.a_at_ref
  63.2 0.6 add.222.b_at_ref
  63.8 0.1 stack_reshape.6
  63.9 0.1 stack_reshape.7
  64.0 0.1 copy.47
  64.1 0.1 reshape.639.e_row_ref
  64.2 0.1 sub.76
  64.4 0.6 reshape.641.gain_ref
  65.0 0.6 pad_add_fusion.cell_ref
  65.6 0.1 convert_reduce_fusion.1
  65.7 0.2 convert_reduce_fusion.2
  65.9 12.3 %collective-permute-done.7.ga2 = bf16[896,384]{1,0:T(8,128)(2,1)} collective-permute-done((bf16[896,384]{1,0:T(8,128)(2,1)S(1)}, bf16[896,384]{1,0:T(8,128)(2,1)}, u32[]{:S(2)}, u32[]{:S(2)}) %collective-permute-start.7) | collective-permute-done | bytes 688160 | tf_op jit(solution)/shard_map/ppermute | solution.py:605
  78.2 1.2 collective-permute-done.10.gb2
  79.4 3.8 %collective-permute-done.9.gb1 = bf16[1024,384]{1,0:T(8,128)(2,1)} collective-permute-done((bf16[1024,384]{1,0:T(8,128)(2,1)S(1)}, bf16[1024,384]{1,0:T(8,128)(2,1)}, u32[]{:S(2)}, u32[]{:S(2)}) %collective-permute-start.9) | collective-permute-done | bytes 786464 | tf_op jit(solution)/shard_map/ppermute | solution.py:601
  83.2 4.3 %collective-permute-done.12.other_ref = bf16[4,192,1280]{2,1,0:T(8,128)(2,1)} collective-permute-done((bf16[4,192,1280]{2,1,0:T(8,128)(2,1)}, bf16[4,192,1280]{2,1,0:T(8,128)(2,1)}, u32[]{:S(2)}, u32[]{:S(2)}) %collective-permute-start.12) | collective-permute-done | bytes 1966112 | tf_op jit(solution)/shard_map/ppermute | solution.py:597
  87.6 9.9 %shard_map.123 = bf16[512,896]{1,0:T(8,128)(2,1)} custom-call(s32[16]{0:T(128)} %add.218.a_at_ref, s32[16]{0:T(128)} %add.222.b_at_ref, bf16[896,384]{1,0:T(8,128)(2,1)} %copy-done.4, bf16[896,384]{1,0:T(8,128)(2,1)} %collective-permute-done.6.ga1, bf16[896,384]{1,0:T(8,128)(2,1)} %collective-permute-done.7.ga2, ...), custom_call_target="tpu_custom_call" | custom-call | flops 3000000000 | bytes 11000000 | tf_op jit(solution)/shard_map/pallas_call | solution.py:429
  97.5 7.4 %all-to-all-start = ((bf16[64,8,896]{2,1,0:T(8,128)(2,1)}), bf16[64,8,896]{2,1,0:T(8,128)(2,1)S(1)}, u32[]{:S(2)}, u32[]{:S(2)}) async-start(bf16[64,8,896]{2,1,0:T(8,128)(2,1)} %bitcast.62), calls=%async_computation | async-start | bytes 1835008 | tf_op jit(solution)/shard_map/all_to_all | solution.py:710
  104.9 0.1 copy.51.filled_ref
  105.0 17.2 %all-to-all-done = bf16[64,8,896]{2,1,0:T(8,128)(2,1)S(1)} async-done(((bf16[64,8,896]{2,1,0:T(8,128)(2,1)}), bf16[64,8,896]{2,1,0:T(8,128)(2,1)S(1)}, u32[]{:S(2)}, u32[]{:S(2)}) %all-to-all-start) | async-done | bytes 917536 | tf_op jit(solution)/shard_map/all_to_all | solution.py:710
  122.2 0.9 shard_map.124.own_hbm.rows_hbm
  123.0 0.1 collective-permute-start.13
  123.1 0.8 copy.52.seg_col_ref
  124.0 1.6 collective-permute-done.13.other_hbm
  125.6 0.9 copy-done.11
  126.5 13.4 %shard_map.125 = (bf16[256,1920]{1,0:T(8,128)(2,1)}, bf16[256,1792]{1,0:T(8,128)(2,1)}, f32[256,1]{1,0:T(8,128)}, f32[256,1]{1,0:T(8,128)}) custom-call(s32[1]{0:T(128)} %bitcast.1.half_ref, bf16[256,1792]{1,0:T(8,128)(2,1)} %copy-done, bf16[256,1792]{1,0:T(8,128)(2,1)} %copy-done.11, f32[2,1792]{1,0:T(2,128)} %reshape.641.gain_ref, ...), custom_call_target="tpu_custom_call" | custom-call | flops 5000000000 | bytes 14000000 | tf_op jit(solution)/shard_map/pallas_call | solution.py:147
  139.9 0.2 collective-permute-start.14
  140.1 0.9 copy.53.spot_ref
  141.0 1.8 collective-permute-done.14.taken_hbm
  142.8 1.0 copy-done.2
  143.7 4.9 %shard_map.126 = bf16[512,896]{1,0:T(8,128)(2,1)} custom-call(s32[1]{0:T(128)} %bitcast.1.half_ref, bf16[256,1792]{1,0:T(8,128)(2,1)} %copy-done, bf16[256,1792]{1,0:T(8,128)(2,1)} %get-tuple-element.67.keep_hbm, bf16[256,1920]{1,0:T(8,128)(2,1)} %copy-done.2, f32[256,1]{1,0:T(8,128)} %get-tuple-element.69.inv_ref, f32[256,1]{1,0:T(8,128)} %get-tuple-element.70.stat_ref, ...), custom_call_target="tpu_custom_call" | custom-call | flops 500000000 | bytes 4000000 | tf_op jit(solution)/shard_map/pallas_call | solution.py:548
  148.6 4.8 %all-to-all-start.1 = ((bf16[64,8,896]{2,1,0:T(8,128)(2,1)}), bf16[64,8,896]{2,1,0:T(8,128)(2,1)S(1)}, u32[]{:S(2)}, u32[]{:S(2)}) async-start(bf16[64,8,896]{2,1,0:T(8,128)(2,1)} %bitcast.61), calls=%async_computation.1 | async-start | bytes 1835008 | tf_op jit(solution)/shard_map/all_to_all | solution.py:722
  153.5 0.1 copy.54.cell_ref
  153.6 17.5 %all-to-all-done.1 = bf16[64,8,896]{2,1,0:T(8,128)(2,1)S(1)} async-done(((bf16[64,8,896]{2,1,0:T(8,128)(2,1)}), bf16[64,8,896]{2,1,0:T(8,128)(2,1)S(1)}, u32[]{:S(2)}, u32[]{:S(2)}) %all-to-all-start.1) | async-done | bytes 917536 | tf_op jit(solution)/shard_map/all_to_all | solution.py:722
  171.1 1.5 shard_map.127
  (65 shorter events, 0.9 us)
Async XLA Ops:
  7.2 27.6 %copy-start.5 = (s32[64,192]{1,0:T(8,128)S(1)}, s32[64,192]{1,0:T(8,128)}, u32[]{:S(2)}) copy-start(s32[64,192]{1,0:T(8,128)} %param.16) | copy-start | bytes 147460
  7.2 76.1 %all-gather.3.cloned.1.call-start = ((), (), s32[]{:S(2)}) async-start(), calls=%async_computation.2 | async-start | bytes 2457600 | tf_op jit(solution)/shard_map/all_gather | solution.py:658
  25.4 12.9 %copy-start.7 = (bf16[224,384]{1,0:T(8,128)(2,1)S(1)}, bf16[224,384]{1,0:T(8,128)(2,1)}, u32[]{:S(2)}) copy-start(bf16[224,384]{1,0:T(8,128)(2,1)} %get-tuple-element.39) | copy-start | bytes 516100
  25.4 15.0 %copy-start.10 = (s32[4]{0:T(128)S(1)}, s32[4]{0:T(128)}, u32[]{:S(2)}) copy-start(s32[4]{0:T(128)} %constant.183) | copy-start | bytes 52
  25.4 19.9 %collective-permute-start.3 = (bf16[256,384]{1,0:T(8,128)(2,1)}, bf16[256,384]{1,0:T(8,128)(2,1)S(1)}, u32[]{:S(2)}, u32[]{:S(2)}) collective-permute-start(bf16[256,384]{1,0:T(8,128)(2,1)} %get-tuple-element.43), channel_id=1, source_target_pairs={{0,8},{2,10},{4,12},{6,14},{8,16},{10,18},{12,20},{14,22},{16,24},... | collective-permute-start | bytes 589832 | tf_op jit(solution)/shard_map/ppermute | solution.py:605
  27.5 17.8 %collective-permute-start.4 = (bf16[256,384]{1,0:T(8,128)(2,1)}, bf16[256,384]{1,0:T(8,128)(2,1)S(1)}, u32[]{:S(2)}, u32[]{:S(2)}) collective-permute-start(bf16[256,384]{1,0:T(8,128)(2,1)} %get-tuple-element.43), channel_id=1, source_target_pairs={{0,24},{2,26},{4,28},{6,30},{8,0},{10,2},{12,4},{14,6},{16,8},{18,... | collective-permute-start | bytes 589832 | tf_op jit(solution)/shard_map/ppermute | solution.py:605
  29.7 15.6 %collective-permute-start.5 = (bf16[256,384]{1,0:T(8,128)(2,1)}, bf16[256,384]{1,0:T(8,128)(2,1)S(1)}, u32[]{:S(2)}, u32[]{:S(2)}) collective-permute-start(bf16[256,384]{1,0:T(8,128)(2,1)} %get-tuple-element.43), channel_id=1, source_target_pairs={{0,16},{2,18},{4,20},{6,22},{8,24},{10,26},{12,28},{14,30},{16,0},... | collective-permute-start | bytes 589832 | tf_op jit(solution)/shard_map/ppermute | solution.py:605
  31.4 6.8 %collective-permute-start = (bf16[224,384]{1,0:T(8,128)(2,1)}, bf16[224,384]{1,0:T(8,128)(2,1)S(1)}, u32[]{:S(2)}, u32[]{:S(2)}) collective-permute-start(bf16[224,384]{1,0:T(8,128)(2,1)} %get-tuple-element.39), channel_id=1, source_target_pairs={{0,2},{2,4},{4,6},{6,0},{8,10},{10,12},{12,14},{14,8},{16,18},{18,... | collective-permute-start | bytes 516104 | tf_op jit(solution)/shard_map/ppermute | solution.py:601
  33.0 7.4 %collective-permute-start.1 = (bf16[224,384]{1,0:T(8,128)(2,1)}, bf16[224,384]{1,0:T(8,128)(2,1)S(1)}, u32[]{:S(2)}, u32[]{:S(2)}) collective-permute-start(bf16[224,384]{1,0:T(8,128)(2,1)} %get-tuple-element.39), channel_id=1, source_target_pairs={{0,6},{2,0},{4,2},{6,4},{8,14},{10,8},{12,10},{14,12},{16,22},{18,... | collective-permute-start | bytes 516104 | tf_op jit(solution)/shard_map/ppermute | solution.py:601
  34.7 10.7 %copy-start.6 = (bf16[256,384]{1,0:T(8,128)(2,1)S(1)}, bf16[256,384]{1,0:T(8,128)(2,1)}, u32[]{:S(2)}) copy-start(bf16[256,384]{1,0:T(8,128)(2,1)} %get-tuple-element.43) | copy-start | bytes 589828
  38.3 7.0 %collective-permute-start.2 = (bf16[224,384]{1,0:T(8,128)(2,1)S(1)}, bf16[224,384]{1,0:T(8,128)(2,1)S(1)}, u32[]{:S(2)}, u32[]{:S(2)}) collective-permute-start(bf16[224,384]{1,0:T(8,128)(2,1)S(1)} %copy-done.7), channel_id=1, source_target_pairs={{0,4},{2,6},{4,0},{6,2},{8,12},{10,14},{12,8},{14,10},{16,20},{18,... | collective-permute-start | bytes 516104 | tf_op jit(solution)/shard_map/ppermute | solution.py:601
  40.4 24.0 %copy-start.8 = (f32[3584]{0:T(1024)S(1)}, f32[3584]{0:T(1024)}, u32[]{:S(2)}) copy-start(f32[3584]{0:T(1024)} %param.18) | copy-start | bytes 43012
  45.4 42.2 %copy-start.4 = (bf16[896,384]{1,0:T(8,128)(2,1)}, bf16[896,384]{1,0:T(8,128)(2,1)S(1)}, u32[]{:S(2)}) copy-start(bf16[896,384]{1,0:T(8,128)(2,1)S(1)} %pad_maximum_fusion.1.ga0) | copy-start | bytes 2064388
  45.5 42.1 %copy-start.3 = (bf16[1024,384]{1,0:T(8,128)(2,1)}, bf16[1024,384]{1,0:T(8,128)(2,1)S(1)}, u32[]{:S(2)}) copy-start(bf16[1024,384]{1,0:T(8,128)(2,1)S(1)} %pad_maximum_fusion.gb0) | copy-start | bytes 2359300
  45.5 16.1 %collective-permute-start.6 = (bf16[896,384]{1,0:T(8,128)(2,1)S(1)}, bf16[896,384]{1,0:T(8,128)(2,1)}, u32[]{:S(2)}, u32[]{:S(2)}) collective-permute-start(bf16[896,384]{1,0:T(8,128)(2,1)S(1)} %pad_maximum_fusion.1.ga0), channel_id=1, source_target_pairs={{0,8},{2,10},{4,12},{6,14},{8,16},{10,18},{12,20},{14,22},{16,24},... | collective-permute-start | bytes 2064392 | tf_op jit(solution)/shard_map/ppermute | solution.py:605
  46.7 32.7 %collective-permute-start.10 = (bf16[1024,384]{1,0:T(8,128)(2,1)S(1)}, bf16[1024,384]{1,0:T(8,128)(2,1)S(1)}, u32[]{:S(2)}, u32[]{:S(2)}) collective-permute-start(bf16[1024,384]{1,0:T(8,128)(2,1)S(1)} %pad_maximum_fusion.gb0), channel_id=1, source_target_pairs={{0,6},{2,0},{4,2},{6,4},{8,14},{10,8},{12,10},{14,12},{16,22},{18,... | collective-permute-start | bytes 2359304 | tf_op jit(solution)/shard_map/ppermute | solution.py:601
  48.6 30.9 %collective-permute-start.11 = (bf16[1024,384]{1,0:T(8,128)(2,1)S(1)}, bf16[1024,384]{1,0:T(8,128)(2,1)}, u32[]{:S(2)}, u32[]{:S(2)}) collective-permute-start(bf16[1024,384]{1,0:T(8,128)(2,1)S(1)} %pad_maximum_fusion.gb0), channel_id=1, source_target_pairs={{0,4},{2,6},{4,0},{6,2},{8,12},{10,14},{12,8},{14,10},{16,20},{18,... | collective-permute-start | bytes 2359304 | tf_op jit(solution)/shard_map/ppermute | solution.py:601
  49.2 34.0 %collective-permute-start.9 = (bf16[1024,384]{1,0:T(8,128)(2,1)S(1)}, bf16[1024,384]{1,0:T(8,128)(2,1)}, u32[]{:S(2)}, u32[]{:S(2)}) collective-permute-start(bf16[1024,384]{1,0:T(8,128)(2,1)S(1)} %pad_maximum_fusion.gb0), channel_id=1, source_target_pairs={{0,2},{2,4},{4,6},{6,0},{8,10},{10,12},{12,14},{14,8},{16,18},{18,... | collective-permute-start | bytes 2359304 | tf_op jit(solution)/shard_map/ppermute | solution.py:601
  50.2 28.0 %collective-permute-start.7 = (bf16[896,384]{1,0:T(8,128)(2,1)S(1)}, bf16[896,384]{1,0:T(8,128)(2,1)}, u32[]{:S(2)}, u32[]{:S(2)}) collective-permute-start(bf16[896,384]{1,0:T(8,128)(2,1)S(1)} %pad_maximum_fusion.1.ga0), channel_id=1, source_target_pairs={{0,24},{2,26},{4,28},{6,30},{8,0},{10,2},{12,4},{14,6},{16,8},{18,... | collective-permute-start | bytes 2064392 | tf_op jit(solution)/shard_map/ppermute | solution.py:605
  61.6 16.7 %collective-permute-start.8 = (bf16[896,384]{1,0:T(8,128)(2,1)S(1)}, bf16[896,384]{1,0:T(8,128)(2,1)}, u32[]{:S(2)}, u32[]{:S(2)}) collective-permute-start(bf16[896,384]{1,0:T(8,128)(2,1)S(1)} %pad_maximum_fusion.1.ga0), channel_id=1, source_target_pairs={{0,16},{2,18},{4,20},{6,22},{8,24},{10,26},{12,28},{14,30},{16,0},... | collective-permute-start | bytes 2064392 | tf_op jit(solution)/shard_map/ppermute | solution.py:605
  79.4 8.1 %copy-start.12 = (bf16[1024,384]{1,0:T(8,128)(2,1)}, bf16[1024,384]{1,0:T(8,128)(2,1)S(1)}, u32[]{:S(2)}) copy-start(bf16[1024,384]{1,0:T(8,128)(2,1)S(1)} %collective-permute-done.10.gb2) | copy-start | bytes 2359300
  83.2 4.3 %collective-permute-start.12 = (bf16[4,192,1280]{2,1,0:T(8,128)(2,1)}, bf16[4,192,1280]{2,1,0:T(8,128)(2,1)}, u32[]{:S(2)}, u32[]{:S(2)}) collective-permute-start(bf16[4,192,1280]{2,1,0:T(8,128)(2,1)} %bitcast.71), channel_id=1, source_target_pairs={{0,1},{1,0},{2,3},{3,2},{4,5},{5,4},{6,7},{7,6},{8,9},{9,8},{10,11... | collective-permute-start | bytes 5898248 | tf_op jit(solution)/shard_map/ppermute | solution.py:597
  97.5 24.7 %copy-start.1 = (bf16[256,1792]{1,0:T(8,128)(2,1)S(1)}, bf16[256,1792]{1,0:T(8,128)(2,1)}, u32[]{:S(2)}) copy-start(bf16[256,1792]{1,0:T(8,128)(2,1)} %text_hbm.1) | copy-start | bytes 2752516
  97.5 24.7 %all-to-all-start = ((bf16[64,8,896]{2,1,0:T(8,128)(2,1)}), bf16[64,8,896]{2,1,0:T(8,128)(2,1)S(1)}, u32[]{:S(2)}, u32[]{:S(2)}) async-start(bf16[64,8,896]{2,1,0:T(8,128)(2,1)} %bitcast.62), calls=%async_computation | async-start | bytes 1835008 | tf_op jit(solution)/shard_map/all_to_all | solution.py:710
  104.8 18.3 %copy-start.9 = (s32[1,256]{1,0:T(1,128)S(1)}, s32[1,256]{1,0:T(1,128)}, u32[]{:S(2)}) copy-start(s32[1,256]{1,0:T(1,128)} %seg_row_ref.1) | copy-start | bytes 3076
  123.0 2.6 %copy-start = (bf16[256,1792]{1,0:T(8,128)(2,1)}, bf16[256,1792]{1,0:T(8,128)(2,1)S(1)}, u32[]{:S(2)}) copy-start(bf16[256,1792]{1,0:T(8,128)(2,1)S(1)} %shard_map.124.own_hbm.rows_hbm) | copy-start | bytes 2752516
  123.0 2.6 %collective-permute-start.13 = (bf16[256,1792]{1,0:T(8,128)(2,1)S(1)}, bf16[256,1792]{1,0:T(8,128)(2,1)S(1)}, u32[]{:S(2)}, u32[]{:S(2)}) collective-permute-start(bf16[256,1792]{1,0:T(8,128)(2,1)S(1)} %shard_map.124.own_hbm.rows_hbm), channel_id=1, source_target_pairs={{0,1},{1,0},{2,3},{3,2},{4,5},{5,4},{6,7},{7,6},{8,9},{9,8},{10,11... | collective-permute-start | bytes 2752520 | tf_op jit(solution)/shard_map/ppermute | solution.py:597
  125.6 0.9 copy-start.11
  139.9 2.9 %collective-permute-start.14 = (bf16[256,1920]{1,0:T(8,128)(2,1)}, bf16[256,1920]{1,0:T(8,128)(2,1)S(1)}, u32[]{:S(2)}, u32[]{:S(2)}) collective-permute-start(bf16[256,1920]{1,0:T(8,128)(2,1)} %get-tuple-element.68), channel_id=1, source_target_pairs={{0,1},{1,0},{2,3},{3,2},{4,5},{5,4},{6,7},{7,6},{8,9},{9,8},{10,11... | collective-permute-start | bytes 2949128 | tf_op jit(solution)/shard_map/ppermute | solution.py:597
  142.7 1.0 copy-start.2
  148.6 22.4 %all-to-all-start.1 = ((bf16[64,8,896]{2,1,0:T(8,128)(2,1)}), bf16[64,8,896]{2,1,0:T(8,128)(2,1)S(1)}, u32[]{:S(2)}, u32[]{:S(2)}) async-start(bf16[64,8,896]{2,1,0:T(8,128)(2,1)} %bitcast.61), calls=%async_computation.1 | async-start | bytes 1835008 | tf_op jit(solution)/shard_map/all_to_all | solution.py:722
Sparse Core Ops, SparseCore 0:
  34.8 28.6 all-gather.2

commit v6 on v5

--- a/solution.py
+++ b/solution.py
@@ -3,6 +3,7 @@
 from jax import lax
 from jax.experimental import pallas as pl
 from jax.experimental.pallas import tpu as pltpu
+from jax.sharding import Mesh
 from jax.sharding import PartitionSpec as P
 
 HEAD_DIM = 128
@@ -13,7 +14,11 @@
 NT = (((1,), (1,)), ((), ()))
 NN = (((1,), (0,)), ((), ()))
 TAIL = 128
-BIG = 60 * 1024 * 1024
+BIG = 26 * 1024 * 1024
+
+
+def in_hbm(x):
+    return pltpu.with_memory_space_constraint(x, pltpu.HBM)
 
 
 def dot(x, y, dims=NN):
@@ -22,15 +27,15 @@
 
 def attend_kernel(
     half_ref,
-    own_hbm,
-    other_hbm,
+    own_ref,
+    other_ref,
     gain_ref,
     weight_ref,
     upstream_hbm,
     seg_row_ref,
     seg_col_ref,
-    give_hbm,
-    keep_hbm,
+    give_ref,
+    keep_ref,
     inv_ref,
     stat_ref,
     normed_ref,
@@ -39,15 +44,11 @@
     sgrad_ref,
     bias_ref,
     held_ref,
-    own_ref,
-    other_ref,
     upstream_ref,
-    give_ref,
-    keep_ref,
     sems,
 ):
     bf16, f32 = jnp.bfloat16, jnp.float32
-    rows, slab = own_hbm.shape
+    rows, slab = own_ref.shape
     group = weight_ref.shape[1]
     heads = group // HEAD_DIM - 2
     chunks = [(at, min(512, group - at)) for at in range(0, group, 512)]
@@ -58,20 +59,14 @@
         )
         for n, (at, size) in enumerate(chunks)
     ]
-    small = [
-        pltpu.make_async_copy(own_hbm, own_ref, sems.at[pieces]),
-        pltpu.make_async_copy(other_hbm, other_ref, sems.at[pieces + 1]),
-        pltpu.make_async_copy(upstream_hbm, upstream_ref, sems.at[pieces + 2]),
-    ]
-    for copy in small[:2] + copies + small[2:]:
+    last = pltpu.make_async_copy(upstream_hbm, upstream_ref, sems.at[pieces])
+    for copy in copies + [last]:
         copy.start()
     place_u = lax.broadcasted_iota(jnp.int32, (rows, rows), 0)
     place_t = lax.broadcasted_iota(jnp.int32, (rows, rows), 1)
     allowed = (seg_col_ref[...] == seg_row_ref[...]) & (place_u <= place_t)
     bias_ref[...] = jnp.where(allowed, 0.0, -1e30)
 
-    small[0].wait()
-    small[1].wait()
     t = half_ref[0]
     own_at = pl.multiple_of(t * slab, HEAD_DIM)
     other_at = pl.multiple_of((1 - t) * slab, HEAD_DIM)
@@ -94,7 +89,7 @@
         unscaled_ref[:, at : at + size] = value
         scaled_ref[:, at : at + size] = (value * inv).astype(bf16)
 
-    small[2].wait()
+    last.wait()
     key = scaled_ref[:, heads * HEAD_DIM : (heads + 1) * HEAD_DIM]
     val = scaled_ref[:, (heads + 1) * HEAD_DIM :]
     grad_key = jnp.zeros((rows, HEAD_DIM), f32)
@@ -129,13 +124,7 @@
     give_ref[:, slab:] = jnp.where(lane == 0, high.astype(f32), low.astype(f32)).astype(bf16)
 
     keep_ref[...] = dot(sgrad_ref[...], held_ref[pl.ds(own_at, slab), :], NT).astype(bf16)
-    keep_out = pltpu.make_async_copy(keep_ref, keep_hbm, sems.at[pieces + 3])
-    keep_out.start()
     give_ref[:, :slab] = dot(sgrad_ref[...], held_ref[pl.ds(other_at, slab), :], NT).astype(bf16)
-    give_out = pltpu.make_async_copy(give_ref, give_hbm, sems.at[pieces + 4])
-    give_out.start()
-    keep_out.wait()
-    give_out.wait()
 
 
 def attend(half, own, other, gain, qkv_weight, upstream, seg_row, seg_col):
@@ -152,9 +141,9 @@
             jax.ShapeDtypeStruct((rows, 1), f32),
             jax.ShapeDtypeStruct((rows, 1), f32),
         ),
-        in_specs=[pl.BlockSpec(memory_space=pltpu.SMEM), anywhere, anywhere, vmem]
+        in_specs=[pl.BlockSpec(memory_space=pltpu.SMEM), vmem, vmem, vmem]
         + [anywhere, anywhere, vmem, vmem],
-        out_specs=(anywhere, anywhere, vmem, vmem),
+        out_specs=(vmem,) * 4,
         scratch_shapes=[
             pltpu.VMEM((rows, 2 * slab), bf16),
             pltpu.VMEM((rows, group), f32),
@@ -162,12 +151,8 @@
             pltpu.VMEM((rows, group), bf16),
             pltpu.VMEM((rows, rows), f32),
             pltpu.VMEM((2 * slab, group), bf16),
-            pltpu.VMEM((rows, slab), bf16),
-            pltpu.VMEM((rows, slab), bf16),
             pltpu.VMEM(upstream.shape, bf16),
-            pltpu.VMEM((rows, slab + TAIL), bf16),
-            pltpu.VMEM((rows, slab), bf16),
-            pltpu.SemaphoreType.DMA((8,)),
+            pltpu.SemaphoreType.DMA((4,)),
         ],
         compiler_params=pltpu.CompilerParams(vmem_limit_bytes=BIG),
         cost_estimate=pl.CostEstimate(flops=5_000_000_000, bytes_accessed=14_000_000, transcendentals=500_000),
@@ -176,8 +161,8 @@
         own,
         other,
         gain,
-        qkv_weight,
-        upstream,
+        in_hbm(qkv_weight),
+        in_hbm(upstream),
         seg_row,
         seg_col,
     )
@@ -284,7 +269,7 @@
             ),
         ),
         in_specs=[pl.BlockSpec(memory_space=pltpu.SMEM)] + [anywhere] * 4,
-        out_specs=(vmem, vmem, anywhere),
+        out_specs=(vmem, vmem, vmem),
         scratch_shapes=[
             pltpu.VMEM((k, 384), bf16),
             pltpu.VMEM((k, 128), bf16),
@@ -295,16 +280,12 @@
         ],
         compiler_params=pltpu.CompilerParams(vmem_limit_bytes=BIG),
         cost_estimate=pl.CostEstimate(flops=0, bytes_accessed=1_800_000, transcendentals=0),
-    )(where, audio_weight, vision_weight, audio_rows, vision_rows)
+    )(where, in_hbm(audio_weight), in_hbm(vision_weight), in_hbm(audio_rows), in_hbm(vision_rows))
 
 
 def encode_kernel(
-    a_at_ref,
     b_at_ref,
-    ga0,
-    ga1,
-    ga2,
-    ga3,
+    ga,
     gb0,
     gb1,
     gb2,
@@ -313,59 +294,36 @@
     other_ref,
     cell_ref,
     out_ref,
-    w_ref,
-    wt_ref,
+    wa_ref,
+    wv_ref,
     ta_ref,
-    tb_ref,
+    tv_ref,
+    ra_ref,
+    rb_ref,
     x_ref,
     enc_ref,
     sems,
 ):
     bf16, f32 = jnp.bfloat16, jnp.float32
     audio_width = x_ref.shape[3]
-    audio_k = audio_width // 16
-    vision_k = 4 * audio_k
+    audio_k = wa_ref.shape[1]
     cut = A_ROWS - audio_k
-    sources = ((ga0, gb0), (ga1, gb1), (ga2, gb2), (ga3, gb3))
-
-    def spots(p):
-        audio_at = pl.multiple_of(a_at_ref[p] * audio_k, 16)
-        low_at = pl.multiple_of(audio_width + a_at_ref[p] * vision_k, 16)
-        high_at = pl.multiple_of(audio_width + b_at_ref[p] * vision_k + cut, 16)
-        return audio_at, low_at, high_at
-
-    def bases(n):
-        return pl.multiple_of(n * A_PIECE, 16), pl.multiple_of(n * B_PIECE, 16)
-
-    for m, (ga, gb) in enumerate(sources):
-
-        @pl.loop(0, 4)
-        def _(n):
-            p = m * 4 + n
-            base_a, base_b = bases(n)
-            pltpu.make_async_copy(
-                ga.at[pl.ds(base_a + A_ROWS, A_TAIL), :], ta_ref.at[p], sems.at[2]
-            ).start()
-            pltpu.make_async_copy(
-                gb.at[pl.ds(base_b + B_ROWS, B_TAIL), :], tb_ref.at[p], sems.at[3]
-            ).start()
-
+    shards_b = (gb0, gb1, gb2, gb3)
+    pltpu.make_async_copy(ga.at[:, A_ROWS:, :], ra_ref, sems.at[2]).start()
+    for m, gb in enumerate(shards_b):
+        pltpu.make_async_copy(
+            gb.at[:, B_ROWS:, :], rb_ref.at[4 * m : 4 * m + 4], sems.at[3]
+        ).start()
     pltpu.make_async_copy(own_ref, x_ref.at[0], sems.at[0]).start()
     pltpu.make_async_copy(other_ref, x_ref.at[1], sems.at[1]).start()
-    for m, (ga, gb) in enumerate(sources):
-
-        @pl.loop(0, 4)
-        def _(n):
-            base_a, base_b = bases(n)
-            audio_at, low_at, high_at = spots(m * 4 + n)
+    audio_copy = pltpu.make_async_copy(ga.at[:, :audio_k, :], wa_ref, sems.at[4])
+    audio_copy.start()
+    low_copy = pltpu.make_async_copy(ga.at[:, audio_k:A_ROWS, :], wv_ref.at[:, :cut, :], sems.at[5])
+    low_copy.start()
+    for m, gb in enumerate(shards_b):
+        for n in range(4):
             pltpu.make_async_copy(
-                ga.at[pl.ds(base_a, audio_k), :], w_ref.at[pl.ds(audio_at, audio_k), :], sems.at[4]
-            ).start()
-            pltpu.make_async_copy(
-                ga.at[pl.ds(base_a + audio_k, cut), :], w_ref.at[pl.ds(low_at, cut), :], sems.at[5]
-            ).start()
-            pltpu.make_async_copy(
-                gb.at[pl.ds(base_b, B_ROWS), :], w_ref.at[pl.ds(high_at, B_ROWS), :], sems.at[5]
+                gb.at[n, :B_ROWS, :], wv_ref.at[b_at_ref[4 * m + n], cut:, :], sems.at[6]
             ).start()
 
     count = cell_ref.shape[1]
@@ -374,20 +332,24 @@
     first = jnp.where(line == cell_ref[0:1, :], 1.0, 0.0).astype(bf16)
     second = jnp.where(line == cell_ref[1:2, :], 1.0, 0.0).astype(bf16)
 
-    pltpu.make_async_copy(ta_ref, ta_ref, sems.at[2]).wait()
-    pltpu.make_async_copy(tb_ref, tb_ref, sems.at[3]).wait()
+    pltpu.make_async_copy(ra_ref, ra_ref, sems.at[2]).wait()
 
     @pl.loop(0, 16)
     def _(p):
-        audio_at, low_at, high_at = spots(p)
-        ta = jnp.concatenate([ta_ref[p, :, q * 128 : (q + 1) * 128] for q in range(3)], axis=0)
-        wt_ref[pl.ds(audio_at, audio_k), :] = ta[:audio_k]
-        wt_ref[pl.ds(low_at, 96 - audio_k), :] = ta[audio_k:]
-        wt_ref[pl.ds(low_at + (96 - audio_k), 96), :] = roll_half(ta)
-        tb = jnp.concatenate([tb_ref[p, :, q * 128 : (q + 1) * 128] for q in range(2)], axis=0)
-        wt_ref[pl.ds(high_at, 96), :] = tb
-        wt_ref[pl.ds(high_at + 96, 16), :] = tb_ref[p, :16, 256:]
-        wt_ref[pl.ds(high_at + 112, 96), :] = roll_half(tb)
+        ta = jnp.concatenate([ra_ref[p, :, q * 128 : (q + 1) * 128] for q in range(3)], axis=0)
+        ta_ref[p, :, :] = ta[:audio_k]
+        tv_ref[p, : 96 - audio_k, :] = ta[audio_k:]
+        tv_ref[p, 96 - audio_k : cut, :] = roll_half(ta)
+
+    pltpu.make_async_copy(rb_ref, rb_ref, sems.at[3]).wait()
+
+    @pl.loop(0, 16)
+    def _(p):
+        at = b_at_ref[p]
+        tb = jnp.concatenate([rb_ref[p, :, q * 128 : (q + 1) * 128] for q in range(2)], axis=0)
+        tv_ref[at, cut : cut + 96, :] = tb
+        tv_ref[at, cut + 96 : cut + 112, :] = rb_ref[p, :16, 256:]
+        tv_ref[at, cut + 112 :, :] = roll_half(tb)
 
     halves, n_enc = x_ref.shape[:2]
     audio = 64
@@ -395,56 +357,67 @@
     n_audio = halves * n_enc * audio
     n_vision = halves * n_enc * vision
 
-    def weights(at):
-        return jnp.concatenate([w_ref[at : at + audio_width, :], wt_ref[at : at + audio_width, :]], axis=1)
+    def weights(main, last):
+        size = main.shape[0] * main.shape[1]
+        return jnp.concatenate([main.reshape(size, 384), last.reshape(size, 128)], axis=1)
+
+    def keep_rows(value, base, each):
+        run = 2 * each
+        for h in range(2):
+            for g in range(2):
+                at = g * count + base + h * run
+                enc_ref[at : at + run, :] = value[(2 * h + g) * run : (2 * h + g + 1) * run]
 
     pltpu.make_async_copy(own_ref, x_ref.at[0], sems.at[0]).wait()
     pltpu.make_async_copy(other_ref, x_ref.at[1], sems.at[1]).wait()
-    pltpu.make_async_copy(w_ref.at[:audio_width], w_ref.at[:audio_width], sems.at[4]).wait()
+    audio_copy.wait()
     rows = x_ref[:, :, :audio, :].reshape(n_audio, audio_width)
-    enc_ref[:n_audio, :] = dot(rows, weights(0)).astype(bf16)
-    pltpu.make_async_copy(w_ref.at[audio_width:], w_ref.at[audio_width:], sems.at[5]).wait()
+    keep_rows(dot(rows, weights(wa_ref[...], ta_ref[...])).astype(bf16), 0, audio)
+    low_copy.wait()
+    pltpu.make_async_copy(wv_ref.at[:, cut:, :], wv_ref.at[:, cut:, :], sems.at[6]).wait()
     total = jnp.zeros((n_vision, 512), f32)
     for i in range(4):
         rows = x_ref[:, :, audio + i * vision : audio + (i + 1) * vision, :]
-        total = total + dot(rows.reshape(n_vision, audio_width), weights((i + 1) * audio_width))
-    enc_ref[n_audio:, :] = total.astype(bf16)
-
-    main = enc_ref[:, :384]
-    out_ref[:, :384] = dot(first, main).astype(bf16)
-    out_ref[:, 384:768] = dot(second, main).astype(bf16)
-    last = enc_ref[:, 384:].astype(f32)
-    lane = lax.broadcasted_iota(jnp.int32, last.shape, 1)
-    last = jnp.where(lane < 64, last, 0.0)
-    moved = pltpu.roll(last, 64, 1)
-    out_ref[:, 768:] = (dot(first, last.astype(bf16)) + dot(second, moved.astype(bf16))).astype(bf16)
-
-
-def encode(a_at, b_at, pieces_a, pieces_b, own, other, cells, n_cells):
+        part = weights(wv_ref[4 * i : 4 * i + 4], tv_ref[4 * i : 4 * i + 4])
+        total = total + dot(rows.reshape(n_vision, audio_width), part)
+    keep_rows(total.astype(bf16), 4 * audio, vision)
+
+    out_ref[:, :384] = dot(first, enc_ref[:count, :384]).astype(bf16)
+    out_ref[:, 384:768] = dot(second, enc_ref[count:, :384]).astype(bf16)
+    low = dot(first, enc_ref[:count, 384:])
+    high = dot(second, enc_ref[count:, 384:])
+    lane = lax.broadcasted_iota(jnp.int32, low.shape, 1)
+    out_ref[:, 768:] = jnp.where(lane < 64, low, pltpu.roll(high, 64, 1)).astype(bf16)
+
+
+def encode(b_at, shards_a, shards_b, own, other, cells, n_cells):
     bf16 = jnp.bfloat16
     n_enc, rows, width = own.shape
     smem = pl.BlockSpec(memory_space=pltpu.SMEM)
     vmem = pl.BlockSpec(memory_space=pltpu.VMEM)
     anywhere = pl.BlockSpec(memory_space=pl.ANY)
+    k = width // 16
     return pl.pallas_call(
         encode_kernel,
         out_shape=jax.ShapeDtypeStruct((n_cells, 896), bf16),
-        in_specs=[smem, smem] + [anywhere] * 10 + [vmem],
+        in_specs=[smem] + [anywhere] * 7 + [vmem],
         out_specs=vmem,
         scratch_shapes=[
-            pltpu.VMEM((5 * width, 384), bf16),
-            pltpu.VMEM((5 * width, 128), bf16),
+            pltpu.VMEM((16, k, 384), bf16),
+            pltpu.VMEM((16, 4 * k, 384), bf16),
+            pltpu.VMEM((16, k, 128), bf16),
+            pltpu.VMEM((16, 4 * k, 128), bf16),
             pltpu.VMEM((16, A_TAIL, 384), bf16),
             pltpu.VMEM((16, B_TAIL, 384), bf16),
             pltpu.VMEM((2, n_enc, rows, width), bf16),
-            pltpu.VMEM((cells.shape[1], 512), bf16),
-            pltpu.SemaphoreType.DMA((6,)),
+            pltpu.VMEM((2 * cells.shape[1], 512), bf16),
+            pltpu.SemaphoreType.DMA((7,)),
         ],
         compiler_params=pltpu.CompilerParams(vmem_limit_bytes=BIG),
         cost_estimate=pl.CostEstimate(
             flops=3_000_000_000, bytes_accessed=11_000_000, transcendentals=0
         ),
-    )(a_at, b_at, *pieces_a, *pieces_b, own, other, cells)
+    )(b_at, in_hbm(shards_a), *(in_hbm(x) for x in shards_b), in_hbm(own), other, cells)
 
 
 def place_kernel(e_row_ref, arrived_ref, text_hbm, filled_ref, out_ref, text_ref, sem):
@@ -494,28 +467,17 @@
 
 def finish_kernel(
     half_ref,
-    rows_hbm,
-    keep_hbm,
-    taken_hbm,
+    rows_ref,
+    keep_ref,
+    taken_ref,
     inv_ref,
     stat_ref,
     gain_ref,
     spot_ref,
     out_ref,
-    rows_ref,
-    keep_ref,
-    taken_ref,
     grad_ref,
-    sems,
 ):
     bf16, f32 = jnp.bfloat16, jnp.float32
-    copies = [
-        pltpu.make_async_copy(taken_hbm, taken_ref, sems.at[0]),
-        pltpu.make_async_copy(rows_hbm, rows_ref, sems.at[1]),
-        pltpu.make_async_copy(keep_hbm, keep_ref, sems.at[2]),
-    ]
-    for copy in copies:
-        copy.start()
     rows, slab = rows_ref.shape
     cells = out_ref.shape[0]
     half = slab // 2
@@ -525,8 +487,6 @@
     first = jnp.where(line == spot_ref[:, 0:1], 1.0, 0.0).astype(bf16)
     second = jnp.where(line == spot_ref[:, 1:2], 1.0, 0.0).astype(bf16)
     both = jnp.concatenate([first, second], axis=1)
-    for copy in copies:
-        copy.wait()
     sent = taken_ref[:, slab:].astype(f32)
     stat = stat_ref[...] + sent[:, 0:1] + sent[:, 1:2]
     factor = inv * inv * inv / (2 * slab) * stat
@@ -542,22 +502,15 @@
 def finish(half, rows, keep, taken, inv, stat, gain, spots):
     bf16 = jnp.bfloat16
     vmem = pl.BlockSpec(memory_space=pltpu.VMEM)
-    anywhere = pl.BlockSpec(memory_space=pl.ANY)
     cells = spots.shape[0]
     count, slab = rows.shape
     return pl.pallas_call(
         finish_kernel,
         out_shape=jax.ShapeDtypeStruct((cells, slab // 2), bf16),
-        in_specs=[pl.BlockSpec(memory_space=pltpu.SMEM)] + [anywhere] * 3 + [vmem] * 4,
+        in_specs=[pl.BlockSpec(memory_space=pltpu.SMEM)] + [vmem] * 7,
         out_specs=vmem,
-        scratch_shapes=[
-            pltpu.VMEM((count, slab), bf16),
-            pltpu.VMEM((count, slab), bf16),
-            pltpu.VMEM((count, slab + TAIL), bf16),
-            pltpu.VMEM((2 * count, slab // 2), bf16),
-            pltpu.SemaphoreType.DMA((3,)),
-        ],
-        compiler_params=pltpu.CompilerParams(vmem_limit_bytes=BIG),
+        scratch_shapes=[pltpu.VMEM((2 * count, slab // 2), bf16)],
+        compiler_params=pltpu.CompilerParams(vmem_limit_bytes=16 * 1024 * 1024),
         cost_estimate=pl.CostEstimate(flops=500_000_000, bytes_accessed=4_000_000, transcendentals=0),
     )(half.reshape(1), rows, keep, taken, inv, stat, gain, spots)
 
@@ -597,12 +550,8 @@
     return lax.ppermute(x, "tp", [(0, 1), (1, 0)])
 
 
-def shift_y(x, k):
-    return lax.ppermute(x, "seq", [(i, i // 4 * 4 + (i % 4 + k) % 4) for i in range(16)])
-
-
-def shift_z(x, k):
-    return lax.ppermute(x, "seq", [(i, (i // 4 + k) % 4 * 4 + i % 4) for i in range(16)])
+def shift(x, axis, k):
+    return lax.ppermute(x, axis, [(i, (i + k) % 4) for i in range(4)])
 
 
 def ranks(dest):
@@ -627,7 +576,7 @@
     bf16, f32 = jnp.bfloat16, jnp.float32
     t = lax.axis_index("tp")
     e = lax.axis_index("enc")
-    j = lax.axis_index("seq")
+    j = lax.axis_index(("z", "y"))
     n_enc = 4
     n_seq = 16
     self_index = e * n_seq + j
@@ -646,35 +595,22 @@
         audio_rows,
         vision_rows,
     )
+    z, y = lax.axis_index("z"), lax.axis_index("y")
     hops = (1, 3, 2)
-    along_y = [piece_a] + [shift_y(piece_a, k) for k in hops]
-    along_z = [piece_b] + [shift_z(piece_b, k) for k in hops]
-    along_y, along_z = lax.optimization_barrier((along_y, along_z))
-    stack_a = jnp.concatenate(along_y, axis=0)
-    stack_b = jnp.concatenate(along_z, axis=0)
-    stack_a, stack_b = lax.optimization_barrier((stack_a, stack_b))
-    pieces_a = [stack_a] + [shift_z(stack_a, k) for k in hops]
-    pieces_b = [stack_b] + [shift_y(stack_b, k) for k in hops]
-    own = lax.all_gather(packed, "enc", axis=0, tiled=False)
-    z, y = j // 4, j % 4
     back = jnp.array((0,) + hops, jnp.int32)
-    a_at = (((z - back) % 4)[:, None] * 4 + ((y - back) % 4)[None, :]).reshape(-1)
     b_at = (((y - back) % 4)[:, None] + ((z - back) % 4)[None, :] * 4).reshape(-1)
-
     ah, vh = audio_count // 2, vision_count // 2
 
     line = row_target.reshape(n_enc, n_seq, enc_rows)[:, j]
     line_dest = line // length
     line_slot = line_dest * (n_enc * cap) + jnp.arange(n_enc)[:, None] * cap + ranks(line_dest)
-    a_slot = line_slot[:, :audio_count].reshape(n_enc, 2, ah)
-    v_slot = line_slot[:, audio_count:].reshape(n_enc, 2, vh)
+    a_slot = line_slot[:, :audio_count].reshape(2, 2, 2, ah)
+    v_slot = line_slot[:, audio_count:].reshape(2, 2, 2, vh)
     halves = jnp.stack([t, 1 - t])
-    a_slot = jnp.moveaxis(a_slot, 1, 0)[halves].reshape(-1)
-    v_slot = jnp.moveaxis(v_slot, 1, 0)[halves].reshape(-1)
-    row_slot = jnp.concatenate([a_slot, v_slot])
-    cell = row_slot // 16 * 8 + row_slot % 8
-    part = row_slot // 8 % 2
-    cells = jnp.stack([jnp.where(part == 0, cell, -1), jnp.where(part == 1, cell, -1)])
+    a_slot = jnp.moveaxis(a_slot, 2, 1)[:, halves].reshape(2, -1)
+    v_slot = jnp.moveaxis(v_slot, 2, 1)[:, halves].reshape(2, -1)
+    row_slot = jnp.concatenate([a_slot, v_slot], axis=1)
+    cells = row_slot // 16 * 8 + row_slot % 8
 
     dest = row_target // length
     mine = (dest == self_index).astype(jnp.int32)
@@ -700,15 +636,28 @@
     gain = norm_gain.reshape(2, slab)
     seg_row = segment_ids
     seg_col = segment_ids.reshape(length, 1)
-    pieces_a, pieces_b, own, cells, by_line, filled, spots, own_cell, gain, seg_col, a_at, b_at = (
+
+    def gather(x, axis):
+        return lax.all_to_all(
+            jnp.broadcast_to(x[None], (4,) + x.shape), axis, split_axis=0, concat_axis=0, tiled=True
+        )
+
+    along_z = [piece_b] + [shift(piece_b, "z", k) for k in hops]
+    along_y = gather(piece_a, "y")
+    along_y, along_z, cells, by_line, filled, spots, own_cell, gain, seg_col, b_at = (
         lax.optimization_barrier(
-            (pieces_a, pieces_b, own, cells, by_line, filled, spots, own_cell, gain, seg_col, a_at, b_at)
+            (along_y, along_z, cells, by_line, filled, spots, own_cell, gain, seg_col, b_at)
         )
     )
+    along_y, stack_b = lax.optimization_barrier((along_y, jnp.stack(along_z)))
+    shards_b = [stack_b] + [shift(stack_b, "y", k) for k in hops]
+    shards_a = gather(along_y.reshape(4 * A_PIECE, 384), "z").reshape(n_seq, A_PIECE, 384)
+    own = lax.all_gather(packed, "enc", axis=0, tiled=False)
+    shards_a, shards_b, own = lax.optimization_barrier((shards_a, shards_b, own))
     other = swap(own)
-    outgoing = encode(a_at, b_at, pieces_a, pieces_b, own, other, cells, senders * 8)
+    outgoing = encode(b_at, shards_a, shards_b, own, other, cells, senders * 8)
     arrived = lax.all_to_all(
-        outgoing.reshape(senders, 8, slab // 2), ("enc", "seq"), split_axis=0, concat_axis=0, tiled=True
+        outgoing.reshape(senders, 8, slab // 2), SPREAD, split_axis=0, concat_axis=0, tiled=True
     )
     row_slab = place(by_line, arrived.reshape(senders * 8, slab // 2), text_rows, filled)
 
@@ -720,23 +669,27 @@
 
     out8 = finish(t, row_slab, keep, taken, inv_rms, row_part, gain, spots)
     returned = lax.all_to_all(
-        out8.reshape(senders, 2 * cap, half), ("enc", "seq"), split_axis=0, concat_axis=0, tiled=True
+        out8.reshape(senders, 2 * cap, half), SPREAD, split_axis=0, concat_axis=0, tiled=True
     )
     return collect(own_cell, returned.reshape(senders * 2 * cap, half), audio_count)
 
 
+SPREAD = ("enc", "z", "y")
+
+
 def solution(mesh):
+    torus = Mesh(mesh.devices.reshape(4, 4, 4, 2), ("enc", "z", "y", "tp"))
     in_specs = (
-        P(("enc", "seq"), None),
-        P(("enc", "seq"), None),
-        P("seq", "tp"),
-        P("seq", None, "tp"),
-        P(("enc", "seq"), "tp"),
+        P(SPREAD, None),
+        P(SPREAD, None),
+        P(("z", "y"), "tp"),
+        P(("z", "y"), None, "tp"),
+        P(SPREAD, "tp"),
         P(),
-        P(("enc", "seq"), None),
+        P(SPREAD, None),
         P(),
         P(None, "tp"),
-        P(("enc", "seq"), "tp"),
-    )
-    out_specs = (P(("enc", "seq"), "tp"), P(("enc", "seq"), "tp"))
-    return jax.shard_map(local, mesh=mesh, in_specs=in_specs, out_specs=out_specs, check_vma=False)
+        P(SPREAD, "tp"),
+    )
+    out_specs = (P(SPREAD, "tp"), P(SPREAD, "tp"))
+    return jax.shard_map(local, mesh=torus, in_specs=in_specs, out_specs=out_specs, check_vma=False)

time: 180 us -> 168 us (0.933)
  Pallas kernels: 48 us -> 27.2 us
  waiting for transfers between devices: 73.7 us -> 81.3 us
    pallas_call x1, Pallas kernels: 17.5 us -> 2.69 us  [pack(): pl.pallas_call(pack_kernel, out_shape=(jax.ShapeDtypeStruct((A_PIECE, 384...]
    all_to_all x2 -> x4, starting transfers between devices: 12.2 us -> 22.3 us  [the longest x1 9.37 us: local(): lax.all_to_all(outgoing.reshape(senders, 8, slab // 2), SPREAD, split_axi...]
    ppermute x12 -> x6, starting transfers between devices: 18.9 us -> 9.36 us  [shift(): return lax.ppermute(x, axis, [(i, (i + k) % 4) for i in range(4)])]
    all_to_all x2 -> x4, waiting for transfers between devices: 34.7 us -> 39.6 us  [the longest x1 17.5 us: local(): lax.all_to_all(out8.reshape(senders, 2 * cap, half), SPREAD, split_axis=0...]
    pallas_call x1, Pallas kernels: 4.93 us -> 2.07 us  [finish(): pl.pallas_call(finish_kernel, out_shape=jax.ShapeDtypeStruct((cells, slab...]
    broadcast_in_dim x0 -> x2, local copies, waits for them, and re-layouts: none -> 2.69 us  [gather(): jnp.broadcast_to(x[None], (4,) + x.shape)]
    ppermute x12 -> x6, waiting for transfers between devices: 31.4 us -> 32 us  [shift(): return lax.ppermute(x, axis, [(i, (i + k) % 4) for i in range(4)])]
  transfers between devices with their start and end apart: 18 -> 14, of which waited for: 10 -> 7; matrix products, arithmetic and copies ran while one was open for 5% -> 5% of each run, Pallas kernels for 0% -> 0%
where the time goes in v6:
time: 168 us; the launch traced here: 167 us
  waiting for transfers between devices  81.3 us (48%)
  starting transfers between devices  32.1 us (19%)
  Pallas kernels  27.2 us (16%)
  between operations  14.4 us (9%)
  local copies, waits for them, and re-layouts  9.31 us (6%)
  other arithmetic  3.12 us (2%)
    ppermute x6, waiting for transfers between devices, shift(): return lax.ppermute(x, axis, [(i, (i + k) % 4) for i in range(4)])  32 us
    all_to_all x1, waiting for transfers between devices, local(): lax.all_to_all(out8.reshape(senders, 2 * cap, half), SPREAD, split_axis=0...  17.5 us
    all_to_all x1, waiting for transfers between devices, local(): lax.all_to_all(outgoing.reshape(senders, 8, slab // 2), SPREAD, split_axi...  17.4 us
    pallas_call x1, Pallas kernels, attend(): pl.pallas_call(attend_kernel, out_shape=(jax.ShapeDtypeStruct((rows, slab...  11.9 us
    all_to_all x1, starting transfers between devices, local(): lax.all_to_all(outgoing.reshape(senders, 8, slab // 2), SPREAD, split_axi...  9.37 us
    ppermute x6, starting transfers between devices, shift(): return lax.ppermute(x, axis, [(i, (i + k) % 4) for i in range(4)])  9.36 us
    ppermute x3, waiting for transfers between devices, swap(): return lax.ppermute(x, 'tp', [(0, 1), (1, 0)])  8.98 us
    pallas_call x1, Pallas kernels, encode(): pl.pallas_call(encode_kernel, out_shape=jax.ShapeDtypeStruct((n_cells, 89...  8.2 us
  transfers between devices with their start and end apart: 14, of which 7 were waited for; matrix products, arithmetic and copies ran while one was open for 5% of the time, Pallas kernels for 0%

profile of v6, /device:TPU:0, one launch (start us, length us, event | category | flops | bytes accessed | tf_op | source)
XLA Modules:
  0.0 167.4 jit_solution(11433614587765297604)
XLA Ops:
  7.2 0.1 pad_add_fusion.1.place_ref
  7.3 2.7 %shard_map.122 = (bf16[224,384]{1,0:T(8,128)(2,1)S(1)}, bf16[256,384]{1,0:T(8,128)(2,1)S(1)}, bf16[192,1280]{1,0:T(8,128)(2,1)}) custom-call(s32[2]{0:T(128)S(1)} %pad_add_fusion.1.place_ref, bf16[80,1792]{1,0:T(8,128)(2,1)} %audio_w_ref.1, bf16[80,4,1792]{2,1,0:T(4,128)(2,1)} %vision_w_ref.1, bf16[128,1280]{1,0:T(8,128)(2,1)} %audio_ref.1, ...), custom_call_target="tpu_custom_call" | custom-call | bytes 1800000 | tf_op jit(solution)/shard_map/pallas_call | solution.py:262
  10.0 2.1 %collective-permute-start = (bf16[256,384]{1,0:T(8,128)(2,1)S(1)}, bf16[256,384]{1,0:T(8,128)(2,1)S(1)}, u32[]{:S(2)}, u32[]{:S(2)}) collective-permute-start(bf16[256,384]{1,0:T(8,128)(2,1)S(1)} %get-tuple-element.36), channel_id=1, source_target_pairs={{0,8},{8,16},{16,24},{24,0},{1,9},{9,17},{17,25},{25,1},{2,10},{10... | collective-permute-start | bytes 589832 | tf_op jit(solution)/shard_map/ppermute | solution.py:554
  12.1 2.2 %collective-permute-start.1 = (bf16[256,384]{1,0:T(8,128)(2,1)S(1)}, bf16[256,384]{1,0:T(8,128)(2,1)S(1)}, u32[]{:S(2)}, u32[]{:S(2)}) collective-permute-start(bf16[256,384]{1,0:T(8,128)(2,1)S(1)} %get-tuple-element.36), channel_id=1, source_target_pairs={{0,24},{8,0},{16,8},{24,16},{1,25},{9,1},{17,9},{25,17},{2,26},{10... | collective-permute-start | bytes 589832 | tf_op jit(solution)/shard_map/ppermute | solution.py:554
  14.3 1.8 %collective-permute-start.2 = (bf16[256,384]{1,0:T(8,128)(2,1)S(1)}, bf16[256,384]{1,0:T(8,128)(2,1)S(1)}, u32[]{:S(2)}, u32[]{:S(2)}) collective-permute-start(bf16[256,384]{1,0:T(8,128)(2,1)S(1)} %get-tuple-element.36), channel_id=1, source_target_pairs={{0,16},{8,24},{16,0},{24,8},{1,17},{9,25},{17,1},{25,9},{2,18},{10... | collective-permute-start | bytes 589832 | tf_op jit(solution)/shard_map/ppermute | solution.py:554
  16.0 0.9 broadcast_in_dim.16
  17.0 4.5 %all-to-all-start = ((bf16[4,224,384]{2,1,0:T(8,128)(2,1)}), bf16[4,224,384]{2,1,0:T(8,128)(2,1)S(1)}, u32[]{:S(2)}, u32[]{:S(2)}) async-start(bf16[4,224,384]{2,1,0:T(8,128)(2,1)} %broadcast_in_dim.16), calls=%async_computation | async-start | bytes 1376256 | tf_op jit(solution)/shard_map/all_to_all | solution.py:641
  21.4 0.7 all-gather.3.cloned.1.call-update
  22.2 0.4 convert_reduce_fusion
  22.6 0.1 add_add_fusion
  22.7 0.1 broadcast_compare_fusion
  22.8 0.6 reduce-window.6
  23.4 0.2 slice_reduce_fusion
  23.6 0.1 copy_bitcast_fusion
  23.8 0.2 select_reduce_fusion
  23.9 0.1 sub.62
  24.0 0.1 copy.56
  24.1 0.1 copy.64
  24.2 0.1 fusion.20
  24.3 0.1 stack_reshape.6
  24.4 0.1 stack_reshape.7
  24.6 0.1 reshape.304
  24.6 0.1 fusion.17
  24.7 0.6 gather_fusion
  25.3 0.1 reshape.305
  25.4 0.1 reshape.306
  25.5 0.6 gather_fusion.1
  26.1 0.1 reshape.307
  26.2 0.1 copy.55
  26.3 0.1 reshape.310.e_row_ref
  26.4 0.1 sub.63
  26.5 0.1 convert_reduce_fusion.1
  26.6 0.1 broadcast_add_fusion
  26.7 0.1 add.134.b_at_ref
  26.9 0.2 convert_reduce_fusion.2
  27.1 4.7 %all-to-all-done = bf16[4,224,384]{2,1,0:T(8,128)(2,1)S(1)} async-done(((bf16[4,224,384]{2,1,0:T(8,128)(2,1)}), bf16[4,224,384]{2,1,0:T(8,128)(2,1)S(1)}, u32[]{:S(2)}, u32[]{:S(2)}) %all-to-all-start) | async-done | bytes 688160 | tf_op jit(solution)/shard_map/all_to_all | solution.py:641
  31.8 1.0 pad_maximum_fusion.gb0
  32.8 1.8 %broadcast_in_dim.25 = bf16[4,896,384]{2,1,0:T(8,128)(2,1)} broadcast(bf16[896,384]{1,0:T(8,128)(2,1)S(1)} %bitcast.72), dimensions={1,2} | broadcast | bytes 3440640 | tf_op jit(solution)/shard_map/broadcast_in_dim | solution.py:642
  34.6 3.7 %all-to-all-start.1 = ((bf16[4,896,384]{2,1,0:T(8,128)(2,1)}), bf16[4,896,384]{2,1,0:T(8,128)(2,1)S(1)}, u32[]{:S(2)}, u32[]{:S(2)}) async-start(bf16[4,896,384]{2,1,0:T(8,128)(2,1)} %broadcast_in_dim.25), calls=%async_computation.1 | async-start | bytes 5505024 | tf_op jit(solution)/shard_map/all_to_all | solution.py:641
  38.3 0.6 collective-permute-start.3
  38.9 2.7 %collective-permute-start.4 = (bf16[4,256,384]{2,1,0:T(8,128)(2,1)}, bf16[4,256,384]{2,1,0:T(8,128)(2,1)S(1)}, u32[]{:S(2)}, u32[]{:S(2)}) collective-permute-start(bf16[4,256,384]{2,1,0:T(8,128)(2,1)} %pad_maximum_fusion.gb0), channel_id=1, source_target_pairs={{0,6},{2,0},{4,2},{6,4},{1,7},{3,1},{5,3},{7,5},{8,14},{10,8},{12,... | collective-permute-start | bytes 2359304 | tf_op jit(solution)/shard_map/ppermute | solution.py:554
  41.6 32.0 %collective-permute-done.3.gb1 = bf16[4,256,384]{2,1,0:T(8,128)(2,1)S(1)} collective-permute-done((bf16[4,256,384]{2,1,0:T(8,128)(2,1)}, bf16[4,256,384]{2,1,0:T(8,128)(2,1)S(1)}, u32[]{:S(2)}, u32[]{:S(2)}) %collective-permute-start.3) | collective-permute-done | bytes 786464 | tf_op jit(solution)/shard_map/ppermute | solution.py:554
  73.6 0.9 copy-done.6
  74.5 0.9 copy-done.7
  75.4 0.0 all-gather.3.cloned.1.call-done
  75.4 1.5 copy-done.2
  77.0 4.2 %collective-permute-done.6.other_ref = bf16[4,192,1280]{2,1,0:T(8,128)(2,1)S(1)} collective-permute-done((bf16[4,192,1280]{2,1,0:T(8,128)(2,1)}, bf16[4,192,1280]{2,1,0:T(8,128)(2,1)S(1)}, u32[]{:S(2)}, u32[]{:S(2)}) %collective-permute-start.6) | collective-permute-done | bytes 1966112 | tf_op jit(solution)/shard_map/ppermute | solution.py:550
  81.1 8.2 %shard_map.123 = bf16[512,896]{1,0:T(8,128)(2,1)} custom-call(s32[16]{0:T(128)S(1)} %add.134.b_at_ref, bf16[16,224,384]{2,1,0:T(8,128)(2,1)} %bitcast.71, bf16[4,256,384]{2,1,0:T(8,128)(2,1)} %pad_maximum_fusion.gb0, bf16[4,256,384]{2,1,0:T(8,128)(2,1)} %copy-done.6, bf16[4,256,384]{2,1,0:T(8,128)(2,1)} %copy-done.7, ...), custom_call_target="tpu_custom_call" | custom-call | flops 3000000000 | bytes 11000000 | tf_op jit(solution)/shard_map/pallas_call | solution.py:400
  89.4 9.4 %all-to-all-start.2 = ((bf16[64,8,896]{2,1,0:T(8,128)(2,1)}), bf16[64,8,896]{2,1,0:T(8,128)(2,1)S(1)}, u32[]{:S(2)}, u32[]{:S(2)}) async-start(bf16[64,8,896]{2,1,0:T(8,128)(2,1)} %bitcast.26), calls=%async_computation.2 | async-start | bytes 1835008 | tf_op jit(solution)/shard_map/all_to_all | solution.py:659
  98.7 0.1 copy.59.filled_ref
  98.9 17.4 %all-to-all-done.2 = bf16[64,8,896]{2,1,0:T(8,128)(2,1)S(1)} async-done(((bf16[64,8,896]{2,1,0:T(8,128)(2,1)}), bf16[64,8,896]{2,1,0:T(8,128)(2,1)S(1)}, u32[]{:S(2)}, u32[]{:S(2)}) %all-to-all-start.2) | async-done | bytes 917536 | tf_op jit(solution)/shard_map/all_to_all | solution.py:659
  116.2 0.9 shard_map.124.own_ref.rows_ref
  117.1 0.3 collective-permute-start.7
  117.4 0.1 copy.60.seg_col_ref
  117.5 2.3 %collective-permute-done.7.other_ref = bf16[256,1792]{1,0:T(8,128)(2,1)S(1)} collective-permute-done((bf16[256,1792]{1,0:T(8,128)(2,1)S(1)}, bf16[256,1792]{1,0:T(8,128)(2,1)S(1)}, u32[]{:S(2)}, u32[]{:S(2)}) %collective-permute-start.7) | collective-permute-done | bytes 917536 | tf_op jit(solution)/shard_map/ppermute | solution.py:550
  119.8 11.9 %shard_map.125 = (bf16[256,1920]{1,0:T(8,128)(2,1)}, bf16[256,1792]{1,0:T(8,128)(2,1)S(1)}, f32[256,1]{1,0:T(8,128)S(1)}, f32[256,1]{1,0:T(8,128)S(1)}) custom-call(s32[1]{0:T(128)} %bitcast.1.half_ref, bf16[256,1792]{1,0:T(8,128)(2,1)S(1)} %shard_map.124.own_ref.rows_ref, bf16[256,1792]{1,0:T(8,128)(2,1)S(1)} %collective-permute-done.7.other_ref, ...), custom_call_target="tpu_custom_call" | custom-call | flops 5000000000 | bytes 14000000 | tf_op jit(solution)/shard_map/pallas_call | solution.py:136
  131.7 0.2 collective-permute-start.8
  131.9 0.1 copy.61.spot_ref
  132.1 2.5 %collective-permute-done.8.taken_ref = bf16[256,1920]{1,0:T(8,128)(2,1)S(1)} collective-permute-done((bf16[256,1920]{1,0:T(8,128)(2,1)}, bf16[256,1920]{1,0:T(8,128)(2,1)S(1)}, u32[]{:S(2)}, u32[]{:S(2)}) %collective-permute-start.8) | collective-permute-done | bytes 983072 | tf_op jit(solution)/shard_map/ppermute | solution.py:550
  134.6 2.1 %shard_map.126 = bf16[512,896]{1,0:T(8,128)(2,1)} custom-call(s32[1]{0:T(128)} %bitcast.1.half_ref, bf16[256,1792]{1,0:T(8,128)(2,1)S(1)} %shard_map.124.own_ref.rows_ref, bf16[256,1792]{1,0:T(8,128)(2,1)S(1)} %get-tuple-element.53.keep_ref, bf16[256,1920]{1,0:T(8,128)(2,1)S(1)} %collective-permute-done.8.taken_ref, f32[256,1]{1,0:T(8,128)S(1)} %get-tuple-element.55.inv_ref, ...), custom_call_target="tpu_custom_call" | custom-call | flops 500000000 | bytes 4000000 | tf_op jit(solution)/shard_map/pallas_call | solution.py:507
  136.7 4.8 %all-to-all-start.3 = ((bf16[64,8,896]{2,1,0:T(8,128)(2,1)}), bf16[64,8,896]{2,1,0:T(8,128)(2,1)S(1)}, u32[]{:S(2)}, u32[]{:S(2)}) async-start(bf16[64,8,896]{2,1,0:T(8,128)(2,1)} %bitcast.28), calls=%async_computation.3 | async-start | bytes 1835008 | tf_op jit(solution)/shard_map/all_to_all | solution.py:671
  141.4 0.1 copy.62.cell_ref
  141.6 17.5 %all-to-all-done.3 = bf16[64,8,896]{2,1,0:T(8,128)(2,1)S(1)} async-done(((bf16[64,8,896]{2,1,0:T(8,128)(2,1)}), bf16[64,8,896]{2,1,0:T(8,128)(2,1)S(1)}, u32[]{:S(2)}, u32[]{:S(2)}) %all-to-all-start.3) | async-done | bytes 917536 | tf_op jit(solution)/shard_map/all_to_all | solution.py:671
  159.1 1.5 shard_map.127
  (47 shorter events, 0.3 us)
Async XLA Ops:
  7.2 15.0 %copy-start.3 = (s32[64,192]{1,0:T(8,128)S(1)}, s32[64,192]{1,0:T(8,128)}, u32[]{:S(2)}) copy-start(s32[64,192]{1,0:T(8,128)} %param.16) | copy-start | bytes 147460
  10.0 16.7 %copy-start.5 = (s32[4]{0:T(128)S(1)}, s32[4]{0:T(128)}, u32[]{:S(2)}) copy-start(s32[4]{0:T(128)} %constant.142) | copy-start | bytes 52
  10.0 16.8 %copy-start.4 = (f32[3584]{0:T(1024)S(1)}, f32[3584]{0:T(1024)}, u32[]{:S(2)}) copy-start(f32[3584]{0:T(1024)} %param.18) | copy-start | bytes 43012
  10.0 17.1 %collective-permute-start = (bf16[256,384]{1,0:T(8,128)(2,1)S(1)}, bf16[256,384]{1,0:T(8,128)(2,1)S(1)}, u32[]{:S(2)}, u32[]{:S(2)}) collective-permute-start(bf16[256,384]{1,0:T(8,128)(2,1)S(1)} %get-tuple-element.36), channel_id=1, source_target_pairs={{0,8},{8,16},{16,24},{24,0},{1,9},{9,17},{17,25},{25,1},{2,10},{10... | collective-permute-start | bytes 589832 | tf_op jit(solution)/shard_map/ppermute | solution.py:554
  12.1 15.1 %collective-permute-start.1 = (bf16[256,384]{1,0:T(8,128)(2,1)S(1)}, bf16[256,384]{1,0:T(8,128)(2,1)S(1)}, u32[]{:S(2)}, u32[]{:S(2)}) collective-permute-start(bf16[256,384]{1,0:T(8,128)(2,1)S(1)} %get-tuple-element.36), channel_id=1, source_target_pairs={{0,24},{8,0},{16,8},{24,16},{1,25},{9,1},{17,9},{25,17},{2,26},{10... | collective-permute-start | bytes 589832 | tf_op jit(solution)/shard_map/ppermute | solution.py:554
  14.3 12.9 %collective-permute-start.2 = (bf16[256,384]{1,0:T(8,128)(2,1)S(1)}, bf16[256,384]{1,0:T(8,128)(2,1)S(1)}, u32[]{:S(2)}, u32[]{:S(2)}) collective-permute-start(bf16[256,384]{1,0:T(8,128)(2,1)S(1)} %get-tuple-element.36), channel_id=1, source_target_pairs={{0,16},{8,24},{16,0},{24,8},{1,17},{9,25},{17,1},{25,9},{2,18},{10... | collective-permute-start | bytes 589832 | tf_op jit(solution)/shard_map/ppermute | solution.py:554
  17.0 14.9 %all-to-all-start = ((bf16[4,224,384]{2,1,0:T(8,128)(2,1)}), bf16[4,224,384]{2,1,0:T(8,128)(2,1)S(1)}, u32[]{:S(2)}, u32[]{:S(2)}) async-start(bf16[4,224,384]{2,1,0:T(8,128)(2,1)} %broadcast_in_dim.16), calls=%async_computation | async-start | bytes 1376256 | tf_op jit(solution)/shard_map/all_to_all | solution.py:641
  21.4 54.0 %all-gather.3.cloned.1.call-start = ((), (), s32[]{:S(2)}) async-start(), calls=%async_computation.4 | async-start | bytes 2457600 | tf_op jit(solution)/shard_map/all_gather | solution.py:655
  34.6 40.8 %all-to-all-start.1 = ((bf16[4,896,384]{2,1,0:T(8,128)(2,1)}), bf16[4,896,384]{2,1,0:T(8,128)(2,1)S(1)}, u32[]{:S(2)}, u32[]{:S(2)}) async-start(bf16[4,896,384]{2,1,0:T(8,128)(2,1)} %broadcast_in_dim.25), calls=%async_computation.1 | async-start | bytes 5505024 | tf_op jit(solution)/shard_map/all_to_all | solution.py:641
  38.3 35.3 %collective-permute-start.3 = (bf16[4,256,384]{2,1,0:T(8,128)(2,1)}, bf16[4,256,384]{2,1,0:T(8,128)(2,1)S(1)}, u32[]{:S(2)}, u32[]{:S(2)}) collective-permute-start(bf16[4,256,384]{2,1,0:T(8,128)(2,1)} %pad_maximum_fusion.gb0), channel_id=1, source_target_pairs={{0,2},{2,4},{4,6},{6,0},{1,3},{3,5},{5,7},{7,1},{8,10},{10,12},{12... | collective-permute-start | bytes 2359304 | tf_op jit(solution)/shard_map/ppermute | solution.py:554
  38.9 34.7 %collective-permute-start.4 = (bf16[4,256,384]{2,1,0:T(8,128)(2,1)}, bf16[4,256,384]{2,1,0:T(8,128)(2,1)S(1)}, u32[]{:S(2)}, u32[]{:S(2)}) collective-permute-start(bf16[4,256,384]{2,1,0:T(8,128)(2,1)} %pad_maximum_fusion.gb0), channel_id=1, source_target_pairs={{0,6},{2,0},{4,2},{6,4},{1,7},{3,1},{5,3},{7,5},{8,14},{10,8},{12,... | collective-permute-start | bytes 2359304 | tf_op jit(solution)/shard_map/ppermute | solution.py:554
  41.6 33.8 %collective-permute-start.5 = (bf16[4,256,384]{2,1,0:T(8,128)(2,1)}, bf16[4,256,384]{2,1,0:T(8,128)(2,1)}, u32[]{:S(2)}, u32[]{:S(2)}) collective-permute-start(bf16[4,256,384]{2,1,0:T(8,128)(2,1)} %pad_maximum_fusion.gb0), channel_id=1, source_target_pairs={{0,4},{2,6},{4,0},{6,2},{1,5},{3,7},{5,1},{7,3},{8,12},{10,14},{12... | collective-permute-start | bytes 2359304 | tf_op jit(solution)/shard_map/ppermute | solution.py:554
  73.6 0.9 copy-start.6
  74.5 0.9 copy-start.7
  75.4 1.5 copy-start.2
  77.0 39.3 %copy-start = (bf16[256,1792]{1,0:T(8,128)(2,1)S(1)}, bf16[256,1792]{1,0:T(8,128)(2,1)}, u32[]{:S(2)}) copy-start(bf16[256,1792]{1,0:T(8,128)(2,1)} %text_hbm.1) | copy-start | bytes 2752516
  77.0 4.2 %collective-permute-start.6 = (bf16[4,192,1280]{2,1,0:T(8,128)(2,1)}, bf16[4,192,1280]{2,1,0:T(8,128)(2,1)S(1)}, u32[]{:S(2)}, u32[]{:S(2)}) collective-permute-start(bf16[4,192,1280]{2,1,0:T(8,128)(2,1)} %bitcast.85), channel_id=1, source_target_pairs={{0,1},{1,0},{2,3},{3,2},{4,5},{5,4},{6,7},{7,6},{8,9},{9,8},{10,11... | collective-permute-start | bytes 5898248 | tf_op jit(solution)/shard_map/ppermute | solution.py:550
  89.3 28.0 %copy-start.1 = (s32[1,256]{1,0:T(1,128)S(1)}, s32[1,256]{1,0:T(1,128)}, u32[]{:S(2)}) copy-start(s32[1,256]{1,0:T(1,128)} %seg_row_ref.1) | copy-start | bytes 3076
  89.4 26.9 %all-to-all-start.2 = ((bf16[64,8,896]{2,1,0:T(8,128)(2,1)}), bf16[64,8,896]{2,1,0:T(8,128)(2,1)S(1)}, u32[]{:S(2)}, u32[]{:S(2)}) async-start(bf16[64,8,896]{2,1,0:T(8,128)(2,1)} %bitcast.26), calls=%async_computation.2 | async-start | bytes 1835008 | tf_op jit(solution)/shard_map/all_to_all | solution.py:659
  117.1 2.7 %collective-permute-start.7 = (bf16[256,1792]{1,0:T(8,128)(2,1)S(1)}, bf16[256,1792]{1,0:T(8,128)(2,1)S(1)}, u32[]{:S(2)}, u32[]{:S(2)}) collective-permute-start(bf16[256,1792]{1,0:T(8,128)(2,1)S(1)} %shard_map.124.own_ref.rows_ref), channel_id=1, source_target_pairs={{0,1},{1,0},{2,3},{3,2},{4,5},{5,4},{6,7},{7,6},{8,9},{9,8},{10,11... | collective-permute-start | bytes 2752520 | tf_op jit(solution)/shard_map/ppermute | solution.py:550
  131.7 2.9 %collective-permute-start.8 = (bf16[256,1920]{1,0:T(8,128)(2,1)}, bf16[256,1920]{1,0:T(8,128)(2,1)S(1)}, u32[]{:S(2)}, u32[]{:S(2)}) collective-permute-start(bf16[256,1920]{1,0:T(8,128)(2,1)} %get-tuple-element.54), channel_id=1, source_target_pairs={{0,1},{1,0},{2,3},{3,2},{4,5},{5,4},{6,7},{7,6},{8,9},{9,8},{10,11... | collective-permute-start | bytes 2949128 | tf_op jit(solution)/shard_map/ppermute | solution.py:550
  136.7 22.4 %all-to-all-start.3 = ((bf16[64,8,896]{2,1,0:T(8,128)(2,1)}), bf16[64,8,896]{2,1,0:T(8,128)(2,1)S(1)}, u32[]{:S(2)}, u32[]{:S(2)}) async-start(bf16[64,8,896]{2,1,0:T(8,128)(2,1)} %bitcast.28), calls=%async_computation.3 | async-start | bytes 1835008 | tf_op jit(solution)/shard_map/all_to_all | solution.py:671
Sparse Core Ops, SparseCore 0:
  23.9 30.1 all-gather.2

commit v7 on v6

--- a/solution.py
+++ b/solution.py
@@ -284,12 +284,18 @@
 
 
 def encode_kernel(
+    a_at_ref,
     b_at_ref,
-    ga,
+    ga0,
+    ga1,
+    ga2,
+    ga3,
+    ga4,
     gb0,
     gb1,
     gb2,
     gb3,
+    gb4,
     own_ref,
     other_ref,
     cell_ref,
@@ -308,22 +314,28 @@
     audio_width = x_ref.shape[3]
     audio_k = wa_ref.shape[1]
     cut = A_ROWS - audio_k
-    shards_b = (gb0, gb1, gb2, gb3)
-    pltpu.make_async_copy(ga.at[:, A_ROWS:, :], ra_ref, sems.at[2]).start()
-    for m, gb in enumerate(shards_b):
+    sources = ((ga0, gb0, 0, 4), (ga1, gb1, 4, 4), (ga2, gb2, 8, 4), (ga3, gb3, 12, 2), (ga4, gb4, 14, 2))
+    for ga, gb, start, size in sources:
         pltpu.make_async_copy(
-            gb.at[:, B_ROWS:, :], rb_ref.at[4 * m : 4 * m + 4], sems.at[3]
+            ga.at[:, A_ROWS:, :], ra_ref.at[start : start + size], sems.at[2]
+        ).start()
+        pltpu.make_async_copy(
+            gb.at[:, B_ROWS:, :], rb_ref.at[start : start + size], sems.at[3]
         ).start()
     pltpu.make_async_copy(own_ref, x_ref.at[0], sems.at[0]).start()
     pltpu.make_async_copy(other_ref, x_ref.at[1], sems.at[1]).start()
-    audio_copy = pltpu.make_async_copy(ga.at[:, :audio_k, :], wa_ref, sems.at[4])
-    audio_copy.start()
-    low_copy = pltpu.make_async_copy(ga.at[:, audio_k:A_ROWS, :], wv_ref.at[:, :cut, :], sems.at[5])
-    low_copy.start()
-    for m, gb in enumerate(shards_b):
-        for n in range(4):
+    for ga, _, start, size in sources:
+        for n in range(size):
             pltpu.make_async_copy(
-                gb.at[n, :B_ROWS, :], wv_ref.at[b_at_ref[4 * m + n], cut:, :], sems.at[6]
+                ga.at[n, :audio_k, :], wa_ref.at[a_at_ref[start + n]], sems.at[4]
+            ).start()
+    for ga, gb, start, size in sources:
+        for n in range(size):
+            pltpu.make_async_copy(
+                ga.at[n, audio_k:A_ROWS, :], wv_ref.at[a_at_ref[start + n], :cut, :], sems.at[5]
+            ).start()
+            pltpu.make_async_copy(
+                gb.at[n, :B_ROWS, :], wv_ref.at[b_at_ref[start + n], cut:, :], sems.at[6]
             ).start()
 
     count = cell_ref.shape[1]
@@ -337,9 +349,10 @@
     @pl.loop(0, 16)
     def _(p):
         ta = jnp.concatenate([ra_ref[p, :, q * 128 : (q + 1) * 128] for q in range(3)], axis=0)
-        ta_ref[p, :, :] = ta[:audio_k]
-        tv_ref[p, : 96 - audio_k, :] = ta[audio_k:]
-        tv_ref[p, 96 - audio_k : cut, :] = roll_half(ta)
+        at = a_at_ref[p]
+        ta_ref[at, :, :] = ta[:audio_k]
+        tv_ref[at, : 96 - audio_k, :] = ta[audio_k:]
+        tv_ref[at, 96 - audio_k : cut, :] = roll_half(ta)
 
     pltpu.make_async_copy(rb_ref, rb_ref, sems.at[3]).wait()
 
@@ -370,10 +383,10 @@
 
     pltpu.make_async_copy(own_ref, x_ref.at[0], sems.at[0]).wait()
     pltpu.make_async_copy(other_ref, x_ref.at[1], sems.at[1]).wait()
-    audio_copy.wait()
+    pltpu.make_async_copy(wa_ref, wa_ref, sems.at[4]).wait()
     rows = x_ref[:, :, :audio, :].reshape(n_audio, audio_width)
     keep_rows(dot(rows, weights(wa_ref[...], ta_ref[...])).astype(bf16), 0, audio)
-    low_copy.wait()
+    pltpu.make_async_copy(wv_ref.at[:, :cut, :], wv_ref.at[:, :cut, :], sems.at[5]).wait()
     pltpu.make_async_copy(wv_ref.at[:, cut:, :], wv_ref.at[:, cut:, :], sems.at[6]).wait()
     total = jnp.zeros((n_vision, 512), f32)
     for i in range(4):
@@ -390,7 +403,7 @@
     out_ref[:, 768:] = jnp.where(lane < 64, low, pltpu.roll(high, 64, 1)).astype(bf16)
 
 
-def encode(b_at, shards_a, shards_b, own, other, cells, n_cells):
+def encode(a_at, b_at, shards_a, shards_b, own, other, cells, n_cells):
     bf16 = jnp.bfloat16
     n_enc, rows, width = own.shape
     smem = pl.BlockSpec(memory_space=pltpu.SMEM)
@@ -400,7 +413,7 @@
     return pl.pallas_call(
         encode_kernel,
         out_shape=jax.ShapeDtypeStruct((n_cells, 896), bf16),
-        in_specs=[smem] + [anywhere] * 7 + [vmem],
+        in_specs=[smem, smem] + [anywhere] * 12 + [vmem],
         out_specs=vmem,
         scratch_shapes=[
             pltpu.VMEM((16, k, 384), bf16),
@@ -417,7 +430,7 @@
         cost_estimate=pl.CostEstimate(
             flops=3_000_000_000, bytes_accessed=11_000_000, transcendentals=0
         ),
-    )(b_at, in_hbm(shards_a), *(in_hbm(x) for x in shards_b), in_hbm(own), other, cells)
+    )(a_at, b_at, *shards_a, *shards_b, in_hbm(own), other, cells)
 
 
 def place_kernel(e_row_ref, arrived_ref, text_hbm, filled_ref, out_ref, text_ref, sem):
@@ -598,6 +611,7 @@
     z, y = lax.axis_index("z"), lax.axis_index("y")
     hops = (1, 3, 2)
     back = jnp.array((0,) + hops, jnp.int32)
+    a_at = (((z - back) % 4)[:, None] * 4 + ((y - back) % 4)[None, :]).reshape(-1)
     b_at = (((y - back) % 4)[:, None] + ((z - back) % 4)[None, :] * 4).reshape(-1)
     ah, vh = audio_count // 2, vision_count // 2
 
@@ -636,26 +650,24 @@
     gain = norm_gain.reshape(2, slab)
     seg_row = segment_ids
     seg_col = segment_ids.reshape(length, 1)
-
-    def gather(x, axis):
-        return lax.all_to_all(
-            jnp.broadcast_to(x[None], (4,) + x.shape), axis, split_axis=0, concat_axis=0, tiled=True
+    along_y = [piece_a] + [shift(piece_a, "y", k) for k in hops]
+    along_z = [piece_b] + [shift(piece_b, "z", k) for k in hops]
+    along_y, along_z, cells, by_line, filled, spots, own_cell, gain, seg_col, a_at, b_at = (
+        lax.optimization_barrier(
+            (along_y, along_z, cells, by_line, filled, spots, own_cell, gain, seg_col, a_at, b_at)
         )
-
-    along_z = [piece_b] + [shift(piece_b, "z", k) for k in hops]
-    along_y = gather(piece_a, "y")
-    along_y, along_z, cells, by_line, filled, spots, own_cell, gain, seg_col, b_at = (
-        lax.optimization_barrier(
-            (along_y, along_z, cells, by_line, filled, spots, own_cell, gain, seg_col, b_at)
-        )
-    )
-    along_y, stack_b = lax.optimization_barrier((along_y, jnp.stack(along_z)))
-    shards_b = [stack_b] + [shift(stack_b, "y", k) for k in hops]
-    shards_a = gather(along_y.reshape(4 * A_PIECE, 384), "z").reshape(n_seq, A_PIECE, 384)
+    )
+    stack_a, stack_b = lax.optimization_barrier((jnp.stack(along_y), jnp.stack(along_z)))
+    near_a = [shift(stack_a, "z", 1), shift(stack_a, "z", 3)]
+    near_b = [shift(stack_b, "y", 1), shift(stack_b, "y", 3)]
     own = lax.all_gather(packed, "enc", axis=0, tiled=False)
-    shards_a, shards_b, own = lax.optimization_barrier((shards_a, shards_b, own))
+    near_a, near_b, own = lax.optimization_barrier((near_a, near_b, own))
+    far_a = [shift(near_a[0][:2], "z", 1), shift(near_a[1][2:], "z", 3)]
+    far_b = [shift(near_b[0][:2], "y", 1), shift(near_b[1][2:], "y", 3)]
+    shards_a = [stack_a] + near_a + far_a
+    shards_b = [stack_b] + near_b + far_b
     other = swap(own)
-    outgoing = encode(b_at, shards_a, shards_b, own, other, cells, senders * 8)
+    outgoing = encode(a_at, b_at, shards_a, shards_b, own, other, cells, senders * 8)
     arrived = lax.all_to_all(
         outgoing.reshape(senders, 8, slab // 2), SPREAD, split_axis=0, concat_axis=0, tiled=True
     )

time: 168 us -> 158 us (0.940)
  waiting for transfers between devices: 81.3 us -> 62.5 us
  Pallas kernels: 27.2 us -> 33.6 us
  starting transfers between devices: 32.1 us -> 37.8 us
  local copies, waits for them, and re-layouts: 9.31 us -> 5.64 us
    ppermute x6 -> x14, starting transfers between devices: 9.36 us -> 24.6 us  [shift(): return lax.ppermute(x, axis, [(i, (i + k) % 4) for i in range(4)])]
    all_to_all x2 -> x0, starting transfers between devices: 8.13 us -> none  [gather(): lax.all_to_all(jnp.broadcast_to(x[None], (4,) + x.shape), axis, split_axi...]
    ppermute x6 -> x14, waiting for transfers between devices: 32 us -> 24.2 us  [shift(): return lax.ppermute(x, axis, [(i, (i + k) % 4) for i in range(4)])]
    pallas_call x1, Pallas kernels: 8.2 us -> 14.6 us  [encode(): pl.pallas_call(encode_kernel, out_shape=jax.ShapeDtypeStruct((n_cells, 89...]
    all_to_all x2 -> x0, waiting for transfers between devices: 4.7 us -> none  [gather(): lax.all_to_all(jnp.broadcast_to(x[None], (4,) + x.shape), axis, split_axi...]
    ppermute x3, waiting for transfers between devices: 8.98 us -> 4.79 us  [swap(): return lax.ppermute(x, 'tp', [(0, 1), (1, 0)])]
    broadcast_in_dim x2 -> x0, local copies, waits for them, and re-layouts: 2.69 us -> none  [gather(): jnp.broadcast_to(x[None], (4,) + x.shape)]
    unnamed x18 -> x24, local copies, waits for them, and re-layouts: 3.42 us -> 1.22 us
  transfers between devices with their start and end apart: 14 -> 20, of which waited for: 7 -> 7; matrix products, arithmetic and copies ran while one was open for 5% -> 5% of each run, Pallas kernels for 0% -> 0%
where the time goes in v7:
time: 158 us
  waiting for transfers between devices  62.5 us (40%)
  starting transfers between devices  37.8 us (24%)
  Pallas kernels  33.6 us (21%)
  between operations  14.4 us (9%)
  local copies, waits for them, and re-layouts  5.64 us (4%)
  other arithmetic  3.5 us (2%)
    ppermute x14, starting transfers between devices, shift(): return lax.ppermute(x, axis, [(i, (i + k) % 4) for i in range(4)])  24.6 us
    ppermute x14, waiting for transfers between devices, shift(): return lax.ppermute(x, axis, [(i, (i + k) % 4) for i in range(4)])  24.2 us
    all_to_all x1, waiting for transfers between devices, local(): lax.all_to_all(out8.reshape(senders, 2 * cap, half), SPREAD, split_axis=0...  17.5 us
    all_to_all x1, waiting for transfers between devices, local(): lax.all_to_all(outgoing.reshape(senders, 8, slab // 2), SPREAD, split_axi...  16 us
    pallas_call x1, Pallas kernels, encode(): pl.pallas_call(encode_kernel, out_shape=jax.ShapeDtypeStruct((n_cells, 89...  14.6 us
    pallas_call x1, Pallas kernels, attend(): pl.pallas_call(attend_kernel, out_shape=(jax.ShapeDtypeStruct((rows, slab...  11.9 us
    all_to_all x1, starting transfers between devices, local(): lax.all_to_all(outgoing.reshape(senders, 8, slab // 2), SPREAD, split_axi...  7.94 us
    all_to_all x1, starting transfers between devices, local(): lax.all_to_all(out8.reshape(senders, 2 * cap, half), SPREAD, split_axis=0...  4.82 us
  transfers between devices with their start and end apart: 20, of which 7 were waited for; matrix products, arithmetic and copies ran while one was open for 5% of the time, Pallas kernels for 0%

profile of v7, /device:TPU:0, one launch (start us, length us, event | category | flops | bytes accessed | tf_op | source)
XLA Modules:
  0.0 157.5 jit_solution(11372076685877971363)
XLA Ops:
  7.3 2.7 %shard_map.122 = (bf16[224,384]{1,0:T(8,128)(2,1)S(1)}, bf16[256,384]{1,0:T(8,128)(2,1)S(1)}, bf16[192,1280]{1,0:T(8,128)(2,1)}) custom-call(s32[2]{0:T(128)S(1)} %pad_add_fusion.1.place_ref, bf16[80,1792]{1,0:T(8,128)(2,1)} %audio_w_ref.1, bf16[80,4,1792]{2,1,0:T(4,128)(2,1)} %vision_w_ref.1, bf16[128,1280]{1,0:T(8,128)(2,1)} %audio_ref.1, ...), custom_call_target="tpu_custom_call" | custom-call | bytes 1800000 | tf_op jit(solution)/shard_map/pallas_call | solution.py:262
  10.0 2.1 %collective-permute-start.3 = (bf16[256,384]{1,0:T(8,128)(2,1)S(1)}, bf16[256,384]{1,0:T(8,128)(2,1)S(1)}, u32[]{:S(2)}, u32[]{:S(2)}) collective-permute-start(bf16[256,384]{1,0:T(8,128)(2,1)S(1)} %get-tuple-element.43), channel_id=1, source_target_pairs={{0,8},{8,16},{16,24},{24,0},{1,9},{9,17},{17,25},{25,1},{2,10},{10... | collective-permute-start | bytes 589832 | tf_op jit(solution)/shard_map/ppermute | solution.py:567
  12.1 2.2 %collective-permute-start.4 = (bf16[256,384]{1,0:T(8,128)(2,1)S(1)}, bf16[256,384]{1,0:T(8,128)(2,1)S(1)}, u32[]{:S(2)}, u32[]{:S(2)}) collective-permute-start(bf16[256,384]{1,0:T(8,128)(2,1)S(1)} %get-tuple-element.43), channel_id=1, source_target_pairs={{0,24},{8,0},{16,8},{24,16},{1,25},{9,1},{17,9},{25,17},{2,26},{10... | collective-permute-start | bytes 589832 | tf_op jit(solution)/shard_map/ppermute | solution.py:567
  14.3 1.8 %collective-permute-start.5 = (bf16[256,384]{1,0:T(8,128)(2,1)S(1)}, bf16[256,384]{1,0:T(8,128)(2,1)S(1)}, u32[]{:S(2)}, u32[]{:S(2)}) collective-permute-start(bf16[256,384]{1,0:T(8,128)(2,1)S(1)} %get-tuple-element.43), channel_id=1, source_target_pairs={{0,16},{8,24},{16,0},{24,8},{1,17},{9,25},{17,1},{25,9},{2,18},{10... | collective-permute-start | bytes 589832 | tf_op jit(solution)/shard_map/ppermute | solution.py:567
  16.1 1.6 %collective-permute-start = (bf16[224,384]{1,0:T(8,128)(2,1)S(1)}, bf16[224,384]{1,0:T(8,128)(2,1)S(1)}, u32[]{:S(2)}, u32[]{:S(2)}) collective-permute-start(bf16[224,384]{1,0:T(8,128)(2,1)S(1)} %get-tuple-element.39), channel_id=1, source_target_pairs={{0,2},{2,4},{4,6},{6,0},{1,3},{3,5},{5,7},{7,1},{8,10},{10,12},{12... | collective-permute-start | bytes 516104 | tf_op jit(solution)/shard_map/ppermute | solution.py:567
  17.7 1.7 %collective-permute-start.1 = (bf16[224,384]{1,0:T(8,128)(2,1)S(1)}, bf16[224,384]{1,0:T(8,128)(2,1)S(1)}, u32[]{:S(2)}, u32[]{:S(2)}) collective-permute-start(bf16[224,384]{1,0:T(8,128)(2,1)S(1)} %get-tuple-element.39), channel_id=1, source_target_pairs={{0,6},{2,0},{4,2},{6,4},{1,7},{3,1},{5,3},{7,5},{8,14},{10,8},{12,... | collective-permute-start | bytes 516104 | tf_op jit(solution)/shard_map/ppermute | solution.py:567
  19.5 0.4 convert_reduce_fusion
  20.0 0.6 reduce-window.6
  20.6 0.2 slice_reduce_fusion
  20.8 0.1 copy_bitcast_fusion
  21.0 0.2 select_reduce_fusion
  21.1 0.1 sub.66
  21.2 0.1 copy.56
  21.3 0.1 reshape.306
  21.5 0.6 gather_fusion
  22.1 0.1 reshape.307
  22.3 0.6 gather_fusion.1
  22.8 0.1 reshape.309
  22.9 0.1 copy.64
  23.1 0.1 stack_reshape.6
  23.2 0.1 stack_reshape.7
  23.4 0.1 copy.55
  23.5 0.1 reshape.312.e_row_ref
  23.6 0.1 sub.67
  23.8 0.1 add.155.a_at_ref
  23.9 0.1 add.159.b_at_ref
  24.0 0.6 pad_add_fusion
  24.6 0.1 convert_reduce_fusion.1
  24.7 0.2 convert_reduce_fusion.2
  25.0 2.1 %collective-permute-start.2 = (bf16[224,384]{1,0:T(8,128)(2,1)S(1)}, bf16[224,384]{1,0:T(8,128)(2,1)S(1)}, u32[]{:S(2)}, u32[]{:S(2)}) collective-permute-start(bf16[224,384]{1,0:T(8,128)(2,1)S(1)} %get-tuple-element.39), channel_id=1, source_target_pairs={{0,4},{2,6},{4,0},{6,2},{1,5},{3,7},{5,1},{7,3},{8,12},{10,14},{12... | collective-permute-start | bytes 516104 | tf_op jit(solution)/shard_map/ppermute | solution.py:567
  27.0 0.6 add_bitcast_fusion.1
  27.6 4.3 %collective-permute-done.2 = bf16[224,384]{1,0:T(8,128)(2,1)S(1)} collective-permute-done((bf16[224,384]{1,0:T(8,128)(2,1)S(1)}, bf16[224,384]{1,0:T(8,128)(2,1)S(1)}, u32[]{:S(2)}, u32[]{:S(2)}) %collective-permute-start.2) | collective-permute-done | bytes 172064 | tf_op jit(solution)/shard_map/ppermute | solution.py:567
  32.0 0.1 pad_maximum_fusion.1.ga0
  32.1 0.1 pad_maximum_fusion.gb0
  32.2 0.4 collective-permute-start.8
  32.7 2.9 %collective-permute-start.9 = (bf16[4,256,384]{2,1,0:T(8,128)(2,1)S(1)}, bf16[4,256,384]{2,1,0:T(8,128)(2,1)S(1)}, u32[]{:S(2)}, u32[]{:S(2)}) collective-permute-start(bf16[4,256,384]{2,1,0:T(8,128)(2,1)S(1)} %pad_maximum_fusion.gb0), channel_id=1, source_target_pairs={{0,6},{2,0},{4,2},{6,4},{1,7},{3,1},{5,3},{7,5},{8,14},{10,8},{12,... | collective-permute-start | bytes 2359304 | tf_op jit(solution)/shard_map/ppermute | solution.py:567
  35.5 1.0 collective-permute-start.6
  36.5 2.2 %collective-permute-start.7 = (bf16[4,224,384]{2,1,0:T(8,128)(2,1)S(1)}, bf16[4,224,384]{2,1,0:T(8,128)(2,1)S(1)}, u32[]{:S(2)}, u32[]{:S(2)}) collective-permute-start(bf16[4,224,384]{2,1,0:T(8,128)(2,1)S(1)} %pad_maximum_fusion.1.ga0), channel_id=1, source_target_pairs={{0,24},{8,0},{16,8},{24,16},{1,25},{9,1},{17,9},{25,17},{2,26},{10... | collective-permute-start | bytes 2064392 | tf_op jit(solution)/shard_map/ppermute | solution.py:567
  38.8 12.1 %collective-permute-done.6.ga1 = bf16[4,224,384]{2,1,0:T(8,128)(2,1)S(1)} collective-permute-done((bf16[4,224,384]{2,1,0:T(8,128)(2,1)S(1)}, bf16[4,224,384]{2,1,0:T(8,128)(2,1)S(1)}, u32[]{:S(2)}, u32[]{:S(2)}) %collective-permute-start.6) | collective-permute-done | bytes 688160 | tf_op jit(solution)/shard_map/ppermute | solution.py:567
  50.9 0.8 copy-done.1
  51.7 0.2 copy-done.3
  52.0 0.1 collective-permute-start.14
  52.2 3.3 %collective-permute-start.13 = (bf16[2,256,384]{2,1,0:T(8,128)(2,1)S(1)}, bf16[2,256,384]{2,1,0:T(8,128)(2,1)S(1)}, u32[]{:S(2)}, u32[]{:S(2)}) collective-permute-start(bf16[2,256,384]{2,1,0:T(8,128)(2,1)S(1)} %slice.35), channel_id=1, source_target_pairs={{0,6},{2,0},{4,2},{6,4},{1,7},{3,1},{5,3},{7,5},{8,14},{10,8},{12,... | collective-permute-start | bytes 1179656 | tf_op jit(solution)/shard_map/ppermute | solution.py:567
  55.5 1.0 slice.32
  56.5 0.3 collective-permute-start.10
  56.9 3.1 %collective-permute-start.11 = (bf16[2,224,384]{2,1,0:T(8,128)(2,1)S(1)}, bf16[2,224,384]{2,1,0:T(8,128)(2,1)S(1)}, u32[]{:S(2)}, u32[]{:S(2)}) collective-permute-start(bf16[2,224,384]{2,1,0:T(8,128)(2,1)S(1)} %slice.33), channel_id=1, source_target_pairs={{0,24},{8,0},{16,8},{24,16},{1,25},{9,1},{17,9},{25,17},{2,26},{10... | collective-permute-start | bytes 1032200 | tf_op jit(solution)/shard_map/ppermute | solution.py:567
  60.0 7.8 %collective-permute-done.10.ga3 = bf16[2,224,384]{2,1,0:T(8,128)(2,1)S(1)} collective-permute-done((bf16[2,224,384]{2,1,0:T(8,128)(2,1)S(1)}, bf16[2,224,384]{2,1,0:T(8,128)(2,1)S(1)}, u32[]{:S(2)}, u32[]{:S(2)}) %collective-permute-start.10) | collective-permute-done | bytes 344096 | tf_op jit(solution)/shard_map/ppermute | solution.py:567
  67.8 14.6 %shard_map.123 = bf16[512,896]{1,0:T(8,128)(2,1)} custom-call(s32[16]{0:T(128)S(1)} %add.155.a_at_ref, s32[16]{0:T(128)S(1)} %add.159.b_at_ref, bf16[4,224,384]{2,1,0:T(8,128)(2,1)S(1)} %pad_maximum_fusion.1.ga0, bf16[4,224,384]{2,1,0:T(8,128)(2,1)S(1)} %copy-done.2, bf16[4,224,384]{2,1,0:T(8,128)(2,1)S(1)} %copy-done.4, ...), custom_call_target="tpu_custom_call" | custom-call | flops 3000000000 | bytes 11000000 | tf_op jit(solution)/shard_map/pallas_call | solution.py:413
  82.4 7.9 %all-to-all-start = ((bf16[64,8,896]{2,1,0:T(8,128)(2,1)}), bf16[64,8,896]{2,1,0:T(8,128)(2,1)S(1)}, u32[]{:S(2)}, u32[]{:S(2)}) async-start(bf16[64,8,896]{2,1,0:T(8,128)(2,1)} %bitcast.28), calls=%async_computation | async-start | bytes 1835008 | tf_op jit(solution)/shard_map/all_to_all | solution.py:671
  90.4 0.1 copy.59.filled_ref
  90.5 16.0 %all-to-all-done = bf16[64,8,896]{2,1,0:T(8,128)(2,1)S(1)} async-done(((bf16[64,8,896]{2,1,0:T(8,128)(2,1)}), bf16[64,8,896]{2,1,0:T(8,128)(2,1)S(1)}, u32[]{:S(2)}, u32[]{:S(2)}) %all-to-all-start) | async-done | bytes 917536 | tf_op jit(solution)/shard_map/all_to_all | solution.py:671
  106.5 0.9 shard_map.124.own_ref.rows_ref
  107.4 0.1 collective-permute-start.15
  107.5 0.1 copy.60.seg_col_ref
  107.6 2.3 %collective-permute-done.15.other_ref = bf16[256,1792]{1,0:T(8,128)(2,1)S(1)} collective-permute-done((bf16[256,1792]{1,0:T(8,128)(2,1)S(1)}, bf16[256,1792]{1,0:T(8,128)(2,1)S(1)}, u32[]{:S(2)}, u32[]{:S(2)}) %collective-permute-start.15) | collective-permute-done | bytes 917536 | tf_op jit(solution)/shard_map/ppermute | solution.py:563
  109.9 11.9 %shard_map.125 = (bf16[256,1920]{1,0:T(8,128)(2,1)}, bf16[256,1792]{1,0:T(8,128)(2,1)S(1)}, f32[256,1]{1,0:T(8,128)S(1)}, f32[256,1]{1,0:T(8,128)S(1)}) custom-call(s32[1]{0:T(128)} %bitcast.1.half_ref, bf16[256,1792]{1,0:T(8,128)(2,1)S(1)} %shard_map.124.own_ref.rows_ref, bf16[256,1792]{1,0:T(8,128)(2,1)S(1)} %collective-permute-done.15.other_ref, ...), custom_call_target="tpu_custom_call" | custom-call | flops 5000000000 | bytes 14000000 | tf_op jit(solution)/shard_map/pallas_call | solution.py:136
  121.8 0.2 collective-permute-start.16
  122.0 0.1 copy.61.spot_ref
  122.2 2.5 %collective-permute-done.16.taken_ref = bf16[256,1920]{1,0:T(8,128)(2,1)S(1)} collective-permute-done((bf16[256,1920]{1,0:T(8,128)(2,1)}, bf16[256,1920]{1,0:T(8,128)(2,1)S(1)}, u32[]{:S(2)}, u32[]{:S(2)}) %collective-permute-start.16) | collective-permute-done | bytes 983072 | tf_op jit(solution)/shard_map/ppermute | solution.py:563
  124.7 2.1 %shard_map.126 = bf16[512,896]{1,0:T(8,128)(2,1)} custom-call(s32[1]{0:T(128)} %bitcast.1.half_ref, bf16[256,1792]{1,0:T(8,128)(2,1)S(1)} %shard_map.124.own_ref.rows_ref, bf16[256,1792]{1,0:T(8,128)(2,1)S(1)} %get-tuple-element.59.keep_ref, bf16[256,1920]{1,0:T(8,128)(2,1)S(1)} %collective-permute-done.16.taken_ref, ...), custom_call_target="tpu_custom_call" | custom-call | flops 500000000 | bytes 4000000 | tf_op jit(solution)/shard_map/pallas_call | solution.py:520
  126.8 4.8 %all-to-all-start.1 = ((bf16[64,8,896]{2,1,0:T(8,128)(2,1)}), bf16[64,8,896]{2,1,0:T(8,128)(2,1)S(1)}, u32[]{:S(2)}, u32[]{:S(2)}) async-start(bf16[64,8,896]{2,1,0:T(8,128)(2,1)} %bitcast.30), calls=%async_computation.1 | async-start | bytes 1835008 | tf_op jit(solution)/shard_map/all_to_all | solution.py:683
  131.6 0.1 copy.62.cell_ref
  131.7 17.5 %all-to-all-done.1 = bf16[64,8,896]{2,1,0:T(8,128)(2,1)S(1)} async-done(((bf16[64,8,896]{2,1,0:T(8,128)(2,1)}), bf16[64,8,896]{2,1,0:T(8,128)(2,1)S(1)}, u32[]{:S(2)}, u32[]{:S(2)}) %all-to-all-start.1) | async-done | bytes 917536 | tf_op jit(solution)/shard_map/all_to_all | solution.py:683
  149.2 1.5 shard_map.127
  (69 shorter events, 1.1 us)
Async XLA Ops:
  7.2 12.2 %copy-start.6 = (s32[64,192]{1,0:T(8,128)S(1)}, s32[64,192]{1,0:T(8,128)}, u32[]{:S(2)}) copy-start(s32[64,192]{1,0:T(8,128)} %param.16) | copy-start | bytes 147460
  7.2 44.8 %all-gather.3.cloned.1.call-start = ((), (), s32[]{:S(2)}) async-start(), calls=%async_computation.2 | async-start | bytes 2457600 | tf_op jit(solution)/shard_map/all_gather | solution.py:663
  7.3 16.4 %copy-start.10 = (s32[4]{0:T(128)S(1)}, s32[4]{0:T(128)}, u32[]{:S(2)}) copy-start(s32[4]{0:T(128)} %constant.148) | copy-start | bytes 52
  7.3 16.7 %copy-start.8 = (f32[3584]{0:T(1024)S(1)}, f32[3584]{0:T(1024)}, u32[]{:S(2)}) copy-start(f32[3584]{0:T(1024)} %param.18) | copy-start | bytes 43012
  10.0 21.9 %collective-permute-start.3 = (bf16[256,384]{1,0:T(8,128)(2,1)S(1)}, bf16[256,384]{1,0:T(8,128)(2,1)S(1)}, u32[]{:S(2)}, u32[]{:S(2)}) collective-permute-start(bf16[256,384]{1,0:T(8,128)(2,1)S(1)} %get-tuple-element.43), channel_id=1, source_target_pairs={{0,8},{8,16},{16,24},{24,0},{1,9},{9,17},{17,25},{25,1},{2,10},{10... | collective-permute-start | bytes 589832 | tf_op jit(solution)/shard_map/ppermute | solution.py:567
  12.1 19.9 %collective-permute-start.4 = (bf16[256,384]{1,0:T(8,128)(2,1)S(1)}, bf16[256,384]{1,0:T(8,128)(2,1)S(1)}, u32[]{:S(2)}, u32[]{:S(2)}) collective-permute-start(bf16[256,384]{1,0:T(8,128)(2,1)S(1)} %get-tuple-element.43), channel_id=1, source_target_pairs={{0,24},{8,0},{16,8},{24,16},{1,25},{9,1},{17,9},{25,17},{2,26},{10... | collective-permute-start | bytes 589832 | tf_op jit(solution)/shard_map/ppermute | solution.py:567
  14.3 17.7 %collective-permute-start.5 = (bf16[256,384]{1,0:T(8,128)(2,1)S(1)}, bf16[256,384]{1,0:T(8,128)(2,1)S(1)}, u32[]{:S(2)}, u32[]{:S(2)}) collective-permute-start(bf16[256,384]{1,0:T(8,128)(2,1)S(1)} %get-tuple-element.43), channel_id=1, source_target_pairs={{0,16},{8,24},{16,0},{24,8},{1,17},{9,25},{17,1},{25,9},{2,18},{10... | collective-permute-start | bytes 589832 | tf_op jit(solution)/shard_map/ppermute | solution.py:567
  16.1 8.9 %collective-permute-start = (bf16[224,384]{1,0:T(8,128)(2,1)S(1)}, bf16[224,384]{1,0:T(8,128)(2,1)S(1)}, u32[]{:S(2)}, u32[]{:S(2)}) collective-permute-start(bf16[224,384]{1,0:T(8,128)(2,1)S(1)} %get-tuple-element.39), channel_id=1, source_target_pairs={{0,2},{2,4},{4,6},{6,0},{1,3},{3,5},{5,7},{7,1},{8,10},{10,12},{12... | collective-permute-start | bytes 516104 | tf_op jit(solution)/shard_map/ppermute | solution.py:567
  17.7 10.0 %collective-permute-start.1 = (bf16[224,384]{1,0:T(8,128)(2,1)S(1)}, bf16[224,384]{1,0:T(8,128)(2,1)S(1)}, u32[]{:S(2)}, u32[]{:S(2)}) collective-permute-start(bf16[224,384]{1,0:T(8,128)(2,1)S(1)} %get-tuple-element.39), channel_id=1, source_target_pairs={{0,6},{2,0},{4,2},{6,4},{1,7},{3,1},{5,3},{7,5},{8,14},{10,8},{12,... | collective-permute-start | bytes 516104 | tf_op jit(solution)/shard_map/ppermute | solution.py:567
  25.0 7.0 %collective-permute-start.2 = (bf16[224,384]{1,0:T(8,128)(2,1)S(1)}, bf16[224,384]{1,0:T(8,128)(2,1)S(1)}, u32[]{:S(2)}, u32[]{:S(2)}) collective-permute-start(bf16[224,384]{1,0:T(8,128)(2,1)S(1)} %get-tuple-element.39), channel_id=1, source_target_pairs={{0,4},{2,6},{4,0},{6,2},{1,5},{3,7},{5,1},{7,3},{8,12},{10,14},{12... | collective-permute-start | bytes 516104 | tf_op jit(solution)/shard_map/ppermute | solution.py:567
  32.2 18.7 %collective-permute-start.8 = (bf16[4,256,384]{2,1,0:T(8,128)(2,1)S(1)}, bf16[4,256,384]{2,1,0:T(8,128)(2,1)S(1)}, u32[]{:S(2)}, u32[]{:S(2)}) collective-permute-start(bf16[4,256,384]{2,1,0:T(8,128)(2,1)S(1)} %pad_maximum_fusion.gb0), channel_id=1, source_target_pairs={{0,2},{2,4},{4,6},{6,0},{1,3},{3,5},{5,7},{7,1},{8,10},{10,12},{12... | collective-permute-start | bytes 2359304 | tf_op jit(solution)/shard_map/ppermute | solution.py:567
  32.7 19.3 %collective-permute-start.9 = (bf16[4,256,384]{2,1,0:T(8,128)(2,1)S(1)}, bf16[4,256,384]{2,1,0:T(8,128)(2,1)S(1)}, u32[]{:S(2)}, u32[]{:S(2)}) collective-permute-start(bf16[4,256,384]{2,1,0:T(8,128)(2,1)S(1)} %pad_maximum_fusion.gb0), channel_id=1, source_target_pairs={{0,6},{2,0},{4,2},{6,4},{1,7},{3,1},{5,3},{7,5},{8,14},{10,8},{12,... | collective-permute-start | bytes 2359304 | tf_op jit(solution)/shard_map/ppermute | solution.py:567
  35.5 15.3 %collective-permute-start.6 = (bf16[4,224,384]{2,1,0:T(8,128)(2,1)S(1)}, bf16[4,224,384]{2,1,0:T(8,128)(2,1)S(1)}, u32[]{:S(2)}, u32[]{:S(2)}) collective-permute-start(bf16[4,224,384]{2,1,0:T(8,128)(2,1)S(1)} %pad_maximum_fusion.1.ga0), channel_id=1, source_target_pairs={{0,8},{8,16},{16,24},{24,0},{1,9},{9,17},{17,25},{25,1},{2,10},{10... | collective-permute-start | bytes 2064392 | tf_op jit(solution)/shard_map/ppermute | solution.py:567
  36.5 14.3 %collective-permute-start.7 = (bf16[4,224,384]{2,1,0:T(8,128)(2,1)S(1)}, bf16[4,224,384]{2,1,0:T(8,128)(2,1)S(1)}, u32[]{:S(2)}, u32[]{:S(2)}) collective-permute-start(bf16[4,224,384]{2,1,0:T(8,128)(2,1)S(1)} %pad_maximum_fusion.1.ga0), channel_id=1, source_target_pairs={{0,24},{8,0},{16,8},{24,16},{1,25},{9,1},{17,9},{25,17},{2,26},{10... | collective-permute-start | bytes 2064392 | tf_op jit(solution)/shard_map/ppermute | solution.py:567
  50.9 0.9 copy-start.1
  50.9 1.1 copy-start.3
  52.0 4.9 %copy-start.4 = (bf16[4,224,384]{2,1,0:T(8,128)(2,1)S(1)}, bf16[4,224,384]{2,1,0:T(8,128)(2,1)}, u32[]{:S(2)}) copy-start(bf16[4,224,384]{2,1,0:T(8,128)(2,1)} %copy-done.3) | copy-start | bytes 2064388
  52.0 15.8 %copy-start.2 = (bf16[4,224,384]{2,1,0:T(8,128)(2,1)S(1)}, bf16[4,224,384]{2,1,0:T(8,128)(2,1)}, u32[]{:S(2)}) copy-start(bf16[4,224,384]{2,1,0:T(8,128)(2,1)} %copy-done.1) | copy-start | bytes 2064388
  52.0 15.8 %collective-permute-start.14 = (bf16[4,192,1280]{2,1,0:T(8,128)(2,1)}, bf16[4,192,1280]{2,1,0:T(8,128)(2,1)S(1)}, u32[]{:S(2)}, u32[]{:S(2)}) collective-permute-start(bf16[4,192,1280]{2,1,0:T(8,128)(2,1)} %bitcast.89), channel_id=1, source_target_pairs={{0,1},{1,0},{2,3},{3,2},{4,5},{5,4},{6,7},{7,6},{8,9},{9,8},{10,11... | collective-permute-start | bytes 5898248 | tf_op jit(solution)/shard_map/ppermute | solution.py:563
  52.1 15.6 %collective-permute-start.12 = (bf16[2,256,384]{2,1,0:T(8,128)(2,1)S(1)}, bf16[2,256,384]{2,1,0:T(8,128)(2,1)S(1)}, u32[]{:S(2)}, u32[]{:S(2)}) collective-permute-start(bf16[2,256,384]{2,1,0:T(8,128)(2,1)S(1)} %slice.34), channel_id=1, source_target_pairs={{0,2},{2,4},{4,6},{6,0},{1,3},{3,5},{5,7},{7,1},{8,10},{10,12},{12... | collective-permute-start | bytes 1179656 | tf_op jit(solution)/shard_map/ppermute | solution.py:567
  52.2 15.5 %collective-permute-start.13 = (bf16[2,256,384]{2,1,0:T(8,128)(2,1)S(1)}, bf16[2,256,384]{2,1,0:T(8,128)(2,1)S(1)}, u32[]{:S(2)}, u32[]{:S(2)}) collective-permute-start(bf16[2,256,384]{2,1,0:T(8,128)(2,1)S(1)} %slice.35), channel_id=1, source_target_pairs={{0,6},{2,0},{4,2},{6,4},{1,7},{3,1},{5,3},{7,5},{8,14},{10,8},{12,... | collective-permute-start | bytes 1179656 | tf_op jit(solution)/shard_map/ppermute | solution.py:567
  56.5 11.2 %collective-permute-start.10 = (bf16[2,224,384]{2,1,0:T(8,128)(2,1)S(1)}, bf16[2,224,384]{2,1,0:T(8,128)(2,1)S(1)}, u32[]{:S(2)}, u32[]{:S(2)}) collective-permute-start(bf16[2,224,384]{2,1,0:T(8,128)(2,1)S(1)} %slice.32), channel_id=1, source_target_pairs={{0,8},{8,16},{16,24},{24,0},{1,9},{9,17},{17,25},{25,1},{2,10},{10... | collective-permute-start | bytes 1032200 | tf_op jit(solution)/shard_map/ppermute | solution.py:567
  56.9 10.8 %collective-permute-start.11 = (bf16[2,224,384]{2,1,0:T(8,128)(2,1)S(1)}, bf16[2,224,384]{2,1,0:T(8,128)(2,1)S(1)}, u32[]{:S(2)}, u32[]{:S(2)}) collective-permute-start(bf16[2,224,384]{2,1,0:T(8,128)(2,1)S(1)} %slice.33), channel_id=1, source_target_pairs={{0,24},{8,0},{16,8},{24,16},{1,25},{9,1},{17,9},{25,17},{2,26},{10... | collective-permute-start | bytes 1032200 | tf_op jit(solution)/shard_map/ppermute | solution.py:567
  82.4 24.1 %copy-start = (bf16[256,1792]{1,0:T(8,128)(2,1)S(1)}, bf16[256,1792]{1,0:T(8,128)(2,1)}, u32[]{:S(2)}) copy-start(bf16[256,1792]{1,0:T(8,128)(2,1)} %text_hbm.1) | copy-start | bytes 2752516
  82.4 24.1 %all-to-all-start = ((bf16[64,8,896]{2,1,0:T(8,128)(2,1)}), bf16[64,8,896]{2,1,0:T(8,128)(2,1)S(1)}, u32[]{:S(2)}, u32[]{:S(2)}) async-start(bf16[64,8,896]{2,1,0:T(8,128)(2,1)} %bitcast.28), calls=%async_computation | async-start | bytes 1835008 | tf_op jit(solution)/shard_map/all_to_all | solution.py:671
  90.3 17.1 %copy-start.5 = (s32[1,256]{1,0:T(1,128)S(1)}, s32[1,256]{1,0:T(1,128)}, u32[]{:S(2)}) copy-start(s32[1,256]{1,0:T(1,128)} %seg_row_ref.1) | copy-start | bytes 3076
  107.4 2.6 %collective-permute-start.15 = (bf16[256,1792]{1,0:T(8,128)(2,1)S(1)}, bf16[256,1792]{1,0:T(8,128)(2,1)S(1)}, u32[]{:S(2)}, u32[]{:S(2)}) collective-permute-start(bf16[256,1792]{1,0:T(8,128)(2,1)S(1)} %shard_map.124.own_ref.rows_ref), channel_id=1, source_target_pairs={{0,1},{1,0},{2,3},{3,2},{4,5},{5,4},{6,7},{7,6},{8,9},{9,8},{10,11... | collective-permute-start | bytes 2752520 | tf_op jit(solution)/shard_map/ppermute | solution.py:563
  107.6 14.4 %copy-start.7 = (s32[512,2]{0,1:T(2,128)S(1)}, s32[512,2]{0,1:T(2,128)}, u32[]{:S(2)}) copy-start(s32[512,2]{0,1:T(2,128)} %pad_add_fusion) | copy-start | bytes 12292
  121.8 2.9 %collective-permute-start.16 = (bf16[256,1920]{1,0:T(8,128)(2,1)}, bf16[256,1920]{1,0:T(8,128)(2,1)S(1)}, u32[]{:S(2)}, u32[]{:S(2)}) collective-permute-start(bf16[256,1920]{1,0:T(8,128)(2,1)} %get-tuple-element.60), channel_id=1, source_target_pairs={{0,1},{1,0},{2,3},{3,2},{4,5},{5,4},{6,7},{7,6},{8,9},{9,8},{10,11... | collective-permute-start | bytes 2949128 | tf_op jit(solution)/shard_map/ppermute | solution.py:563
  124.7 6.9 %copy-start.9 = (s32[192,1]{0,1:T(1,128)S(1)}, s32[192,1]{0,1:T(1,128)}, u32[]{:S(2)}) copy-start(s32[192,1]{0,1:T(1,128)} %add_bitcast_fusion.1) | copy-start | bytes 2308
  126.8 22.4 %all-to-all-start.1 = ((bf16[64,8,896]{2,1,0:T(8,128)(2,1)}), bf16[64,8,896]{2,1,0:T(8,128)(2,1)S(1)}, u32[]{:S(2)}, u32[]{:S(2)}) async-start(bf16[64,8,896]{2,1,0:T(8,128)(2,1)} %bitcast.30), calls=%async_computation.1 | async-start | bytes 1835008 | tf_op jit(solution)/shard_map/all_to_all | solution.py:683
Sparse Core Ops, SparseCore 0:
  19.5 28.5 all-gather.2

commit v8 on v7

--- a/solution.py
+++ b/solution.py
@@ -304,39 +304,35 @@
     wv_ref,
     ta_ref,
     tv_ref,
-    ra_ref,
-    rb_ref,
     x_ref,
     enc_ref,
     sems,
 ):
     bf16, f32 = jnp.bfloat16, jnp.float32
-    audio_width = x_ref.shape[3]
+    audio_width = x_ref.shape[2]
     audio_k = wa_ref.shape[1]
     cut = A_ROWS - audio_k
     sources = ((ga0, gb0, 0, 4), (ga1, gb1, 4, 4), (ga2, gb2, 8, 4), (ga3, gb3, 12, 2), (ga4, gb4, 14, 2))
+    own_copy = pltpu.make_async_copy(own_ref, x_ref, sems.at[0])
+    own_copy.start()
+
     for ga, gb, start, size in sources:
-        pltpu.make_async_copy(
-            ga.at[:, A_ROWS:, :], ra_ref.at[start : start + size], sems.at[2]
-        ).start()
-        pltpu.make_async_copy(
-            gb.at[:, B_ROWS:, :], rb_ref.at[start : start + size], sems.at[3]
-        ).start()
-    pltpu.make_async_copy(own_ref, x_ref.at[0], sems.at[0]).start()
-    pltpu.make_async_copy(other_ref, x_ref.at[1], sems.at[1]).start()
-    for ga, _, start, size in sources:
-        for n in range(size):
-            pltpu.make_async_copy(
-                ga.at[n, :audio_k, :], wa_ref.at[a_at_ref[start + n]], sems.at[4]
-            ).start()
-    for ga, gb, start, size in sources:
-        for n in range(size):
-            pltpu.make_async_copy(
-                ga.at[n, audio_k:A_ROWS, :], wv_ref.at[a_at_ref[start + n], :cut, :], sems.at[5]
-            ).start()
-            pltpu.make_async_copy(
-                gb.at[n, :B_ROWS, :], wv_ref.at[b_at_ref[start + n], cut:, :], sems.at[6]
-            ).start()
+
+        @pl.loop(0, size)
+        def _(n):
+            at = a_at_ref[start + n]
+            wa_ref[at] = ga[n, :audio_k, :]
+            wv_ref[at, :cut, :] = ga[n, audio_k:A_ROWS, :]
+            ta = jnp.concatenate([ga[n, A_ROWS:, q * 128 : (q + 1) * 128] for q in range(3)], axis=0)
+            ta_ref[at] = ta[:audio_k]
+            tv_ref[at, : 96 - audio_k, :] = ta[audio_k:]
+            tv_ref[at, 96 - audio_k : cut, :] = roll_half(ta)
+            at = b_at_ref[start + n]
+            wv_ref[at, cut:, :] = gb[n, :B_ROWS, :]
+            tb = jnp.concatenate([gb[n, B_ROWS:, q * 128 : (q + 1) * 128] for q in range(2)], axis=0)
+            tv_ref[at, cut : cut + 96, :] = tb
+            tv_ref[at, cut + 96 : cut + 112, :] = gb[n, B_ROWS : B_ROWS + 16, 256:]
+            tv_ref[at, cut + 112 :, :] = roll_half(tb)
 
     count = cell_ref.shape[1]
     cells = out_ref.shape[0]
@@ -344,30 +340,9 @@
     first = jnp.where(line == cell_ref[0:1, :], 1.0, 0.0).astype(bf16)
     second = jnp.where(line == cell_ref[1:2, :], 1.0, 0.0).astype(bf16)
 
-    pltpu.make_async_copy(ra_ref, ra_ref, sems.at[2]).wait()
-
-    @pl.loop(0, 16)
-    def _(p):
-        ta = jnp.concatenate([ra_ref[p, :, q * 128 : (q + 1) * 128] for q in range(3)], axis=0)
-        at = a_at_ref[p]
-        ta_ref[at, :, :] = ta[:audio_k]
-        tv_ref[at, : 96 - audio_k, :] = ta[audio_k:]
-        tv_ref[at, 96 - audio_k : cut, :] = roll_half(ta)
-
-    pltpu.make_async_copy(rb_ref, rb_ref, sems.at[3]).wait()
-
-    @pl.loop(0, 16)
-    def _(p):
-        at = b_at_ref[p]
-        tb = jnp.concatenate([rb_ref[p, :, q * 128 : (q + 1) * 128] for q in range(2)], axis=0)
-        tv_ref[at, cut : cut + 96, :] = tb
-        tv_ref[at, cut + 96 : cut + 112, :] = rb_ref[p, :16, 256:]
-        tv_ref[at, cut + 112 :, :] = roll_half(tb)
-
-    halves, n_enc = x_ref.shape[:2]
+    halves, n_enc = 2, x_ref.shape[0]
     audio = 64
     vision = 32
-    n_audio = halves * n_enc * audio
     n_vision = halves * n_enc * vision
 
     def weights(main, last):
@@ -381,18 +356,16 @@
                 at = g * count + base + h * run
                 enc_ref[at : at + run, :] = value[(2 * h + g) * run : (2 * h + g + 1) * run]
 
-    pltpu.make_async_copy(own_ref, x_ref.at[0], sems.at[0]).wait()
-    pltpu.make_async_copy(other_ref, x_ref.at[1], sems.at[1]).wait()
-    pltpu.make_async_copy(wa_ref, wa_ref, sems.at[4]).wait()
-    rows = x_ref[:, :, :audio, :].reshape(n_audio, audio_width)
-    keep_rows(dot(rows, weights(wa_ref[...], ta_ref[...])).astype(bf16), 0, audio)
-    pltpu.make_async_copy(wv_ref.at[:, :cut, :], wv_ref.at[:, :cut, :], sems.at[5]).wait()
-    pltpu.make_async_copy(wv_ref.at[:, cut:, :], wv_ref.at[:, cut:, :], sems.at[6]).wait()
+    def rows(at, each):
+        parts = [ref[:, at : at + each, :].reshape(n_enc * each, audio_width) for ref in (x_ref, other_ref)]
+        return jnp.concatenate(parts, axis=0)
+
+    own_copy.wait()
+    keep_rows(dot(rows(0, audio), weights(wa_ref[...], ta_ref[...])).astype(bf16), 0, audio)
     total = jnp.zeros((n_vision, 512), f32)
     for i in range(4):
-        rows = x_ref[:, :, audio + i * vision : audio + (i + 1) * vision, :]
         part = weights(wv_ref[4 * i : 4 * i + 4], tv_ref[4 * i : 4 * i + 4])
-        total = total + dot(rows.reshape(n_vision, audio_width), part)
+        total = total + dot(rows(audio + i * vision, vision), part)
     keep_rows(total.astype(bf16), 4 * audio, vision)
 
     out_ref[:, :384] = dot(first, enc_ref[:count, :384]).astype(bf16)
@@ -413,18 +386,16 @@
     return pl.pallas_call(
         encode_kernel,
         out_shape=jax.ShapeDtypeStruct((n_cells, 896), bf16),
-        in_specs=[smem, smem] + [anywhere] * 12 + [vmem],
+        in_specs=[smem, smem] + [vmem] * 10 + [anywhere] + [vmem] * 2,
         out_specs=vmem,
         scratch_shapes=[
             pltpu.VMEM((16, k, 384), bf16),
             pltpu.VMEM((16, 4 * k, 384), bf16),
             pltpu.VMEM((16, k, 128), bf16),
             pltpu.VMEM((16, 4 * k, 128), bf16),
-            pltpu.VMEM((16, A_TAIL, 384), bf16),
-            pltpu.VMEM((16, B_TAIL, 384), bf16),
-            pltpu.VMEM((2, n_enc, rows, width), bf16),
+            pltpu.VMEM((n_enc, rows, width), bf16),
             pltpu.VMEM((2 * cells.shape[1], 512), bf16),
-            pltpu.SemaphoreType.DMA((7,)),
+            pltpu.SemaphoreType.DMA((1,)),
         ],
         compiler_params=pltpu.CompilerParams(vmem_limit_bytes=BIG),
         cost_estimate=pl.CostEstimate(

time: 158 us -> 150 us (0.949)
  Pallas kernels: 33.6 us -> 25.5 us
    pallas_call x1, Pallas kernels: 14.6 us -> 6.47 us  [encode(): pl.pallas_call(encode_kernel, out_shape=jax.ShapeDtypeStruct((n_cells, 89...]
where the time goes in v8:
time: 150 us; the launch traced here: 149 us
  waiting for transfers between devices  62.4 us (42%)
  starting transfers between devices  38 us (25%)
  Pallas kernels  25.5 us (17%)
  between operations  14.4 us (10%)
  local copies, waits for them, and re-layouts  5.64 us (4%)
  other arithmetic  3.5 us (2%)
    ppermute x14, starting transfers between devices, shift(): return lax.ppermute(x, axis, [(i, (i + k) % 4) for i in range(4)])  24.6 us
    ppermute x14, waiting for transfers between devices, shift(): return lax.ppermute(x, axis, [(i, (i + k) % 4) for i in range(4)])  24.2 us
    all_to_all x1, waiting for transfers between devices, local(): lax.all_to_all(out8.reshape(senders, 2 * cap, half), SPREAD, split_axis=0...  17.5 us
    all_to_all x1, waiting for transfers between devices, local(): lax.all_to_all(outgoing.reshape(senders, 8, slab // 2), SPREAD, split_axi...  15.8 us
    pallas_call x1, Pallas kernels, attend(): pl.pallas_call(attend_kernel, out_shape=(jax.ShapeDtypeStruct((rows, slab...  11.9 us
    all_to_all x1, starting transfers between devices, local(): lax.all_to_all(outgoing.reshape(senders, 8, slab // 2), SPREAD, split_axi...  8.13 us
    pallas_call x1, Pallas kernels, encode(): pl.pallas_call(encode_kernel, out_shape=jax.ShapeDtypeStruct((n_cells, 89...  6.47 us
    all_to_all x1, starting transfers between devices, local(): lax.all_to_all(out8.reshape(senders, 2 * cap, half), SPREAD, split_axis=0...  4.82 us
  transfers between devices with their start and end apart: 20, of which 7 were waited for; matrix products, arithmetic and copies ran while one was open for 5% of the time, Pallas kernels for 0%

profile of v8, /device:TPU:0, one launch (start us, length us, event | category | flops | bytes accessed | tf_op | source)
XLA Modules:
  0.0 149.4 jit_solution(15145956450979330987)
XLA Ops:
  7.3 2.7 %shard_map.122 = (bf16[224,384]{1,0:T(8,128)(2,1)S(1)}, bf16[256,384]{1,0:T(8,128)(2,1)S(1)}, bf16[192,1280]{1,0:T(8,128)(2,1)}) custom-call(s32[2]{0:T(128)S(1)} %pad_add_fusion.1.place_ref, bf16[80,1792]{1,0:T(8,128)(2,1)} %audio_w_ref.1, bf16[80,4,1792]{2,1,0:T(4,128)(2,1)} %vision_w_ref.1, bf16[128,1280]{1,0:T(8,128)(2,1)} %audio_ref.1, ...), custom_call_target="tpu_custom_call" | custom-call | bytes 1800000 | tf_op jit(solution)/shard_map/pallas_call | solution.py:262
  10.0 2.1 %collective-permute-start.3 = (bf16[256,384]{1,0:T(8,128)(2,1)S(1)}, bf16[256,384]{1,0:T(8,128)(2,1)S(1)}, u32[]{:S(2)}, u32[]{:S(2)}) collective-permute-start(bf16[256,384]{1,0:T(8,128)(2,1)S(1)} %get-tuple-element.43), channel_id=1, source_target_pairs={{0,8},{8,16},{16,24},{24,0},{1,9},{9,17},{17,25},{25,1},{2,10},{10... | collective-permute-start | bytes 589832 | tf_op jit(solution)/shard_map/ppermute | solution.py:538
  12.1 2.2 %collective-permute-start.4 = (bf16[256,384]{1,0:T(8,128)(2,1)S(1)}, bf16[256,384]{1,0:T(8,128)(2,1)S(1)}, u32[]{:S(2)}, u32[]{:S(2)}) collective-permute-start(bf16[256,384]{1,0:T(8,128)(2,1)S(1)} %get-tuple-element.43), channel_id=1, source_target_pairs={{0,24},{8,0},{16,8},{24,16},{1,25},{9,1},{17,9},{25,17},{2,26},{10... | collective-permute-start | bytes 589832 | tf_op jit(solution)/shard_map/ppermute | solution.py:538
  14.3 1.8 %collective-permute-start.5 = (bf16[256,384]{1,0:T(8,128)(2,1)S(1)}, bf16[256,384]{1,0:T(8,128)(2,1)S(1)}, u32[]{:S(2)}, u32[]{:S(2)}) collective-permute-start(bf16[256,384]{1,0:T(8,128)(2,1)S(1)} %get-tuple-element.43), channel_id=1, source_target_pairs={{0,16},{8,24},{16,0},{24,8},{1,17},{9,25},{17,1},{25,9},{2,18},{10... | collective-permute-start | bytes 589832 | tf_op jit(solution)/shard_map/ppermute | solution.py:538
  16.1 1.6 %collective-permute-start = (bf16[224,384]{1,0:T(8,128)(2,1)S(1)}, bf16[224,384]{1,0:T(8,128)(2,1)S(1)}, u32[]{:S(2)}, u32[]{:S(2)}) collective-permute-start(bf16[224,384]{1,0:T(8,128)(2,1)S(1)} %get-tuple-element.39), channel_id=1, source_target_pairs={{0,2},{2,4},{4,6},{6,0},{1,3},{3,5},{5,7},{7,1},{8,10},{10,12},{12... | collective-permute-start | bytes 516104 | tf_op jit(solution)/shard_map/ppermute | solution.py:538
  17.7 1.7 %collective-permute-start.1 = (bf16[224,384]{1,0:T(8,128)(2,1)S(1)}, bf16[224,384]{1,0:T(8,128)(2,1)S(1)}, u32[]{:S(2)}, u32[]{:S(2)}) collective-permute-start(bf16[224,384]{1,0:T(8,128)(2,1)S(1)} %get-tuple-element.39), channel_id=1, source_target_pairs={{0,6},{2,0},{4,2},{6,4},{1,7},{3,1},{5,3},{7,5},{8,14},{10,8},{12,... | collective-permute-start | bytes 516104 | tf_op jit(solution)/shard_map/ppermute | solution.py:538
  19.5 0.4 convert_reduce_fusion
  20.0 0.6 reduce-window.6
  20.6 0.2 slice_reduce_fusion
  20.8 0.1 copy_bitcast_fusion
  21.0 0.2 select_reduce_fusion
  21.1 0.1 sub.66
  21.2 0.1 copy.56
  21.3 0.1 reshape.306
  21.5 0.6 gather_fusion
  22.1 0.1 reshape.307
  22.3 0.6 gather_fusion.1
  22.8 0.1 reshape.309
  22.9 0.1 copy.64
  23.1 0.1 stack_reshape.6
  23.2 0.1 stack_reshape.7
  23.4 0.1 copy.55
  23.5 0.1 reshape.312.e_row_ref
  23.6 0.1 sub.67
  23.8 0.1 add.155.a_at_ref
  23.9 0.1 add.159.b_at_ref
  24.0 0.6 pad_add_fusion
  24.6 0.1 convert_reduce_fusion.1
  24.7 0.2 convert_reduce_fusion.2
  25.0 2.1 %collective-permute-start.2 = (bf16[224,384]{1,0:T(8,128)(2,1)S(1)}, bf16[224,384]{1,0:T(8,128)(2,1)S(1)}, u32[]{:S(2)}, u32[]{:S(2)}) collective-permute-start(bf16[224,384]{1,0:T(8,128)(2,1)S(1)} %get-tuple-element.39), channel_id=1, source_target_pairs={{0,4},{2,6},{4,0},{6,2},{1,5},{3,7},{5,1},{7,3},{8,12},{10,14},{12... | collective-permute-start | bytes 516104 | tf_op jit(solution)/shard_map/ppermute | solution.py:538
  27.0 0.6 add_bitcast_fusion.1
  27.6 4.3 %collective-permute-done.2 = bf16[224,384]{1,0:T(8,128)(2,1)S(1)} collective-permute-done((bf16[224,384]{1,0:T(8,128)(2,1)S(1)}, bf16[224,384]{1,0:T(8,128)(2,1)S(1)}, u32[]{:S(2)}, u32[]{:S(2)}) %collective-permute-start.2) | collective-permute-done | bytes 172064 | tf_op jit(solution)/shard_map/ppermute | solution.py:538
  32.0 0.1 pad_maximum_fusion.1.ga0
  32.1 0.1 pad_maximum_fusion.gb0
  32.2 0.4 collective-permute-start.8
  32.7 2.9 %collective-permute-start.9 = (bf16[4,256,384]{2,1,0:T(8,128)(2,1)S(1)}, bf16[4,256,384]{2,1,0:T(8,128)(2,1)S(1)}, u32[]{:S(2)}, u32[]{:S(2)}) collective-permute-start(bf16[4,256,384]{2,1,0:T(8,128)(2,1)S(1)} %pad_maximum_fusion.gb0), channel_id=1, source_target_pairs={{0,6},{2,0},{4,2},{6,4},{1,7},{3,1},{5,3},{7,5},{8,14},{10,8},{12,... | collective-permute-start | bytes 2359304 | tf_op jit(solution)/shard_map/ppermute | solution.py:538
  35.5 1.0 collective-permute-start.6
  36.5 2.2 %collective-permute-start.7 = (bf16[4,224,384]{2,1,0:T(8,128)(2,1)S(1)}, bf16[4,224,384]{2,1,0:T(8,128)(2,1)S(1)}, u32[]{:S(2)}, u32[]{:S(2)}) collective-permute-start(bf16[4,224,384]{2,1,0:T(8,128)(2,1)S(1)} %pad_maximum_fusion.1.ga0), channel_id=1, source_target_pairs={{0,24},{8,0},{16,8},{24,16},{1,25},{9,1},{17,9},{25,17},{2,26},{10... | collective-permute-start | bytes 2064392 | tf_op jit(solution)/shard_map/ppermute | solution.py:538
  38.8 12.1 %collective-permute-done.6.ga1 = bf16[4,224,384]{2,1,0:T(8,128)(2,1)S(1)} collective-permute-done((bf16[4,224,384]{2,1,0:T(8,128)(2,1)S(1)}, bf16[4,224,384]{2,1,0:T(8,128)(2,1)S(1)}, u32[]{:S(2)}, u32[]{:S(2)}) %collective-permute-start.6) | collective-permute-done | bytes 688160 | tf_op jit(solution)/shard_map/ppermute | solution.py:538
  50.9 0.8 copy-done.1
  51.7 0.2 copy-done.3
  52.0 0.1 collective-permute-start.14
  52.2 3.3 %collective-permute-start.13 = (bf16[2,256,384]{2,1,0:T(8,128)(2,1)S(1)}, bf16[2,256,384]{2,1,0:T(8,128)(2,1)S(1)}, u32[]{:S(2)}, u32[]{:S(2)}) collective-permute-start(bf16[2,256,384]{2,1,0:T(8,128)(2,1)S(1)} %slice.35), channel_id=1, source_target_pairs={{0,6},{2,0},{4,2},{6,4},{1,7},{3,1},{5,3},{7,5},{8,14},{10,8},{12,... | collective-permute-start | bytes 1179656 | tf_op jit(solution)/shard_map/ppermute | solution.py:538
  55.5 1.0 slice.32
  56.5 0.3 collective-permute-start.10
  56.9 3.1 %collective-permute-start.11 = (bf16[2,224,384]{2,1,0:T(8,128)(2,1)S(1)}, bf16[2,224,384]{2,1,0:T(8,128)(2,1)S(1)}, u32[]{:S(2)}, u32[]{:S(2)}) collective-permute-start(bf16[2,224,384]{2,1,0:T(8,128)(2,1)S(1)} %slice.33), channel_id=1, source_target_pairs={{0,24},{8,0},{16,8},{24,16},{1,25},{9,1},{17,9},{25,17},{2,26},{10... | collective-permute-start | bytes 1032200 | tf_op jit(solution)/shard_map/ppermute | solution.py:538
  60.0 7.8 %collective-permute-done.10.ga3 = bf16[2,224,384]{2,1,0:T(8,128)(2,1)S(1)} collective-permute-done((bf16[2,224,384]{2,1,0:T(8,128)(2,1)S(1)}, bf16[2,224,384]{2,1,0:T(8,128)(2,1)S(1)}, u32[]{:S(2)}, u32[]{:S(2)}) %collective-permute-start.10) | collective-permute-done | bytes 344096 | tf_op jit(solution)/shard_map/ppermute | solution.py:538
  67.8 6.5 %shard_map.123 = bf16[512,896]{1,0:T(8,128)(2,1)} custom-call(s32[16]{0:T(128)S(1)} %add.155.a_at_ref, s32[16]{0:T(128)S(1)} %add.159.b_at_ref, bf16[4,224,384]{2,1,0:T(8,128)(2,1)S(1)} %pad_maximum_fusion.1.ga0, bf16[4,224,384]{2,1,0:T(8,128)(2,1)S(1)} %copy-done.2, bf16[4,224,384]{2,1,0:T(8,128)(2,1)S(1)} %copy-done.4, ...), custom_call_target="tpu_custom_call" | custom-call | flops 3000000000 | bytes 11000000 | tf_op jit(solution)/shard_map/pallas_call | solution.py:386
  74.3 8.1 %all-to-all-start = ((bf16[64,8,896]{2,1,0:T(8,128)(2,1)}), bf16[64,8,896]{2,1,0:T(8,128)(2,1)S(1)}, u32[]{:S(2)}, u32[]{:S(2)}) async-start(bf16[64,8,896]{2,1,0:T(8,128)(2,1)} %bitcast.28), calls=%async_computation | async-start | bytes 1835008 | tf_op jit(solution)/shard_map/all_to_all | solution.py:642
  82.4 0.1 copy.59.filled_ref
  82.5 15.8 %all-to-all-done = bf16[64,8,896]{2,1,0:T(8,128)(2,1)S(1)} async-done(((bf16[64,8,896]{2,1,0:T(8,128)(2,1)}), bf16[64,8,896]{2,1,0:T(8,128)(2,1)S(1)}, u32[]{:S(2)}, u32[]{:S(2)}) %all-to-all-start) | async-done | bytes 917536 | tf_op jit(solution)/shard_map/all_to_all | solution.py:642
  98.4 0.9 shard_map.124.own_ref.rows_ref
  99.2 0.1 collective-permute-start.15
  99.3 0.1 copy.60.seg_col_ref
  99.5 2.3 %collective-permute-done.15.other_ref = bf16[256,1792]{1,0:T(8,128)(2,1)S(1)} collective-permute-done((bf16[256,1792]{1,0:T(8,128)(2,1)S(1)}, bf16[256,1792]{1,0:T(8,128)(2,1)S(1)}, u32[]{:S(2)}, u32[]{:S(2)}) %collective-permute-start.15) | collective-permute-done | bytes 917536 | tf_op jit(solution)/shard_map/ppermute | solution.py:534
  101.8 11.9 %shard_map.125 = (bf16[256,1920]{1,0:T(8,128)(2,1)}, bf16[256,1792]{1,0:T(8,128)(2,1)S(1)}, f32[256,1]{1,0:T(8,128)S(1)}, f32[256,1]{1,0:T(8,128)S(1)}) custom-call(s32[1]{0:T(128)} %bitcast.1.half_ref, bf16[256,1792]{1,0:T(8,128)(2,1)S(1)} %shard_map.124.own_ref.rows_ref, bf16[256,1792]{1,0:T(8,128)(2,1)S(1)} %collective-permute-done.15.other_ref, ...), custom_call_target="tpu_custom_call" | custom-call | flops 5000000000 | bytes 14000000 | tf_op jit(solution)/shard_map/pallas_call | solution.py:136
  113.7 0.2 collective-permute-start.16
  113.9 0.1 copy.61.spot_ref
  114.1 2.5 %collective-permute-done.16.taken_ref = bf16[256,1920]{1,0:T(8,128)(2,1)S(1)} collective-permute-done((bf16[256,1920]{1,0:T(8,128)(2,1)}, bf16[256,1920]{1,0:T(8,128)(2,1)S(1)}, u32[]{:S(2)}, u32[]{:S(2)}) %collective-permute-start.16) | collective-permute-done | bytes 983072 | tf_op jit(solution)/shard_map/ppermute | solution.py:534
  116.6 2.1 %shard_map.126 = bf16[512,896]{1,0:T(8,128)(2,1)} custom-call(s32[1]{0:T(128)} %bitcast.1.half_ref, bf16[256,1792]{1,0:T(8,128)(2,1)S(1)} %shard_map.124.own_ref.rows_ref, bf16[256,1792]{1,0:T(8,128)(2,1)S(1)} %get-tuple-element.59.keep_ref, bf16[256,1920]{1,0:T(8,128)(2,1)S(1)} %collective-permute-done.16.taken_ref, ...), custom_call_target="tpu_custom_call" | custom-call | flops 500000000 | bytes 4000000 | tf_op jit(solution)/shard_map/pallas_call | solution.py:491
  118.6 4.8 %all-to-all-start.1 = ((bf16[64,8,896]{2,1,0:T(8,128)(2,1)}), bf16[64,8,896]{2,1,0:T(8,128)(2,1)S(1)}, u32[]{:S(2)}, u32[]{:S(2)}) async-start(bf16[64,8,896]{2,1,0:T(8,128)(2,1)} %bitcast.30), calls=%async_computation.1 | async-start | bytes 1835008 | tf_op jit(solution)/shard_map/all_to_all | solution.py:654
  123.5 0.1 copy.62.cell_ref
  123.6 17.5 %all-to-all-done.1 = bf16[64,8,896]{2,1,0:T(8,128)(2,1)S(1)} async-done(((bf16[64,8,896]{2,1,0:T(8,128)(2,1)}), bf16[64,8,896]{2,1,0:T(8,128)(2,1)S(1)}, u32[]{:S(2)}, u32[]{:S(2)}) %all-to-all-start.1) | async-done | bytes 917536 | tf_op jit(solution)/shard_map/all_to_all | solution.py:654
  141.1 1.5 shard_map.127
  (69 shorter events, 1.1 us)
Async XLA Ops:
  7.2 12.2 %copy-start.6 = (s32[64,192]{1,0:T(8,128)S(1)}, s32[64,192]{1,0:T(8,128)}, u32[]{:S(2)}) copy-start(s32[64,192]{1,0:T(8,128)} %param.16) | copy-start | bytes 147460
  7.2 44.8 %all-gather.3.cloned.1.call-start = ((), (), s32[]{:S(2)}) async-start(), calls=%async_computation.2 | async-start | bytes 2457600 | tf_op jit(solution)/shard_map/all_gather | solution.py:634
  7.3 16.4 %copy-start.10 = (s32[4]{0:T(128)S(1)}, s32[4]{0:T(128)}, u32[]{:S(2)}) copy-start(s32[4]{0:T(128)} %constant.148) | copy-start | bytes 52
  7.3 16.7 %copy-start.8 = (f32[3584]{0:T(1024)S(1)}, f32[3584]{0:T(1024)}, u32[]{:S(2)}) copy-start(f32[3584]{0:T(1024)} %param.18) | copy-start | bytes 43012
  10.0 21.9 %collective-permute-start.3 = (bf16[256,384]{1,0:T(8,128)(2,1)S(1)}, bf16[256,384]{1,0:T(8,128)(2,1)S(1)}, u32[]{:S(2)}, u32[]{:S(2)}) collective-permute-start(bf16[256,384]{1,0:T(8,128)(2,1)S(1)} %get-tuple-element.43), channel_id=1, source_target_pairs={{0,8},{8,16},{16,24},{24,0},{1,9},{9,17},{17,25},{25,1},{2,10},{10... | collective-permute-start | bytes 589832 | tf_op jit(solution)/shard_map/ppermute | solution.py:538
  12.1 19.9 %collective-permute-start.4 = (bf16[256,384]{1,0:T(8,128)(2,1)S(1)}, bf16[256,384]{1,0:T(8,128)(2,1)S(1)}, u32[]{:S(2)}, u32[]{:S(2)}) collective-permute-start(bf16[256,384]{1,0:T(8,128)(2,1)S(1)} %get-tuple-element.43), channel_id=1, source_target_pairs={{0,24},{8,0},{16,8},{24,16},{1,25},{9,1},{17,9},{25,17},{2,26},{10... | collective-permute-start | bytes 589832 | tf_op jit(solution)/shard_map/ppermute | solution.py:538
  14.3 17.7 %collective-permute-start.5 = (bf16[256,384]{1,0:T(8,128)(2,1)S(1)}, bf16[256,384]{1,0:T(8,128)(2,1)S(1)}, u32[]{:S(2)}, u32[]{:S(2)}) collective-permute-start(bf16[256,384]{1,0:T(8,128)(2,1)S(1)} %get-tuple-element.43), channel_id=1, source_target_pairs={{0,16},{8,24},{16,0},{24,8},{1,17},{9,25},{17,1},{25,9},{2,18},{10... | collective-permute-start | bytes 589832 | tf_op jit(solution)/shard_map/ppermute | solution.py:538
  16.1 8.9 %collective-permute-start = (bf16[224,384]{1,0:T(8,128)(2,1)S(1)}, bf16[224,384]{1,0:T(8,128)(2,1)S(1)}, u32[]{:S(2)}, u32[]{:S(2)}) collective-permute-start(bf16[224,384]{1,0:T(8,128)(2,1)S(1)} %get-tuple-element.39), channel_id=1, source_target_pairs={{0,2},{2,4},{4,6},{6,0},{1,3},{3,5},{5,7},{7,1},{8,10},{10,12},{12... | collective-permute-start | bytes 516104 | tf_op jit(solution)/shard_map/ppermute | solution.py:538
  17.7 10.0 %collective-permute-start.1 = (bf16[224,384]{1,0:T(8,128)(2,1)S(1)}, bf16[224,384]{1,0:T(8,128)(2,1)S(1)}, u32[]{:S(2)}, u32[]{:S(2)}) collective-permute-start(bf16[224,384]{1,0:T(8,128)(2,1)S(1)} %get-tuple-element.39), channel_id=1, source_target_pairs={{0,6},{2,0},{4,2},{6,4},{1,7},{3,1},{5,3},{7,5},{8,14},{10,8},{12,... | collective-permute-start | bytes 516104 | tf_op jit(solution)/shard_map/ppermute | solution.py:538
  25.0 7.0 %collective-permute-start.2 = (bf16[224,384]{1,0:T(8,128)(2,1)S(1)}, bf16[224,384]{1,0:T(8,128)(2,1)S(1)}, u32[]{:S(2)}, u32[]{:S(2)}) collective-permute-start(bf16[224,384]{1,0:T(8,128)(2,1)S(1)} %get-tuple-element.39), channel_id=1, source_target_pairs={{0,4},{2,6},{4,0},{6,2},{1,5},{3,7},{5,1},{7,3},{8,12},{10,14},{12... | collective-permute-start | bytes 516104 | tf_op jit(solution)/shard_map/ppermute | solution.py:538
  32.2 18.7 %collective-permute-start.8 = (bf16[4,256,384]{2,1,0:T(8,128)(2,1)S(1)}, bf16[4,256,384]{2,1,0:T(8,128)(2,1)S(1)}, u32[]{:S(2)}, u32[]{:S(2)}) collective-permute-start(bf16[4,256,384]{2,1,0:T(8,128)(2,1)S(1)} %pad_maximum_fusion.gb0), channel_id=1, source_target_pairs={{0,2},{2,4},{4,6},{6,0},{1,3},{3,5},{5,7},{7,1},{8,10},{10,12},{12... | collective-permute-start | bytes 2359304 | tf_op jit(solution)/shard_map/ppermute | solution.py:538
  32.7 19.3 %collective-permute-start.9 = (bf16[4,256,384]{2,1,0:T(8,128)(2,1)S(1)}, bf16[4,256,384]{2,1,0:T(8,128)(2,1)S(1)}, u32[]{:S(2)}, u32[]{:S(2)}) collective-permute-start(bf16[4,256,384]{2,1,0:T(8,128)(2,1)S(1)} %pad_maximum_fusion.gb0), channel_id=1, source_target_pairs={{0,6},{2,0},{4,2},{6,4},{1,7},{3,1},{5,3},{7,5},{8,14},{10,8},{12,... | collective-permute-start | bytes 2359304 | tf_op jit(solution)/shard_map/ppermute | solution.py:538
  35.5 15.3 %collective-permute-start.6 = (bf16[4,224,384]{2,1,0:T(8,128)(2,1)S(1)}, bf16[4,224,384]{2,1,0:T(8,128)(2,1)S(1)}, u32[]{:S(2)}, u32[]{:S(2)}) collective-permute-start(bf16[4,224,384]{2,1,0:T(8,128)(2,1)S(1)} %pad_maximum_fusion.1.ga0), channel_id=1, source_target_pairs={{0,8},{8,16},{16,24},{24,0},{1,9},{9,17},{17,25},{25,1},{2,10},{10... | collective-permute-start | bytes 2064392 | tf_op jit(solution)/shard_map/ppermute | solution.py:538
  36.5 14.3 %collective-permute-start.7 = (bf16[4,224,384]{2,1,0:T(8,128)(2,1)S(1)}, bf16[4,224,384]{2,1,0:T(8,128)(2,1)S(1)}, u32[]{:S(2)}, u32[]{:S(2)}) collective-permute-start(bf16[4,224,384]{2,1,0:T(8,128)(2,1)S(1)} %pad_maximum_fusion.1.ga0), channel_id=1, source_target_pairs={{0,24},{8,0},{16,8},{24,16},{1,25},{9,1},{17,9},{25,17},{2,26},{10... | collective-permute-start | bytes 2064392 | tf_op jit(solution)/shard_map/ppermute | solution.py:538
  50.9 0.9 copy-start.1
  50.9 1.1 copy-start.3
  52.0 4.9 %copy-start.4 = (bf16[4,224,384]{2,1,0:T(8,128)(2,1)S(1)}, bf16[4,224,384]{2,1,0:T(8,128)(2,1)}, u32[]{:S(2)}) copy-start(bf16[4,224,384]{2,1,0:T(8,128)(2,1)} %copy-done.3) | copy-start | bytes 2064388
  52.0 15.8 %copy-start.2 = (bf16[4,224,384]{2,1,0:T(8,128)(2,1)S(1)}, bf16[4,224,384]{2,1,0:T(8,128)(2,1)}, u32[]{:S(2)}) copy-start(bf16[4,224,384]{2,1,0:T(8,128)(2,1)} %copy-done.1) | copy-start | bytes 2064388
  52.0 15.8 %collective-permute-start.14 = (bf16[4,192,1280]{2,1,0:T(8,128)(2,1)}, bf16[4,192,1280]{2,1,0:T(8,128)(2,1)S(1)}, u32[]{:S(2)}, u32[]{:S(2)}) collective-permute-start(bf16[4,192,1280]{2,1,0:T(8,128)(2,1)} %bitcast.89), channel_id=1, source_target_pairs={{0,1},{1,0},{2,3},{3,2},{4,5},{5,4},{6,7},{7,6},{8,9},{9,8},{10,11... | collective-permute-start | bytes 5898248 | tf_op jit(solution)/shard_map/ppermute | solution.py:534
  52.1 15.6 %collective-permute-start.12 = (bf16[2,256,384]{2,1,0:T(8,128)(2,1)S(1)}, bf16[2,256,384]{2,1,0:T(8,128)(2,1)S(1)}, u32[]{:S(2)}, u32[]{:S(2)}) collective-permute-start(bf16[2,256,384]{2,1,0:T(8,128)(2,1)S(1)} %slice.34), channel_id=1, source_target_pairs={{0,2},{2,4},{4,6},{6,0},{1,3},{3,5},{5,7},{7,1},{8,10},{10,12},{12... | collective-permute-start | bytes 1179656 | tf_op jit(solution)/shard_map/ppermute | solution.py:538
  52.2 15.5 %collective-permute-start.13 = (bf16[2,256,384]{2,1,0:T(8,128)(2,1)S(1)}, bf16[2,256,384]{2,1,0:T(8,128)(2,1)S(1)}, u32[]{:S(2)}, u32[]{:S(2)}) collective-permute-start(bf16[2,256,384]{2,1,0:T(8,128)(2,1)S(1)} %slice.35), channel_id=1, source_target_pairs={{0,6},{2,0},{4,2},{6,4},{1,7},{3,1},{5,3},{7,5},{8,14},{10,8},{12,... | collective-permute-start | bytes 1179656 | tf_op jit(solution)/shard_map/ppermute | solution.py:538
  56.5 11.2 %collective-permute-start.10 = (bf16[2,224,384]{2,1,0:T(8,128)(2,1)S(1)}, bf16[2,224,384]{2,1,0:T(8,128)(2,1)S(1)}, u32[]{:S(2)}, u32[]{:S(2)}) collective-permute-start(bf16[2,224,384]{2,1,0:T(8,128)(2,1)S(1)} %slice.32), channel_id=1, source_target_pairs={{0,8},{8,16},{16,24},{24,0},{1,9},{9,17},{17,25},{25,1},{2,10},{10... | collective-permute-start | bytes 1032200 | tf_op jit(solution)/shard_map/ppermute | solution.py:538
  56.9 10.8 %collective-permute-start.11 = (bf16[2,224,384]{2,1,0:T(8,128)(2,1)S(1)}, bf16[2,224,384]{2,1,0:T(8,128)(2,1)S(1)}, u32[]{:S(2)}, u32[]{:S(2)}) collective-permute-start(bf16[2,224,384]{2,1,0:T(8,128)(2,1)S(1)} %slice.33), channel_id=1, source_target_pairs={{0,24},{8,0},{16,8},{24,16},{1,25},{9,1},{17,9},{25,17},{2,26},{10... | collective-permute-start | bytes 1032200 | tf_op jit(solution)/shard_map/ppermute | solution.py:538
  74.2 24.1 %copy-start = (bf16[256,1792]{1,0:T(8,128)(2,1)S(1)}, bf16[256,1792]{1,0:T(8,128)(2,1)}, u32[]{:S(2)}) copy-start(bf16[256,1792]{1,0:T(8,128)(2,1)} %text_hbm.1) | copy-start | bytes 2752516
  74.3 24.1 %all-to-all-start = ((bf16[64,8,896]{2,1,0:T(8,128)(2,1)}), bf16[64,8,896]{2,1,0:T(8,128)(2,1)S(1)}, u32[]{:S(2)}, u32[]{:S(2)}) async-start(bf16[64,8,896]{2,1,0:T(8,128)(2,1)} %bitcast.28), calls=%async_computation | async-start | bytes 1835008 | tf_op jit(solution)/shard_map/all_to_all | solution.py:642
  82.4 16.9 %copy-start.5 = (s32[1,256]{1,0:T(1,128)S(1)}, s32[1,256]{1,0:T(1,128)}, u32[]{:S(2)}) copy-start(s32[1,256]{1,0:T(1,128)} %seg_row_ref.1) | copy-start | bytes 3076
  99.2 2.6 %collective-permute-start.15 = (bf16[256,1792]{1,0:T(8,128)(2,1)S(1)}, bf16[256,1792]{1,0:T(8,128)(2,1)S(1)}, u32[]{:S(2)}, u32[]{:S(2)}) collective-permute-start(bf16[256,1792]{1,0:T(8,128)(2,1)S(1)} %shard_map.124.own_ref.rows_ref), channel_id=1, source_target_pairs={{0,1},{1,0},{2,3},{3,2},{4,5},{5,4},{6,7},{7,6},{8,9},{9,8},{10,11... | collective-permute-start | bytes 2752520 | tf_op jit(solution)/shard_map/ppermute | solution.py:534
  99.5 14.4 %copy-start.7 = (s32[512,2]{0,1:T(2,128)S(1)}, s32[512,2]{0,1:T(2,128)}, u32[]{:S(2)}) copy-start(s32[512,2]{0,1:T(2,128)} %pad_add_fusion) | copy-start | bytes 12292
  113.7 2.9 %collective-permute-start.16 = (bf16[256,1920]{1,0:T(8,128)(2,1)}, bf16[256,1920]{1,0:T(8,128)(2,1)S(1)}, u32[]{:S(2)}, u32[]{:S(2)}) collective-permute-start(bf16[256,1920]{1,0:T(8,128)(2,1)} %get-tuple-element.60), channel_id=1, source_target_pairs={{0,1},{1,0},{2,3},{3,2},{4,5},{5,4},{6,7},{7,6},{8,9},{9,8},{10,11... | collective-permute-start | bytes 2949128 | tf_op jit(solution)/shard_map/ppermute | solution.py:534
  116.6 6.9 %copy-start.9 = (s32[192,1]{0,1:T(1,128)S(1)}, s32[192,1]{0,1:T(1,128)}, u32[]{:S(2)}) copy-start(s32[192,1]{0,1:T(1,128)} %add_bitcast_fusion.1) | copy-start | bytes 2308
  118.6 22.4 %all-to-all-start.1 = ((bf16[64,8,896]{2,1,0:T(8,128)(2,1)}), bf16[64,8,896]{2,1,0:T(8,128)(2,1)S(1)}, u32[]{:S(2)}, u32[]{:S(2)}) async-start(bf16[64,8,896]{2,1,0:T(8,128)(2,1)} %bitcast.30), calls=%async_computation.1 | async-start | bytes 1835008 | tf_op jit(solution)/shard_map/all_to_all | solution.py:654
Sparse Core Ops, SparseCore 0:
  19.5 28.5 all-gather.2

commit v9 on v8

--- a/solution.py
+++ b/solution.py
@@ -25,13 +25,43 @@
     return lax.dot_general(x, y, dims, preferred_element_type=jnp.float32)
 
 
+EARLY = 640
+
+
+def fetch_kernel(weight_hbm, upstream_hbm, weight_ref, upstream_ref, sems):
+    copies = [
+        pltpu.make_async_copy(weight_hbm.at[:, :EARLY], weight_ref, sems.at[0]),
+        pltpu.make_async_copy(upstream_hbm, upstream_ref, sems.at[1]),
+    ]
+    for copy in copies:
+        copy.start()
+    for copy in copies:
+        copy.wait()
+
+
+def fetch(weight, upstream):
+    return pl.pallas_call(
+        fetch_kernel,
+        out_shape=(
+            pltpu.VMEM((weight.shape[0], EARLY), weight.dtype),
+            pltpu.VMEM(upstream.shape, upstream.dtype),
+        ),
+        in_specs=[pl.BlockSpec(memory_space=pl.ANY)] * 2,
+        out_specs=(pl.BlockSpec(memory_space=pltpu.VMEM),) * 2,
+        scratch_shapes=[pltpu.SemaphoreType.DMA((2,))],
+        compiler_params=pltpu.CompilerParams(vmem_limit_bytes=1024 * 1024),
+        cost_estimate=pl.CostEstimate(flops=0, bytes_accessed=10_000_000, transcendentals=0),
+    )(in_hbm(weight), in_hbm(upstream))
+
+
 def attend_kernel(
     half_ref,
     own_ref,
     other_ref,
     gain_ref,
-    weight_ref,
-    upstream_hbm,
+    early_ref,
+    weight_hbm,
+    upstream_ref,
     seg_row_ref,
     seg_col_ref,
     give_ref,
@@ -43,25 +73,16 @@
     scaled_ref,
     sgrad_ref,
     bias_ref,
-    held_ref,
-    upstream_ref,
-    sems,
+    late_ref,
+    sem,
 ):
     bf16, f32 = jnp.bfloat16, jnp.float32
     rows, slab = own_ref.shape
-    group = weight_ref.shape[1]
+    group = weight_hbm.shape[1]
     heads = group // HEAD_DIM - 2
-    chunks = [(at, min(512, group - at)) for at in range(0, group, 512)]
-    pieces = len(chunks)
-    copies = [
-        pltpu.make_async_copy(
-            weight_ref.at[:, at : at + size], held_ref.at[:, at : at + size], sems.at[n]
-        )
-        for n, (at, size) in enumerate(chunks)
-    ]
-    last = pltpu.make_async_copy(upstream_hbm, upstream_ref, sems.at[pieces])
-    for copy in copies + [last]:
-        copy.start()
+    split = early_ref.shape[1]
+    load = pltpu.make_async_copy(weight_hbm.at[:, split:], late_ref, sem)
+    load.start()
     place_u = lax.broadcasted_iota(jnp.int32, (rows, rows), 0)
     place_t = lax.broadcasted_iota(jnp.int32, (rows, rows), 1)
     allowed = (seg_col_ref[...] == seg_row_ref[...]) & (place_u <= place_t)
@@ -83,13 +104,13 @@
     inv = lax.rsqrt(jnp.sum(squares, axis=1, keepdims=True) / (2 * slab) + epsilon)
     inv_ref[...] = inv
 
-    for n, (at, size) in enumerate(chunks):
-        copies[n].wait()
-        value = dot(normed_ref[...], held_ref[:, at : at + size])
-        unscaled_ref[:, at : at + size] = value
-        scaled_ref[:, at : at + size] = (value * inv).astype(bf16)
-
-    last.wait()
+    for ref, at, end in ((early_ref, 0, split), (late_ref, split, group)):
+        if at:
+            load.wait()
+        value = dot(normed_ref[...], ref[...])
+        unscaled_ref[:, at:end] = value
+        scaled_ref[:, at:end] = (value * inv).astype(bf16)
+
     key = scaled_ref[:, heads * HEAD_DIM : (heads + 1) * HEAD_DIM]
     val = scaled_ref[:, (heads + 1) * HEAD_DIM :]
     grad_key = jnp.zeros((rows, HEAD_DIM), f32)
@@ -123,11 +144,19 @@
     low = (total - high.astype(f32)).astype(bf16)
     give_ref[:, slab:] = jnp.where(lane == 0, high.astype(f32), low.astype(f32)).astype(bf16)
 
-    keep_ref[...] = dot(sgrad_ref[...], held_ref[pl.ds(own_at, slab), :], NT).astype(bf16)
-    give_ref[:, :slab] = dot(sgrad_ref[...], held_ref[pl.ds(other_at, slab), :], NT).astype(bf16)
-
-
-def attend(half, own, other, gain, qkv_weight, upstream, seg_row, seg_col):
+
+    def back(at):
+        rows_at = pl.ds(at, slab)
+        return (
+            dot(sgrad_ref[:, :split], early_ref[rows_at, :], NT)
+            + dot(sgrad_ref[:, split:], late_ref[rows_at, :], NT)
+        ).astype(bf16)
+
+    keep_ref[...] = back(own_at)
+    give_ref[:, :slab] = back(other_at)
+
+
+def attend(half, own, other, gain, early, qkv_weight, upstream, seg_row, seg_col):
     rows, slab = own.shape
     group = qkv_weight.shape[1]
     f32, bf16 = jnp.float32, jnp.bfloat16
@@ -142,7 +171,7 @@
             jax.ShapeDtypeStruct((rows, 1), f32),
         ),
         in_specs=[pl.BlockSpec(memory_space=pltpu.SMEM), vmem, vmem, vmem]
-        + [anywhere, anywhere, vmem, vmem],
+        + [vmem, anywhere, vmem, vmem, vmem],
         out_specs=(vmem,) * 4,
         scratch_shapes=[
             pltpu.VMEM((rows, 2 * slab), bf16),
@@ -150,9 +179,8 @@
             pltpu.VMEM((rows, group), bf16),
             pltpu.VMEM((rows, group), bf16),
             pltpu.VMEM((rows, rows), f32),
-            pltpu.VMEM((2 * slab, group), bf16),
-            pltpu.VMEM(upstream.shape, bf16),
-            pltpu.SemaphoreType.DMA((4,)),
+            pltpu.VMEM((2 * slab, group - early.shape[1]), bf16),
+            pltpu.SemaphoreType.DMA,
         ],
         compiler_params=pltpu.CompilerParams(vmem_limit_bytes=BIG),
         cost_estimate=pl.CostEstimate(flops=5_000_000_000, bytes_accessed=14_000_000, transcendentals=500_000),
@@ -161,8 +189,9 @@
         own,
         other,
         gain,
+        early,
         in_hbm(qkv_weight),
-        in_hbm(upstream),
+        upstream,
         seg_row,
         seg_col,
     )
@@ -579,8 +608,16 @@
         audio_rows,
         vision_rows,
     )
+    hops = (1, 3, 2)
+    along_y = [piece_a] + [shift(piece_a, "y", k) for k in hops]
+    along_z = [piece_b] + [shift(piece_b, "z", k) for k in hops]
+    along_y, along_z = lax.optimization_barrier((along_y, along_z))
+    stack_a, stack_b, row_target = lax.optimization_barrier(
+        (jnp.stack(along_y), jnp.stack(along_z), row_target)
+    )
+    near_a = [shift(stack_a, "z", 1), shift(stack_a, "z", 3)]
+    near_b = [shift(stack_b, "y", 1), shift(stack_b, "y", 3)]
     z, y = lax.axis_index("z"), lax.axis_index("y")
-    hops = (1, 3, 2)
     back = jnp.array((0,) + hops, jnp.int32)
     a_at = (((z - back) % 4)[:, None] * 4 + ((y - back) % 4)[None, :]).reshape(-1)
     b_at = (((y - back) % 4)[:, None] + ((z - back) % 4)[None, :] * 4).reshape(-1)
@@ -621,20 +658,16 @@
     gain = norm_gain.reshape(2, slab)
     seg_row = segment_ids
     seg_col = segment_ids.reshape(length, 1)
-    along_y = [piece_a] + [shift(piece_a, "y", k) for k in hops]
-    along_z = [piece_b] + [shift(piece_b, "z", k) for k in hops]
-    along_y, along_z, cells, by_line, filled, spots, own_cell, gain, seg_col, a_at, b_at = (
-        lax.optimization_barrier(
-            (along_y, along_z, cells, by_line, filled, spots, own_cell, gain, seg_col, a_at, b_at)
-        )
-    )
-    stack_a, stack_b = lax.optimization_barrier((jnp.stack(along_y), jnp.stack(along_z)))
-    near_a = [shift(stack_a, "z", 1), shift(stack_a, "z", 3)]
-    near_b = [shift(stack_b, "y", 1), shift(stack_b, "y", 3)]
     own = lax.all_gather(packed, "enc", axis=0, tiled=False)
-    near_a, near_b, own = lax.optimization_barrier((near_a, near_b, own))
-    far_a = [shift(near_a[0][:2], "z", 1), shift(near_a[1][2:], "z", 3)]
-    far_b = [shift(near_b[0][:2], "y", 1), shift(near_b[1][2:], "y", 3)]
+    pass_a = [near_a[0][:2], near_a[1][2:]]
+    pass_b = [near_b[0][:2], near_b[1][2:]]
+    (
+        near_a, near_b, pass_a, pass_b, own, cells, by_line, filled, spots, own_cell, gain, seg_col, a_at, b_at
+    ) = lax.optimization_barrier(
+        (near_a, near_b, pass_a, pass_b, own, cells, by_line, filled, spots, own_cell, gain, seg_col, a_at, b_at)
+    )
+    far_a = [shift(pass_a[0], "z", 1), shift(pass_a[1], "z", 3)]
+    far_b = [shift(pass_b[0], "y", 1), shift(pass_b[1], "y", 3)]
     shards_a = [stack_a] + near_a + far_a
     shards_b = [stack_b] + near_b + far_b
     other = swap(own)
@@ -644,9 +677,11 @@
     )
     row_slab = place(by_line, arrived.reshape(senders * 8, slab // 2), text_rows, filled)
 
+    row_slab, qkv_weight, attn_grad = lax.optimization_barrier((row_slab, qkv_weight, attn_grad))
     other_slab = swap(row_slab)
+    early, upstream = fetch(qkv_weight, attn_grad)
     give, keep, inv_rms, row_part = attend(
-        t, row_slab, other_slab, gain, qkv_weight, attn_grad, seg_row, seg_col
+        t, row_slab, other_slab, gain, early, qkv_weight, upstream, seg_row, seg_col
     )
     taken = swap(give)
 

time: 150 us -> 150 us (level)
  waiting for transfers between devices: 62.4 us -> 59.3 us
  Pallas kernels: 25.5 us -> 28 us
  local copies, waits for them, and re-layouts: 5.64 us -> 7.72 us
    slice x5, local copies, waits for them, and re-layouts: 1.32 us -> 4.51 us  [the longest x2 3.5 us: local(): pass_a = [near_a[0][:2], near_a[1][2:]]]
    ppermute x3, waiting for transfers between devices: 4.79 us -> 2.26 us  [swap(): return lax.ppermute(x, 'tp', [(0, 1), (1, 0)])]
    pallas_call x0 -> x1, Pallas kernels: none -> 2.42 us  [fetch(): pl.pallas_call(fetch_kernel, out_shape=(pltpu.VMEM((weight.shape[0], EARL...]
  transfers between devices with their start and end apart: 20 -> 20, of which waited for: 7 -> 7; matrix products, arithmetic and copies ran while one was open for 5% -> 7% of each run, Pallas kernels for 0% -> 2%
where the time goes in v9:
time: 150 us
  waiting for transfers between devices  59.3 us (40%)
  starting transfers between devices  37.8 us (25%)
  Pallas kernels  28 us (19%)
  between operations  14.4 us (10%)
  local copies, waits for them, and re-layouts  7.72 us (5%)
  other arithmetic  2.33 us (2%)
    ppermute x14, starting transfers between devices, shift(): return lax.ppermute(x, axis, [(i, (i + k) % 4) for i in range(4)])  24.2 us
    ppermute x14, waiting for transfers between devices, shift(): return lax.ppermute(x, axis, [(i, (i + k) % 4) for i in range(4)])  23.5 us
    all_to_all x1, waiting for transfers between devices, local(): lax.all_to_all(out8.reshape(senders, 2 * cap, half), SPREAD, split_axis=0...  17.7 us
    all_to_all x1, waiting for transfers between devices, local(): lax.all_to_all(outgoing.reshape(senders, 8, slab // 2), SPREAD, split_axi...  15.8 us
    pallas_call x1, Pallas kernels, attend(): pl.pallas_call(attend_kernel, out_shape=(jax.ShapeDtypeStruct((rows, slab...  11.2 us
    all_to_all x1, starting transfers between devices, local(): lax.all_to_all(outgoing.reshape(senders, 8, slab // 2), SPREAD, split_axi...  7.99 us
    pallas_call x1, Pallas kernels, encode(): pl.pallas_call(encode_kernel, out_shape=jax.ShapeDtypeStruct((n_cells, 89...  7.24 us
    all_to_all x1, starting transfers between devices, local(): lax.all_to_all(out8.reshape(senders, 2 * cap, half), SPREAD, split_axis=0...  4.83 us
  transfers between devices with their start and end apart: 20, of which 7 were waited for; matrix products, arithmetic and copies ran while one was open for 7% of the time, Pallas kernels for 2%

profile of v9, /device:TPU:0, one launch (start us, length us, event | category | flops | bytes accessed | tf_op | source)
XLA Modules:
  0.0 149.6 jit_solution(10350483888700052542)
XLA Ops:
  7.2 0.1 pad_add_fusion.1.place_ref
  7.3 2.7 %shard_map.122 = (bf16[224,384]{1,0:T(8,128)(2,1)S(1)}, bf16[256,384]{1,0:T(8,128)(2,1)S(1)}, bf16[192,1280]{1,0:T(8,128)(2,1)}) custom-call(s32[2]{0:T(128)S(1)} %pad_add_fusion.1.place_ref, bf16[80,1792]{1,0:T(8,128)(2,1)} %audio_w_ref.1, bf16[80,4,1792]{2,1,0:T(4,128)(2,1)} %vision_w_ref.1, bf16[128,1280]{1,0:T(8,128)(2,1)} %audio_ref.1, ...), custom_call_target="tpu_custom_call" | custom-call | bytes 1800000 | tf_op jit(solution)/shard_map/pallas_call | solution.py:291
  10.0 2.1 %collective-permute-start.3 = (bf16[256,384]{1,0:T(8,128)(2,1)S(1)}, bf16[256,384]{1,0:T(8,128)(2,1)S(1)}, u32[]{:S(2)}, u32[]{:S(2)}) collective-permute-start(bf16[256,384]{1,0:T(8,128)(2,1)S(1)} %get-tuple-element.49), channel_id=1, source_target_pairs={{0,8},{8,16},{16,24},{24,0},{1,9},{9,17},{17,25},{25,1},{2,10},{10... | collective-permute-start | bytes 589832 | tf_op jit(solution)/shard_map/ppermute | solution.py:567
  12.1 2.2 %collective-permute-start.4 = (bf16[256,384]{1,0:T(8,128)(2,1)S(1)}, bf16[256,384]{1,0:T(8,128)(2,1)S(1)}, u32[]{:S(2)}, u32[]{:S(2)}) collective-permute-start(bf16[256,384]{1,0:T(8,128)(2,1)S(1)} %get-tuple-element.49), channel_id=1, source_target_pairs={{0,24},{8,0},{16,8},{24,16},{1,25},{9,1},{17,9},{25,17},{2,26},{10... | collective-permute-start | bytes 589832 | tf_op jit(solution)/shard_map/ppermute | solution.py:567
  14.3 1.8 %collective-permute-start.5 = (bf16[256,384]{1,0:T(8,128)(2,1)S(1)}, bf16[256,384]{1,0:T(8,128)(2,1)S(1)}, u32[]{:S(2)}, u32[]{:S(2)}) collective-permute-start(bf16[256,384]{1,0:T(8,128)(2,1)S(1)} %get-tuple-element.49), channel_id=1, source_target_pairs={{0,16},{8,24},{16,0},{24,8},{1,17},{9,25},{17,1},{25,9},{2,18},{10... | collective-permute-start | bytes 589832 | tf_op jit(solution)/shard_map/ppermute | solution.py:567
  16.1 1.6 %collective-permute-start = (bf16[224,384]{1,0:T(8,128)(2,1)S(1)}, bf16[224,384]{1,0:T(8,128)(2,1)S(1)}, u32[]{:S(2)}, u32[]{:S(2)}) collective-permute-start(bf16[224,384]{1,0:T(8,128)(2,1)S(1)} %get-tuple-element.45), channel_id=1, source_target_pairs={{0,2},{2,4},{4,6},{6,0},{1,3},{3,5},{5,7},{7,1},{8,10},{10,12},{12... | collective-permute-start | bytes 516104 | tf_op jit(solution)/shard_map/ppermute | solution.py:567
  17.7 1.7 %collective-permute-start.1 = (bf16[224,384]{1,0:T(8,128)(2,1)S(1)}, bf16[224,384]{1,0:T(8,128)(2,1)S(1)}, u32[]{:S(2)}, u32[]{:S(2)}) collective-permute-start(bf16[224,384]{1,0:T(8,128)(2,1)S(1)} %get-tuple-element.45), channel_id=1, source_target_pairs={{0,6},{2,0},{4,2},{6,4},{1,7},{3,1},{5,3},{7,5},{8,14},{10,8},{12,... | collective-permute-start | bytes 516104 | tf_op jit(solution)/shard_map/ppermute | solution.py:567
  19.5 0.1 add.155.a_at_ref
  19.6 0.1 add.159.b_at_ref
  19.7 0.1 fusion.17
  19.7 3.0 %collective-permute-done = bf16[224,384]{1,0:T(8,128)(2,1)S(1)} collective-permute-done((bf16[224,384]{1,0:T(8,128)(2,1)S(1)}, bf16[224,384]{1,0:T(8,128)(2,1)S(1)}, u32[]{:S(2)}, u32[]{:S(2)}) %collective-permute-start) | collective-permute-done | bytes 172064 | tf_op jit(solution)/shard_map/ppermute | solution.py:567
  22.7 2.0 %collective-permute-start.2 = (bf16[224,384]{1,0:T(8,128)(2,1)S(1)}, bf16[224,384]{1,0:T(8,128)(2,1)S(1)}, u32[]{:S(2)}, u32[]{:S(2)}) collective-permute-start(bf16[224,384]{1,0:T(8,128)(2,1)S(1)} %get-tuple-element.45), channel_id=1, source_target_pairs={{0,4},{2,6},{4,0},{6,2},{1,5},{3,7},{5,1},{7,3},{8,12},{10,14},{12... | collective-permute-start | bytes 516104 | tf_op jit(solution)/shard_map/ppermute | solution.py:567
  24.7 4.9 %collective-permute-done.2 = bf16[224,384]{1,0:T(8,128)(2,1)S(1)} collective-permute-done((bf16[224,384]{1,0:T(8,128)(2,1)S(1)}, bf16[224,384]{1,0:T(8,128)(2,1)S(1)}, u32[]{:S(2)}, u32[]{:S(2)}) %collective-permute-start.2) | collective-permute-done | bytes 172064 | tf_op jit(solution)/shard_map/ppermute | solution.py:567
  29.6 0.1 pad_maximum_fusion.gb0
  29.8 0.1 pad_maximum_fusion.1.ga0
  29.9 0.4 convert_reduce_fusion
  30.4 0.4 collective-permute-start.8
  30.8 2.9 %collective-permute-start.9 = (bf16[4,256,384]{2,1,0:T(8,128)(2,1)S(1)}, bf16[4,256,384]{2,1,0:T(8,128)(2,1)S(1)}, u32[]{:S(2)}, u32[]{:S(2)}) collective-permute-start(bf16[4,256,384]{2,1,0:T(8,128)(2,1)S(1)} %pad_maximum_fusion.gb0), channel_id=1, source_target_pairs={{0,6},{2,0},{4,2},{6,4},{1,7},{3,1},{5,3},{7,5},{8,14},{10,8},{12,... | collective-permute-start | bytes 2359304 | tf_op jit(solution)/shard_map/ppermute | solution.py:567
  33.7 1.0 collective-permute-start.6
  34.7 2.2 %collective-permute-start.7 = (bf16[4,224,384]{2,1,0:T(8,128)(2,1)S(1)}, bf16[4,224,384]{2,1,0:T(8,128)(2,1)}, u32[]{:S(2)}, u32[]{:S(2)}) collective-permute-start(bf16[4,224,384]{2,1,0:T(8,128)(2,1)S(1)} %pad_maximum_fusion.1.ga0), channel_id=1, source_target_pairs={{0,24},{8,0},{16,8},{24,16},{1,25},{9,1},{17,9},{25,17},{2,26},{10... | collective-permute-start | bytes 2064392 | tf_op jit(solution)/shard_map/ppermute | solution.py:567
  37.0 0.6 reduce-window.6
  37.6 0.2 slice_reduce_fusion
  37.9 0.1 copy_bitcast_fusion
  38.0 0.2 select_reduce_fusion
  38.1 0.1 copy.64
  38.3 0.1 stack_reshape.6
  38.4 0.1 stack_reshape.7
  38.6 0.1 reshape.306
  38.7 0.6 gather_fusion
  39.2 0.1 reshape.307
  39.3 0.1 reshape.308
  39.4 0.6 gather_fusion.1
  40.0 0.1 reshape.309
  40.1 0.1 sub.66
  40.2 0.1 copy.56
  40.3 0.1 copy.55
  40.4 0.1 reshape.312.e_row_ref
  40.5 0.1 sub.67
  40.6 0.1 convert_reduce_fusion.1
  40.8 0.2 convert_reduce_fusion.2
  41.0 7.5 %collective-permute-done.6.ga1 = bf16[4,224,384]{2,1,0:T(8,128)(2,1)} collective-permute-done((bf16[4,224,384]{2,1,0:T(8,128)(2,1)S(1)}, bf16[4,224,384]{2,1,0:T(8,128)(2,1)}, u32[]{:S(2)}, u32[]{:S(2)}) %collective-permute-start.6) | collective-permute-done | bytes 688160 | tf_op jit(solution)/shard_map/ppermute | solution.py:567
  48.5 1.7 %slice.40 = bf16[2,224,384]{2,1,0:T(8,128)(2,1)} slice(bf16[4,224,384]{2,1,0:T(8,128)(2,1)} %collective-permute-done.6.ga1), slice={[0:2], [0:224], [0:384]} | slice | bytes 688128 | tf_op jit(solution)/shard_map/slice | solution.py:662
  50.3 1.8 %slice.41 = bf16[2,224,384]{2,1,0:T(8,128)(2,1)} slice(bf16[4,224,384]{2,1,0:T(8,128)(2,1)} %collective-permute-done.7.ga2), slice={[2:4], [0:224], [0:384]} | slice | bytes 688128 | tf_op jit(solution)/shard_map/slice | solution.py:662
  52.1 0.8 slice.43
  52.9 3.2 %collective-permute-start.13 = (bf16[2,256,384]{2,1,0:T(8,128)(2,1)}, bf16[2,256,384]{2,1,0:T(8,128)(2,1)S(1)}, u32[]{:S(2)}, u32[]{:S(2)}) collective-permute-start(bf16[2,256,384]{2,1,0:T(8,128)(2,1)} %slice.43), channel_id=1, source_target_pairs={{0,6},{2,0},{4,2},{6,4},{1,7},{3,1},{5,3},{7,5},{8,14},{10,8},{12,... | collective-permute-start | bytes 1179656 | tf_op jit(solution)/shard_map/ppermute | solution.py:567
  56.1 3.2 %collective-permute-start.11 = (bf16[2,224,384]{2,1,0:T(8,128)(2,1)}, bf16[2,224,384]{2,1,0:T(8,128)(2,1)S(1)}, u32[]{:S(2)}, u32[]{:S(2)}) collective-permute-start(bf16[2,224,384]{2,1,0:T(8,128)(2,1)} %slice.41), channel_id=1, source_target_pairs={{0,24},{8,0},{16,8},{24,16},{1,25},{9,1},{17,9},{25,17},{2,26},{10... | collective-permute-start | bytes 1032200 | tf_op jit(solution)/shard_map/ppermute | solution.py:567
  59.4 8.1 %collective-permute-done.10.ga3 = bf16[2,224,384]{2,1,0:T(8,128)(2,1)S(1)} collective-permute-done((bf16[2,224,384]{2,1,0:T(8,128)(2,1)}, bf16[2,224,384]{2,1,0:T(8,128)(2,1)S(1)}, u32[]{:S(2)}, u32[]{:S(2)}) %collective-permute-start.10) | collective-permute-done | bytes 344096 | tf_op jit(solution)/shard_map/ppermute | solution.py:567
  67.5 7.2 %shard_map.123 = bf16[512,896]{1,0:T(8,128)(2,1)} custom-call(s32[16]{0:T(128)S(1)} %add.155.a_at_ref, s32[16]{0:T(128)S(1)} %add.159.b_at_ref, bf16[4,224,384]{2,1,0:T(8,128)(2,1)S(1)} %pad_maximum_fusion.1.ga0, bf16[4,224,384]{2,1,0:T(8,128)(2,1)} %collective-permute-done.6.ga1, bf16[4,224,384]{2,1,0:T(8,128)(2,1)} %collective-permute-done.7.ga2, ...), custom_call_target="tpu_custom_call" | custom-call | flops 3000000000 | bytes 11000000 | tf_op jit(solution)/shard_map/pallas_call | solution.py:415
  74.8 8.0 %all-to-all-start = ((bf16[64,8,896]{2,1,0:T(8,128)(2,1)}), bf16[64,8,896]{2,1,0:T(8,128)(2,1)S(1)}, u32[]{:S(2)}, u32[]{:S(2)}) async-start(bf16[64,8,896]{2,1,0:T(8,128)(2,1)} %bitcast.28), calls=%async_computation | async-start | bytes 1835008 | tf_op jit(solution)/shard_map/all_to_all | solution.py:675
  82.8 0.1 copy.59.filled_ref
  82.9 15.8 %all-to-all-done = bf16[64,8,896]{2,1,0:T(8,128)(2,1)S(1)} async-done(((bf16[64,8,896]{2,1,0:T(8,128)(2,1)}), bf16[64,8,896]{2,1,0:T(8,128)(2,1)S(1)}, u32[]{:S(2)}, u32[]{:S(2)}) %all-to-all-start) | async-done | bytes 917536 | tf_op jit(solution)/shard_map/all_to_all | solution.py:675
  98.8 0.9 shard_map.124.own_ref.rows_ref
  99.6 0.1 collective-permute-start.15
  99.7 0.1 copy.60.seg_col_ref
  99.9 2.4 %shard_map.125 = (bf16[3584,640]{1,0:T(8,128)(2,1)S(1)}, bf16[256,896]{1,0:T(8,128)(2,1)S(1)}) custom-call(bf16[3584,1152]{1,0:T(8,128)(2,1)} %weight_hbm.1, bf16[256,896]{1,0:T(8,128)(2,1)} %upstream_hbm), custom_call_target="tpu_custom_call" | custom-call | bytes 10000000 | tf_op jit(solution)/shard_map/pallas_call | solution.py:43
  102.3 11.2 %shard_map.126 = (bf16[256,1920]{1,0:T(8,128)(2,1)}, bf16[256,1792]{1,0:T(8,128)(2,1)S(1)}, f32[256,1]{1,0:T(8,128)S(1)}, f32[256,1]{1,0:T(8,128)S(1)}) custom-call(s32[1]{0:T(128)} %bitcast.1.half_ref, bf16[256,1792]{1,0:T(8,128)(2,1)S(1)} %shard_map.124.own_ref.rows_ref, bf16[256,1792]{1,0:T(8,128)(2,1)S(1)} %collective-permute-done.15.other_ref, ...), custom_call_target="tpu_custom_call" | custom-call | flops 5000000000 | bytes 14000000 | tf_op jit(solution)/shard_map/pallas_call | solution.py:165
  113.5 0.6 collective-permute-start.16
  114.1 0.1 copy.61.spot_ref
  114.2 2.3 %collective-permute-done.16.taken_ref = bf16[256,1920]{1,0:T(8,128)(2,1)S(1)} collective-permute-done((bf16[256,1920]{1,0:T(8,128)(2,1)}, bf16[256,1920]{1,0:T(8,128)(2,1)S(1)}, u32[]{:S(2)}, u32[]{:S(2)}) %collective-permute-start.16) | collective-permute-done | bytes 983072 | tf_op jit(solution)/shard_map/ppermute | solution.py:563
  116.5 2.1 %shard_map.127 = bf16[512,896]{1,0:T(8,128)(2,1)} custom-call(s32[1]{0:T(128)} %bitcast.1.half_ref, bf16[256,1792]{1,0:T(8,128)(2,1)S(1)} %shard_map.124.own_ref.rows_ref, bf16[256,1792]{1,0:T(8,128)(2,1)S(1)} %get-tuple-element.79.keep_ref, bf16[256,1920]{1,0:T(8,128)(2,1)S(1)} %collective-permute-done.16.taken_ref, ...), custom_call_target="tpu_custom_call" | custom-call | flops 500000000 | bytes 4000000 | tf_op jit(solution)/shard_map/pallas_call | solution.py:520
  118.6 4.8 %all-to-all-start.1 = ((bf16[64,8,896]{2,1,0:T(8,128)(2,1)}), bf16[64,8,896]{2,1,0:T(8,128)(2,1)S(1)}, u32[]{:S(2)}, u32[]{:S(2)}) async-start(bf16[64,8,896]{2,1,0:T(8,128)(2,1)} %bitcast.30), calls=%async_computation.1 | async-start | bytes 1835008 | tf_op jit(solution)/shard_map/all_to_all | solution.py:689
  123.4 0.1 copy.62.cell_ref
  123.6 17.7 %all-to-all-done.1 = bf16[64,8,896]{2,1,0:T(8,128)(2,1)S(1)} async-done(((bf16[64,8,896]{2,1,0:T(8,128)(2,1)}), bf16[64,8,896]{2,1,0:T(8,128)(2,1)S(1)}, u32[]{:S(2)}, u32[]{:S(2)}) %all-to-all-start.1) | async-done | bytes 917536 | tf_op jit(solution)/shard_map/all_to_all | solution.py:689
  141.3 1.5 shard_map.128
  (59 shorter events, 0.7 us)
Async XLA Ops:
  7.2 12.2 %copy-start.4 = (s32[4]{0:T(128)S(1)}, s32[4]{0:T(128)}, u32[]{:S(2)}) copy-start(s32[4]{0:T(128)} %constant.148) | copy-start | bytes 52
  7.2 12.5 %copy-start.3 = (f32[3584]{0:T(1024)S(1)}, f32[3584]{0:T(1024)}, u32[]{:S(2)}) copy-start(f32[3584]{0:T(1024)} %param.18) | copy-start | bytes 43012
  7.2 45.7 %all-gather.3.cloned.1.call-start = ((), (), s32[]{:S(2)}) async-start(), calls=%async_computation.2 | async-start | bytes 2457600 | tf_op jit(solution)/shard_map/all_gather | solution.py:661
  10.0 19.9 %copy-start.2 = (s32[64,192]{1,0:T(8,128)S(1)}, s32[64,192]{1,0:T(8,128)}, u32[]{:S(2)}) copy-start(s32[64,192]{1,0:T(8,128)} %param.16) | copy-start | bytes 147460
  10.0 19.6 %collective-permute-start.3 = (bf16[256,384]{1,0:T(8,128)(2,1)S(1)}, bf16[256,384]{1,0:T(8,128)(2,1)S(1)}, u32[]{:S(2)}, u32[]{:S(2)}) collective-permute-start(bf16[256,384]{1,0:T(8,128)(2,1)S(1)} %get-tuple-element.49), channel_id=1, source_target_pairs={{0,8},{8,16},{16,24},{24,0},{1,9},{9,17},{17,25},{25,1},{2,10},{10... | collective-permute-start | bytes 589832 | tf_op jit(solution)/shard_map/ppermute | solution.py:567
  12.1 17.5 %collective-permute-start.4 = (bf16[256,384]{1,0:T(8,128)(2,1)S(1)}, bf16[256,384]{1,0:T(8,128)(2,1)S(1)}, u32[]{:S(2)}, u32[]{:S(2)}) collective-permute-start(bf16[256,384]{1,0:T(8,128)(2,1)S(1)} %get-tuple-element.49), channel_id=1, source_target_pairs={{0,24},{8,0},{16,8},{24,16},{1,25},{9,1},{17,9},{25,17},{2,26},{10... | collective-permute-start | bytes 589832 | tf_op jit(solution)/shard_map/ppermute | solution.py:567
  14.3 15.3 %collective-permute-start.5 = (bf16[256,384]{1,0:T(8,128)(2,1)S(1)}, bf16[256,384]{1,0:T(8,128)(2,1)S(1)}, u32[]{:S(2)}, u32[]{:S(2)}) collective-permute-start(bf16[256,384]{1,0:T(8,128)(2,1)S(1)} %get-tuple-element.49), channel_id=1, source_target_pairs={{0,16},{8,24},{16,0},{24,8},{1,17},{9,25},{17,1},{25,9},{2,18},{10... | collective-permute-start | bytes 589832 | tf_op jit(solution)/shard_map/ppermute | solution.py:567
  16.1 6.6 %collective-permute-start = (bf16[224,384]{1,0:T(8,128)(2,1)S(1)}, bf16[224,384]{1,0:T(8,128)(2,1)S(1)}, u32[]{:S(2)}, u32[]{:S(2)}) collective-permute-start(bf16[224,384]{1,0:T(8,128)(2,1)S(1)} %get-tuple-element.45), channel_id=1, source_target_pairs={{0,2},{2,4},{4,6},{6,0},{1,3},{3,5},{5,7},{7,1},{8,10},{10,12},{12... | collective-permute-start | bytes 516104 | tf_op jit(solution)/shard_map/ppermute | solution.py:567
  17.7 7.1 %collective-permute-start.1 = (bf16[224,384]{1,0:T(8,128)(2,1)S(1)}, bf16[224,384]{1,0:T(8,128)(2,1)S(1)}, u32[]{:S(2)}, u32[]{:S(2)}) collective-permute-start(bf16[224,384]{1,0:T(8,128)(2,1)S(1)} %get-tuple-element.45), channel_id=1, source_target_pairs={{0,6},{2,0},{4,2},{6,4},{1,7},{3,1},{5,3},{7,5},{8,14},{10,8},{12,... | collective-permute-start | bytes 516104 | tf_op jit(solution)/shard_map/ppermute | solution.py:567
  22.7 6.9 %collective-permute-start.2 = (bf16[224,384]{1,0:T(8,128)(2,1)S(1)}, bf16[224,384]{1,0:T(8,128)(2,1)S(1)}, u32[]{:S(2)}, u32[]{:S(2)}) collective-permute-start(bf16[224,384]{1,0:T(8,128)(2,1)S(1)} %get-tuple-element.45), channel_id=1, source_target_pairs={{0,4},{2,6},{4,0},{6,2},{1,5},{3,7},{5,1},{7,3},{8,12},{10,14},{12... | collective-permute-start | bytes 516104 | tf_op jit(solution)/shard_map/ppermute | solution.py:567
  30.4 21.6 %collective-permute-start.8 = (bf16[4,256,384]{2,1,0:T(8,128)(2,1)S(1)}, bf16[4,256,384]{2,1,0:T(8,128)(2,1)S(1)}, u32[]{:S(2)}, u32[]{:S(2)}) collective-permute-start(bf16[4,256,384]{2,1,0:T(8,128)(2,1)S(1)} %pad_maximum_fusion.gb0), channel_id=1, source_target_pairs={{0,2},{2,4},{4,6},{6,0},{1,3},{3,5},{5,7},{7,1},{8,10},{10,12},{12... | collective-permute-start | bytes 2359304 | tf_op jit(solution)/shard_map/ppermute | solution.py:567
  30.8 21.3 %collective-permute-start.9 = (bf16[4,256,384]{2,1,0:T(8,128)(2,1)S(1)}, bf16[4,256,384]{2,1,0:T(8,128)(2,1)S(1)}, u32[]{:S(2)}, u32[]{:S(2)}) collective-permute-start(bf16[4,256,384]{2,1,0:T(8,128)(2,1)S(1)} %pad_maximum_fusion.gb0), channel_id=1, source_target_pairs={{0,6},{2,0},{4,2},{6,4},{1,7},{3,1},{5,3},{7,5},{8,14},{10,8},{12,... | collective-permute-start | bytes 2359304 | tf_op jit(solution)/shard_map/ppermute | solution.py:567
  33.7 14.9 %collective-permute-start.6 = (bf16[4,224,384]{2,1,0:T(8,128)(2,1)S(1)}, bf16[4,224,384]{2,1,0:T(8,128)(2,1)}, u32[]{:S(2)}, u32[]{:S(2)}) collective-permute-start(bf16[4,224,384]{2,1,0:T(8,128)(2,1)S(1)} %pad_maximum_fusion.1.ga0), channel_id=1, source_target_pairs={{0,8},{8,16},{16,24},{24,0},{1,9},{9,17},{17,25},{25,1},{2,10},{10... | collective-permute-start | bytes 2064392 | tf_op jit(solution)/shard_map/ppermute | solution.py:567
  34.7 15.6 %collective-permute-start.7 = (bf16[4,224,384]{2,1,0:T(8,128)(2,1)S(1)}, bf16[4,224,384]{2,1,0:T(8,128)(2,1)}, u32[]{:S(2)}, u32[]{:S(2)}) collective-permute-start(bf16[4,224,384]{2,1,0:T(8,128)(2,1)S(1)} %pad_maximum_fusion.1.ga0), channel_id=1, source_target_pairs={{0,24},{8,0},{16,8},{24,16},{1,25},{9,1},{17,9},{25,17},{2,26},{10... | collective-permute-start | bytes 2064392 | tf_op jit(solution)/shard_map/ppermute | solution.py:567
  52.9 14.6 %collective-permute-start.14 = (bf16[4,192,1280]{2,1,0:T(8,128)(2,1)}, bf16[4,192,1280]{2,1,0:T(8,128)(2,1)S(1)}, u32[]{:S(2)}, u32[]{:S(2)}) collective-permute-start(bf16[4,192,1280]{2,1,0:T(8,128)(2,1)} %bitcast.89), channel_id=1, source_target_pairs={{0,1},{1,0},{2,3},{3,2},{4,5},{5,4},{6,7},{7,6},{8,9},{9,8},{10,11... | collective-permute-start | bytes 5898248 | tf_op jit(solution)/shard_map/ppermute | solution.py:563
  52.9 14.6 %collective-permute-start.12 = (bf16[2,256,384]{2,1,0:T(8,128)(2,1)S(1)}, bf16[2,256,384]{2,1,0:T(8,128)(2,1)S(1)}, u32[]{:S(2)}, u32[]{:S(2)}) collective-permute-start(bf16[2,256,384]{2,1,0:T(8,128)(2,1)S(1)} %slice.42), channel_id=1, source_target_pairs={{0,2},{2,4},{4,6},{6,0},{1,3},{3,5},{5,7},{7,1},{8,10},{10,12},{12... | collective-permute-start | bytes 1179656 | tf_op jit(solution)/shard_map/ppermute | solution.py:567
  52.9 14.6 %collective-permute-start.13 = (bf16[2,256,384]{2,1,0:T(8,128)(2,1)}, bf16[2,256,384]{2,1,0:T(8,128)(2,1)S(1)}, u32[]{:S(2)}, u32[]{:S(2)}) collective-permute-start(bf16[2,256,384]{2,1,0:T(8,128)(2,1)} %slice.43), channel_id=1, source_target_pairs={{0,6},{2,0},{4,2},{6,4},{1,7},{3,1},{5,3},{7,5},{8,14},{10,8},{12,... | collective-permute-start | bytes 1179656 | tf_op jit(solution)/shard_map/ppermute | solution.py:567
  56.1 11.3 %collective-permute-start.10 = (bf16[2,224,384]{2,1,0:T(8,128)(2,1)}, bf16[2,224,384]{2,1,0:T(8,128)(2,1)S(1)}, u32[]{:S(2)}, u32[]{:S(2)}) collective-permute-start(bf16[2,224,384]{2,1,0:T(8,128)(2,1)} %slice.40), channel_id=1, source_target_pairs={{0,8},{8,16},{16,24},{24,0},{1,9},{9,17},{17,25},{25,1},{2,10},{10... | collective-permute-start | bytes 1032200 | tf_op jit(solution)/shard_map/ppermute | solution.py:567
  56.1 11.3 %collective-permute-start.11 = (bf16[2,224,384]{2,1,0:T(8,128)(2,1)}, bf16[2,224,384]{2,1,0:T(8,128)(2,1)S(1)}, u32[]{:S(2)}, u32[]{:S(2)}) collective-permute-start(bf16[2,224,384]{2,1,0:T(8,128)(2,1)} %slice.41), channel_id=1, source_target_pairs={{0,24},{8,0},{16,8},{24,16},{1,25},{9,1},{17,9},{25,17},{2,26},{10... | collective-permute-start | bytes 1032200 | tf_op jit(solution)/shard_map/ppermute | solution.py:567
  74.7 24.0 %copy-start = (bf16[256,1792]{1,0:T(8,128)(2,1)S(1)}, bf16[256,1792]{1,0:T(8,128)(2,1)}, u32[]{:S(2)}) copy-start(bf16[256,1792]{1,0:T(8,128)(2,1)} %text_hbm.1) | copy-start | bytes 2752516
  74.8 24.0 %all-to-all-start = ((bf16[64,8,896]{2,1,0:T(8,128)(2,1)}), bf16[64,8,896]{2,1,0:T(8,128)(2,1)S(1)}, u32[]{:S(2)}, u32[]{:S(2)}) async-start(bf16[64,8,896]{2,1,0:T(8,128)(2,1)} %bitcast.28), calls=%async_computation | async-start | bytes 1835008 | tf_op jit(solution)/shard_map/all_to_all | solution.py:675
  82.8 17.0 %copy-start.1 = (s32[1,256]{1,0:T(1,128)S(1)}, s32[1,256]{1,0:T(1,128)}, u32[]{:S(2)}) copy-start(s32[1,256]{1,0:T(1,128)} %seg_row_ref.1) | copy-start | bytes 3076
  99.6 2.7 %collective-permute-start.15 = (bf16[256,1792]{1,0:T(8,128)(2,1)S(1)}, bf16[256,1792]{1,0:T(8,128)(2,1)S(1)}, u32[]{:S(2)}, u32[]{:S(2)}) collective-permute-start(bf16[256,1792]{1,0:T(8,128)(2,1)S(1)} %shard_map.124.own_ref.rows_ref), channel_id=1, source_target_pairs={{0,1},{1,0},{2,3},{3,2},{4,5},{5,4},{6,7},{7,6},{8,9},{9,8},{10,11... | collective-permute-start | bytes 2752520 | tf_op jit(solution)/shard_map/ppermute | solution.py:563
  113.5 3.0 %collective-permute-start.16 = (bf16[256,1920]{1,0:T(8,128)(2,1)}, bf16[256,1920]{1,0:T(8,128)(2,1)S(1)}, u32[]{:S(2)}, u32[]{:S(2)}) collective-permute-start(bf16[256,1920]{1,0:T(8,128)(2,1)} %get-tuple-element.80), channel_id=1, source_target_pairs={{0,1},{1,0},{2,3},{3,2},{4,5},{5,4},{6,7},{7,6},{8,9},{9,8},{10,11... | collective-permute-start | bytes 2949128 | tf_op jit(solution)/shard_map/ppermute | solution.py:563
  118.6 22.7 %all-to-all-start.1 = ((bf16[64,8,896]{2,1,0:T(8,128)(2,1)}), bf16[64,8,896]{2,1,0:T(8,128)(2,1)S(1)}, u32[]{:S(2)}, u32[]{:S(2)}) async-start(bf16[64,8,896]{2,1,0:T(8,128)(2,1)} %bitcast.30), calls=%async_computation.1 | async-start | bytes 1835008 | tf_op jit(solution)/shard_map/all_to_all | solution.py:689
Sparse Core Ops, SparseCore 0:
  19.5 28.5 all-gather.2

commit v10 on v9

--- a/solution.py
+++ b/solution.py
@@ -433,6 +433,27 @@
     )(a_at, b_at, *shards_a, *shards_b, in_hbm(own), other, cells)
 
 
+def cut_kernel(a0, a1, b0, b1, low_a, high_a, low_b, high_b):
+    low_a[...] = a0[:2]
+    high_a[...] = a1[2:]
+    low_b[...] = b0[:2]
+    high_b[...] = b1[2:]
+
+
+def cut(near_a, near_b):
+    vmem = pl.BlockSpec(memory_space=pltpu.VMEM)
+    shapes = [(2,) + x.shape[1:] for x in near_a + near_b]
+    halves = pl.pallas_call(
+        cut_kernel,
+        out_shape=[jax.ShapeDtypeStruct(shape, jnp.bfloat16) for shape in shapes],
+        in_specs=[vmem] * 4,
+        out_specs=[vmem] * 4,
+        compiler_params=pltpu.CompilerParams(vmem_limit_bytes=8 * 1024 * 1024),
+        cost_estimate=pl.CostEstimate(flops=0, bytes_accessed=3_000_000, transcendentals=0),
+    )(*near_a, *near_b)
+    return halves[:2], halves[2:]
+
+
 def place_kernel(e_row_ref, arrived_ref, text_hbm, filled_ref, out_ref, text_ref, sem):
     bf16, f32 = jnp.bfloat16, jnp.float32
     load = pltpu.make_async_copy(text_hbm, text_ref, sem)
@@ -609,8 +630,9 @@
         vision_rows,
     )
     hops = (1, 3, 2)
-    along_y = [piece_a] + [shift(piece_a, "y", k) for k in hops]
-    along_z = [piece_b] + [shift(piece_b, "z", k) for k in hops]
+    across_y, across_z = shift(piece_a, "y", 2), shift(piece_b, "z", 2)
+    along_y = [piece_a, shift(piece_a, "y", 1), shift(piece_a, "y", 3), across_y]
+    along_z = [piece_b, shift(piece_b, "z", 1), shift(piece_b, "z", 3), across_z]
     along_y, along_z = lax.optimization_barrier((along_y, along_z))
     stack_a, stack_b, row_target = lax.optimization_barrier(
         (jnp.stack(along_y), jnp.stack(along_z), row_target)
@@ -659,8 +681,7 @@
     seg_row = segment_ids
     seg_col = segment_ids.reshape(length, 1)
     own = lax.all_gather(packed, "enc", axis=0, tiled=False)
-    pass_a = [near_a[0][:2], near_a[1][2:]]
-    pass_b = [near_b[0][:2], near_b[1][2:]]
+    pass_a, pass_b = cut(near_a, near_b)
     (
         near_a, near_b, pass_a, pass_b, own, cells, by_line, filled, spots, own_cell, gain, seg_col, a_at, b_at
     ) = lax.optimization_barrier(

time: 150 us -> 151 us (level)
  local copies, waits for them, and re-layouts: 7.72 us -> 5.62 us
    slice x5 -> x1, local copies, waits for them, and re-layouts: 4.51 us -> 0.18 us  [the longest x2 3.5 us: local(): pass_a = [near_a[0][:2], near_a[1][2:]]]
    unnamed x12 -> x18, local copies, waits for them, and re-layouts: 0.13 us -> 2.35 us
  transfers between devices with their start and end apart: 20 -> 20, of which waited for: 7 -> 7; matrix products, arithmetic and copies ran while one was open for 7% -> 4% of each run, Pallas kernels for 2% -> 3%
where the time goes in v10:
time: 151 us; the launch traced here: 150 us
  waiting for transfers between devices  59.9 us (40%)
  starting transfers between devices  38.3 us (25%)
  Pallas kernels  29.5 us (20%)
  between operations  14.4 us (10%)
  local copies, waits for them, and re-layouts  5.62 us (4%)
  other arithmetic  2.33 us (2%)
    ppermute x14, starting transfers between devices, shift(): return lax.ppermute(x, axis, [(i, (i + k) % 4) for i in range(4)])  24.2 us
    ppermute x14, waiting for transfers between devices, shift(): return lax.ppermute(x, axis, [(i, (i + k) % 4) for i in range(4)])  23.5 us
    all_to_all x1, waiting for transfers between devices, local(): lax.all_to_all(out8.reshape(senders, 2 * cap, half), SPREAD, split_axis=0...  17.7 us
    all_to_all x1, waiting for transfers between devices, local(): lax.all_to_all(outgoing.reshape(senders, 8, slab // 2), SPREAD, split_axi...  16.4 us
    pallas_call x1, Pallas kernels, attend(): pl.pallas_call(attend_kernel, out_shape=(jax.ShapeDtypeStruct((rows, slab...  11.2 us
    all_to_all x1, starting transfers between devices, local(): lax.all_to_all(outgoing.reshape(senders, 8, slab // 2), SPREAD, split_axi...  8.53 us
    pallas_call x1, Pallas kernels, encode(): pl.pallas_call(encode_kernel, out_shape=jax.ShapeDtypeStruct((n_cells, 89...  7.23 us
    all_to_all x1, starting transfers between devices, local(): lax.all_to_all(out8.reshape(senders, 2 * cap, half), SPREAD, split_axis=0...  4.83 us
  transfers between devices with their start and end apart: 20, of which 7 were waited for; matrix products, arithmetic and copies ran while one was open for 4% of the time, Pallas kernels for 3%

profile of v10, /device:TPU:0, one launch (start us, length us, event | category | flops | bytes accessed | tf_op | source)
XLA Modules:
  0.0 150.1 jit_solution(10041464392595946450)
XLA Ops:
  7.3 2.7 %shard_map.122 = (bf16[224,384]{1,0:T(8,128)(2,1)S(1)}, bf16[256,384]{1,0:T(8,128)(2,1)S(1)}, bf16[192,1280]{1,0:T(8,128)(2,1)}) custom-call(s32[2]{0:T(128)S(1)} %pad_add_fusion.1.place_ref, bf16[80,1792]{1,0:T(8,128)(2,1)} %audio_w_ref.1, bf16[80,4,1792]{2,1,0:T(4,128)(2,1)} %vision_w_ref.1, bf16[128,1280]{1,0:T(8,128)(2,1)} %audio_ref.1, ...), custom_call_target="tpu_custom_call" | custom-call | bytes 1800000 | tf_op jit(solution)/shard_map/pallas_call | solution.py:291
  10.0 2.1 %collective-permute-start.3 = (bf16[256,384]{1,0:T(8,128)(2,1)S(1)}, bf16[256,384]{1,0:T(8,128)(2,1)S(1)}, u32[]{:S(2)}, u32[]{:S(2)}) collective-permute-start(bf16[256,384]{1,0:T(8,128)(2,1)S(1)} %get-tuple-element.53), channel_id=1, source_target_pairs={{0,8},{8,16},{16,24},{24,0},{1,9},{9,17},{17,25},{25,1},{2,10},{10... | collective-permute-start | bytes 589832 | tf_op jit(solution)/shard_map/ppermute | solution.py:588
  12.1 2.2 %collective-permute-start.4 = (bf16[256,384]{1,0:T(8,128)(2,1)S(1)}, bf16[256,384]{1,0:T(8,128)(2,1)S(1)}, u32[]{:S(2)}, u32[]{:S(2)}) collective-permute-start(bf16[256,384]{1,0:T(8,128)(2,1)S(1)} %get-tuple-element.53), channel_id=1, source_target_pairs={{0,24},{8,0},{16,8},{24,16},{1,25},{9,1},{17,9},{25,17},{2,26},{10... | collective-permute-start | bytes 589832 | tf_op jit(solution)/shard_map/ppermute | solution.py:588
  14.3 1.8 %collective-permute-start.5 = (bf16[256,384]{1,0:T(8,128)(2,1)S(1)}, bf16[256,384]{1,0:T(8,128)(2,1)S(1)}, u32[]{:S(2)}, u32[]{:S(2)}) collective-permute-start(bf16[256,384]{1,0:T(8,128)(2,1)S(1)} %get-tuple-element.53), channel_id=1, source_target_pairs={{0,16},{8,24},{16,0},{24,8},{1,17},{9,25},{17,1},{25,9},{2,18},{10... | collective-permute-start | bytes 589832 | tf_op jit(solution)/shard_map/ppermute | solution.py:588
  16.1 1.6 %collective-permute-start = (bf16[224,384]{1,0:T(8,128)(2,1)S(1)}, bf16[224,384]{1,0:T(8,128)(2,1)S(1)}, u32[]{:S(2)}, u32[]{:S(2)}) collective-permute-start(bf16[224,384]{1,0:T(8,128)(2,1)S(1)} %get-tuple-element.49), channel_id=1, source_target_pairs={{0,2},{2,4},{4,6},{6,0},{1,3},{3,5},{5,7},{7,1},{8,10},{10,12},{12... | collective-permute-start | bytes 516104 | tf_op jit(solution)/shard_map/ppermute | solution.py:588
  17.7 1.7 %collective-permute-start.1 = (bf16[224,384]{1,0:T(8,128)(2,1)S(1)}, bf16[224,384]{1,0:T(8,128)(2,1)S(1)}, u32[]{:S(2)}, u32[]{:S(2)}) collective-permute-start(bf16[224,384]{1,0:T(8,128)(2,1)S(1)} %get-tuple-element.49), channel_id=1, source_target_pairs={{0,6},{2,0},{4,2},{6,4},{1,7},{3,1},{5,3},{7,5},{8,14},{10,8},{12,... | collective-permute-start | bytes 516104 | tf_op jit(solution)/shard_map/ppermute | solution.py:588
  19.5 0.1 add.155.a_at_ref
  19.6 0.1 add.159.b_at_ref
  19.7 0.1 fusion.17
  19.8 3.0 %collective-permute-done = bf16[224,384]{1,0:T(8,128)(2,1)S(1)} collective-permute-done((bf16[224,384]{1,0:T(8,128)(2,1)S(1)}, bf16[224,384]{1,0:T(8,128)(2,1)S(1)}, u32[]{:S(2)}, u32[]{:S(2)}) %collective-permute-start) | collective-permute-done | bytes 172064 | tf_op jit(solution)/shard_map/ppermute | solution.py:588
  22.7 2.0 %collective-permute-start.2 = (bf16[224,384]{1,0:T(8,128)(2,1)S(1)}, bf16[224,384]{1,0:T(8,128)(2,1)S(1)}, u32[]{:S(2)}, u32[]{:S(2)}) collective-permute-start(bf16[224,384]{1,0:T(8,128)(2,1)S(1)} %get-tuple-element.49), channel_id=1, source_target_pairs={{0,4},{2,6},{4,0},{6,2},{1,5},{3,7},{5,1},{7,3},{8,12},{10,14},{12... | collective-permute-start | bytes 516104 | tf_op jit(solution)/shard_map/ppermute | solution.py:588
  24.7 4.9 %collective-permute-done.2 = bf16[224,384]{1,0:T(8,128)(2,1)S(1)} collective-permute-done((bf16[224,384]{1,0:T(8,128)(2,1)S(1)}, bf16[224,384]{1,0:T(8,128)(2,1)S(1)}, u32[]{:S(2)}, u32[]{:S(2)}) %collective-permute-start.2) | collective-permute-done | bytes 172064 | tf_op jit(solution)/shard_map/ppermute | solution.py:588
  29.6 0.1 pad_maximum_fusion.gb0
  29.8 0.1 pad_maximum_fusion.1.ga0
  30.0 0.4 convert_reduce_fusion
  30.4 0.4 collective-permute-start.8
  30.8 2.9 %collective-permute-start.9 = (bf16[4,256,384]{2,1,0:T(8,128)(2,1)S(1)}, bf16[4,256,384]{2,1,0:T(8,128)(2,1)S(1)}, u32[]{:S(2)}, u32[]{:S(2)}) collective-permute-start(bf16[4,256,384]{2,1,0:T(8,128)(2,1)S(1)} %pad_maximum_fusion.gb0), channel_id=1, source_target_pairs={{0,6},{2,0},{4,2},{6,4},{1,7},{3,1},{5,3},{7,5},{8,14},{10,8},{12,... | collective-permute-start | bytes 2359304 | tf_op jit(solution)/shard_map/ppermute | solution.py:588
  33.7 1.0 collective-permute-start.6
  34.7 2.2 %collective-permute-start.7 = (bf16[4,224,384]{2,1,0:T(8,128)(2,1)S(1)}, bf16[4,224,384]{2,1,0:T(8,128)(2,1)}, u32[]{:S(2)}, u32[]{:S(2)}) collective-permute-start(bf16[4,224,384]{2,1,0:T(8,128)(2,1)S(1)} %pad_maximum_fusion.1.ga0), channel_id=1, source_target_pairs={{0,24},{8,0},{16,8},{24,16},{1,25},{9,1},{17,9},{25,17},{2,26},{10... | collective-permute-start | bytes 2064392 | tf_op jit(solution)/shard_map/ppermute | solution.py:588
  37.0 0.6 reduce-window.6
  37.6 0.2 slice_reduce_fusion
  38.0 0.2 select_reduce_fusion
  38.2 0.1 copy.64
  38.3 0.1 stack_reshape.6
  38.5 0.1 stack_reshape.7
  38.6 0.1 reshape.306
  38.7 0.6 gather_fusion
  39.3 0.1 reshape.307
  39.3 0.1 reshape.308
  39.4 0.6 gather_fusion.1
  40.0 0.1 reshape.309
  40.2 0.1 sub.66
  40.2 0.1 copy.56
  40.3 0.1 copy.55
  40.4 0.1 reshape.312.e_row_ref
  40.6 0.1 sub.67
  40.7 0.1 convert_reduce_fusion.1
  40.8 0.2 convert_reduce_fusion.2
  41.0 7.5 %collective-permute-done.6.a0.ga1 = bf16[4,224,384]{2,1,0:T(8,128)(2,1)} collective-permute-done((bf16[4,224,384]{2,1,0:T(8,128)(2,1)S(1)}, bf16[4,224,384]{2,1,0:T(8,128)(2,1)}, u32[]{:S(2)}, u32[]{:S(2)}) %collective-permute-start.6) | collective-permute-done | bytes 688160 | tf_op jit(solution)/shard_map/ppermute | solution.py:588
  48.6 1.4 shard_map.123
  50.0 0.7 copy-done.2
  50.8 0.7 copy-done.3
  51.5 0.7 copy-done.4
  52.3 3.2 %collective-permute-start.13 = (bf16[2,256,384]{2,1,0:T(8,128)(2,1)S(1)}, bf16[2,256,384]{2,1,0:T(8,128)(2,1)S(1)}, u32[]{:S(2)}, u32[]{:S(2)}) collective-permute-start(bf16[2,256,384]{2,1,0:T(8,128)(2,1)S(1)} %get-tuple-element.76), channel_id=1, source_target_pairs={{0,6},{2,0},{4,2},{6,4},{1,7},{3,1},{5,3},{7,5},{8,14},{10,8},{12,... | collective-permute-start | bytes 1179656 | tf_op jit(solution)/shard_map/ppermute | solution.py:588
  55.5 0.9 collective-permute-start.10
  56.4 2.3 %collective-permute-start.11 = (bf16[2,224,384]{2,1,0:T(8,128)(2,1)}, bf16[2,224,384]{2,1,0:T(8,128)(2,1)S(1)}, u32[]{:S(2)}, u32[]{:S(2)}) collective-permute-start(bf16[2,224,384]{2,1,0:T(8,128)(2,1)} %copy-done.3), channel_id=1, source_target_pairs={{0,24},{8,0},{16,8},{24,16},{1,25},{9,1},{17,9},{25,17},{2,26},{10... | collective-permute-start | bytes 1032200 | tf_op jit(solution)/shard_map/ppermute | solution.py:588
  58.7 8.1 %collective-permute-done.10.ga3 = bf16[2,224,384]{2,1,0:T(8,128)(2,1)S(1)} collective-permute-done((bf16[2,224,384]{2,1,0:T(8,128)(2,1)}, bf16[2,224,384]{2,1,0:T(8,128)(2,1)S(1)}, u32[]{:S(2)}, u32[]{:S(2)}) %collective-permute-start.10) | collective-permute-done | bytes 344096 | tf_op jit(solution)/shard_map/ppermute | solution.py:588
  66.8 7.2 %shard_map.124 = bf16[512,896]{1,0:T(8,128)(2,1)} custom-call(s32[16]{0:T(128)S(1)} %add.155.a_at_ref, s32[16]{0:T(128)S(1)} %add.159.b_at_ref, bf16[4,224,384]{2,1,0:T(8,128)(2,1)S(1)} %pad_maximum_fusion.1.ga0, bf16[4,224,384]{2,1,0:T(8,128)(2,1)} %collective-permute-done.6.a0.ga1, bf16[4,224,384]{2,1,0:T(8,128)(2,1)} %collective-permute-done.7.a1.ga2, ...), custom_call_target="tpu_custom_call" | custom-call | flops 3000000000 | bytes 11000000 | tf_op jit(solution)/shard_map/pallas_call | solution.py:415
  74.1 8.5 %all-to-all-start = ((bf16[64,8,896]{2,1,0:T(8,128)(2,1)}), bf16[64,8,896]{2,1,0:T(8,128)(2,1)S(1)}, u32[]{:S(2)}, u32[]{:S(2)}) async-start(bf16[64,8,896]{2,1,0:T(8,128)(2,1)} %bitcast.28), calls=%async_computation | async-start | bytes 1835008 | tf_op jit(solution)/shard_map/all_to_all | solution.py:696
  82.6 0.1 copy.59.filled_ref
  82.8 16.4 %all-to-all-done = bf16[64,8,896]{2,1,0:T(8,128)(2,1)S(1)} async-done(((bf16[64,8,896]{2,1,0:T(8,128)(2,1)}), bf16[64,8,896]{2,1,0:T(8,128)(2,1)S(1)}, u32[]{:S(2)}, u32[]{:S(2)}) %all-to-all-start) | async-done | bytes 917536 | tf_op jit(solution)/shard_map/all_to_all | solution.py:696
  99.2 0.9 shard_map.125.own_ref.rows_ref
  100.1 0.1 collective-permute-start.15
  100.2 0.1 copy.60.seg_col_ref
  100.3 2.4 %shard_map.126 = (bf16[3584,640]{1,0:T(8,128)(2,1)S(1)}, bf16[256,896]{1,0:T(8,128)(2,1)S(1)}) custom-call(bf16[3584,1152]{1,0:T(8,128)(2,1)} %weight_hbm.1, bf16[256,896]{1,0:T(8,128)(2,1)} %upstream_hbm), custom_call_target="tpu_custom_call" | custom-call | bytes 10000000 | tf_op jit(solution)/shard_map/pallas_call | solution.py:43
  102.8 11.2 %shard_map.127 = (bf16[256,1920]{1,0:T(8,128)(2,1)}, bf16[256,1792]{1,0:T(8,128)(2,1)S(1)}, f32[256,1]{1,0:T(8,128)S(1)}, f32[256,1]{1,0:T(8,128)S(1)}) custom-call(s32[1]{0:T(128)} %bitcast.1.half_ref, bf16[256,1792]{1,0:T(8,128)(2,1)S(1)} %shard_map.125.own_ref.rows_ref, bf16[256,1792]{1,0:T(8,128)(2,1)S(1)} %collective-permute-done.15.other_ref, ...), custom_call_target="tpu_custom_call" | custom-call | flops 5000000000 | bytes 14000000 | tf_op jit(solution)/shard_map/pallas_call | solution.py:165
  114.0 0.6 collective-permute-start.16
  114.6 0.1 copy.61.spot_ref
  114.7 2.3 %collective-permute-done.16.taken_ref = bf16[256,1920]{1,0:T(8,128)(2,1)S(1)} collective-permute-done((bf16[256,1920]{1,0:T(8,128)(2,1)}, bf16[256,1920]{1,0:T(8,128)(2,1)S(1)}, u32[]{:S(2)}, u32[]{:S(2)}) %collective-permute-start.16) | collective-permute-done | bytes 983072 | tf_op jit(solution)/shard_map/ppermute | solution.py:584
  117.0 2.1 %shard_map.128 = bf16[512,896]{1,0:T(8,128)(2,1)} custom-call(s32[1]{0:T(128)} %bitcast.1.half_ref, bf16[256,1792]{1,0:T(8,128)(2,1)S(1)} %shard_map.125.own_ref.rows_ref, bf16[256,1792]{1,0:T(8,128)(2,1)S(1)} %get-tuple-element.87.keep_ref, bf16[256,1920]{1,0:T(8,128)(2,1)S(1)} %collective-permute-done.16.taken_ref, ...), custom_call_target="tpu_custom_call" | custom-call | flops 500000000 | bytes 4000000 | tf_op jit(solution)/shard_map/pallas_call | solution.py:541
  119.1 4.8 %all-to-all-start.1 = ((bf16[64,8,896]{2,1,0:T(8,128)(2,1)}), bf16[64,8,896]{2,1,0:T(8,128)(2,1)S(1)}, u32[]{:S(2)}, u32[]{:S(2)}) async-start(bf16[64,8,896]{2,1,0:T(8,128)(2,1)} %bitcast.30), calls=%async_computation.1 | async-start | bytes 1835008 | tf_op jit(solution)/shard_map/all_to_all | solution.py:710
  124.0 0.1 copy.62.cell_ref
  124.1 17.7 %all-to-all-done.1 = bf16[64,8,896]{2,1,0:T(8,128)(2,1)S(1)} async-done(((bf16[64,8,896]{2,1,0:T(8,128)(2,1)}), bf16[64,8,896]{2,1,0:T(8,128)(2,1)S(1)}, u32[]{:S(2)}, u32[]{:S(2)}) %all-to-all-start.1) | async-done | bytes 917536 | tf_op jit(solution)/shard_map/all_to_all | solution.py:710
  141.8 1.5 shard_map.129
  (62 shorter events, 0.8 us)
Async XLA Ops:
  7.2 12.2 %copy-start.7 = (s32[4]{0:T(128)S(1)}, s32[4]{0:T(128)}, u32[]{:S(2)}) copy-start(s32[4]{0:T(128)} %constant.148) | copy-start | bytes 52
  7.2 12.5 %copy-start.6 = (f32[3584]{0:T(1024)S(1)}, f32[3584]{0:T(1024)}, u32[]{:S(2)}) copy-start(f32[3584]{0:T(1024)} %param.18) | copy-start | bytes 43012
  7.2 45.1 %all-gather.3.cloned.1.call-start = ((), (), s32[]{:S(2)}) async-start(), calls=%async_computation.2 | async-start | bytes 2457600 | tf_op jit(solution)/shard_map/all_gather | solution.py:683
  10.0 19.9 %copy-start.5 = (s32[64,192]{1,0:T(8,128)S(1)}, s32[64,192]{1,0:T(8,128)}, u32[]{:S(2)}) copy-start(s32[64,192]{1,0:T(8,128)} %param.16) | copy-start | bytes 147460
  10.0 19.6 %collective-permute-start.3 = (bf16[256,384]{1,0:T(8,128)(2,1)S(1)}, bf16[256,384]{1,0:T(8,128)(2,1)S(1)}, u32[]{:S(2)}, u32[]{:S(2)}) collective-permute-start(bf16[256,384]{1,0:T(8,128)(2,1)S(1)} %get-tuple-element.53), channel_id=1, source_target_pairs={{0,8},{8,16},{16,24},{24,0},{1,9},{9,17},{17,25},{25,1},{2,10},{10... | collective-permute-start | bytes 589832 | tf_op jit(solution)/shard_map/ppermute | solution.py:588
  12.1 17.5 %collective-permute-start.4 = (bf16[256,384]{1,0:T(8,128)(2,1)S(1)}, bf16[256,384]{1,0:T(8,128)(2,1)S(1)}, u32[]{:S(2)}, u32[]{:S(2)}) collective-permute-start(bf16[256,384]{1,0:T(8,128)(2,1)S(1)} %get-tuple-element.53), channel_id=1, source_target_pairs={{0,24},{8,0},{16,8},{24,16},{1,25},{9,1},{17,9},{25,17},{2,26},{10... | collective-permute-start | bytes 589832 | tf_op jit(solution)/shard_map/ppermute | solution.py:588
  14.3 15.3 %collective-permute-start.5 = (bf16[256,384]{1,0:T(8,128)(2,1)S(1)}, bf16[256,384]{1,0:T(8,128)(2,1)S(1)}, u32[]{:S(2)}, u32[]{:S(2)}) collective-permute-start(bf16[256,384]{1,0:T(8,128)(2,1)S(1)} %get-tuple-element.53), channel_id=1, source_target_pairs={{0,16},{8,24},{16,0},{24,8},{1,17},{9,25},{17,1},{25,9},{2,18},{10... | collective-permute-start | bytes 589832 | tf_op jit(solution)/shard_map/ppermute | solution.py:588
  16.1 6.6 %collective-permute-start = (bf16[224,384]{1,0:T(8,128)(2,1)S(1)}, bf16[224,384]{1,0:T(8,128)(2,1)S(1)}, u32[]{:S(2)}, u32[]{:S(2)}) collective-permute-start(bf16[224,384]{1,0:T(8,128)(2,1)S(1)} %get-tuple-element.49), channel_id=1, source_target_pairs={{0,2},{2,4},{4,6},{6,0},{1,3},{3,5},{5,7},{7,1},{8,10},{10,12},{12... | collective-permute-start | bytes 516104 | tf_op jit(solution)/shard_map/ppermute | solution.py:588
  17.7 7.1 %collective-permute-start.1 = (bf16[224,384]{1,0:T(8,128)(2,1)S(1)}, bf16[224,384]{1,0:T(8,128)(2,1)S(1)}, u32[]{:S(2)}, u32[]{:S(2)}) collective-permute-start(bf16[224,384]{1,0:T(8,128)(2,1)S(1)} %get-tuple-element.49), channel_id=1, source_target_pairs={{0,6},{2,0},{4,2},{6,4},{1,7},{3,1},{5,3},{7,5},{8,14},{10,8},{12,... | collective-permute-start | bytes 516104 | tf_op jit(solution)/shard_map/ppermute | solution.py:588
  22.7 6.9 %collective-permute-start.2 = (bf16[224,384]{1,0:T(8,128)(2,1)S(1)}, bf16[224,384]{1,0:T(8,128)(2,1)S(1)}, u32[]{:S(2)}, u32[]{:S(2)}) collective-permute-start(bf16[224,384]{1,0:T(8,128)(2,1)S(1)} %get-tuple-element.49), channel_id=1, source_target_pairs={{0,4},{2,6},{4,0},{6,2},{1,5},{3,7},{5,1},{7,3},{8,12},{10,14},{12... | collective-permute-start | bytes 516104 | tf_op jit(solution)/shard_map/ppermute | solution.py:588
  30.4 18.1 %collective-permute-start.8 = (bf16[4,256,384]{2,1,0:T(8,128)(2,1)S(1)}, bf16[4,256,384]{2,1,0:T(8,128)(2,1)S(1)}, u32[]{:S(2)}, u32[]{:S(2)}) collective-permute-start(bf16[4,256,384]{2,1,0:T(8,128)(2,1)S(1)} %pad_maximum_fusion.gb0), channel_id=1, source_target_pairs={{0,2},{2,4},{4,6},{6,0},{1,3},{3,5},{5,7},{7,1},{8,10},{10,12},{12... | collective-permute-start | bytes 2359304 | tf_op jit(solution)/shard_map/ppermute | solution.py:588
  30.8 17.8 %collective-permute-start.9 = (bf16[4,256,384]{2,1,0:T(8,128)(2,1)S(1)}, bf16[4,256,384]{2,1,0:T(8,128)(2,1)S(1)}, u32[]{:S(2)}, u32[]{:S(2)}) collective-permute-start(bf16[4,256,384]{2,1,0:T(8,128)(2,1)S(1)} %pad_maximum_fusion.gb0), channel_id=1, source_target_pairs={{0,6},{2,0},{4,2},{6,4},{1,7},{3,1},{5,3},{7,5},{8,14},{10,8},{12,... | collective-permute-start | bytes 2359304 | tf_op jit(solution)/shard_map/ppermute | solution.py:588
  33.7 14.9 %collective-permute-start.6 = (bf16[4,224,384]{2,1,0:T(8,128)(2,1)S(1)}, bf16[4,224,384]{2,1,0:T(8,128)(2,1)}, u32[]{:S(2)}, u32[]{:S(2)}) collective-permute-start(bf16[4,224,384]{2,1,0:T(8,128)(2,1)S(1)} %pad_maximum_fusion.1.ga0), channel_id=1, source_target_pairs={{0,8},{8,16},{16,24},{24,0},{1,9},{9,17},{17,25},{25,1},{2,10},{10... | collective-permute-start | bytes 2064392 | tf_op jit(solution)/shard_map/ppermute | solution.py:588
  34.7 13.9 %collective-permute-start.7 = (bf16[4,224,384]{2,1,0:T(8,128)(2,1)S(1)}, bf16[4,224,384]{2,1,0:T(8,128)(2,1)}, u32[]{:S(2)}, u32[]{:S(2)}) collective-permute-start(bf16[4,224,384]{2,1,0:T(8,128)(2,1)S(1)} %pad_maximum_fusion.1.ga0), channel_id=1, source_target_pairs={{0,24},{8,0},{16,8},{24,16},{1,25},{9,1},{17,9},{25,17},{2,26},{10... | collective-permute-start | bytes 2064392 | tf_op jit(solution)/shard_map/ppermute | solution.py:588
  50.0 0.7 copy-start.2
  50.8 0.7 copy-start.3
  51.5 0.7 copy-start.4
  52.2 14.6 %collective-permute-start.14 = (bf16[4,192,1280]{2,1,0:T(8,128)(2,1)}, bf16[4,192,1280]{2,1,0:T(8,128)(2,1)S(1)}, u32[]{:S(2)}, u32[]{:S(2)}) collective-permute-start(bf16[4,192,1280]{2,1,0:T(8,128)(2,1)} %bitcast.89), channel_id=1, source_target_pairs={{0,1},{1,0},{2,3},{3,2},{4,5},{5,4},{6,7},{7,6},{8,9},{9,8},{10,11... | collective-permute-start | bytes 5898248 | tf_op jit(solution)/shard_map/ppermute | solution.py:584
  52.3 14.6 %collective-permute-start.12 = (bf16[2,256,384]{2,1,0:T(8,128)(2,1)}, bf16[2,256,384]{2,1,0:T(8,128)(2,1)S(1)}, u32[]{:S(2)}, u32[]{:S(2)}) collective-permute-start(bf16[2,256,384]{2,1,0:T(8,128)(2,1)} %copy-done.2), channel_id=1, source_target_pairs={{0,2},{2,4},{4,6},{6,0},{1,3},{3,5},{5,7},{7,1},{8,10},{10,12},{12... | collective-permute-start | bytes 1179656 | tf_op jit(solution)/shard_map/ppermute | solution.py:588
  52.3 14.6 %collective-permute-start.13 = (bf16[2,256,384]{2,1,0:T(8,128)(2,1)S(1)}, bf16[2,256,384]{2,1,0:T(8,128)(2,1)S(1)}, u32[]{:S(2)}, u32[]{:S(2)}) collective-permute-start(bf16[2,256,384]{2,1,0:T(8,128)(2,1)S(1)} %get-tuple-element.76), channel_id=1, source_target_pairs={{0,6},{2,0},{4,2},{6,4},{1,7},{3,1},{5,3},{7,5},{8,14},{10,8},{12,... | collective-permute-start | bytes 1179656 | tf_op jit(solution)/shard_map/ppermute | solution.py:588
  55.5 11.3 %collective-permute-start.10 = (bf16[2,224,384]{2,1,0:T(8,128)(2,1)}, bf16[2,224,384]{2,1,0:T(8,128)(2,1)S(1)}, u32[]{:S(2)}, u32[]{:S(2)}) collective-permute-start(bf16[2,224,384]{2,1,0:T(8,128)(2,1)} %copy-done.4), channel_id=1, source_target_pairs={{0,8},{8,16},{16,24},{24,0},{1,9},{9,17},{17,25},{25,1},{2,10},{10... | collective-permute-start | bytes 1032200 | tf_op jit(solution)/shard_map/ppermute | solution.py:588
  56.4 10.4 %collective-permute-start.11 = (bf16[2,224,384]{2,1,0:T(8,128)(2,1)}, bf16[2,224,384]{2,1,0:T(8,128)(2,1)S(1)}, u32[]{:S(2)}, u32[]{:S(2)}) collective-permute-start(bf16[2,224,384]{2,1,0:T(8,128)(2,1)} %copy-done.3), channel_id=1, source_target_pairs={{0,24},{8,0},{16,8},{24,16},{1,25},{9,1},{17,9},{25,17},{2,26},{10... | collective-permute-start | bytes 1032200 | tf_op jit(solution)/shard_map/ppermute | solution.py:588
  74.1 25.1 %copy-start = (bf16[256,1792]{1,0:T(8,128)(2,1)S(1)}, bf16[256,1792]{1,0:T(8,128)(2,1)}, u32[]{:S(2)}) copy-start(bf16[256,1792]{1,0:T(8,128)(2,1)} %text_hbm.1) | copy-start | bytes 2752516
  74.1 25.1 %all-to-all-start = ((bf16[64,8,896]{2,1,0:T(8,128)(2,1)}), bf16[64,8,896]{2,1,0:T(8,128)(2,1)S(1)}, u32[]{:S(2)}, u32[]{:S(2)}) async-start(bf16[64,8,896]{2,1,0:T(8,128)(2,1)} %bitcast.28), calls=%async_computation | async-start | bytes 1835008 | tf_op jit(solution)/shard_map/all_to_all | solution.py:696
  82.6 17.6 %copy-start.1 = (s32[1,256]{1,0:T(1,128)S(1)}, s32[1,256]{1,0:T(1,128)}, u32[]{:S(2)}) copy-start(s32[1,256]{1,0:T(1,128)} %seg_row_ref.1) | copy-start | bytes 3076
  100.1 2.7 %collective-permute-start.15 = (bf16[256,1792]{1,0:T(8,128)(2,1)S(1)}, bf16[256,1792]{1,0:T(8,128)(2,1)S(1)}, u32[]{:S(2)}, u32[]{:S(2)}) collective-permute-start(bf16[256,1792]{1,0:T(8,128)(2,1)S(1)} %shard_map.125.own_ref.rows_ref), channel_id=1, source_target_pairs={{0,1},{1,0},{2,3},{3,2},{4,5},{5,4},{6,7},{7,6},{8,9},{9,8},{10,11... | collective-permute-start | bytes 2752520 | tf_op jit(solution)/shard_map/ppermute | solution.py:584
  114.0 3.0 %collective-permute-start.16 = (bf16[256,1920]{1,0:T(8,128)(2,1)}, bf16[256,1920]{1,0:T(8,128)(2,1)S(1)}, u32[]{:S(2)}, u32[]{:S(2)}) collective-permute-start(bf16[256,1920]{1,0:T(8,128)(2,1)} %get-tuple-element.88), channel_id=1, source_target_pairs={{0,1},{1,0},{2,3},{3,2},{4,5},{5,4},{6,7},{7,6},{8,9},{9,8},{10,11... | collective-permute-start | bytes 2949128 | tf_op jit(solution)/shard_map/ppermute | solution.py:584
  119.1 22.7 %all-to-all-start.1 = ((bf16[64,8,896]{2,1,0:T(8,128)(2,1)}), bf16[64,8,896]{2,1,0:T(8,128)(2,1)S(1)}, u32[]{:S(2)}, u32[]{:S(2)}) async-start(bf16[64,8,896]{2,1,0:T(8,128)(2,1)} %bitcast.30), calls=%async_computation.1 | async-start | bytes 1835008 | tf_op jit(solution)/shard_map/all_to_all | solution.py:710
Sparse Core Ops, SparseCore 0:
  19.5 28.5 all-gather.2

commit v11 on v9

--- a/solution.py
+++ b/solution.py
@@ -659,13 +659,13 @@
     seg_row = segment_ids
     seg_col = segment_ids.reshape(length, 1)
     own = lax.all_gather(packed, "enc", axis=0, tiled=False)
+    (
+        near_a, near_b, own, cells, by_line, filled, spots, own_cell, gain, seg_col, a_at, b_at
+    ) = lax.optimization_barrier(
+        (near_a, near_b, own, cells, by_line, filled, spots, own_cell, gain, seg_col, a_at, b_at)
+    )
     pass_a = [near_a[0][:2], near_a[1][2:]]
     pass_b = [near_b[0][:2], near_b[1][2:]]
-    (
-        near_a, near_b, pass_a, pass_b, own, cells, by_line, filled, spots, own_cell, gain, seg_col, a_at, b_at
-    ) = lax.optimization_barrier(
-        (near_a, near_b, pass_a, pass_b, own, cells, by_line, filled, spots, own_cell, gain, seg_col, a_at, b_at)
-    )
     far_a = [shift(pass_a[0], "z", 1), shift(pass_a[1], "z", 3)]
     far_b = [shift(pass_b[0], "y", 1), shift(pass_b[1], "y", 3)]
     shards_a = [stack_a] + near_a + far_a

time: 150 us -> 148 us (0.987)
  local copies, waits for them, and re-layouts: 7.72 us -> 5.51 us
  transfers between devices with their start and end apart: 20 -> 20, of which waited for: 7 -> 8; matrix products, arithmetic and copies ran while one was open for 7% -> 5% of each run, Pallas kernels for 2% -> 2%
where the time goes in v11:
time: 148 us
  waiting for transfers between devices  58.7 us (40%)
  starting transfers between devices  39 us (26%)
  Pallas kernels  27.9 us (19%)
  between operations  14.4 us (10%)
  local copies, waits for them, and re-layouts  5.51 us (4%)
  other arithmetic  2.33 us (2%)
    ppermute x14, starting transfers between devices, shift(): return lax.ppermute(x, axis, [(i, (i + k) % 4) for i in range(4)])  24.5 us
    ppermute x14, waiting for transfers between devices, shift(): return lax.ppermute(x, axis, [(i, (i + k) % 4) for i in range(4)])  22.8 us
    all_to_all x1, waiting for transfers between devices, local(): lax.all_to_all(out8.reshape(senders, 2 * cap, half), SPREAD, split_axis=0...  17.7 us
    all_to_all x1, waiting for transfers between devices, local(): lax.all_to_all(outgoing.reshape(senders, 8, slab // 2), SPREAD, split_axi...  15.9 us
    pallas_call x1, Pallas kernels, attend(): pl.pallas_call(attend_kernel, out_shape=(jax.ShapeDtypeStruct((rows, slab...  11.2 us
    all_to_all x1, starting transfers between devices, local(): lax.all_to_all(outgoing.reshape(senders, 8, slab // 2), SPREAD, split_axi...  8.89 us
    pallas_call x1, Pallas kernels, encode(): pl.pallas_call(encode_kernel, out_shape=jax.ShapeDtypeStruct((n_cells, 89...  7.26 us
    all_to_all x1, starting transfers between devices, local(): lax.all_to_all(out8.reshape(senders, 2 * cap, half), SPREAD, split_axis=0...  4.82 us
  transfers between devices with their start and end apart: 20, of which 8 were waited for; matrix products, arithmetic and copies ran while one was open for 5% of the time, Pallas kernels for 2%

profile of v11, /device:TPU:0, one launch (start us, length us, event | category | flops | bytes accessed | tf_op | source)
XLA Modules:
  0.0 147.9 jit_solution(6762278338340555104)
XLA Ops:
  7.3 2.7 %shard_map.122 = (bf16[224,384]{1,0:T(8,128)(2,1)S(1)}, bf16[256,384]{1,0:T(8,128)(2,1)S(1)}, bf16[192,1280]{1,0:T(8,128)(2,1)}) custom-call(s32[2]{0:T(128)S(1)} %pad_add_fusion.1.place_ref, bf16[80,1792]{1,0:T(8,128)(2,1)} %audio_w_ref.1, bf16[80,4,1792]{2,1,0:T(4,128)(2,1)} %vision_w_ref.1, bf16[128,1280]{1,0:T(8,128)(2,1)} %audio_ref.1, ...), custom_call_target="tpu_custom_call" | custom-call | bytes 1800000 | tf_op jit(solution)/shard_map/pallas_call | solution.py:291
  10.0 2.1 %collective-permute-start.3 = (bf16[256,384]{1,0:T(8,128)(2,1)S(1)}, bf16[256,384]{1,0:T(8,128)(2,1)S(1)}, u32[]{:S(2)}, u32[]{:S(2)}) collective-permute-start(bf16[256,384]{1,0:T(8,128)(2,1)S(1)} %get-tuple-element.45), channel_id=1, source_target_pairs={{0,8},{8,16},{16,24},{24,0},{1,9},{9,17},{17,25},{25,1},{2,10},{10... | collective-permute-start | bytes 589832 | tf_op jit(solution)/shard_map/ppermute | solution.py:567
  12.1 2.2 %collective-permute-start.4 = (bf16[256,384]{1,0:T(8,128)(2,1)S(1)}, bf16[256,384]{1,0:T(8,128)(2,1)S(1)}, u32[]{:S(2)}, u32[]{:S(2)}) collective-permute-start(bf16[256,384]{1,0:T(8,128)(2,1)S(1)} %get-tuple-element.45), channel_id=1, source_target_pairs={{0,24},{8,0},{16,8},{24,16},{1,25},{9,1},{17,9},{25,17},{2,26},{10... | collective-permute-start | bytes 589832 | tf_op jit(solution)/shard_map/ppermute | solution.py:567
  14.3 1.8 %collective-permute-start.5 = (bf16[256,384]{1,0:T(8,128)(2,1)S(1)}, bf16[256,384]{1,0:T(8,128)(2,1)S(1)}, u32[]{:S(2)}, u32[]{:S(2)}) collective-permute-start(bf16[256,384]{1,0:T(8,128)(2,1)S(1)} %get-tuple-element.45), channel_id=1, source_target_pairs={{0,16},{8,24},{16,0},{24,8},{1,17},{9,25},{17,1},{25,9},{2,18},{10... | collective-permute-start | bytes 589832 | tf_op jit(solution)/shard_map/ppermute | solution.py:567
  16.1 1.6 %collective-permute-start = (bf16[224,384]{1,0:T(8,128)(2,1)S(1)}, bf16[224,384]{1,0:T(8,128)(2,1)S(1)}, u32[]{:S(2)}, u32[]{:S(2)}) collective-permute-start(bf16[224,384]{1,0:T(8,128)(2,1)S(1)} %get-tuple-element.41), channel_id=1, source_target_pairs={{0,2},{2,4},{4,6},{6,0},{1,3},{3,5},{5,7},{7,1},{8,10},{10,12},{12... | collective-permute-start | bytes 516104 | tf_op jit(solution)/shard_map/ppermute | solution.py:567
  17.7 1.7 %collective-permute-start.1 = (bf16[224,384]{1,0:T(8,128)(2,1)S(1)}, bf16[224,384]{1,0:T(8,128)(2,1)S(1)}, u32[]{:S(2)}, u32[]{:S(2)}) collective-permute-start(bf16[224,384]{1,0:T(8,128)(2,1)S(1)} %get-tuple-element.41), channel_id=1, source_target_pairs={{0,6},{2,0},{4,2},{6,4},{1,7},{3,1},{5,3},{7,5},{8,14},{10,8},{12,... | collective-permute-start | bytes 516104 | tf_op jit(solution)/shard_map/ppermute | solution.py:567
  19.5 0.1 add.155.a_at_ref
  19.6 0.1 add.159.b_at_ref
  19.8 3.0 %collective-permute-done = bf16[224,384]{1,0:T(8,128)(2,1)S(1)} collective-permute-done((bf16[224,384]{1,0:T(8,128)(2,1)S(1)}, bf16[224,384]{1,0:T(8,128)(2,1)S(1)}, u32[]{:S(2)}, u32[]{:S(2)}) %collective-permute-start) | collective-permute-done | bytes 172064 | tf_op jit(solution)/shard_map/ppermute | solution.py:567
  22.7 2.0 %collective-permute-start.2 = (bf16[224,384]{1,0:T(8,128)(2,1)S(1)}, bf16[224,384]{1,0:T(8,128)(2,1)S(1)}, u32[]{:S(2)}, u32[]{:S(2)}) collective-permute-start(bf16[224,384]{1,0:T(8,128)(2,1)S(1)} %get-tuple-element.41), channel_id=1, source_target_pairs={{0,4},{2,6},{4,0},{6,2},{1,5},{3,7},{5,1},{7,3},{8,12},{10,14},{12... | collective-permute-start | bytes 516104 | tf_op jit(solution)/shard_map/ppermute | solution.py:567
  24.7 4.9 %collective-permute-done.2 = bf16[224,384]{1,0:T(8,128)(2,1)S(1)} collective-permute-done((bf16[224,384]{1,0:T(8,128)(2,1)S(1)}, bf16[224,384]{1,0:T(8,128)(2,1)S(1)}, u32[]{:S(2)}, u32[]{:S(2)}) %collective-permute-start.2) | collective-permute-done | bytes 172064 | tf_op jit(solution)/shard_map/ppermute | solution.py:567
  29.6 0.1 pad_maximum_fusion.gb0
  29.8 0.1 pad_maximum_fusion.1.ga0
  30.0 0.4 convert_reduce_fusion
  30.4 0.4 collective-permute-start.8
  30.8 2.9 %collective-permute-start.9 = (bf16[4,256,384]{2,1,0:T(8,128)(2,1)S(1)}, bf16[4,256,384]{2,1,0:T(8,128)(2,1)S(1)}, u32[]{:S(2)}, u32[]{:S(2)}) collective-permute-start(bf16[4,256,384]{2,1,0:T(8,128)(2,1)S(1)} %pad_maximum_fusion.gb0), channel_id=1, source_target_pairs={{0,6},{2,0},{4,2},{6,4},{1,7},{3,1},{5,3},{7,5},{8,14},{10,8},{12,... | collective-permute-start | bytes 2359304 | tf_op jit(solution)/shard_map/ppermute | solution.py:567
  33.7 1.0 collective-permute-start.6
  34.7 2.2 %collective-permute-start.7 = (bf16[4,224,384]{2,1,0:T(8,128)(2,1)S(1)}, bf16[4,224,384]{2,1,0:T(8,128)(2,1)}, u32[]{:S(2)}, u32[]{:S(2)}) collective-permute-start(bf16[4,224,384]{2,1,0:T(8,128)(2,1)S(1)} %pad_maximum_fusion.1.ga0), channel_id=1, source_target_pairs={{0,24},{8,0},{16,8},{24,16},{1,25},{9,1},{17,9},{25,17},{2,26},{10... | collective-permute-start | bytes 2064392 | tf_op jit(solution)/shard_map/ppermute | solution.py:567
  37.0 0.6 reduce-window.6
  37.6 0.2 slice_reduce_fusion
  38.0 0.2 select_reduce_fusion
  38.1 0.1 copy.64
  38.3 0.1 stack_reshape.6
  38.5 0.1 stack_reshape.7
  38.6 0.1 reshape.306
  38.7 0.6 gather_fusion
  39.3 0.1 reshape.307
  39.3 0.1 reshape.308
  39.4 0.6 gather_fusion.1
  40.0 0.1 reshape.309
  40.1 0.1 sub.66
  40.2 0.1 copy.56
  40.3 0.1 copy.55
  40.4 0.1 reshape.312.e_row_ref
  40.6 0.1 sub.67
  40.7 0.1 convert_reduce_fusion.1
  40.8 0.2 convert_reduce_fusion.2
  41.0 7.5 %collective-permute-done.6.ga1 = bf16[4,224,384]{2,1,0:T(8,128)(2,1)} collective-permute-done((bf16[4,224,384]{2,1,0:T(8,128)(2,1)S(1)}, bf16[4,224,384]{2,1,0:T(8,128)(2,1)}, u32[]{:S(2)}, u32[]{:S(2)}) %collective-permute-start.6) | collective-permute-done | bytes 688160 | tf_op jit(solution)/shard_map/ppermute | solution.py:567
  48.6 0.1 collective-permute-start.14
  48.7 1.0 collective-permute-start.12
  49.8 2.4 %collective-permute-start.13 = (bf16[2,256,384]{2,1,0:T(8,128)(2,1)S(1)}, bf16[2,256,384]{2,1,0:T(8,128)(2,1)S(1)}, u32[]{:S(2)}, u32[]{:S(2)}) collective-permute-start(bf16[2,256,384]{2,1,0:T(8,128)(2,1)S(1)} %slice.35), channel_id=1, source_target_pairs={{0,6},{2,0},{4,2},{6,4},{1,7},{3,1},{5,3},{7,5},{8,14},{10,8},{12,... | collective-permute-start | bytes 1179656 | tf_op jit(solution)/shard_map/ppermute | solution.py:567
  52.2 1.0 slice.32
  53.2 1.1 collective-permute-start.10
  54.2 1.0 slice.33
  55.2 2.3 %collective-permute-start.11 = (bf16[2,224,384]{2,1,0:T(8,128)(2,1)S(1)}, bf16[2,224,384]{2,1,0:T(8,128)(2,1)S(1)}, u32[]{:S(2)}, u32[]{:S(2)}) collective-permute-start(bf16[2,224,384]{2,1,0:T(8,128)(2,1)S(1)} %slice.33), channel_id=1, source_target_pairs={{0,24},{8,0},{16,8},{24,16},{1,25},{9,1},{17,9},{25,17},{2,26},{10... | collective-permute-start | bytes 1032200 | tf_op jit(solution)/shard_map/ppermute | solution.py:567
  57.6 6.8 %collective-permute-done.10.ga3 = bf16[2,224,384]{2,1,0:T(8,128)(2,1)S(1)} collective-permute-done((bf16[2,224,384]{2,1,0:T(8,128)(2,1)S(1)}, bf16[2,224,384]{2,1,0:T(8,128)(2,1)S(1)}, u32[]{:S(2)}, u32[]{:S(2)}) %collective-permute-start.10) | collective-permute-done | bytes 344096 | tf_op jit(solution)/shard_map/ppermute | solution.py:567
  64.4 0.6 collective-permute-done.11.ga4
  65.0 7.3 %shard_map.123 = bf16[512,896]{1,0:T(8,128)(2,1)} custom-call(s32[16]{0:T(128)S(1)} %add.155.a_at_ref, s32[16]{0:T(128)S(1)} %add.159.b_at_ref, bf16[4,224,384]{2,1,0:T(8,128)(2,1)S(1)} %pad_maximum_fusion.1.ga0, bf16[4,224,384]{2,1,0:T(8,128)(2,1)} %collective-permute-done.6.ga1, bf16[4,224,384]{2,1,0:T(8,128)(2,1)} %collective-permute-done.7.ga2, ...), custom_call_target="tpu_custom_call" | custom-call | flops 3000000000 | bytes 11000000 | tf_op jit(solution)/shard_map/pallas_call | solution.py:415
  72.2 8.9 %all-to-all-start = ((bf16[64,8,896]{2,1,0:T(8,128)(2,1)}), bf16[64,8,896]{2,1,0:T(8,128)(2,1)S(1)}, u32[]{:S(2)}, u32[]{:S(2)}) async-start(bf16[64,8,896]{2,1,0:T(8,128)(2,1)} %bitcast.28), calls=%async_computation | async-start | bytes 1835008 | tf_op jit(solution)/shard_map/all_to_all | solution.py:675
  81.1 0.1 copy.59.filled_ref
  81.3 15.9 %all-to-all-done = bf16[64,8,896]{2,1,0:T(8,128)(2,1)S(1)} async-done(((bf16[64,8,896]{2,1,0:T(8,128)(2,1)}), bf16[64,8,896]{2,1,0:T(8,128)(2,1)S(1)}, u32[]{:S(2)}, u32[]{:S(2)}) %all-to-all-start) | async-done | bytes 917536 | tf_op jit(solution)/shard_map/all_to_all | solution.py:675
  97.1 0.9 shard_map.124.own_ref.rows_ref
  98.0 0.1 collective-permute-start.15
  98.1 0.1 copy.60.seg_col_ref
  98.3 2.4 %shard_map.125 = (bf16[3584,640]{1,0:T(8,128)(2,1)S(1)}, bf16[256,896]{1,0:T(8,128)(2,1)S(1)}) custom-call(bf16[3584,1152]{1,0:T(8,128)(2,1)} %weight_hbm.1, bf16[256,896]{1,0:T(8,128)(2,1)} %upstream_hbm), custom_call_target="tpu_custom_call" | custom-call | bytes 10000000 | tf_op jit(solution)/shard_map/pallas_call | solution.py:43
  100.7 11.2 %shard_map.126 = (bf16[256,1920]{1,0:T(8,128)(2,1)}, bf16[256,1792]{1,0:T(8,128)(2,1)S(1)}, f32[256,1]{1,0:T(8,128)S(1)}, f32[256,1]{1,0:T(8,128)S(1)}) custom-call(s32[1]{0:T(128)} %bitcast.1.half_ref, bf16[256,1792]{1,0:T(8,128)(2,1)S(1)} %shard_map.124.own_ref.rows_ref, bf16[256,1792]{1,0:T(8,128)(2,1)S(1)} %collective-permute-done.15.other_ref, ...), custom_call_target="tpu_custom_call" | custom-call | flops 5000000000 | bytes 14000000 | tf_op jit(solution)/shard_map/pallas_call | solution.py:165
  111.9 0.6 collective-permute-start.16
  112.4 0.1 copy.61.spot_ref
  112.6 2.3 %collective-permute-done.16.taken_ref = bf16[256,1920]{1,0:T(8,128)(2,1)S(1)} collective-permute-done((bf16[256,1920]{1,0:T(8,128)(2,1)}, bf16[256,1920]{1,0:T(8,128)(2,1)S(1)}, u32[]{:S(2)}, u32[]{:S(2)}) %collective-permute-start.16) | collective-permute-done | bytes 983072 | tf_op jit(solution)/shard_map/ppermute | solution.py:563
  114.8 2.1 %shard_map.127 = bf16[512,896]{1,0:T(8,128)(2,1)} custom-call(s32[1]{0:T(128)} %bitcast.1.half_ref, bf16[256,1792]{1,0:T(8,128)(2,1)S(1)} %shard_map.124.own_ref.rows_ref, bf16[256,1792]{1,0:T(8,128)(2,1)S(1)} %get-tuple-element.71.keep_ref, bf16[256,1920]{1,0:T(8,128)(2,1)S(1)} %collective-permute-done.16.taken_ref, ...), custom_call_target="tpu_custom_call" | custom-call | flops 500000000 | bytes 4000000 | tf_op jit(solution)/shard_map/pallas_call | solution.py:520
  116.9 4.8 %all-to-all-start.1 = ((bf16[64,8,896]{2,1,0:T(8,128)(2,1)}), bf16[64,8,896]{2,1,0:T(8,128)(2,1)S(1)}, u32[]{:S(2)}, u32[]{:S(2)}) async-start(bf16[64,8,896]{2,1,0:T(8,128)(2,1)} %bitcast.30), calls=%async_computation.1 | async-start | bytes 1835008 | tf_op jit(solution)/shard_map/all_to_all | solution.py:689
  121.7 0.1 copy.62.cell_ref
  121.8 17.7 %all-to-all-done.1 = bf16[64,8,896]{2,1,0:T(8,128)(2,1)S(1)} async-done(((bf16[64,8,896]{2,1,0:T(8,128)(2,1)}), bf16[64,8,896]{2,1,0:T(8,128)(2,1)S(1)}, u32[]{:S(2)}, u32[]{:S(2)}) %all-to-all-start.1) | async-done | bytes 917536 | tf_op jit(solution)/shard_map/all_to_all | solution.py:689
  139.6 1.5 shard_map.128
  (59 shorter events, 1.0 us)
Async XLA Ops:
  7.2 12.2 %copy-start.4 = (s32[4]{0:T(128)S(1)}, s32[4]{0:T(128)}, u32[]{:S(2)}) copy-start(s32[4]{0:T(128)} %constant.148) | copy-start | bytes 52
  7.2 12.5 %copy-start.3 = (f32[3584]{0:T(1024)S(1)}, f32[3584]{0:T(1024)}, u32[]{:S(2)}) copy-start(f32[3584]{0:T(1024)} %param.18) | copy-start | bytes 43012
  7.2 41.4 %all-gather.3.cloned.1.call-start = ((), (), s32[]{:S(2)}) async-start(), calls=%async_computation.2 | async-start | bytes 2457600 | tf_op jit(solution)/shard_map/all_gather | solution.py:661
  10.0 19.9 %copy-start.2 = (s32[64,192]{1,0:T(8,128)S(1)}, s32[64,192]{1,0:T(8,128)}, u32[]{:S(2)}) copy-start(s32[64,192]{1,0:T(8,128)} %param.16) | copy-start | bytes 147460
  10.0 19.6 %collective-permute-start.3 = (bf16[256,384]{1,0:T(8,128)(2,1)S(1)}, bf16[256,384]{1,0:T(8,128)(2,1)S(1)}, u32[]{:S(2)}, u32[]{:S(2)}) collective-permute-start(bf16[256,384]{1,0:T(8,128)(2,1)S(1)} %get-tuple-element.45), channel_id=1, source_target_pairs={{0,8},{8,16},{16,24},{24,0},{1,9},{9,17},{17,25},{25,1},{2,10},{10... | collective-permute-start | bytes 589832 | tf_op jit(solution)/shard_map/ppermute | solution.py:567
  12.1 17.5 %collective-permute-start.4 = (bf16[256,384]{1,0:T(8,128)(2,1)S(1)}, bf16[256,384]{1,0:T(8,128)(2,1)S(1)}, u32[]{:S(2)}, u32[]{:S(2)}) collective-permute-start(bf16[256,384]{1,0:T(8,128)(2,1)S(1)} %get-tuple-element.45), channel_id=1, source_target_pairs={{0,24},{8,0},{16,8},{24,16},{1,25},{9,1},{17,9},{25,17},{2,26},{10... | collective-permute-start | bytes 589832 | tf_op jit(solution)/shard_map/ppermute | solution.py:567
  14.3 15.3 %collective-permute-start.5 = (bf16[256,384]{1,0:T(8,128)(2,1)S(1)}, bf16[256,384]{1,0:T(8,128)(2,1)S(1)}, u32[]{:S(2)}, u32[]{:S(2)}) collective-permute-start(bf16[256,384]{1,0:T(8,128)(2,1)S(1)} %get-tuple-element.45), channel_id=1, source_target_pairs={{0,16},{8,24},{16,0},{24,8},{1,17},{9,25},{17,1},{25,9},{2,18},{10... | collective-permute-start | bytes 589832 | tf_op jit(solution)/shard_map/ppermute | solution.py:567
  16.1 6.6 %collective-permute-start = (bf16[224,384]{1,0:T(8,128)(2,1)S(1)}, bf16[224,384]{1,0:T(8,128)(2,1)S(1)}, u32[]{:S(2)}, u32[]{:S(2)}) collective-permute-start(bf16[224,384]{1,0:T(8,128)(2,1)S(1)} %get-tuple-element.41), channel_id=1, source_target_pairs={{0,2},{2,4},{4,6},{6,0},{1,3},{3,5},{5,7},{7,1},{8,10},{10,12},{12... | collective-permute-start | bytes 516104 | tf_op jit(solution)/shard_map/ppermute | solution.py:567
  17.7 7.1 %collective-permute-start.1 = (bf16[224,384]{1,0:T(8,128)(2,1)S(1)}, bf16[224,384]{1,0:T(8,128)(2,1)S(1)}, u32[]{:S(2)}, u32[]{:S(2)}) collective-permute-start(bf16[224,384]{1,0:T(8,128)(2,1)S(1)} %get-tuple-element.41), channel_id=1, source_target_pairs={{0,6},{2,0},{4,2},{6,4},{1,7},{3,1},{5,3},{7,5},{8,14},{10,8},{12,... | collective-permute-start | bytes 516104 | tf_op jit(solution)/shard_map/ppermute | solution.py:567
  22.7 6.9 %collective-permute-start.2 = (bf16[224,384]{1,0:T(8,128)(2,1)S(1)}, bf16[224,384]{1,0:T(8,128)(2,1)S(1)}, u32[]{:S(2)}, u32[]{:S(2)}) collective-permute-start(bf16[224,384]{1,0:T(8,128)(2,1)S(1)} %get-tuple-element.41), channel_id=1, source_target_pairs={{0,4},{2,6},{4,0},{6,2},{1,5},{3,7},{5,1},{7,3},{8,12},{10,14},{12... | collective-permute-start | bytes 516104 | tf_op jit(solution)/shard_map/ppermute | solution.py:567
  30.4 18.1 %collective-permute-start.8 = (bf16[4,256,384]{2,1,0:T(8,128)(2,1)S(1)}, bf16[4,256,384]{2,1,0:T(8,128)(2,1)S(1)}, u32[]{:S(2)}, u32[]{:S(2)}) collective-permute-start(bf16[4,256,384]{2,1,0:T(8,128)(2,1)S(1)} %pad_maximum_fusion.gb0), channel_id=1, source_target_pairs={{0,2},{2,4},{4,6},{6,0},{1,3},{3,5},{5,7},{7,1},{8,10},{10,12},{12... | collective-permute-start | bytes 2359304 | tf_op jit(solution)/shard_map/ppermute | solution.py:567
  30.8 17.8 %collective-permute-start.9 = (bf16[4,256,384]{2,1,0:T(8,128)(2,1)S(1)}, bf16[4,256,384]{2,1,0:T(8,128)(2,1)S(1)}, u32[]{:S(2)}, u32[]{:S(2)}) collective-permute-start(bf16[4,256,384]{2,1,0:T(8,128)(2,1)S(1)} %pad_maximum_fusion.gb0), channel_id=1, source_target_pairs={{0,6},{2,0},{4,2},{6,4},{1,7},{3,1},{5,3},{7,5},{8,14},{10,8},{12,... | collective-permute-start | bytes 2359304 | tf_op jit(solution)/shard_map/ppermute | solution.py:567
  33.7 14.9 %collective-permute-start.6 = (bf16[4,224,384]{2,1,0:T(8,128)(2,1)S(1)}, bf16[4,224,384]{2,1,0:T(8,128)(2,1)}, u32[]{:S(2)}, u32[]{:S(2)}) collective-permute-start(bf16[4,224,384]{2,1,0:T(8,128)(2,1)S(1)} %pad_maximum_fusion.1.ga0), channel_id=1, source_target_pairs={{0,8},{8,16},{16,24},{24,0},{1,9},{9,17},{17,25},{25,1},{2,10},{10... | collective-permute-start | bytes 2064392 | tf_op jit(solution)/shard_map/ppermute | solution.py:567
  34.7 13.9 %collective-permute-start.7 = (bf16[4,224,384]{2,1,0:T(8,128)(2,1)S(1)}, bf16[4,224,384]{2,1,0:T(8,128)(2,1)}, u32[]{:S(2)}, u32[]{:S(2)}) collective-permute-start(bf16[4,224,384]{2,1,0:T(8,128)(2,1)S(1)} %pad_maximum_fusion.1.ga0), channel_id=1, source_target_pairs={{0,24},{8,0},{16,8},{24,16},{1,25},{9,1},{17,9},{25,17},{2,26},{10... | collective-permute-start | bytes 2064392 | tf_op jit(solution)/shard_map/ppermute | solution.py:567
  48.6 16.4 %collective-permute-start.14 = (bf16[4,192,1280]{2,1,0:T(8,128)(2,1)}, bf16[4,192,1280]{2,1,0:T(8,128)(2,1)S(1)}, u32[]{:S(2)}, u32[]{:S(2)}) collective-permute-start(bf16[4,192,1280]{2,1,0:T(8,128)(2,1)} %bitcast.89), channel_id=1, source_target_pairs={{0,1},{1,0},{2,3},{3,2},{4,5},{5,4},{6,7},{7,6},{8,9},{9,8},{10,11... | collective-permute-start | bytes 5898248 | tf_op jit(solution)/shard_map/ppermute | solution.py:563
  48.7 16.2 %collective-permute-start.12 = (bf16[2,256,384]{2,1,0:T(8,128)(2,1)S(1)}, bf16[2,256,384]{2,1,0:T(8,128)(2,1)S(1)}, u32[]{:S(2)}, u32[]{:S(2)}) collective-permute-start(bf16[2,256,384]{2,1,0:T(8,128)(2,1)S(1)} %slice.34), channel_id=1, source_target_pairs={{0,2},{2,4},{4,6},{6,0},{1,3},{3,5},{5,7},{7,1},{8,10},{10,12},{12... | collective-permute-start | bytes 1179656 | tf_op jit(solution)/shard_map/ppermute | solution.py:567
  49.8 15.2 %collective-permute-start.13 = (bf16[2,256,384]{2,1,0:T(8,128)(2,1)S(1)}, bf16[2,256,384]{2,1,0:T(8,128)(2,1)S(1)}, u32[]{:S(2)}, u32[]{:S(2)}) collective-permute-start(bf16[2,256,384]{2,1,0:T(8,128)(2,1)S(1)} %slice.35), channel_id=1, source_target_pairs={{0,6},{2,0},{4,2},{6,4},{1,7},{3,1},{5,3},{7,5},{8,14},{10,8},{12,... | collective-permute-start | bytes 1179656 | tf_op jit(solution)/shard_map/ppermute | solution.py:567
  53.2 11.2 %collective-permute-start.10 = (bf16[2,224,384]{2,1,0:T(8,128)(2,1)S(1)}, bf16[2,224,384]{2,1,0:T(8,128)(2,1)S(1)}, u32[]{:S(2)}, u32[]{:S(2)}) collective-permute-start(bf16[2,224,384]{2,1,0:T(8,128)(2,1)S(1)} %slice.32), channel_id=1, source_target_pairs={{0,8},{8,16},{16,24},{24,0},{1,9},{9,17},{17,25},{25,1},{2,10},{10... | collective-permute-start | bytes 1032200 | tf_op jit(solution)/shard_map/ppermute | solution.py:567
  55.2 9.7 %collective-permute-start.11 = (bf16[2,224,384]{2,1,0:T(8,128)(2,1)S(1)}, bf16[2,224,384]{2,1,0:T(8,128)(2,1)S(1)}, u32[]{:S(2)}, u32[]{:S(2)}) collective-permute-start(bf16[2,224,384]{2,1,0:T(8,128)(2,1)S(1)} %slice.33), channel_id=1, source_target_pairs={{0,24},{8,0},{16,8},{24,16},{1,25},{9,1},{17,9},{25,17},{2,26},{10... | collective-permute-start | bytes 1032200 | tf_op jit(solution)/shard_map/ppermute | solution.py:567
  72.2 24.9 %copy-start = (bf16[256,1792]{1,0:T(8,128)(2,1)S(1)}, bf16[256,1792]{1,0:T(8,128)(2,1)}, u32[]{:S(2)}) copy-start(bf16[256,1792]{1,0:T(8,128)(2,1)} %text_hbm.1) | copy-start | bytes 2752516
  72.2 24.9 %all-to-all-start = ((bf16[64,8,896]{2,1,0:T(8,128)(2,1)}), bf16[64,8,896]{2,1,0:T(8,128)(2,1)S(1)}, u32[]{:S(2)}, u32[]{:S(2)}) async-start(bf16[64,8,896]{2,1,0:T(8,128)(2,1)} %bitcast.28), calls=%async_computation | async-start | bytes 1835008 | tf_op jit(solution)/shard_map/all_to_all | solution.py:675
  81.1 17.0 %copy-start.1 = (s32[1,256]{1,0:T(1,128)S(1)}, s32[1,256]{1,0:T(1,128)}, u32[]{:S(2)}) copy-start(s32[1,256]{1,0:T(1,128)} %seg_row_ref.1) | copy-start | bytes 3076
  98.0 2.7 %collective-permute-start.15 = (bf16[256,1792]{1,0:T(8,128)(2,1)S(1)}, bf16[256,1792]{1,0:T(8,128)(2,1)S(1)}, u32[]{:S(2)}, u32[]{:S(2)}) collective-permute-start(bf16[256,1792]{1,0:T(8,128)(2,1)S(1)} %shard_map.124.own_ref.rows_ref), channel_id=1, source_target_pairs={{0,1},{1,0},{2,3},{3,2},{4,5},{5,4},{6,7},{7,6},{8,9},{9,8},{10,11... | collective-permute-start | bytes 2752520 | tf_op jit(solution)/shard_map/ppermute | solution.py:563
  111.9 3.0 %collective-permute-start.16 = (bf16[256,1920]{1,0:T(8,128)(2,1)}, bf16[256,1920]{1,0:T(8,128)(2,1)S(1)}, u32[]{:S(2)}, u32[]{:S(2)}) collective-permute-start(bf16[256,1920]{1,0:T(8,128)(2,1)} %get-tuple-element.72), channel_id=1, source_target_pairs={{0,1},{1,0},{2,3},{3,2},{4,5},{5,4},{6,7},{7,6},{8,9},{9,8},{10,11... | collective-permute-start | bytes 2949128 | tf_op jit(solution)/shard_map/ppermute | solution.py:563
  116.9 22.7 %all-to-all-start.1 = ((bf16[64,8,896]{2,1,0:T(8,128)(2,1)}), bf16[64,8,896]{2,1,0:T(8,128)(2,1)S(1)}, u32[]{:S(2)}, u32[]{:S(2)}) async-start(bf16[64,8,896]{2,1,0:T(8,128)(2,1)} %bitcast.30), calls=%async_computation.1 | async-start | bytes 1835008 | tf_op jit(solution)/shard_map/all_to_all | solution.py:689
Sparse Core Ops, SparseCore 0:
  19.5 28.5 all-gather.2
